TPU v7x, 32 devices: a whole 2x2x4 slice. The times are simulated.
32 devices in a mesh: seg: 8 (over z, y), head: 4 (over x, core).
Axes of the slice: x: 2, y: 2, z: 4, core: 2. Of those that a mesh axis runs over, the one named last changes fastest.
Arguments:
- queries: bfloat16 [2048, 2048], P('seg', 'head'), may hold values from -20 to 20
- keys: bfloat16 [2048, 2048], P('seg', 'head'), may hold values from -12 to 12
- values: bfloat16 [2048, 2048], P('seg', 'head'), may hold values from -6 to 6
- out_grad: bfloat16 [2048, 2048], P('seg', 'head'), may hold values from -2.5 to 2.5
- out_weight: bfloat16 [2048, 2048], P('head'), may hold values from -1 to 1
- retr_owner: int32 [8, 4], replicated, may hold values from 0 to 7, as said below
- retr_block: int32 [8, 4], replicated, may hold values from -1 to 1, as said below
Outputs:
- layer_out: bfloat16 [2048, 2048], P('seg', 'head')
- query_grad: bfloat16 [2048, 2048], P('seg', 'head')
- key_grad: bfloat16 [2048, 2048], P('seg', 'head')
- value_grad: bfloat16 [2048, 2048], P('seg', 'head')
- proj_grad_t: float32 [2048, 2048], P('seg', 'head')
Inputs may be any that keep to these rules, and one draw needn't show every extreme that they name: `retr_owner`: row s lists 4 owners, all different from one another and from s. `retr_block`: padding (-1) comes after the live entries of a row; every row has at least 3 live entries.
All inputs are finite; a program needn't handle non-finite values.
Results may differ from a plain program's by a relative error of at most 0.012.
Values may be sent and summed in bfloat16 or wider, within the bound.
No kernel may reach another device: no remote copies, remote signals or barrier semaphores. Data moves between devices by JAX's collectives and lax.ppermute only.
A program may use at most 128 MiB of HBM per device.

v0:
```python
import math

import jax
import jax.numpy as jnp
from jax import lax
from jax.sharding import PartitionSpec as P

DH = 128
BLOCK = 128


def shifted(block, axis, distance):
    devices = range(lax.axis_size(axis))
    route = [(i - distance, i) for i in devices if i - distance in devices]
    return lax.ppermute(block, axis, route)


def split_heads(tok_rows, count):
    return tok_rows.reshape(tok_rows.shape[0], count, -1).transpose(1, 0, 2)


def join_heads(stacked):
    return stacked.transpose(1, 0, 2).reshape(stacked.shape[1], -1)


def product(form, left_side, right_side):
    return jnp.einsum(form, left_side, right_side, preferred_element_type=jnp.float32)


def attend(packed, mem_live, has_cache, score_scale):
    queries, keys, values, cache_k, cache_v, mem_k, mem_v, d_attn = packed
    length = queries.shape[1]
    causal = jnp.arange(length)[:, None] >= jnp.arange(length)[None, :]
    own = jnp.where(causal[None], product("hqd,hkd->hqk", queries, keys) * score_scale, -jnp.inf)
    cached = jnp.where(has_cache, product("hqd,hkd->hqk", queries, cache_k) * score_scale, -jnp.inf)
    stored = jnp.where(
        mem_live[None, None, :], product("hqd,hkd->hqk", queries, mem_k) * score_scale, -jnp.inf
    )
    row_top = jnp.maximum(jnp.maximum(jnp.max(own, -1), jnp.max(cached, -1)), jnp.max(stored, -1))[
        ..., None
    ]
    row_total = (
        jnp.sum(jnp.exp(own - row_top), -1)
        + jnp.sum(jnp.exp(cached - row_top), -1)
        + jnp.sum(jnp.exp(stored - row_top), -1)
    )
    log_total = row_top + jnp.log(row_total)[..., None]
    weights = [jnp.exp(group_scores - log_total) for group_scores in (own, cached, stored)]
    rounded = [entry.astype(jnp.bfloat16) for entry in weights]
    sources = (values, cache_v, mem_v)
    mixed_sum = (
        product("hqk,hkd->hqd", rounded[0], sources[0])
        + product("hqk,hkd->hqd", rounded[1], sources[1])
        + product("hqk,hkd->hqd", rounded[2], sources[2])
    )
    attn = mixed_sum.astype(jnp.bfloat16)
    row_delta = jnp.sum(d_attn.astype(jnp.float32) * attn.astype(jnp.float32), -1)[..., None]
    slopes = [
        (entry * (product("hqd,hkd->hqk", d_attn, source) - row_delta)).astype(jnp.bfloat16)
        for entry, source in zip(weights, sources)
    ]
    grad_q = score_scale * (
        product("hqk,hkd->hqd", slopes[0], keys)
        + product("hqk,hkd->hqd", slopes[1], cache_k)
        + product("hqk,hkd->hqd", slopes[2], mem_k)
    )
    grad_k = score_scale * product("hqk,hqd->hkd", slopes[0], queries)
    grad_v = product("hqk,hqd->hkd", rounded[0], d_attn)
    grad_k_cache = score_scale * product("hqk,hqd->hkd", slopes[1], queries)
    grad_v_cache = product("hqk,hqd->hkd", rounded[1], d_attn)
    return (
        attn,
        grad_q,
        grad_k,
        grad_v,
        grad_k_cache,
        grad_v_cache,
        log_total[..., 0],
        row_delta[..., 0],
    )


def per_device(queries, keys, values, out_grad, out_weight, retr_owner, retr_block):
    my_index = lax.axis_index("seg")
    tok_count = queries.shape[0]
    full_width = queries.shape[1]
    head_dev = full_width // DH
    per_group = 2
    group_count = head_dev // per_group
    score_scale = 1.0 / math.sqrt(DH)
    cache_k, cache_v = shifted((keys, values), "seg", 1)
    matches = (retr_owner == my_index) & (retr_block >= 0)
    wanted = jnp.sum(jnp.where(matches, retr_block, 0), axis=1)
    served = jnp.any(matches, axis=1)[:, None, None]
    key_blocks = keys.reshape(tok_count // BLOCK, BLOCK, full_width)
    value_blocks = values.reshape(tok_count // BLOCK, BLOCK, full_width)
    zero_fill = jnp.zeros((), keys.dtype)
    send_k = jnp.where(served, key_blocks[wanted], zero_fill)
    send_v = jnp.where(served, value_blocks[wanted], zero_fill)
    recv_k, recv_v = (
        lax.all_to_all(send_k, "seg", split_axis=0, concat_axis=0, tiled=True),
        lax.all_to_all(send_v, "seg", split_axis=0, concat_axis=0, tiled=True),
    )
    my_owner = lax.dynamic_index_in_dim(retr_owner, my_index, 0, False)
    my_block = lax.dynamic_index_in_dim(retr_block, my_index, 0, False)
    mem_k = recv_k[my_owner].reshape(-1, full_width)
    mem_v = recv_v[my_owner].reshape(-1, full_width)
    mem_live = jnp.repeat(my_block >= 0, BLOCK)
    full_grad = lax.all_gather(out_grad, "head", axis=1, tiled=True)
    d_attn = lax.dot_general(
        full_grad, out_weight, (((1,), (1,)), ((), ())), preferred_element_type=jnp.float32
    ).astype(jnp.bfloat16)

    def grouped(tok_rows):
        stacked = split_heads(tok_rows, head_dev)
        return stacked.reshape(group_count, per_group, stacked.shape[1], stacked.shape[2])

    packed = tuple(
        (
            grouped(entry)
            for entry in (queries, keys, values, cache_k, cache_v, mem_k, mem_v, d_attn)
        )
    )
    results = lax.map(
        lambda group_args: attend(group_args, mem_live, my_index > 0, score_scale), packed
    )

    def ungrouped(stacked):
        return join_heads(stacked.reshape(head_dev, stacked.shape[2], stacked.shape[3]))

    attn_rows = ungrouped(results[0])
    grad_q = ungrouped(results[1])
    grad_k = ungrouped(results[2])
    grad_v = ungrouped(results[3])
    partial_out = jnp.dot(attn_rows, out_weight, preferred_element_type=jnp.float32)
    layer_out = lax.psum_scatter(
        partial_out.astype(jnp.bfloat16), "head", scatter_dimension=1, tiled=True
    )
    proj_grad_t = lax.psum_scatter(
        lax.dot_general(
            full_grad, attn_rows, (((0,), (0,)), ((), ())), preferred_element_type=jnp.float32
        ),
        "seg",
        scatter_dimension=0,
        tiled=True,
    )
    carried_k, carried_v = (
        shifted(ungrouped(results[4]).astype(jnp.bfloat16), "seg", -1).astype(jnp.float32),
        shifted(ungrouped(results[5]).astype(jnp.bfloat16), "seg", -1).astype(jnp.float32),
    )
    query_grad = grad_q.astype(jnp.bfloat16)
    key_grad = (grad_k + carried_k).astype(jnp.bfloat16)
    value_grad = (grad_v + carried_v).astype(jnp.bfloat16)
    return (layer_out, query_grad, key_grad, value_grad, proj_grad_t)


def solution(mesh):
    in_specs = (
        P("seg", "head"),
        P("seg", "head"),
        P("seg", "head"),
        P("seg", "head"),
        P("head", None),
        P(),
        P(),
    )
    out_specs = (
        P("seg", "head"),
        P("seg", "head"),
        P("seg", "head"),
        P("seg", "head"),
        P("seg", "head"),
    )
    return jax.shard_map(
        per_device, mesh=mesh, in_specs=in_specs, out_specs=out_specs, check_vma=False
    )
```

profile of v0, /device:TPU:0, one launch (start us, length us, event | category | flops | bytes accessed | tf_op | source)
XLA Modules:
  0.0 271.7 jit_solution(10845235894447655318)
XLA Ops:
  8.8 2.5 gather_fusion.2
  11.3 1.6 gather_fusion
  12.9 3.1 %broadcast_select_fusion = (bf16[8,128,512]{2,1,0:T(8,128)(2,1)}, bf16[8,128,512]{2,1,0:T(8,128)(2,1)}) fusion(bf16[8,128,512]{2,1,0:T(8,128)(2,1)} %gather_fusion.2, pred[8]{0:T(512)(128)(4,1)S(1)} %get-tuple-element.309, bf16[8,128,512]{2,1,0:T(8,128)(2,1)} %gather_fusion), kind=kLoop, calls=%fused_computation.120 | loop fusion | flops 1048576 | bytes 4194312 | tf_op jit(solution)/shard_map/jit(_where)/select_n | solution.py:99
  16.0 7.4 %all-to-all-start.1 = ((bf16[8,128,512]{2,1,0:T(8,128)(2,1)}), bf16[8,128,512]{2,1,0:T(8,128)(2,1)}, u32[]{:S(2)}, u32[]{:S(2)}) async-start(bf16[8,128,512]{2,1,0:T(8,128)(2,1)} %get-tuple-element.319), calls=%async_computation.1 | async-start | bytes 2097152 | tf_op jit(solution)/shard_map/all_to_all | solution.py:102
  24.2 25.1 %all-to-all-done.1 = bf16[8,128,512]{2,1,0:T(8,128)(2,1)} async-done(((bf16[8,128,512]{2,1,0:T(8,128)(2,1)}), bf16[8,128,512]{2,1,0:T(8,128)(2,1)}, u32[]{:S(2)}, u32[]{:S(2)}) %all-to-all-start.1) | async-done | bytes 1048608 | tf_op jit(solution)/shard_map/all_to_all | solution.py:102
  49.3 4.2 %all-to-all-start = ((bf16[8,128,512]{2,1,0:T(8,128)(2,1)}), bf16[8,128,512]{2,1,0:T(8,128)(2,1)}, u32[]{:S(2)}, u32[]{:S(2)}) async-start(bf16[8,128,512]{2,1,0:T(8,128)(2,1)} %get-tuple-element.320), calls=%async_computation | async-start | bytes 2097152 | tf_op jit(solution)/shard_map/all_to_all | solution.py:101
  53.6 3.8 %collective-permute-start = (bf16[256,512]{1,0:T(8,128)(2,1)S(1)}, bf16[256,512]{1,0:T(8,128)(2,1)S(1)}, u32[]{:S(2)}, u32[]{:S(2)}) collective-permute-start(bf16[256,512]{1,0:T(8,128)(2,1)S(1)} %copy-done.8), channel_id=1, source_target_pairs={{0,4},{4,8},{8,12},{12,16},{16,20},{20,24},{24,28},{1,5},{5,9},{9,... | collective-permute-start | bytes 786440 | tf_op jit(solution)/shard_map/ppermute | solution.py:15
  57.4 3.4 %collective-permute-start.1 = (bf16[256,512]{1,0:T(8,128)(2,1)S(1)}, bf16[256,512]{1,0:T(8,128)(2,1)S(1)}, u32[]{:S(2)}, u32[]{:S(2)}) collective-permute-start(bf16[256,512]{1,0:T(8,128)(2,1)S(1)} %copy-done.7), channel_id=1, source_target_pairs={{0,4},{4,8},{8,12},{12,16},{16,20},{20,24},{24,28},{1,5},{5,9},{9,... | collective-permute-start | bytes 786440 | tf_op jit(solution)/shard_map/ppermute | solution.py:15
  63.5 10.9 %collective-permute-done.1 = bf16[256,512]{1,0:T(8,128)(2,1)S(1)} collective-permute-done((bf16[256,512]{1,0:T(8,128)(2,1)S(1)}, bf16[256,512]{1,0:T(8,128)(2,1)S(1)}, u32[]{:S(2)}, u32[]{:S(2)}) %collective-permute-start.1) | collective-permute-done | bytes 262176 | tf_op jit(solution)/shard_map/ppermute | solution.py:15
  76.0 2.0 convolution_convert_fusion.1
  78.2 1.8 gather_fusion.3
  81.3 1.8 gather_fusion.1
  84.1 36.6 %while.23 = (s32[]{:T(128)}, bf16[2,2,256,128]{2,3,1,0:T(8,128)(2,1)}, bf16[2,2,256,128]{3,2,1,0:T(8,128)(2,1)}, f32[2,2,256,128]{3,2,1,0:T(8,128)}, f32[2,2,256...) while((s32[]{:T(128)}, ...), condition=%wide.region_10.11_spmd.clone, body=%wide.region_2.10_spmd.clone.sunk | while | flops 678231040 | bytes 32709092 | solution.py:124
  85.3 1.3 fusion.178
  87.9 1.3 fusion.177
  94.4 1.9 convolution_add_fusion.3
  96.3 2.3 fusion.185
  98.6 1.8 fusion.188
  100.5 1.9 fusion.186
  106.2 1.3 fusion.177
  112.7 1.9 convolution_add_fusion.3
  114.6 2.3 fusion.185
  116.9 1.8 fusion.188
  118.7 1.9 fusion.186
  120.7 4.0 %convolution_bitcast_fusion.2 = f32[2048,512]{0,1:T(8,128)} fusion(bf16[256,512]{0,1:T(8,128)(2,1)} %bitcast.269, bf16[256,2048]{1,0:T(8,128)(2,1)} %all-gather.2.cloned.1.call-done), kind=kOutput, calls=%fused_computation.117 | convolution fusion | flops 536870912 | bytes 5505024 | tf_op jit(solution)/shard_map/dot_general | solution.py:140
  125.6 1.7 convolution_convert_fusion
  127.6 1.4 collective-permute-start.2
  133.2 14.1 %collective-permute-done.2 = bf16[256,512]{1,0:T(8,128)(2,1)S(1)} collective-permute-done((bf16[256,512]{1,0:T(8,128)(2,1)S(1)}, bf16[256,512]{1,0:T(8,128)(2,1)S(1)}, u32[]{:S(2)}, u32[]{:S(2)}) %collective-permute-start.2) | collective-permute-done | bytes 262176 | tf_op jit(solution)/shard_map/ppermute | solution.py:15
  148.0 7.4 %collective-permute-done.3 = bf16[256,512]{1,0:T(8,128)(2,1)S(1)} collective-permute-done((bf16[256,512]{1,0:T(8,128)(2,1)S(1)}, bf16[256,512]{1,0:T(8,128)(2,1)S(1)}, u32[]{:S(2)}, u32[]{:S(2)}) %collective-permute-start.3) | collective-permute-done | bytes 262176 | tf_op jit(solution)/shard_map/ppermute | solution.py:15
  156.2 81.0 %reduce-scatter.5.cloned.1.call-done = f32[256,512]{0,1:T(8,128)} async-done(((f32[2048,512]{0,1:T(8,128)}), f32[256,512]{0,1:T(8,128)}) %reduce-scatter.5.cloned.1.call-update) | async-done | bytes 524304 | tf_op jit(solution)/shard_map/reduce_scatter | solution.py:139
  237.2 2.0 copy.62
  239.2 25.9 %reduce-scatter.3.cloned.1.call-done = bf16[256,512]{1,0:T(8,128)(2,1)} async-done(((bf16[256,2048]{1,0:T(8,128)(2,1)}), bf16[256,512]{1,0:T(8,128)(2,1)}) %reduce-scatter.3.cloned.1.call-update) | async-done | bytes 262160 | tf_op jit(solution)/shard_map/reduce_scatter | solution.py:136
  (141 shorter events, 32.3 us)
Async XLA Ops:
  7.2 68.9 %copy-start = (bf16[512,2048]{1,0:T(8,128)(2,1)S(1)}, bf16[512,2048]{1,0:T(8,128)(2,1)}, u32[]{:S(2)}) copy-start(bf16[512,2048]{1,0:T(8,128)(2,1)} %param.13) | copy-start | bytes 6291460
  7.2 4.1 %copy-start.8 = (bf16[256,512]{1,0:T(8,128)(2,1)S(1)}, bf16[256,512]{1,0:T(8,128)(2,1)}, u32[]{:S(2)}) copy-start(bf16[256,512]{1,0:T(8,128)(2,1)} %param.10) | copy-start | bytes 786436
  16.0 41.4 %copy-start.7 = (bf16[256,512]{1,0:T(8,128)(2,1)S(1)}, bf16[256,512]{1,0:T(8,128)(2,1)}, u32[]{:S(2)}) copy-start(bf16[256,512]{1,0:T(8,128)(2,1)} %param.11) | copy-start | bytes 786436
  16.0 44.7 %copy-start.20 = (s32[8,4]{0,1:T(4,128)S(1)}, s32[8,4]{0,1:T(4,128)}, u32[]{:S(2)}) copy-start(s32[8,4]{0,1:T(4,128)} %param.14) | copy-start | bytes 388
  16.0 33.3 %all-to-all-start.1 = ((bf16[8,128,512]{2,1,0:T(8,128)(2,1)}), bf16[8,128,512]{2,1,0:T(8,128)(2,1)}, u32[]{:S(2)}, u32[]{:S(2)}) async-start(bf16[8,128,512]{2,1,0:T(8,128)(2,1)} %get-tuple-element.319), calls=%async_computation.1 | async-start | bytes 2097152 | tf_op jit(solution)/shard_map/all_to_all | solution.py:102
  23.4 39.1 %copy-start.19 = (s32[8,4]{0,1:T(4,128)S(1)}, s32[8,4]{0,1:T(4,128)}, u32[]{:S(2)}) copy-start(s32[8,4]{0,1:T(4,128)} %param.15) | copy-start | bytes 388
  23.4 39.3 %copy-start.16 = (bf16[256,512]{1,0:T(8,128)(2,1)S(1)}, bf16[256,512]{1,0:T(8,128)(2,1)}, u32[]{:S(2)}) copy-start(bf16[256,512]{1,0:T(8,128)(2,1)} %param.9) | copy-start | bytes 786436
  23.5 52.6 %all-gather.2.cloned.1.call-start = ((), (), s32[]{:S(2)}) async-start(), calls=%async_computation.4 | async-start | bytes 1310720 | tf_op jit(solution)/shard_map/all_gather | solution.py:109
  49.3 32.0 %all-to-all-start = ((bf16[8,128,512]{2,1,0:T(8,128)(2,1)}), bf16[8,128,512]{2,1,0:T(8,128)(2,1)}, u32[]{:S(2)}, u32[]{:S(2)}) async-start(bf16[8,128,512]{2,1,0:T(8,128)(2,1)} %get-tuple-element.320), calls=%async_computation | async-start | bytes 2097152 | tf_op jit(solution)/shard_map/all_to_all | solution.py:101
  53.6 183.6 %reduce-scatter.5.cloned.1.call-start = ((), (), s32[]{:S(2)}) async-start(), calls=%async_computation.6 | async-start | bytes 4718592 | tf_op jit(solution)/shard_map/reduce_scatter | solution.py:139
  53.6 21.7 %collective-permute-start = (bf16[256,512]{1,0:T(8,128)(2,1)S(1)}, bf16[256,512]{1,0:T(8,128)(2,1)S(1)}, u32[]{:S(2)}, u32[]{:S(2)}) collective-permute-start(bf16[256,512]{1,0:T(8,128)(2,1)S(1)} %copy-done.8), channel_id=1, source_target_pairs={{0,4},{4,8},{8,12},{12,16},{16,20},{20,24},{24,28},{1,5},{5,9},{9,... | collective-permute-start | bytes 786440 | tf_op jit(solution)/shard_map/ppermute | solution.py:15
  57.4 17.1 %collective-permute-start.1 = (bf16[256,512]{1,0:T(8,128)(2,1)S(1)}, bf16[256,512]{1,0:T(8,128)(2,1)S(1)}, u32[]{:S(2)}, u32[]{:S(2)}) collective-permute-start(bf16[256,512]{1,0:T(8,128)(2,1)S(1)} %copy-done.7), channel_id=1, source_target_pairs={{0,4},{4,8},{8,12},{12,16},{16,20},{20,24},{24,28},{1,5},{5,9},{9,... | collective-permute-start | bytes 786440 | tf_op jit(solution)/shard_map/ppermute | solution.py:15
  85.3 2.6 copy-start.1
  87.9 2.8 %copy-start.5 = (bf16[2,2,256,128]{2,3,1,0:T(8,128)(2,1)S(1)}, bf16[2,2,256,128]{2,3,1,0:T(8,128)(2,1)}, u32[]{:S(2)}) copy-start(bf16[2,2,256,128]{2,3,1,0:T(8,128)(2,1)} %get-tuple-element.492) | copy-start | bytes 786436 | tf_op jit(solution)/shard_map/while
  89.2 1.7 copy-start.4
  89.5 1.8 copy-start.6
  89.5 1.8 copy-start.9
  91.6 2.8 %copy-start.10 = (bf16[2,2,256,128]{2,3,1,0:T(8,128)(2,1)}, bf16[2,2,256,128]{2,3,1,0:T(8,128)(2,1)S(1)}, u32[]{:S(2)}) copy-start(bf16[2,2,256,128]{2,3,1,0:T(8,128)(2,1)S(1)} %get-tuple-element.481) | copy-start | bytes 786436 | tf_op jit(solution)/shard_map/while
  92.0 2.4 copy-start.2
  103.6 2.6 copy-start.1
  106.2 2.8 %copy-start.5 = (bf16[2,2,256,128]{2,3,1,0:T(8,128)(2,1)S(1)}, bf16[2,2,256,128]{2,3,1,0:T(8,128)(2,1)}, u32[]{:S(2)}) copy-start(bf16[2,2,256,128]{2,3,1,0:T(8,128)(2,1)} %get-tuple-element.492) | copy-start | bytes 786436 | tf_op jit(solution)/shard_map/while
  107.8 1.8 copy-start.6
  107.8 1.8 copy-start.9
  109.9 2.8 %copy-start.10 = (bf16[2,2,256,128]{2,3,1,0:T(8,128)(2,1)}, bf16[2,2,256,128]{2,3,1,0:T(8,128)(2,1)S(1)}, u32[]{:S(2)}) copy-start(bf16[2,2,256,128]{2,3,1,0:T(8,128)(2,1)S(1)} %get-tuple-element.481) | copy-start | bytes 786436 | tf_op jit(solution)/shard_map/while
  110.3 2.4 copy-start.2
  124.6 2.7 copy-start.17
  124.7 140.5 %reduce-scatter.3.cloned.1.call-start = ((), (), s32[]{:S(2)}) async-start(), calls=%async_computation.5 | async-start | bytes 1310720 | tf_op jit(solution)/shard_map/reduce_scatter | solution.py:136
  127.3 4.2 %copy-start.18 = (bf16[2,2,256,128]{3,2,1,0:T(8,128)(2,1)S(1)}, bf16[2,2,256,128]{3,2,1,0:T(8,128)(2,1)}, u32[]{:S(2)}) copy-start(bf16[2,2,256,128]{3,2,1,0:T(8,128)(2,1)} %get-tuple-element.204) | copy-start | bytes 786436
  127.3 5.2 %copy-start.15 = (f32[2,2,256,128]{3,2,1,0:T(8,128)S(1)}, f32[2,2,256,128]{3,2,1,0:T(8,128)}, u32[]{:S(2)}) copy-start(f32[2,2,256,128]{3,2,1,0:T(8,128)} %get-tuple-element.205) | copy-start | bytes 1572868
  127.3 5.5 %copy-start.14 = (f32[2,2,256,128]{3,2,1,0:T(8,128)S(1)}, f32[2,2,256,128]{3,2,1,0:T(8,128)}, u32[]{:S(2)}) copy-start(f32[2,2,256,128]{3,2,1,0:T(8,128)} %get-tuple-element.207) | copy-start | bytes 1572868
  127.6 19.7 %collective-permute-start.2 = (bf16[256,512]{1,0:T(8,128)(2,1)S(1)}, bf16[256,512]{1,0:T(8,128)(2,1)S(1)}, u32[]{:S(2)}, u32[]{:S(2)}) collective-permute-start(bf16[256,512]{1,0:T(8,128)(2,1)S(1)} %bitcast.280), channel_id=1, source_target_pairs={{4,0},{8,4},{12,8},{16,12},{20,16},{24,20},{28,24},{5,1},{9,5},{13... | collective-permute-start | bytes 786440 | tf_op jit(solution)/shard_map/ppermute | solution.py:15
  130.2 25.2 %collective-permute-start.3 = (bf16[256,512]{1,0:T(8,128)(2,1)S(1)}, bf16[256,512]{1,0:T(8,128)(2,1)S(1)}, u32[]{:S(2)}, u32[]{:S(2)}) collective-permute-start(bf16[256,512]{1,0:T(8,128)(2,1)S(1)} %bitcast.281), channel_id=1, source_target_pairs={{4,0},{8,4},{12,8},{16,12},{20,16},{24,20},{28,24},{5,1},{9,5},{13... | collective-permute-start | bytes 786440 | tf_op jit(solution)/shard_map/ppermute | solution.py:15
  (8 other events, 8.7 us)
Sparse Core Ops, SparseCore 0:
  25.9 18.1 all-gather.1
  124.8 112.3 reduce-scatter.4
  240.4 24.6 reduce-scatter.2
where the time goes:
time: 273 us; the launch traced here: 272 us
  waiting for transfers between devices  165 us (60%)
  matrix products  39 us (14%)
  local copies, waits for them, and re-layouts  23.9 us (9%)
  starting transfers between devices  21.6 us (8%)
  between operations  14 us (5%)
  other arithmetic  7.6 us (3%)
    reduce_scatter x1, waiting for transfers between devices, per_device(): lax.psum_scatter(lax.dot_general(full_grad, attn_rows, (((0,), (0,)), (()...  81 us
    ppermute x4, waiting for transfers between devices, shifted(): return lax.ppermute(block, axis, route)  32.4 us
    dot_general x30, matrix products, product(): jnp.einsum(form, left_side, right_side, preferred_element_type=jnp.float32)  31.4 us
    reduce_scatter x1, waiting for transfers between devices, per_device(): lax.psum_scatter(partial_out.astype(jnp.bfloat16), 'head', scatter_dimens...  25.9 us
    all_to_all x1, waiting for transfers between devices, per_device(): lax.all_to_all(send_v, 'seg', split_axis=0, concat_axis=0, tiled=True)  25.1 us
    ppermute x4, starting transfers between devices, shifted(): return lax.ppermute(block, axis, route)  9.85 us
    all_to_all x1, starting transfers between devices, per_device(): lax.all_to_all(send_v, 'seg', split_axis=0, concat_axis=0, tiled=True)  7.41 us
  transfers between devices with their start and end apart: 9, of which 6 were waited for; matrix products, arithmetic and copies ran while one was open for 7% of the time, Pallas kernels for 0%

commit v1 on v0

v1 whole, which is shorter than its diff:
```python
import functools
import math

import jax
import jax.numpy as jnp
from jax import lax
from jax.experimental import pallas as pl
from jax.experimental.pallas import tpu as pltpu
from jax.sharding import PartitionSpec as P

DH = 128
BLOCK = 128
F32 = jnp.float32
BF16 = jnp.bfloat16
HIDDEN = -1e30
VMEM = pl.BlockSpec(memory_space=pltpu.VMEM)
SMEM = pl.BlockSpec(memory_space=pltpu.SMEM)


def dot(left, right, dims):
    return lax.dot_general(left, right, ((dims[:1], dims[1:]), ((), ())), preferred_element_type=F32)


def lanes(block, width):
    return pl.ds(pl.multiple_of(block * width, width), width)


def call(body, outs, operands, specs=None, scratch=(), flops=0):
    nbytes = sum(x.size * x.dtype.itemsize for x in (*operands, *outs))
    return pl.pallas_call(
        body,
        out_shape=outs,
        in_specs=specs or [VMEM] * len(operands),
        out_specs=[VMEM] * len(outs),
        scratch_shapes=list(scratch),
        compiler_params=pltpu.CompilerParams(vmem_limit_bytes=56 * 2**20),
        cost_estimate=pl.CostEstimate(flops=flops, bytes_accessed=nbytes, transcendentals=0),
    )(*operands)


def shape(dims, dtype):
    return jax.ShapeDtypeStruct(dims, dtype)


def cut_body(A, B, q_ref, k_ref, v_ref, *outs):
    a = lax.axis_index("seg") // B
    for m in range(A):
        head = lanes(a ^ m, DH)
        outs[m][:, :DH] = k_ref[:, head]
        outs[m][:, DH:] = v_ref[:, head]
        outs[A + m][...] = q_ref[:, head]


def slope_body(A, B, H, *refs):
    grads, weight_ref, outs = refs[:H], refs[H], refs[H + 1 : H + 1 + A]
    full, mixed = refs[H + 1 + A :]
    a = lax.axis_index("seg") // B
    h = lax.axis_index("head")
    width = grads[0].shape[1]
    for k in range(H):
        full[:, lanes(h ^ k, width)] = grads[k][...]
    mixed[...] = dot(full[...], weight_ref[...], (1, 1)).astype(BF16)
    for m in range(A):
        outs[m][:, :DH] = mixed[:, lanes(a ^ m, DH)]
        outs[m][:, DH:] = full[:, lanes((a ^ m) * H + h, width // H)]


def attend_body(A, B, R, score_scale, owner_ref, block_ref, *refs):
    pair = B == 2
    q_refs, dag_refs, refs = refs[:A], refs[A : 2 * A], refs[2 * A :]
    kv_refs, refs = (refs[: 2 * A], refs[2 * A :]) if pair else (refs[:1], refs[1:])
    attn_ref, dq_ref, own_ref, carry_ref, q_all, da_all, kv, kvcat = refs
    SEG = q_refs[0].shape[0]
    parts = SEG // BLOCK
    count = 2 * SEG + R * BLOCK
    seg = lax.axis_index("seg")
    a, b = seg // B, seg % B
    for m in range(A):
        q_all[m] = q_refs[m][...]
        da_all[m] = dag_refs[m][:, :DH]
    if pair:
        for i in range(2 * A):
            for part in range(parts):
                kv[i * parts + part] = kv_refs[i][part * BLOCK : (part + 1) * BLOCK, :]
    else:
        kv = kv_refs[0]

    def place(other_a, other_b):
        slot = (other_b ^ b) * A + (other_a ^ a) if pair else other_b * A + (other_a ^ a)
        return slot * parts

    def segment(m):
        seg_a = a ^ m
        s = seg_a * B + b
        prev_b = jnp.where(b == 0, B - 1, b - 1)
        prev_a = jnp.where(b == 0, (seg_a + A - 1) % A, seg_a)
        column = lax.broadcasted_iota(jnp.int32, (1, count), 1)
        hidden = (column >= SEG) & (column < 2 * SEG) & (s == 0)
        for part in range(parts):
            at = part * BLOCK
            kvcat[at : at + BLOCK] = kv[place(seg_a, b) + part]
            kvcat[SEG + at : SEG + at + BLOCK] = kv[place(prev_a, prev_b) + part]
        for j in range(R):
            at = 2 * SEG + j * BLOCK
            owner, block = owner_ref[s, j], block_ref[s, j]
            kvcat[at : at + BLOCK] = kv[place(owner // B, owner % B) + jnp.maximum(block, 0)]
            hidden |= (column >= at) & (column < at + BLOCK) & (block < 0)
        bias = jnp.where(hidden, HIDDEN, 0.0)
        q, da = q_all[m], da_all[m]
        keys, values = kvcat[:, :DH], kvcat[:, DH:]
        scores = dot(q, keys, (1, 1)) * score_scale + bias
        row = lax.broadcasted_iota(jnp.int32, (SEG, SEG), 0)
        col = lax.broadcasted_iota(jnp.int32, (SEG, SEG), 1)
        scores = jnp.concatenate([jnp.where(row >= col, scores[:, :SEG], HIDDEN), scores[:, SEG:]], 1)
        top = jnp.max(scores, -1, keepdims=True)
        grown = jnp.exp(scores - top)
        weights = grown * (1.0 / jnp.sum(grown, -1, keepdims=True))
        rounded = weights.astype(BF16)
        attn = dot(rounded, values, (1, 0)).astype(BF16)
        attn_ref[m] = attn
        row_delta = jnp.sum(da.astype(F32) * attn.astype(F32), -1, keepdims=True)
        slopes = (weights * (dot(da, values, (1, 1)) - row_delta)).astype(BF16)
        dq_ref[m] = (score_scale * dot(slopes, keys, (1, 0))).astype(BF16)
        dk = score_scale * dot(slopes[:, : 2 * SEG], q, (0, 0))
        dv = dot(rounded[:, : 2 * SEG], da, (0, 0))
        own_ref[m, :, :DH] = dk[:SEG]
        own_ref[m, :, DH:] = dv[:SEG]
        slot = prev_a ^ a
        carry_ref[slot, :, :DH] = dk[SEG:].astype(BF16)
        carry_ref[slot, :, DH:] = dv[SEG:].astype(BF16)

    if pair:
        for m in range(A):
            segment(m)
    else:
        lax.fori_loop(0, A, lambda m, _: segment(m), None)


def project_body(A, B, H, *refs):
    attns, gs, weight_ref, refs = refs[:A], refs[A : A + H], refs[A + H], refs[A + H + 1 :]
    keep_ref, send_ref, *proj_refs = refs[:-3]
    own, mixed, cots = refs[-3:]
    seg = lax.axis_index("seg")
    a, b = seg // B, seg % B
    h = lax.axis_index("head")
    SEG = attns[0].shape[1]
    for m in range(A):
        head = lanes(a ^ m, DH)
        own[:, head] = attns[m][m]
        for i in range(A):
            mixed[(m ^ i) * SEG : (m ^ i) * SEG + SEG, head] = attns[m][i]
    width = keep_ref.shape[1] // (H // 2)
    for k in range(0, H, 2):
        at = k // 2 * width
        keep_ref[:, at : at + width] = dot(own[...], weight_ref[:, lanes(h ^ k, width)], (1, 0))
        send_ref[:, at : at + width] = dot(own[...], weight_ref[:, lanes(h ^ (k + 1), width)], (1, 0)).astype(BF16)
    piece = gs[0].shape[2]
    for k in range(H):
        for m in range(A):
            cots[m * SEG : (m + 1) * SEG, lanes(h ^ k, piece)] = gs[k][m]
    if B == 2:
        rows = piece * H // 2
        proj_refs[0][...] = dot(cots[:, lanes(b, rows)], mixed[...], (0, 0))
        proj_refs[1][...] = dot(cots[:, lanes(1 - b, rows)], mixed[...], (0, 0)).astype(BF16)
    else:
        proj_refs[0][...] = dot(cots[...], mixed[...], (0, 0))


def merge_body(A, dq_ref, own_ref, carry_ref, *outs):
    for m in range(A):
        outs[m][:, :DH] = dq_ref[m]
        outs[m][:, DH:] = (own_ref[m] + carry_ref[m].astype(F32)).astype(BF16)


def place_body(A, B, *refs):
    pieces, outs = refs[:A], refs[A:]
    a = lax.axis_index("seg") // B
    for m in range(A):
        for i in range(3):
            outs[i][:, lanes(a ^ m, DH)] = pieces[m][:, i * DH : (i + 1) * DH]


def per_device(queries, keys, values, out_grad, out_weight, retr_owner, retr_block):
    n, H = lax.axis_size("seg"), lax.axis_size("head")
    SEG, width = queries.shape
    A = width // DH
    B = n // A
    R = retr_owner.shape[1]
    D = out_weight.shape[1]
    score_scale = 1.0 / math.sqrt(DH)

    def over_a(x, m):
        return lax.ppermute(x, "seg", [(i, (i // B ^ m) * B + i % B) for i in range(n)])

    def back_b(x):
        return lax.ppermute(x, "seg", [(i, i // B * B + (i % B - 1) % B) for i in range(n)])

    def over_head(x, k):
        return lax.ppermute(x, "head", [(i, i ^ k) for i in range(H)])

    def over_heads(x):
        parts = {0: x}
        for bit in (2, 1):
            parts |= {k | bit: over_head(parts[k], bit) for k in sorted(parts)}
        return [parts[k] for k in range(H)]

    grads = over_heads(out_grad)
    cut = call(
        functools.partial(cut_body, A, B),
        [shape((SEG, 2 * DH), BF16)] * A + [shape((SEG, DH), BF16)] * A,
        [queries, keys, values],
    )
    kvs = [cut[0]] + [over_a(cut[m], m) for m in range(1, A)]
    qs = [cut[A]] + [over_a(cut[A + m], m) for m in range(1, A)]
    if B == 2:
        kvs = kvs + [back_b(piece) for piece in kvs]
    else:
        groups = [[i * B + j for j in range(B)] for i in range(A)]
        gathered = lax.all_gather(jnp.stack(kvs), "seg", axis_index_groups=groups)
        kvs = [gathered.reshape(B * A * (SEG // BLOCK), BLOCK, 2 * DH)]
    dag = call(
        functools.partial(slope_body, A, B, H),
        [shape((SEG, 2 * DH), BF16)] * A,
        [*grads, out_weight],
        scratch=[pltpu.VMEM((SEG, D), BF16), pltpu.VMEM((SEG, width), BF16)],
        flops=2 * SEG * D * width,
    )
    dags = [dag[0]] + [over_a(dag[m], m) for m in range(1, A)]
    count = 2 * SEG + R * BLOCK
    attn, dq, own, carry = call(
        functools.partial(attend_body, A, B, R, score_scale),
        [
            shape((A, SEG, DH), BF16),
            shape((A, SEG, DH), BF16),
            shape((A, SEG, 2 * DH), F32),
            shape((A, SEG, 2 * DH), BF16),
        ],
        [retr_owner, retr_block, *qs, *dags, *kvs],
        specs=[SMEM] * 2 + [VMEM] * (2 * A + len(kvs)),
        scratch=[
            pltpu.VMEM((A, SEG, DH), BF16),
            pltpu.VMEM((A, SEG, DH), BF16),
            pltpu.VMEM((2 * A * (SEG // BLOCK), BLOCK, 2 * DH), BF16),
            pltpu.VMEM((count, 2 * DH), BF16),
        ],
        flops=10 * A * SEG * count * DH,
    )
    attns = [attn] + [over_a(attn, m) for m in range(1, A)]
    carried = back_b(carry)
    gs = over_heads(jnp.stack([piece[:, DH:] for piece in dags]))
    partials = [shape((SEG, D // 2), F32), shape((SEG, D // 2), BF16)]
    rows = D // A
    if B == 2:
        projs = [shape((rows // 2, width), F32), shape((rows // 2, width), BF16)]
    else:
        projs = [shape((rows, width), F32)]
    keep, send, *proj = call(
        functools.partial(project_body, A, B, H),
        partials + projs,
        [*attns, *gs, out_weight],
        scratch=[
            pltpu.VMEM((SEG, width), BF16),
            pltpu.VMEM((A * SEG, width), BF16),
            pltpu.VMEM((A * SEG, rows), BF16),
        ],
        flops=2 * SEG * width * D + 2 * A * SEG * rows * width,
    )
    block = D // H
    summed = keep + over_head(send, 1).astype(F32)
    layer_out = (summed[:, :block] + over_head(summed[:, block:].astype(BF16), 2).astype(F32)).astype(BF16)
    if B == 2:
        proj_grad_t = proj[0] + back_b(proj[1]).astype(F32)
    else:
        proj_grad_t = lax.psum_scatter(proj[0], "seg", scatter_dimension=0, axis_index_groups=groups, tiled=True)
    merged = call(
        functools.partial(merge_body, A), [shape((SEG, 3 * DH), BF16)] * A, [dq, own, carried]
    )
    placed = call(
        functools.partial(place_body, A, B),
        [shape((SEG, width), BF16)] * 3,
        [merged[0]] + [over_a(merged[m], m) for m in range(1, A)],
    )
    return (layer_out, *placed, proj_grad_t)


def solution(mesh):
    both = P("seg", "head")
    return jax.shard_map(
        per_device,
        mesh=mesh,
        in_specs=(both, both, both, both, P("head", None), P(), P()),
        out_specs=(both,) * 5,
        check_vma=False,
    )
```

time: 273 us -> 125 us (0.46)
  waiting for transfers between devices: 165 us -> 55.8 us
  matrix products: 39 us -> 0 us
  Pallas kernels: 0 us -> 22 us
  local copies, waits for them, and re-layouts: 23.9 us -> 7.09 us
  starting transfers between devices: 21.6 us -> 35.6 us
  between operations: 14 us -> 0.91 us
  other arithmetic: 7.6 us -> 1.86 us
    reduce_scatter x2 -> x0, waiting for transfers between devices: 107 us -> none  [the longest x1 81 us: per_device(): lax.psum_scatter(lax.dot_general(full_grad, attn_rows, (((0,), (0,)), (()...]
    dot_general x33 -> x0, matrix products: 39 us -> none  [the longest x30 31.4 us: product(): jnp.einsum(form, left_side, right_side, preferred_element_type=jnp.float32)]
    ppermute x4 -> x29, starting transfers between devices: 9.85 us -> 35.6 us  [the longest x15 22.4 us: over_a(): lax.ppermute(x, 'seg', [(i, (i // B ^ m) * B + i % B) for i in range(n)])]
    all_to_all x2 -> x0, waiting for transfers between devices: 25.1 us -> none  [the longest x1 25.1 us: per_device(): lax.all_to_all(send_v, 'seg', split_axis=0, concat_axis=0, tiled=True)]
    ppermute x4 -> x29, waiting for transfers between devices: 32.4 us -> 55.8 us  [the longest x15 44 us: over_a(): lax.ppermute(x, 'seg', [(i, (i // B ^ m) * B + i % B) for i in range(n)])]
    pallas_call x0 -> x6, Pallas kernels: none -> 22 us  [call(): pl.pallas_call(body, out_shape=outs, in_specs=specs or [VMEM] * len(opera...]
    all_to_all x2 -> x0, starting transfers between devices: 11.7 us -> none  [the longest x1 7.41 us: per_device(): lax.all_to_all(send_v, 'seg', split_axis=0, concat_axis=0, tiled=True)]
    gather x4 -> x0, local copies, waits for them, and re-layouts: 7.74 us -> none  [the longest x1 2.53 us: per_device(): send_v = jnp.where(served, value_blocks[wanted], zero_fill)]
  transfers between devices with their start and end apart: 9 -> 29, of which waited for: 6 -> 13; matrix products, arithmetic and copies ran while one was open for 7% -> 3% of each run, Pallas kernels for 0% -> 18%
where the time goes in v1:
time: 125 us; the launch traced here: 123 us
  waiting for transfers between devices  55.8 us (45%)
  starting transfers between devices  35.6 us (28%)
  Pallas kernels  22 us (18%)
  local copies, waits for them, and re-layouts  7.09 us (6%)
  other arithmetic  1.86 us (1%)
    ppermute x15, waiting for transfers between devices, over_a(): lax.ppermute(x, 'seg', [(i, (i // B ^ m) * B + i % B) for i in range(n)])  44 us
    ppermute x15, starting transfers between devices, over_a(): lax.ppermute(x, 'seg', [(i, (i // B ^ m) * B + i % B) for i in range(n)])  22.4 us
    pallas_call x6, Pallas kernels, call(): pl.pallas_call(body, out_shape=outs, in_specs=specs or [VMEM] * len(opera...  22 us
    ppermute x6, starting transfers between devices, back_b(): lax.ppermute(x, 'seg', [(i, i // B * B + (i % B - 1) % B) for i in range(...  7.12 us
    ppermute x8, waiting for transfers between devices, over_head(): return lax.ppermute(x, 'head', [(i, i ^ k) for i in range(H)])  6.53 us
    unnamed x70, local copies, waits for them, and re-layouts  6.2 us
    ppermute x8, starting transfers between devices, over_head(): return lax.ppermute(x, 'head', [(i, i ^ k) for i in range(H)])  6.11 us
    ppermute x6, waiting for transfers between devices, back_b(): lax.ppermute(x, 'seg', [(i, i // B * B + (i % B - 1) % B) for i in range(...  5.18 us
  transfers between devices with their start and end apart: 29, of which 13 were waited for; matrix products, arithmetic and copies ran while one was open for 3% of the time, Pallas kernels for 18%

profile of v1, /device:TPU:0, one launch (start us, length us, event | category | flops | bytes accessed | tf_op | source)
XLA Modules:
  0.0 123.2 jit_solution(11038153605327605198)
XLA Ops:
  0.6 3.0 %collective-permute-start.4 = (bf16[256,512]{1,0:T(8,128)(2,1)}, bf16[256,512]{1,0:T(8,128)(2,1)S(1)}, u32[]{:S(2)}, u32[]{:S(2)}) collective-permute-start(bf16[256,512]{1,0:T(8,128)(2,1)} %refs_0_.1), channel_id=1, source_target_pairs={{0,2},{1,3},{2,0},{3,1},{4,6},{5,7},{6,4},{7,5},{8,10},{9,11},{10,... | collective-permute-start | bytes 786440 | tf_op jit(solution)/shard_map/ppermute | solution.py:199
  3.6 6.5 %collective-permute-done.4.refs_2_ = bf16[256,512]{1,0:T(8,128)(2,1)S(1)} collective-permute-done((bf16[256,512]{1,0:T(8,128)(2,1)}, bf16[256,512]{1,0:T(8,128)(2,1)S(1)}, u32[]{:S(2)}, u32[]{:S(2)}) %collective-permute-start.4) | collective-permute-done | bytes 262176 | tf_op jit(solution)/shard_map/ppermute | solution.py:199
  10.2 2.2 %shard_map.110 = (bf16[256,256]{1,0:T(8,128)(2,1)}, bf16[256,256]{1,0:T(8,128)(2,1)}, bf16[256,256]{1,0:T(8,128)(2,1)}, bf16[256,256]{1,0:T(8,128)(2,1)}, bf16[2...) custom-call(bf16[256,512]{1,0:T(8,128)(2,1)} %q_ref.1, ...), custom_call_target="tpu_custom_call" | custom-call | bytes 1572864 | tf_op jit(solution)/shard_map/pallas_call | solution.py:30
  12.4 1.9 %collective-permute-start = (bf16[256,128]{1,0:T(8,128)(2,1)}, bf16[256,128]{1,0:T(8,128)(2,1)S(1)}, u32[]{:S(2)}, u32[]{:S(2)}) collective-permute-start(bf16[256,128]{1,0:T(8,128)(2,1)} %get-tuple-element.33), channel_id=1, source_target_pairs={{0,8},{4,12},{8,0},{12,4},{16,24},{20,28},{24,16},{28,20},{1,9},{5... | collective-permute-start | bytes 196616 | tf_op jit(solution)/shard_map/ppermute | solution.py:193
  14.2 2.6 %collective-permute-start.1 = (bf16[256,128]{1,0:T(8,128)(2,1)}, bf16[256,128]{1,0:T(8,128)(2,1)S(1)}, u32[]{:S(2)}, u32[]{:S(2)}) collective-permute-start(bf16[256,128]{1,0:T(8,128)(2,1)} %get-tuple-element.34), channel_id=1, source_target_pairs={{0,16},{4,20},{8,24},{12,28},{16,0},{20,4},{24,8},{28,12},{1,17},{... | collective-permute-start | bytes 196616 | tf_op jit(solution)/shard_map/ppermute | solution.py:193
  18.7 3.5 %shard_map.111 = (bf16[256,256]{1,0:T(8,128)(2,1)}, bf16[256,256]{1,0:T(8,128)(2,1)}, bf16[256,256]{1,0:T(8,128)(2,1)}, bf16[256,256]{1,0:T(8,128)(2,1)}) custom-call(bf16[256,512]{1,0:T(8,128)(2,1)} %refs_0_.1, bf16[256,512]{1,0:T(8,128)(2,1)} %copy-done.7, bf16[256,512]{1,0:T(8,128)(2,1)} %copy-done.6, bf16[256,512]{1,0:T(8,128)(2,1)} %copy-done.10, ...), custom_call_target="tpu_custom_call" | custom-call | flops 536870912 | bytes 3670016 | tf_op jit(solution)/shard_map/pallas_call | solution.py:30
  22.2 1.6 %collective-permute-start.6 = (bf16[256,256]{1,0:T(8,128)(2,1)}, bf16[256,256]{1,0:T(8,128)(2,1)S(1)}, u32[]{:S(2)}, u32[]{:S(2)}) collective-permute-start(bf16[256,256]{1,0:T(8,128)(2,1)} %get-tuple-element.37), channel_id=1, source_target_pairs={{0,8},{4,12},{8,0},{12,4},{16,24},{20,28},{24,16},{28,20},{1,9},{5... | collective-permute-start | bytes 393224 | tf_op jit(solution)/shard_map/ppermute | solution.py:193
  24.6 3.7 %collective-permute-done.6.refs_5_ = bf16[256,256]{1,0:T(8,128)(2,1)S(1)} collective-permute-done((bf16[256,256]{1,0:T(8,128)(2,1)}, bf16[256,256]{1,0:T(8,128)(2,1)S(1)}, u32[]{:S(2)}, u32[]{:S(2)}) %collective-permute-start.6) | collective-permute-done | bytes 131104 | tf_op jit(solution)/shard_map/ppermute | solution.py:193
  29.8 7.3 %collective-permute-done.7.refs_6_ = bf16[256,256]{1,0:T(8,128)(2,1)S(1)} collective-permute-done((bf16[256,256]{1,0:T(8,128)(2,1)}, bf16[256,256]{1,0:T(8,128)(2,1)S(1)}, u32[]{:S(2)}, u32[]{:S(2)}) %collective-permute-start.7) | collective-permute-done | bytes 131104 | tf_op jit(solution)/shard_map/ppermute | solution.py:193
  37.1 1.6 %collective-permute-start.8 = (bf16[256,256]{1,0:T(8,128)(2,1)}, bf16[256,256]{1,0:T(8,128)(2,1)S(1)}, u32[]{:S(2)}, u32[]{:S(2)}) collective-permute-start(bf16[256,256]{1,0:T(8,128)(2,1)} %get-tuple-element.39), channel_id=1, source_target_pairs={{0,24},{4,28},{8,16},{12,20},{16,8},{20,12},{24,0},{28,4},{1,25},{... | collective-permute-start | bytes 393224 | tf_op jit(solution)/shard_map/ppermute | solution.py:193
  38.7 5.4 %collective-permute-done.8.refs_7_ = bf16[256,256]{1,0:T(8,128)(2,1)S(1)} collective-permute-done((bf16[256,256]{1,0:T(8,128)(2,1)}, bf16[256,256]{1,0:T(8,128)(2,1)S(1)}, u32[]{:S(2)}, u32[]{:S(2)}) %collective-permute-start.8) | collective-permute-done | bytes 131104 | tf_op jit(solution)/shard_map/ppermute | solution.py:193
  44.1 1.6 %collective-permute-start.11 = (bf16[256,256]{1,0:T(8,128)(2,1)S(1)}, bf16[256,256]{1,0:T(8,128)(2,1)S(1)}, u32[]{:S(2)}, u32[]{:S(2)}) collective-permute-start(bf16[256,256]{1,0:T(8,128)(2,1)S(1)} %copy-done.24), channel_id=1, source_target_pairs={{0,24},{4,28},{8,16},{12,20},{16,8},{20,12},{24,0},{28,4},{1,25},{... | collective-permute-start | bytes 393224 | tf_op jit(solution)/shard_map/ppermute | solution.py:193
  45.8 2.3 %collective-permute-start.2 = (bf16[256,128]{1,0:T(8,128)(2,1)S(1)}, bf16[256,128]{1,0:T(8,128)(2,1)S(1)}, u32[]{:S(2)}, u32[]{:S(2)}) collective-permute-start(bf16[256,128]{1,0:T(8,128)(2,1)S(1)} %copy-done.32), channel_id=1, source_target_pairs={{0,24},{4,28},{8,16},{12,20},{16,8},{20,12},{24,0},{28,4},{1,25},{... | collective-permute-start | bytes 196616 | tf_op jit(solution)/shard_map/ppermute | solution.py:193
  48.1 1.6 %collective-permute-start.20 = (bf16[4,256,128]{2,1,0:T(8,128)(2,1)S(1)}, bf16[4,256,128]{2,1,0:T(8,128)(2,1)S(1)}, u32[]{:S(2)}, u32[]{:S(2)}) collective-permute-start(bf16[4,256,128]{2,1,0:T(8,128)(2,1)S(1)} %pad_maximum_fusion.refs_4_), channel_id=1, source_target_pairs={{0,2},{1,3},{2,0},{3,1},{4,6},{5,7},{6,4},{7,5},{8,10},{9,11},{10,... | collective-permute-start | bytes 786440 | tf_op jit(solution)/shard_map/ppermute | solution.py:199
  49.7 2.3 %collective-permute-done.2.refs_3_ = bf16[256,128]{1,0:T(8,128)(2,1)S(1)} collective-permute-done((bf16[256,128]{1,0:T(8,128)(2,1)S(1)}, bf16[256,128]{1,0:T(8,128)(2,1)S(1)}, u32[]{:S(2)}, u32[]{:S(2)}) %collective-permute-start.2) | collective-permute-done | bytes 65568 | tf_op jit(solution)/shard_map/ppermute | solution.py:193
  52.0 1.5 %collective-permute-start.12 = (bf16[256,256]{1,0:T(8,128)(2,1)S(1)}, bf16[256,256]{1,0:T(8,128)(2,1)S(1)}, u32[]{:S(2)}, u32[]{:S(2)}) collective-permute-start(bf16[256,256]{1,0:T(8,128)(2,1)S(1)} %copy-done.21), channel_id=1, source_target_pairs={{0,4},{4,0},{8,12},{12,8},{16,20},{20,16},{24,28},{28,24},{1,5},{5... | collective-permute-start | bytes 393224 | tf_op jit(solution)/shard_map/ppermute | solution.py:196
  54.0 1.5 %collective-permute-start.14 = (bf16[256,256]{1,0:T(8,128)(2,1)S(1)}, bf16[256,256]{1,0:T(8,128)(2,1)S(1)}, u32[]{:S(2)}, u32[]{:S(2)}) collective-permute-start(bf16[256,256]{1,0:T(8,128)(2,1)S(1)} %collective-permute-done.10.refs_10_), channel_id=1, source_target_pairs={{0,4},{4,0},{8,12},{12,8},{16,20},{20,16},{24,28},{28,24},{1,5},{5... | collective-permute-start | bytes 393224 | tf_op jit(solution)/shard_map/ppermute | solution.py:196
  63.2 7.1 %shard_map.112 = (bf16[4,256,128]{2,1,0:T(8,128)(2,1)}, bf16[4,256,128]{2,1,0:T(8,128)(2,1)}, f32[4,256,256]{2,1,0:T(8,128)}, bf16[4,256,256]{2,1,0:T(8,128)(2,1)}) custom-call(s32[8,4]{1,0:T(8,128)} %copy.12.owner_ref, s32[8,4]{1,0:T(8,128)} %copy.13.block_ref, bf16[256,128]{1,0:T(8,128)(2,1)} %get-tuple-element.32.refs_0_, bf16[256,128]{1,0:T(8,128)(2,1)} %copy-done.30, ...), custom_call_target="tpu_custom_call" | custom-call | flops 1342177280 | bytes 3932416 | tf_op jit(solution)/shard_map/pallas_call | solution.py:30
  70.3 2.3 %collective-permute-start.18 = (bf16[4,256,128]{2,1,0:T(8,128)(2,1)}, bf16[4,256,128]{2,1,0:T(8,128)(2,1)S(1)}, u32[]{:S(2)}, u32[]{:S(2)}) collective-permute-start(bf16[4,256,128]{2,1,0:T(8,128)(2,1)} %get-tuple-element.44.refs_0_), channel_id=1, source_target_pairs={{0,24},{4,28},{8,16},{12,20},{16,8},{20,12},{24,0},{28,4},{1,25},{... | collective-permute-start | bytes 786440 | tf_op jit(solution)/shard_map/ppermute | solution.py:193
  72.6 2.2 %collective-permute-start.16 = (bf16[4,256,128]{2,1,0:T(8,128)(2,1)}, bf16[4,256,128]{2,1,0:T(8,128)(2,1)S(1)}, u32[]{:S(2)}, u32[]{:S(2)}) collective-permute-start(bf16[4,256,128]{2,1,0:T(8,128)(2,1)} %get-tuple-element.44.refs_0_), channel_id=1, source_target_pairs={{0,8},{4,12},{8,0},{12,4},{16,24},{20,28},{24,16},{28,20},{1,9},{5... | collective-permute-start | bytes 786440 | tf_op jit(solution)/shard_map/ppermute | solution.py:193
  74.8 1.6 %collective-permute-start.24 = (bf16[4,256,256]{2,1,0:T(8,128)(2,1)}, bf16[4,256,256]{2,1,0:T(8,128)(2,1)S(1)}, u32[]{:S(2)}, u32[]{:S(2)}) collective-permute-start(bf16[4,256,256]{2,1,0:T(8,128)(2,1)} %get-tuple-element.49), channel_id=1, source_target_pairs={{0,4},{4,0},{8,12},{12,8},{16,20},{20,16},{24,28},{28,24},{1,5},{5... | collective-permute-start | bytes 1572872 | tf_op jit(solution)/shard_map/ppermute | solution.py:196
  76.3 5.3 %collective-permute-done.18.refs_3_ = bf16[4,256,128]{2,1,0:T(8,128)(2,1)S(1)} collective-permute-done((bf16[4,256,128]{2,1,0:T(8,128)(2,1)}, bf16[4,256,128]{2,1,0:T(8,128)(2,1)S(1)}, u32[]{:S(2)}, u32[]{:S(2)}) %collective-permute-start.18) | collective-permute-done | bytes 262176 | tf_op jit(solution)/shard_map/ppermute | solution.py:193
  81.6 10.4 %collective-permute-done.17.refs_2_ = bf16[4,256,128]{2,1,0:T(8,128)(2,1)S(1)} collective-permute-done((bf16[4,256,128]{2,1,0:T(8,128)(2,1)}, bf16[4,256,128]{2,1,0:T(8,128)(2,1)S(1)}, u32[]{:S(2)}, u32[]{:S(2)}) %collective-permute-start.17) | collective-permute-done | bytes 262176 | tf_op jit(solution)/shard_map/ppermute | solution.py:193
  93.5 4.6 %shard_map.113 = (f32[256,1024]{1,0:T(8,128)}, bf16[256,1024]{1,0:T(8,128)(2,1)}, f32[256,512]{1,0:T(8,128)}, bf16[256,512]{1,0:T(8,128)(2,1)}) custom-call(bf16[4,256,128]{2,1,0:T(8,128)(2,1)} %get-tuple-element.44.refs_0_, bf16[4,256,128]{2,1,0:T(8,128)(2,1)} %copy-done.11, bf16[4,256,128]{2,1,0:T(8,128)(2,1)} %copy-done.9, ...), custom_call_target="tpu_custom_call" | custom-call | flops 1073741824 | bytes 6553600 | tf_op jit(solution)/shard_map/pallas_call | solution.py:30
  98.9 2.3 %shard_map.114 = (bf16[256,384]{1,0:T(8,128)(2,1)}, bf16[256,384]{1,0:T(8,128)(2,1)}, bf16[256,384]{1,0:T(8,128)(2,1)}, bf16[256,384]{1,0:T(8,128)(2,1)}) custom-call(bf16[4,256,128]{2,1,0:T(8,128)(2,1)} %get-tuple-element.47.dq_ref, f32[4,256,256]{2,1,0:T(8,128)} %get-tuple-element.48.own_ref, bf16[4,256,256]{2,1,0:T(8,128)(2,1)} %copy-done.2), custom_call_target="tpu_custom_call" | custom-call | bytes 2621440 | tf_op jit(solution)/shard_map/pallas_call | solution.py:30
  101.3 2.1 %collective-permute-start.26 = (bf16[256,384]{1,0:T(8,128)(2,1)}, bf16[256,384]{1,0:T(8,128)(2,1)S(1)}, u32[]{:S(2)}, u32[]{:S(2)}) collective-permute-start(bf16[256,384]{1,0:T(8,128)(2,1)} %get-tuple-element.52), channel_id=1, source_target_pairs={{0,16},{4,20},{8,24},{12,28},{16,0},{20,4},{24,8},{28,12},{1,17},{... | collective-permute-start | bytes 589832 | tf_op jit(solution)/shard_map/ppermute | solution.py:193
  103.3 2.3 %collective-permute-start.27 = (bf16[256,384]{1,0:T(8,128)(2,1)}, bf16[256,384]{1,0:T(8,128)(2,1)S(1)}, u32[]{:S(2)}, u32[]{:S(2)}) collective-permute-start(bf16[256,384]{1,0:T(8,128)(2,1)} %get-tuple-element.53), channel_id=1, source_target_pairs={{0,24},{4,28},{8,16},{12,20},{16,8},{20,12},{24,0},{28,4},{1,25},{... | collective-permute-start | bytes 589832 | tf_op jit(solution)/shard_map/ppermute | solution.py:193
  105.6 1.5 %collective-permute-start.28 = (bf16[256,512]{1,0:T(8,128)(2,1)}, bf16[256,512]{1,0:T(8,128)(2,1)S(1)}, u32[]{:S(2)}, u32[]{:S(2)}) collective-permute-start(bf16[256,512]{1,0:T(8,128)(2,1)} %get-tuple-element.58), channel_id=1, source_target_pairs={{0,4},{4,0},{8,12},{12,8},{16,20},{20,16},{24,28},{28,24},{1,5},{5... | collective-permute-start | bytes 786440 | tf_op jit(solution)/shard_map/ppermute | solution.py:196
  107.4 1.5 %collective-permute-start.23 = (bf16[256,512]{1,0:T(8,128)(2,1)S(1)}, bf16[256,512]{1,0:T(8,128)(2,1)S(1)}, u32[]{:S(2)}, u32[]{:S(2)}) collective-permute-start(bf16[256,512]{1,0:T(8,128)(2,1)S(1)} %slice.38), channel_id=1, source_target_pairs={{0,2},{1,3},{2,0},{3,1},{4,6},{5,7},{6,4},{7,5},{8,10},{9,11},{10,... | collective-permute-start | bytes 786440 | tf_op jit(solution)/shard_map/ppermute | solution.py:199
  108.9 2.9 %collective-permute-done.25.refs_1_ = bf16[256,384]{1,0:T(8,128)(2,1)S(1)} collective-permute-done((bf16[256,384]{1,0:T(8,128)(2,1)}, bf16[256,384]{1,0:T(8,128)(2,1)S(1)}, u32[]{:S(2)}, u32[]{:S(2)}) %collective-permute-start.25) | collective-permute-done | bytes 196640 | tf_op jit(solution)/shard_map/ppermute | solution.py:193
  111.9 6.7 %collective-permute-done.26.refs_2_ = bf16[256,384]{1,0:T(8,128)(2,1)S(1)} collective-permute-done((bf16[256,384]{1,0:T(8,128)(2,1)}, bf16[256,384]{1,0:T(8,128)(2,1)S(1)}, u32[]{:S(2)}, u32[]{:S(2)}) %collective-permute-start.26) | collective-permute-done | bytes 196640 | tf_op jit(solution)/shard_map/ppermute | solution.py:193
  119.3 2.2 %shard_map.115 = (bf16[256,512]{1,0:T(8,128)(2,1)}, bf16[256,512]{1,0:T(8,128)(2,1)}, bf16[256,512]{1,0:T(8,128)(2,1)}) custom-call(bf16[256,384]{1,0:T(8,128)(2,1)} %get-tuple-element.50.refs_0_, bf16[256,384]{1,0:T(8,128)(2,1)} %copy-done.13, bf16[256,384]{1,0:T(8,128)(2,1)} %copy-done.14, bf16[256,384]{1,0:T(8,128)(2,1)} %copy-done.15), custom_call_target="tpu_custom_call" | custom-call | bytes 1572864 | tf_op jit(solution)/shard_map/pallas_call | solution.py:30
  (111 shorter events, 17.2 us)
Async XLA Ops:
  0.6 9.5 %collective-permute-start.4 = (bf16[256,512]{1,0:T(8,128)(2,1)}, bf16[256,512]{1,0:T(8,128)(2,1)S(1)}, u32[]{:S(2)}, u32[]{:S(2)}) collective-permute-start(bf16[256,512]{1,0:T(8,128)(2,1)} %refs_0_.1), channel_id=1, source_target_pairs={{0,2},{1,3},{2,0},{3,1},{4,6},{5,7},{6,4},{7,5},{8,10},{9,11},{10,... | collective-permute-start | bytes 786440 | tf_op jit(solution)/shard_map/ppermute | solution.py:199
  3.6 13.6 %collective-permute-start.3 = (bf16[256,512]{1,0:T(8,128)(2,1)}, bf16[256,512]{1,0:T(8,128)(2,1)S(1)}, u32[]{:S(2)}, u32[]{:S(2)}) collective-permute-start(bf16[256,512]{1,0:T(8,128)(2,1)} %refs_0_.1), channel_id=1, source_target_pairs={{0,1},{1,0},{2,3},{3,2},{4,5},{5,4},{6,7},{7,6},{8,9},{9,8},{10,11... | collective-permute-start | bytes 786440 | tf_op jit(solution)/shard_map/ppermute | solution.py:199
  10.2 7.3 %collective-permute-start.5 = (bf16[256,512]{1,0:T(8,128)(2,1)S(1)}, bf16[256,512]{1,0:T(8,128)(2,1)S(1)}, u32[]{:S(2)}, u32[]{:S(2)}) collective-permute-start(bf16[256,512]{1,0:T(8,128)(2,1)S(1)} %collective-permute-done.4.refs_2_), channel_id=1, source_target_pairs={{0,1},{1,0},{2,3},{3,2},{4,5},{5,4},{6,7},{7,6},{8,9},{9,8},{10,11... | collective-permute-start | bytes 786440 | tf_op jit(solution)/shard_map/ppermute | solution.py:199
  12.4 33.4 %collective-permute-start = (bf16[256,128]{1,0:T(8,128)(2,1)}, bf16[256,128]{1,0:T(8,128)(2,1)S(1)}, u32[]{:S(2)}, u32[]{:S(2)}) collective-permute-start(bf16[256,128]{1,0:T(8,128)(2,1)} %get-tuple-element.33), channel_id=1, source_target_pairs={{0,8},{4,12},{8,0},{12,4},{16,24},{20,28},{24,16},{28,20},{1,9},{5... | collective-permute-start | bytes 196616 | tf_op jit(solution)/shard_map/ppermute | solution.py:193
  14.2 33.9 %collective-permute-start.1 = (bf16[256,128]{1,0:T(8,128)(2,1)}, bf16[256,128]{1,0:T(8,128)(2,1)S(1)}, u32[]{:S(2)}, u32[]{:S(2)}) collective-permute-start(bf16[256,128]{1,0:T(8,128)(2,1)} %get-tuple-element.34), channel_id=1, source_target_pairs={{0,16},{4,20},{8,24},{12,28},{16,0},{20,4},{24,8},{28,12},{1,17},{... | collective-permute-start | bytes 196616 | tf_op jit(solution)/shard_map/ppermute | solution.py:193
  16.8 36.6 %collective-permute-start.9 = (bf16[256,256]{1,0:T(8,128)(2,1)}, bf16[256,256]{1,0:T(8,128)(2,1)S(1)}, u32[]{:S(2)}, u32[]{:S(2)}) collective-permute-start(bf16[256,256]{1,0:T(8,128)(2,1)} %get-tuple-element.41), channel_id=1, source_target_pairs={{0,8},{4,12},{8,0},{12,4},{16,24},{20,28},{24,16},{28,20},{1,9},{5... | collective-permute-start | bytes 393224 | tf_op jit(solution)/shard_map/ppermute | solution.py:193
  17.3 34.7 %copy-start.21 = (bf16[256,256]{1,0:T(8,128)(2,1)S(1)}, bf16[256,256]{1,0:T(8,128)(2,1)}, u32[]{:S(2)}) copy-start(bf16[256,256]{1,0:T(8,128)(2,1)} %get-tuple-element.40.refs_8_) | copy-start | bytes 393220
  17.3 38.7 %copy-start.19 = (s32[8,4]{0,1:T(4,128)S(1)}, s32[8,4]{0,1:T(4,128)}, u32[]{:S(2)}) copy-start(s32[8,4]{0,1:T(4,128)} %param.12) | copy-start | bytes 388
  17.3 39.4 %copy-start.20 = (s32[8,4]{0,1:T(4,128)S(1)}, s32[8,4]{0,1:T(4,128)}, u32[]{:S(2)}) copy-start(s32[8,4]{0,1:T(4,128)} %param.13) | copy-start | bytes 388
  17.3 36.7 %collective-permute-start.10 = (bf16[256,256]{1,0:T(8,128)(2,1)}, bf16[256,256]{1,0:T(8,128)(2,1)S(1)}, u32[]{:S(2)}, u32[]{:S(2)}) collective-permute-start(bf16[256,256]{1,0:T(8,128)(2,1)} %get-tuple-element.42), channel_id=1, source_target_pairs={{0,16},{4,20},{8,24},{12,28},{16,0},{20,4},{24,8},{28,12},{1,17},{... | collective-permute-start | bytes 393224 | tf_op jit(solution)/shard_map/ppermute | solution.py:193
  22.2 6.1 %collective-permute-start.6 = (bf16[256,256]{1,0:T(8,128)(2,1)}, bf16[256,256]{1,0:T(8,128)(2,1)S(1)}, u32[]{:S(2)}, u32[]{:S(2)}) collective-permute-start(bf16[256,256]{1,0:T(8,128)(2,1)} %get-tuple-element.37), channel_id=1, source_target_pairs={{0,8},{4,12},{8,0},{12,4},{16,24},{20,28},{24,16},{28,20},{1,9},{5... | collective-permute-start | bytes 393224 | tf_op jit(solution)/shard_map/ppermute | solution.py:193
  28.3 8.8 %collective-permute-start.7 = (bf16[256,256]{1,0:T(8,128)(2,1)}, bf16[256,256]{1,0:T(8,128)(2,1)S(1)}, u32[]{:S(2)}, u32[]{:S(2)}) collective-permute-start(bf16[256,256]{1,0:T(8,128)(2,1)} %get-tuple-element.38), channel_id=1, source_target_pairs={{0,16},{4,20},{8,24},{12,28},{16,0},{20,4},{24,8},{28,12},{1,17},{... | collective-permute-start | bytes 393224 | tf_op jit(solution)/shard_map/ppermute | solution.py:193
  37.1 7.0 %collective-permute-start.8 = (bf16[256,256]{1,0:T(8,128)(2,1)}, bf16[256,256]{1,0:T(8,128)(2,1)S(1)}, u32[]{:S(2)}, u32[]{:S(2)}) collective-permute-start(bf16[256,256]{1,0:T(8,128)(2,1)} %get-tuple-element.39), channel_id=1, source_target_pairs={{0,24},{4,28},{8,16},{12,20},{16,8},{20,12},{24,0},{28,4},{1,25},{... | collective-permute-start | bytes 393224 | tf_op jit(solution)/shard_map/ppermute | solution.py:193
  44.1 11.4 %collective-permute-start.11 = (bf16[256,256]{1,0:T(8,128)(2,1)S(1)}, bf16[256,256]{1,0:T(8,128)(2,1)S(1)}, u32[]{:S(2)}, u32[]{:S(2)}) collective-permute-start(bf16[256,256]{1,0:T(8,128)(2,1)S(1)} %copy-done.24), channel_id=1, source_target_pairs={{0,24},{4,28},{8,16},{12,20},{16,8},{20,12},{24,0},{28,4},{1,25},{... | collective-permute-start | bytes 393224 | tf_op jit(solution)/shard_map/ppermute | solution.py:193
  45.8 6.2 %collective-permute-start.2 = (bf16[256,128]{1,0:T(8,128)(2,1)S(1)}, bf16[256,128]{1,0:T(8,128)(2,1)S(1)}, u32[]{:S(2)}, u32[]{:S(2)}) collective-permute-start(bf16[256,128]{1,0:T(8,128)(2,1)S(1)} %copy-done.32), channel_id=1, source_target_pairs={{0,24},{4,28},{8,16},{12,20},{16,8},{20,12},{24,0},{28,4},{1,25},{... | collective-permute-start | bytes 196616 | tf_op jit(solution)/shard_map/ppermute | solution.py:193
  48.1 26.6 %collective-permute-start.20 = (bf16[4,256,128]{2,1,0:T(8,128)(2,1)S(1)}, bf16[4,256,128]{2,1,0:T(8,128)(2,1)S(1)}, u32[]{:S(2)}, u32[]{:S(2)}) collective-permute-start(bf16[4,256,128]{2,1,0:T(8,128)(2,1)S(1)} %pad_maximum_fusion.refs_4_), channel_id=1, source_target_pairs={{0,2},{1,3},{2,0},{3,1},{4,6},{5,7},{6,4},{7,5},{8,10},{9,11},{10,... | collective-permute-start | bytes 786440 | tf_op jit(solution)/shard_map/ppermute | solution.py:199
  52.0 6.4 %collective-permute-start.12 = (bf16[256,256]{1,0:T(8,128)(2,1)S(1)}, bf16[256,256]{1,0:T(8,128)(2,1)S(1)}, u32[]{:S(2)}, u32[]{:S(2)}) collective-permute-start(bf16[256,256]{1,0:T(8,128)(2,1)S(1)} %copy-done.21), channel_id=1, source_target_pairs={{0,4},{4,0},{8,12},{12,8},{16,20},{20,16},{24,28},{28,24},{1,5},{5... | collective-permute-start | bytes 393224 | tf_op jit(solution)/shard_map/ppermute | solution.py:196
  53.5 6.3 %collective-permute-start.13 = (bf16[256,256]{1,0:T(8,128)(2,1)S(1)}, bf16[256,256]{1,0:T(8,128)(2,1)S(1)}, u32[]{:S(2)}, u32[]{:S(2)}) collective-permute-start(bf16[256,256]{1,0:T(8,128)(2,1)S(1)} %collective-permute-done.9.refs_9_), channel_id=1, source_target_pairs={{0,4},{4,0},{8,12},{12,8},{16,20},{20,16},{24,28},{28,24},{1,5},{5... | collective-permute-start | bytes 393224 | tf_op jit(solution)/shard_map/ppermute | solution.py:196
  54.0 7.2 %collective-permute-start.14 = (bf16[256,256]{1,0:T(8,128)(2,1)S(1)}, bf16[256,256]{1,0:T(8,128)(2,1)S(1)}, u32[]{:S(2)}, u32[]{:S(2)}) collective-permute-start(bf16[256,256]{1,0:T(8,128)(2,1)S(1)} %collective-permute-done.10.refs_10_), channel_id=1, source_target_pairs={{0,4},{4,0},{8,12},{12,8},{16,20},{20,16},{24,28},{28,24},{1,5},{5... | collective-permute-start | bytes 393224 | tf_op jit(solution)/shard_map/ppermute | solution.py:196
  55.5 7.0 %collective-permute-start.15 = (bf16[256,256]{1,0:T(8,128)(2,1)S(1)}, bf16[256,256]{1,0:T(8,128)(2,1)S(1)}, u32[]{:S(2)}, u32[]{:S(2)}) collective-permute-start(bf16[256,256]{1,0:T(8,128)(2,1)S(1)} %collective-permute-done.11.refs_11_), channel_id=1, source_target_pairs={{0,4},{4,0},{8,12},{12,8},{16,20},{20,16},{24,28},{28,24},{1,5},{5... | collective-permute-start | bytes 393224 | tf_op jit(solution)/shard_map/ppermute | solution.py:196
  58.3 16.4 %collective-permute-start.19 = (bf16[4,256,128]{2,1,0:T(8,128)(2,1)S(1)}, bf16[4,256,128]{2,1,0:T(8,128)(2,1)S(1)}, u32[]{:S(2)}, u32[]{:S(2)}) collective-permute-start(bf16[4,256,128]{2,1,0:T(8,128)(2,1)S(1)} %pad_maximum_fusion.refs_4_), channel_id=1, source_target_pairs={{0,1},{1,0},{2,3},{3,2},{4,5},{5,4},{6,7},{7,6},{8,9},{9,8},{10,11... | collective-permute-start | bytes 786440 | tf_op jit(solution)/shard_map/ppermute | solution.py:199
  70.3 11.3 %collective-permute-start.18 = (bf16[4,256,128]{2,1,0:T(8,128)(2,1)}, bf16[4,256,128]{2,1,0:T(8,128)(2,1)S(1)}, u32[]{:S(2)}, u32[]{:S(2)}) collective-permute-start(bf16[4,256,128]{2,1,0:T(8,128)(2,1)} %get-tuple-element.44.refs_0_), channel_id=1, source_target_pairs={{0,24},{4,28},{8,16},{12,20},{16,8},{20,12},{24,0},{28,4},{1,25},{... | collective-permute-start | bytes 786440 | tf_op jit(solution)/shard_map/ppermute | solution.py:193
  72.6 19.4 %collective-permute-start.17 = (bf16[4,256,128]{2,1,0:T(8,128)(2,1)}, bf16[4,256,128]{2,1,0:T(8,128)(2,1)S(1)}, u32[]{:S(2)}, u32[]{:S(2)}) collective-permute-start(bf16[4,256,128]{2,1,0:T(8,128)(2,1)} %get-tuple-element.44.refs_0_), channel_id=1, source_target_pairs={{0,16},{4,20},{8,24},{12,28},{16,0},{20,4},{24,8},{28,12},{1,17},{... | collective-permute-start | bytes 786440 | tf_op jit(solution)/shard_map/ppermute | solution.py:193
  72.6 19.4 %collective-permute-start.16 = (bf16[4,256,128]{2,1,0:T(8,128)(2,1)}, bf16[4,256,128]{2,1,0:T(8,128)(2,1)S(1)}, u32[]{:S(2)}, u32[]{:S(2)}) collective-permute-start(bf16[4,256,128]{2,1,0:T(8,128)(2,1)} %get-tuple-element.44.refs_0_), channel_id=1, source_target_pairs={{0,8},{4,12},{8,0},{12,4},{16,24},{20,28},{24,16},{28,20},{1,9},{5... | collective-permute-start | bytes 786440 | tf_op jit(solution)/shard_map/ppermute | solution.py:193
  74.7 17.3 %collective-permute-start.21 = (bf16[4,256,128]{2,1,0:T(8,128)(2,1)S(1)}, bf16[4,256,128]{2,1,0:T(8,128)(2,1)S(1)}, u32[]{:S(2)}, u32[]{:S(2)}) collective-permute-start(bf16[4,256,128]{2,1,0:T(8,128)(2,1)S(1)} %collective-permute-done.20.refs_6_), channel_id=1, source_target_pairs={{0,1},{1,0},{2,3},{3,2},{4,5},{5,4},{6,7},{7,6},{8,9},{9,8},{10,11... | collective-permute-start | bytes 786440 | tf_op jit(solution)/shard_map/ppermute | solution.py:199
  74.8 23.3 %collective-permute-start.24 = (bf16[4,256,256]{2,1,0:T(8,128)(2,1)}, bf16[4,256,256]{2,1,0:T(8,128)(2,1)S(1)}, u32[]{:S(2)}, u32[]{:S(2)}) collective-permute-start(bf16[4,256,256]{2,1,0:T(8,128)(2,1)} %get-tuple-element.49), channel_id=1, source_target_pairs={{0,4},{4,0},{8,12},{12,8},{16,20},{20,16},{24,28},{28,24},{1,5},{5... | collective-permute-start | bytes 1572872 | tf_op jit(solution)/shard_map/ppermute | solution.py:196
  98.1 9.0 %collective-permute-start.22 = (bf16[256,1024]{1,0:T(8,128)(2,1)}, bf16[256,1024]{1,0:T(8,128)(2,1)S(1)}, u32[]{:S(2)}, u32[]{:S(2)}) collective-permute-start(bf16[256,1024]{1,0:T(8,128)(2,1)} %get-tuple-element.46), channel_id=1, source_target_pairs={{0,1},{1,0},{2,3},{3,2},{4,5},{5,4},{6,7},{7,6},{8,9},{9,8},{10,11... | collective-permute-start | bytes 1572872 | tf_op jit(solution)/shard_map/ppermute | solution.py:199
  101.3 10.6 %collective-permute-start.25 = (bf16[256,384]{1,0:T(8,128)(2,1)}, bf16[256,384]{1,0:T(8,128)(2,1)S(1)}, u32[]{:S(2)}, u32[]{:S(2)}) collective-permute-start(bf16[256,384]{1,0:T(8,128)(2,1)} %get-tuple-element.51), channel_id=1, source_target_pairs={{0,8},{4,12},{8,0},{12,4},{16,24},{20,28},{24,16},{28,20},{1,9},{5... | collective-permute-start | bytes 589832 | tf_op jit(solution)/shard_map/ppermute | solution.py:193
  101.3 17.3 %collective-permute-start.26 = (bf16[256,384]{1,0:T(8,128)(2,1)}, bf16[256,384]{1,0:T(8,128)(2,1)S(1)}, u32[]{:S(2)}, u32[]{:S(2)}) collective-permute-start(bf16[256,384]{1,0:T(8,128)(2,1)} %get-tuple-element.52), channel_id=1, source_target_pairs={{0,16},{4,20},{8,24},{12,28},{16,0},{20,4},{24,8},{28,12},{1,17},{... | collective-permute-start | bytes 589832 | tf_op jit(solution)/shard_map/ppermute | solution.py:193
  103.3 15.2 %collective-permute-start.27 = (bf16[256,384]{1,0:T(8,128)(2,1)}, bf16[256,384]{1,0:T(8,128)(2,1)S(1)}, u32[]{:S(2)}, u32[]{:S(2)}) collective-permute-start(bf16[256,384]{1,0:T(8,128)(2,1)} %get-tuple-element.53), channel_id=1, source_target_pairs={{0,24},{4,28},{8,16},{12,20},{16,8},{20,12},{24,0},{28,4},{1,25},{... | collective-permute-start | bytes 589832 | tf_op jit(solution)/shard_map/ppermute | solution.py:193
  105.6 15.9 %collective-permute-start.28 = (bf16[256,512]{1,0:T(8,128)(2,1)}, bf16[256,512]{1,0:T(8,128)(2,1)S(1)}, u32[]{:S(2)}, u32[]{:S(2)}) collective-permute-start(bf16[256,512]{1,0:T(8,128)(2,1)} %get-tuple-element.58), channel_id=1, source_target_pairs={{0,4},{4,0},{8,12},{12,8},{16,20},{20,16},{24,28},{28,24},{1,5},{5... | collective-permute-start | bytes 786440 | tf_op jit(solution)/shard_map/ppermute | solution.py:196
  107.4 15.1 %collective-permute-start.23 = (bf16[256,512]{1,0:T(8,128)(2,1)S(1)}, bf16[256,512]{1,0:T(8,128)(2,1)S(1)}, u32[]{:S(2)}, u32[]{:S(2)}) collective-permute-start(bf16[256,512]{1,0:T(8,128)(2,1)S(1)} %slice.38), channel_id=1, source_target_pairs={{0,2},{1,3},{2,0},{3,1},{4,6},{5,7},{6,4},{7,5},{8,10},{9,11},{10,... | collective-permute-start | bytes 786440 | tf_op jit(solution)/shard_map/ppermute | solution.py:199
  (31 other events, 335.8 us)

commit v2 on v1

--- a/solution.py
+++ b/solution.py
@@ -14,6 +14,8 @@
 BF16 = jnp.bfloat16
 HIDDEN = -1e30
 VMEM = pl.BlockSpec(memory_space=pltpu.VMEM)
+ANY = pl.BlockSpec(memory_space=pl.ANY)
+HBM = pl.BlockSpec(memory_space=pltpu.HBM)
 SMEM = pl.BlockSpec(memory_space=pltpu.SMEM)
 
 
@@ -25,35 +27,32 @@
     return pl.ds(pl.multiple_of(block * width, width), width)
 
 
-def call(body, outs, operands, specs=None, scratch=(), flops=0):
-    nbytes = sum(x.size * x.dtype.itemsize for x in (*operands, *outs))
-    return pl.pallas_call(
+def call(body, outs, operands, specs=None, scratch=(), limit=20):
+    return list(pl.pallas_call(
         body,
         out_shape=outs,
         in_specs=specs or [VMEM] * len(operands),
         out_specs=[VMEM] * len(outs),
         scratch_shapes=list(scratch),
-        compiler_params=pltpu.CompilerParams(vmem_limit_bytes=56 * 2**20),
-        cost_estimate=pl.CostEstimate(flops=flops, bytes_accessed=nbytes, transcendentals=0),
-    )(*operands)
+        compiler_params=pltpu.CompilerParams(vmem_limit_bytes=limit * 2**20),
+        cost_estimate=pl.CostEstimate(flops=1, bytes_accessed=1, transcendentals=0),
+    )(*operands))
 
 
 def shape(dims, dtype):
     return jax.ShapeDtypeStruct(dims, dtype)
 
 
-def cut_body(A, B, q_ref, k_ref, v_ref, *outs):
+def cut_body(A, B, k_ref, v_ref, *outs):
     a = lax.axis_index("seg") // B
     for m in range(A):
         head = lanes(a ^ m, DH)
         outs[m][:, :DH] = k_ref[:, head]
         outs[m][:, DH:] = v_ref[:, head]
-        outs[A + m][...] = q_ref[:, head]
 
 
 def slope_body(A, B, H, *refs):
-    grads, weight_ref, outs = refs[:H], refs[H], refs[H + 1 : H + 1 + A]
-    full, mixed = refs[H + 1 + A :]
+    grads, weight_ref, q_ref, outs, full, mixed = refs[:H], refs[H], refs[H + 1], refs[H + 2 : H + 2 + A], refs[-2], refs[-1]
     a = lax.axis_index("seg") // B
     h = lax.axis_index("head")
     width = grads[0].shape[1]
@@ -61,23 +60,26 @@
         full[:, lanes(h ^ k, width)] = grads[k][...]
     mixed[...] = dot(full[...], weight_ref[...], (1, 1)).astype(BF16)
     for m in range(A):
-        outs[m][:, :DH] = mixed[:, lanes(a ^ m, DH)]
-        outs[m][:, DH:] = full[:, lanes((a ^ m) * H + h, width // H)]
+        head = lanes(a ^ m, DH)
+        outs[m][:, :DH] = q_ref[:, head]
+        outs[m][:, DH : 2 * DH] = mixed[:, head]
+        outs[m][:, 2 * DH :] = full[:, lanes((a ^ m) * H + h, width // H)]
 
 
 def attend_body(A, B, R, score_scale, owner_ref, block_ref, *refs):
     pair = B == 2
-    q_refs, dag_refs, refs = refs[:A], refs[A : 2 * A], refs[2 * A :]
+    qdag_refs, refs = refs[:A], refs[A:]
     kv_refs, refs = (refs[: 2 * A], refs[2 * A :]) if pair else (refs[:1], refs[1:])
-    attn_ref, dq_ref, own_ref, carry_ref, q_all, da_all, kv, kvcat = refs
-    SEG = q_refs[0].shape[0]
+    attn_ref, dq_ref, own_ref, carry_ref, cot_ref, q_all, da_all, kv, kvcat = refs
+    SEG = qdag_refs[0].shape[0]
     parts = SEG // BLOCK
     count = 2 * SEG + R * BLOCK
     seg = lax.axis_index("seg")
     a, b = seg // B, seg % B
     for m in range(A):
-        q_all[m] = q_refs[m][...]
-        da_all[m] = dag_refs[m][:, :DH]
+        q_all[m] = qdag_refs[m][:, :DH]
+        da_all[m] = qdag_refs[m][:, DH : 2 * DH]
+        cot_ref[m] = qdag_refs[m][:, 2 * DH :]
     if pair:
         for i in range(2 * A):
             for part in range(parts):
@@ -137,8 +139,8 @@
 
 
 def project_body(A, B, H, *refs):
-    attns, gs, weight_ref, refs = refs[:A], refs[A : A + H], refs[A + H], refs[A + H + 1 :]
-    keep_ref, send_ref, *proj_refs = refs[:-3]
+    attns, gs, weight_ref, refs = refs[:A], refs[A : A + H], refs[A + H], refs[A + H + 2 :]
+    keep_ref, pass_ref, send_ref, *proj_refs = refs[:-3]
     own, mixed, cots = refs[-3:]
     seg = lax.axis_index("seg")
     a, b = seg // B, seg % B
@@ -149,11 +151,12 @@
         own[:, head] = attns[m][m]
         for i in range(A):
             mixed[(m ^ i) * SEG : (m ^ i) * SEG + SEG, head] = attns[m][i]
-    width = keep_ref.shape[1] // (H // 2)
-    for k in range(0, H, 2):
+    width = keep_ref.shape[1]
+    keep_ref[...] = dot(own[...], weight_ref[:, lanes(h, width)], (1, 0))
+    pass_ref[...] = dot(own[...], weight_ref[:, lanes(h ^ 2, width)], (1, 0))
+    for k in (1, 3):
         at = k // 2 * width
-        keep_ref[:, at : at + width] = dot(own[...], weight_ref[:, lanes(h ^ k, width)], (1, 0))
-        send_ref[:, at : at + width] = dot(own[...], weight_ref[:, lanes(h ^ (k + 1), width)], (1, 0)).astype(BF16)
+        send_ref[:, at : at + width] = dot(own[...], weight_ref[:, lanes(h ^ k, width)], (1, 0)).astype(BF16)
     piece = gs[0].shape[2]
     for k in range(H):
         for m in range(A):
@@ -173,11 +176,13 @@
 
 
 def place_body(A, B, *refs):
-    pieces, outs = refs[:A], refs[A:]
+    pieces, terms, projs, outs = refs[:A], refs[A : A + 3], refs[A + 3 : -5], refs[-5:]
     a = lax.axis_index("seg") // B
     for m in range(A):
         for i in range(3):
-            outs[i][:, lanes(a ^ m, DH)] = pieces[m][:, i * DH : (i + 1) * DH]
+            outs[1 + i][:, lanes(a ^ m, DH)] = pieces[m][:, i * DH : (i + 1) * DH]
+    outs[0][...] = sum(term[...].astype(F32) for term in terms).astype(BF16)
+    outs[4][...] = sum(term[...].astype(F32) for term in projs)
 
 
 def per_device(queries, keys, values, out_grad, out_weight, retr_owner, retr_block):
@@ -198,89 +203,92 @@
     def over_head(x, k):
         return lax.ppermute(x, "head", [(i, i ^ k) for i in range(H)])
 
-    def over_heads(x):
-        parts = {0: x}
-        for bit in (2, 1):
-            parts |= {k | bit: over_head(parts[k], bit) for k in sorted(parts)}
-        return [parts[k] for k in range(H)]
-
-    grads = over_heads(out_grad)
+    def exchange(pieces):
+        moved = {m: over_a(pieces[m], m) for m in reversed(range(1, A))}
+        return [pieces[0]] + [moved[m] for m in range(1, A)]
+
+    def direct(x):
+        return [x] + [over_head(x, k) for k in range(1, H)]
+
+    grads = direct(out_grad)
     cut = call(
         functools.partial(cut_body, A, B),
-        [shape((SEG, 2 * DH), BF16)] * A + [shape((SEG, DH), BF16)] * A,
-        [queries, keys, values],
-    )
-    kvs = [cut[0]] + [over_a(cut[m], m) for m in range(1, A)]
-    qs = [cut[A]] + [over_a(cut[A + m], m) for m in range(1, A)]
+        [shape((SEG, 2 * DH), BF16)] * A,
+        [keys, values],
+        limit=60,
+    )
+    kvs = exchange(cut)
+    sloped = call(
+        functools.partial(slope_body, A, B, H),
+        [shape((SEG, 2 * DH + width // H), BF16)] * A,
+        [*grads, out_weight, queries],
+        scratch=[pltpu.VMEM((SEG, D), BF16), pltpu.VMEM((SEG, width), BF16)],
+    )
     if B == 2:
-        kvs = kvs + [back_b(piece) for piece in kvs]
+        sloped[0], *kvs = lax.optimization_barrier((sloped[0], *kvs))
+        kvs = [*kvs, *(back_b(piece) for piece in kvs)]
     else:
         groups = [[i * B + j for j in range(B)] for i in range(A)]
-        gathered = lax.all_gather(jnp.stack(kvs), "seg", axis_index_groups=groups)
-        kvs = [gathered.reshape(B * A * (SEG // BLOCK), BLOCK, 2 * DH)]
-    dag = call(
-        functools.partial(slope_body, A, B, H),
-        [shape((SEG, 2 * DH), BF16)] * A,
-        [*grads, out_weight],
-        scratch=[pltpu.VMEM((SEG, D), BF16), pltpu.VMEM((SEG, width), BF16)],
-        flops=2 * SEG * D * width,
-    )
-    dags = [dag[0]] + [over_a(dag[m], m) for m in range(1, A)]
+        kvs = lax.all_gather(jnp.stack(kvs), "seg", axis_index_groups=groups)
+        kvs = [kvs.reshape(B * A * (SEG // BLOCK), BLOCK, 2 * DH)]
+    qdags = exchange(sloped)
     count = 2 * SEG + R * BLOCK
-    attn, dq, own, carry = call(
+    attn, dq, own, carry, cot = call(
         functools.partial(attend_body, A, B, R, score_scale),
         [
             shape((A, SEG, DH), BF16),
             shape((A, SEG, DH), BF16),
             shape((A, SEG, 2 * DH), F32),
             shape((A, SEG, 2 * DH), BF16),
+            shape((A, SEG, width // H), BF16),
         ],
-        [retr_owner, retr_block, *qs, *dags, *kvs],
-        specs=[SMEM] * 2 + [VMEM] * (2 * A + len(kvs)),
+        [retr_owner, retr_block, *qdags, *kvs],
+        specs=[SMEM] * 2 + [VMEM] * (A + len(kvs)),
         scratch=[
             pltpu.VMEM((A, SEG, DH), BF16),
             pltpu.VMEM((A, SEG, DH), BF16),
             pltpu.VMEM((2 * A * (SEG // BLOCK), BLOCK, 2 * DH), BF16),
             pltpu.VMEM((count, 2 * DH), BF16),
         ],
-        flops=10 * A * SEG * count * DH,
-    )
-    attns = [attn] + [over_a(attn, m) for m in range(1, A)]
+    )
+    attns = exchange([attn] * A)
     carried = back_b(carry)
-    gs = over_heads(jnp.stack([piece[:, DH:] for piece in dags]))
-    partials = [shape((SEG, D // 2), F32), shape((SEG, D // 2), BF16)]
+    gs = direct(cot)
+    merged = call(
+        functools.partial(merge_body, A), [shape((SEG, 3 * DH), BF16)] * A, [dq, own, carried]
+    )
+    partials = [shape((SEG, D // H), F32)] * 2 + [shape((SEG, D // 2), BF16)]
     rows = D // A
     if B == 2:
         projs = [shape((rows // 2, width), F32), shape((rows // 2, width), BF16)]
     else:
         projs = [shape((rows, width), F32)]
-    keep, send, *proj = call(
+    keep, passed, send, *proj = call(
         functools.partial(project_body, A, B, H),
         partials + projs,
-        [*attns, *gs, out_weight],
+        [*attns, *gs, out_weight, merged[0]],
+        specs=[VMEM] * (A + H + 1) + [ANY],
         scratch=[
             pltpu.VMEM((SEG, width), BF16),
             pltpu.VMEM((A * SEG, width), BF16),
             pltpu.VMEM((A * SEG, rows), BF16),
         ],
-        flops=2 * SEG * width * D + 2 * A * SEG * rows * width,
-    )
+    )
+    moved = exchange(merged)
     block = D // H
-    summed = keep + over_head(send, 1).astype(F32)
-    layer_out = (summed[:, :block] + over_head(summed[:, block:].astype(BF16), 2).astype(F32)).astype(BF16)
+    received = over_head(send, 1)
+    passed = (passed + received[:, block:].astype(F32)).astype(BF16)
     if B == 2:
-        proj_grad_t = proj[0] + back_b(proj[1]).astype(F32)
-    else:
-        proj_grad_t = lax.psum_scatter(proj[0], "seg", scatter_dimension=0, axis_index_groups=groups, tiled=True)
-    merged = call(
-        functools.partial(merge_body, A), [shape((SEG, 3 * DH), BF16)] * A, [dq, own, carried]
-    )
-    placed = call(
-        functools.partial(place_body, A, B),
-        [shape((SEG, width), BF16)] * 3,
-        [merged[0]] + [over_a(merged[m], m) for m in range(1, A)],
-    )
-    return (layer_out, *placed, proj_grad_t)
+        proj = [proj[0], back_b(proj[1])]
+    else:
+        proj = [lax.psum_scatter(proj[0], "seg", scatter_dimension=0, axis_index_groups=groups, tiled=True)]
+    return tuple(
+        call(
+            functools.partial(place_body, A, B),
+            [shape((SEG, width), BF16)] * 4 + [shape(proj[0].shape, F32)],
+            [*moved, keep, received[:, :block], over_head(passed, 2), *proj],
+        )
+    )
 
 
 def solution(mesh):

time: 125 us -> 101 us (0.81)
  waiting for transfers between devices: 55.8 us -> 44.5 us
  Pallas kernels: 22 us -> 12.1 us
  starting transfers between devices: 35.6 us -> 37.6 us
  local copies, waits for them, and re-layouts: 7.09 us -> 5.24 us
  other arithmetic: 1.86 us -> 0.06 us
    pallas_call x6, Pallas kernels: 22 us -> 12.1 us  [call(): pl.pallas_call(body, out_shape=outs, in_specs=specs or [VMEM] * len(opera...]
    ppermute x15 -> x12, waiting for transfers between devices: 44 us -> 38.7 us  [over_a(): lax.ppermute(x, 'seg', [(i, (i // B ^ m) * B + i % B) for i in range(n)])]
    ppermute x8, waiting for transfers between devices: 6.53 us -> 1.96 us  [over_head(): return lax.ppermute(x, 'head', [(i, i ^ k) for i in range(H)])]
    ppermute x15 -> x12, starting transfers between devices: 22.4 us -> 23.8 us  [over_a(): lax.ppermute(x, 'seg', [(i, (i // B ^ m) * B + i % B) for i in range(n)])]
    ppermute x6, waiting for transfers between devices: 5.18 us -> 3.8 us  [back_b(): lax.ppermute(x, 'seg', [(i, i // B * B + (i % B - 1) % B) for i in range(...]
    unnamed x70 -> x20, local copies, waits for them, and re-layouts: 6.2 us -> 5.23 us
  transfers between devices with their start and end apart: 29 -> 26, of which waited for: 13 -> 11; matrix products, arithmetic and copies ran while one was open for 3% -> 0% of each run, Pallas kernels for 18% -> 4%
where the time goes in v2:
time: 101 us; the launch traced here: 100 us
  waiting for transfers between devices  44.5 us (44%)
  starting transfers between devices  37.6 us (37%)
  Pallas kernels  12.1 us (12%)
  local copies, waits for them, and re-layouts  5.24 us (5%)
    ppermute x12, waiting for transfers between devices, over_a(): lax.ppermute(x, 'seg', [(i, (i // B ^ m) * B + i % B) for i in range(n)])  38.7 us
    ppermute x12, starting transfers between devices, over_a(): lax.ppermute(x, 'seg', [(i, (i // B ^ m) * B + i % B) for i in range(n)])  23.8 us
    pallas_call x6, Pallas kernels, call(): pl.pallas_call(body, out_shape=outs, in_specs=specs or [VMEM] * len(opera...  12.1 us
    ppermute x6, starting transfers between devices, back_b(): lax.ppermute(x, 'seg', [(i, i // B * B + (i % B - 1) % B) for i in range(...  7.48 us
    ppermute x8, starting transfers between devices, over_head(): return lax.ppermute(x, 'head', [(i, i ^ k) for i in range(H)])  6.34 us
    unnamed x20, local copies, waits for them, and re-layouts  5.23 us
    ppermute x6, waiting for transfers between devices, back_b(): lax.ppermute(x, 'seg', [(i, i // B * B + (i % B - 1) % B) for i in range(...  3.8 us
  transfers between devices with their start and end apart: 26, of which 11 were waited for; matrix products, arithmetic and copies ran while one was open for 0% of the time, Pallas kernels for 4%

profile of v2, /device:TPU:0, one launch (start us, length us, event | category | flops | bytes accessed | tf_op | source)
XLA Modules:
  0.0 100.3 jit_solution(11434483332906060352)
XLA Ops:
  0.7 3.0 %collective-permute-start.1 = (bf16[256,512]{1,0:T(8,128)(2,1)}, bf16[256,512]{1,0:T(8,128)(2,1)S(1)}, u32[]{:S(2)}, u32[]{:S(2)}) collective-permute-start(bf16[256,512]{1,0:T(8,128)(2,1)} %refs_0_.1), channel_id=1, source_target_pairs={{0,2},{1,3},{2,0},{3,1},{4,6},{5,7},{6,4},{7,5},{8,10},{9,11},{10,... | collective-permute-start | bytes 786440 | tf_op jit(solution)/shard_map/ppermute | solution.py:204
  3.9 1.9 %shard_map.111 = (bf16[256,256]{1,0:T(8,128)(2,1)}, bf16[256,256]{1,0:T(8,128)(2,1)}, bf16[256,256]{1,0:T(8,128)(2,1)}, bf16[256,256]{1,0:T(8,128)(2,1)}) custom-call(bf16[256,512]{1,0:T(8,128)(2,1)} %k_ref.1, bf16[256,512]{1,0:T(8,128)(2,1)} %v_ref.1), custom_call_target="tpu_custom_call" | custom-call | flops 1 | bytes 1 | tf_op jit(solution)/shard_map/pallas_call | solution.py:31
  5.8 2.0 %collective-permute-start.3 = (bf16[256,256]{1,0:T(8,128)(2,1)}, bf16[256,256]{1,0:T(8,128)(2,1)S(1)}, u32[]{:S(2)}, u32[]{:S(2)}) collective-permute-start(bf16[256,256]{1,0:T(8,128)(2,1)} %get-tuple-element.34), channel_id=1, source_target_pairs={{0,8},{4,12},{8,0},{12,4},{16,24},{20,28},{24,16},{28,20},{1,9},{5... | collective-permute-start | bytes 393224 | tf_op jit(solution)/shard_map/ppermute | solution.py:198
  7.8 2.6 %collective-permute-start.4 = (bf16[256,256]{1,0:T(8,128)(2,1)}, bf16[256,256]{1,0:T(8,128)(2,1)S(1)}, u32[]{:S(2)}, u32[]{:S(2)}) collective-permute-start(bf16[256,256]{1,0:T(8,128)(2,1)} %get-tuple-element.35), channel_id=1, source_target_pairs={{0,16},{4,20},{8,24},{12,28},{16,0},{20,4},{24,8},{28,12},{1,17},{... | collective-permute-start | bytes 393224 | tf_op jit(solution)/shard_map/ppermute | solution.py:198
  11.0 4.2 %collective-permute-start.5 = (bf16[256,256]{1,0:T(8,128)(2,1)}, bf16[256,256]{1,0:T(8,128)(2,1)S(1)}, u32[]{:S(2)}, u32[]{:S(2)}) collective-permute-start(bf16[256,256]{1,0:T(8,128)(2,1)} %get-tuple-element.36), channel_id=1, source_target_pairs={{0,24},{4,28},{8,16},{12,20},{16,8},{20,12},{24,0},{28,4},{1,25},{... | collective-permute-start | bytes 393224 | tf_op jit(solution)/shard_map/ppermute | solution.py:198
  15.2 1.6 %copy-done = bf16[512,2048]{1,0:T(8,128)(2,1)S(1)} copy-done((bf16[512,2048]{1,0:T(8,128)(2,1)S(1)}, bf16[512,2048]{1,0:T(8,128)(2,1)}, u32[]{:S(2)}) %copy-start) | copy-done | bytes 2097176
  16.8 0.9 copy-done.2
  17.7 0.9 copy-done.3
  18.7 1.6 %shard_map.110 = (bf16[256,384]{1,0:T(8,128)(2,1)S(1)}, bf16[256,384]{1,0:T(8,128)(2,1)}, bf16[256,384]{1,0:T(8,128)(2,1)}, bf16[256,384]{1,0:T(8,128)(2,1)}) custom-call(bf16[256,512]{1,0:T(8,128)(2,1)S(1)} %copy-done.2, bf16[256,512]{1,0:T(8,128)(2,1)S(1)} %collective-permute-done.refs_1_, bf16[256,512]{1,0:T(8,128)(2,1)S(1)} %collective-permute-done.1.refs_2_, ...), custom_call_target="tpu_custom_call" | custom-call | flops 1 | bytes 1 | tf_op jit(solution)/shard_map/pallas_call | solution.py:31
  20.7 1.5 %collective-permute-start.9 = (bf16[256,256]{1,0:T(8,128)(2,1)S(1)}, bf16[256,256]{1,0:T(8,128)(2,1)S(1)}, u32[]{:S(2)}, u32[]{:S(2)}) collective-permute-start(bf16[256,256]{1,0:T(8,128)(2,1)S(1)} %copy-done.4), channel_id=1, source_target_pairs={{0,4},{4,0},{8,12},{12,8},{16,20},{20,16},{24,28},{28,24},{1,5},{5... | collective-permute-start | bytes 393224 | tf_op jit(solution)/shard_map/ppermute | solution.py:201
  22.8 2.3 %collective-permute-start.6 = (bf16[256,384]{1,0:T(8,128)(2,1)}, bf16[256,384]{1,0:T(8,128)(2,1)S(1)}, u32[]{:S(2)}, u32[]{:S(2)}) collective-permute-start(bf16[256,384]{1,0:T(8,128)(2,1)} %get-tuple-element.38), channel_id=1, source_target_pairs={{0,8},{4,12},{8,0},{12,4},{16,24},{20,28},{24,16},{28,20},{1,9},{5... | collective-permute-start | bytes 589832 | tf_op jit(solution)/shard_map/ppermute | solution.py:198
  25.1 1.5 %collective-permute-start.7 = (bf16[256,384]{1,0:T(8,128)(2,1)}, bf16[256,384]{1,0:T(8,128)(2,1)S(1)}, u32[]{:S(2)}, u32[]{:S(2)}) collective-permute-start(bf16[256,384]{1,0:T(8,128)(2,1)} %get-tuple-element.39), channel_id=1, source_target_pairs={{0,16},{4,20},{8,24},{12,28},{16,0},{20,4},{24,8},{28,12},{1,17},{... | collective-permute-start | bytes 589832 | tf_op jit(solution)/shard_map/ppermute | solution.py:198
  26.6 1.0 collective-permute-start.8
  27.6 1.5 %collective-permute-start.11 = (bf16[256,256]{1,0:T(8,128)(2,1)S(1)}, bf16[256,256]{1,0:T(8,128)(2,1)}, u32[]{:S(2)}, u32[]{:S(2)}) collective-permute-start(bf16[256,256]{1,0:T(8,128)(2,1)S(1)} %collective-permute-done.4.refs_6_), channel_id=1, source_target_pairs={{0,4},{4,0},{8,12},{12,8},{16,20},{20,16},{24,28},{28,24},{1,5},{5... | collective-permute-start | bytes 393224 | tf_op jit(solution)/shard_map/ppermute | solution.py:201
  30.3 1.7 %collective-permute-start.12 = (bf16[256,256]{1,0:T(8,128)(2,1)S(1)}, bf16[256,256]{1,0:T(8,128)(2,1)}, u32[]{:S(2)}, u32[]{:S(2)}) collective-permute-start(bf16[256,256]{1,0:T(8,128)(2,1)S(1)} %collective-permute-done.5.refs_7_), channel_id=1, source_target_pairs={{0,4},{4,0},{8,12},{12,8},{16,20},{20,16},{24,28},{28,24},{1,5},{5... | collective-permute-start | bytes 393224 | tf_op jit(solution)/shard_map/ppermute | solution.py:201
  32.7 2.8 %collective-permute-done.12.refs_11_ = bf16[256,256]{1,0:T(8,128)(2,1)} collective-permute-done((bf16[256,256]{1,0:T(8,128)(2,1)S(1)}, bf16[256,256]{1,0:T(8,128)(2,1)}, u32[]{:S(2)}, u32[]{:S(2)}) %collective-permute-start.12) | collective-permute-done | bytes 131104 | tf_op jit(solution)/shard_map/ppermute | solution.py:201
  35.5 7.0 %collective-permute-done.7.refs_2_ = bf16[256,384]{1,0:T(8,128)(2,1)S(1)} collective-permute-done((bf16[256,384]{1,0:T(8,128)(2,1)}, bf16[256,384]{1,0:T(8,128)(2,1)S(1)}, u32[]{:S(2)}, u32[]{:S(2)}) %collective-permute-start.7) | collective-permute-done | bytes 196640 | tf_op jit(solution)/shard_map/ppermute | solution.py:198
  43.4 5.5 %shard_map.112 = (bf16[4,256,128]{2,1,0:T(8,128)(2,1)S(1)}, bf16[4,256,128]{2,1,0:T(8,128)(2,1)S(1)}, f32[4,256,256]{2,1,0:T(8,128)S(1)}, bf16[4,256,256]{2,1,0:T(8,128)(2,1)S(1)}, bf16[4,256,128]{2,1,0:T(8,128)(2,1)S(1)}) custom-call(s32[8,4]{1,0:T(8,128)S(1)} %copy.12.owner_ref, s32[8,4]{1,0:T(8,128)S(1)} %copy.13.block_ref, ...), custom_call_target="tpu_custom_call" | custom-call | flops 1 | bytes 1 | tf_op jit(solution)/shard_map/pallas_call | solution.py:31
  48.8 1.6 %collective-permute-start.13 = (bf16[4,256,256]{2,1,0:T(8,128)(2,1)S(1)}, bf16[4,256,256]{2,1,0:T(8,128)(2,1)S(1)}, u32[]{:S(2)}, u32[]{:S(2)}) collective-permute-start(bf16[4,256,256]{2,1,0:T(8,128)(2,1)S(1)} %get-tuple-element.47), channel_id=1, source_target_pairs={{0,4},{4,0},{8,12},{12,8},{16,20},{20,16},{24,28},{28,24},{1,5},{5... | collective-permute-start | bytes 1572872 | tf_op jit(solution)/shard_map/ppermute | solution.py:201
  50.4 2.1 %collective-permute-start.19 = (bf16[4,256,128]{2,1,0:T(8,128)(2,1)S(1)}, bf16[4,256,128]{2,1,0:T(8,128)(2,1)S(1)}, u32[]{:S(2)}, u32[]{:S(2)}) collective-permute-start(bf16[4,256,128]{2,1,0:T(8,128)(2,1)S(1)} %get-tuple-element.52.refs_0_), channel_id=1, source_target_pairs={{0,24},{4,28},{8,16},{12,20},{16,8},{20,12},{24,0},{28,4},{1,25},{... | collective-permute-start | bytes 786440 | tf_op jit(solution)/shard_map/ppermute | solution.py:198
  52.6 2.2 %collective-permute-start.18 = (bf16[4,256,128]{2,1,0:T(8,128)(2,1)S(1)}, bf16[4,256,128]{2,1,0:T(8,128)(2,1)S(1)}, u32[]{:S(2)}, u32[]{:S(2)}) collective-permute-start(bf16[4,256,128]{2,1,0:T(8,128)(2,1)S(1)} %get-tuple-element.52.refs_0_), channel_id=1, source_target_pairs={{0,16},{4,20},{8,24},{12,28},{16,0},{20,4},{24,8},{28,12},{1,17},{... | collective-permute-start | bytes 786440 | tf_op jit(solution)/shard_map/ppermute | solution.py:198
  54.8 6.5 %collective-permute-done.19.refs_3_ = bf16[4,256,128]{2,1,0:T(8,128)(2,1)S(1)} collective-permute-done((bf16[4,256,128]{2,1,0:T(8,128)(2,1)S(1)}, bf16[4,256,128]{2,1,0:T(8,128)(2,1)S(1)}, u32[]{:S(2)}, u32[]{:S(2)}) %collective-permute-start.19) | collective-permute-done | bytes 262176 | tf_op jit(solution)/shard_map/ppermute | solution.py:198
  61.4 1.5 %collective-permute-start.21 = (bf16[4,256,128]{2,1,0:T(8,128)(2,1)S(1)}, bf16[4,256,128]{2,1,0:T(8,128)(2,1)S(1)}, u32[]{:S(2)}, u32[]{:S(2)}) collective-permute-start(bf16[4,256,128]{2,1,0:T(8,128)(2,1)S(1)} %get-tuple-element.53.refs_4_), channel_id=1, source_target_pairs={{0,2},{1,3},{2,0},{3,1},{4,6},{5,7},{6,4},{7,5},{8,10},{9,11},{10,... | collective-permute-start | bytes 786440 | tf_op jit(solution)/shard_map/ppermute | solution.py:204
  63.0 9.9 %collective-permute-done.18.refs_2_ = bf16[4,256,128]{2,1,0:T(8,128)(2,1)S(1)} collective-permute-done((bf16[4,256,128]{2,1,0:T(8,128)(2,1)S(1)}, bf16[4,256,128]{2,1,0:T(8,128)(2,1)S(1)}, u32[]{:S(2)}, u32[]{:S(2)}) %collective-permute-start.18) | collective-permute-done | bytes 262176 | tf_op jit(solution)/shard_map/ppermute | solution.py:198
  73.0 1.6 %shard_map.114 = (f32[256,512]{1,0:T(8,128)S(1)}, f32[256,512]{1,0:T(8,128)S(1)}, bf16[256,1024]{1,0:T(8,128)(2,1)S(1)}, f32[256,512]{1,0:T(8,128)S(1)}, bf16[256,512]{1,0:T(8,128)(2,1)S(1)}) custom-call(bf16[4,256,128]{2,1,0:T(8,128)(2,1)S(1)} %get-tuple-element.52.refs_0_, bf16[4,256,128]{2,1,0:T(8,128)(2,1)S(1)} %collective-permute-done.17.refs_1_, ...), custom_call_target="tpu_custom_call" | custom-call | flops 1 | bytes 1 | tf_op jit(solution)/shard_map/pallas_call | solution.py:31
  75.3 1.3 %collective-permute-done.23 = bf16[256,1024]{1,0:T(8,128)(2,1)S(1)} collective-permute-done((bf16[256,1024]{1,0:T(8,128)(2,1)S(1)}, bf16[256,1024]{1,0:T(8,128)(2,1)S(1)}, u32[]{:S(2)}, u32[]{:S(2)}) %collective-permute-start.23) | collective-permute-done | bytes 524320 | tf_op jit(solution)/shard_map/ppermute | solution.py:204
  76.7 1.6 %collective-permute-start.24 = (bf16[256,512]{1,0:T(8,128)(2,1)S(1)}, bf16[256,512]{1,0:T(8,128)(2,1)S(1)}, u32[]{:S(2)}, u32[]{:S(2)}) collective-permute-start(bf16[256,512]{1,0:T(8,128)(2,1)S(1)} %add_convert_fusion), channel_id=1, source_target_pairs={{0,2},{1,3},{2,0},{3,1},{4,6},{5,7},{6,4},{7,5},{8,10},{9,11},{10,... | collective-permute-start | bytes 786440 | tf_op jit(solution)/shard_map/ppermute | solution.py:204
  78.3 3.5 %collective-permute-start.14 = (bf16[256,384]{1,0:T(8,128)(2,1)S(1)}, bf16[256,384]{1,0:T(8,128)(2,1)S(1)}, u32[]{:S(2)}, u32[]{:S(2)}) collective-permute-start(bf16[256,384]{1,0:T(8,128)(2,1)S(1)} %get-tuple-element.49), channel_id=1, source_target_pairs={{0,8},{4,12},{8,0},{12,4},{16,24},{20,28},{24,16},{28,20},{1,9},{5... | collective-permute-start | bytes 589832 | tf_op jit(solution)/shard_map/ppermute | solution.py:198
  81.8 2.4 %collective-permute-start.16 = (bf16[256,384]{1,0:T(8,128)(2,1)S(1)}, bf16[256,384]{1,0:T(8,128)(2,1)S(1)}, u32[]{:S(2)}, u32[]{:S(2)}) collective-permute-start(bf16[256,384]{1,0:T(8,128)(2,1)S(1)} %get-tuple-element.51), channel_id=1, source_target_pairs={{0,24},{4,28},{8,16},{12,20},{16,8},{20,12},{24,0},{28,4},{1,25},{... | collective-permute-start | bytes 589832 | tf_op jit(solution)/shard_map/ppermute | solution.py:198
  84.2 5.4 %collective-permute-done.14.refs_1_ = bf16[256,384]{1,0:T(8,128)(2,1)S(1)} collective-permute-done((bf16[256,384]{1,0:T(8,128)(2,1)S(1)}, bf16[256,384]{1,0:T(8,128)(2,1)S(1)}, u32[]{:S(2)}, u32[]{:S(2)}) %collective-permute-start.14) | collective-permute-done | bytes 196640 | tf_op jit(solution)/shard_map/ppermute | solution.py:198
  89.6 9.4 %collective-permute-done.15.refs_2_ = bf16[256,384]{1,0:T(8,128)(2,1)S(1)} collective-permute-done((bf16[256,384]{1,0:T(8,128)(2,1)S(1)}, bf16[256,384]{1,0:T(8,128)(2,1)S(1)}, u32[]{:S(2)}, u32[]{:S(2)}) %collective-permute-start.15) | collective-permute-done | bytes 196640 | tf_op jit(solution)/shard_map/ppermute | solution.py:198
  98.9 1.4 %shard_map.115 = (bf16[256,512]{1,0:T(8,128)(2,1)}, bf16[256,512]{1,0:T(8,128)(2,1)}, bf16[256,512]{1,0:T(8,128)(2,1)}, bf16[256,512]{1,0:T(8,128)(2,1)}, f32[256,512]{1,0:T(8,128)}) custom-call(bf16[256,384]{1,0:T(8,128)(2,1)S(1)} %get-tuple-element.48.refs_9_.refs_0_, bf16[256,384]{1,0:T(8,128)(2,1)S(1)} %collective-permute-done.14.refs_1_, ...), custom_call_target="tpu_custom_call" | custom-call | flops 1 | bytes 1 | tf_op jit(solution)/shard_map/pallas_call | solution.py:31
  (48 shorter events, 5.6 us)
Async XLA Ops:
  0.6 31.4 %copy-start.7 = (s32[8,4]{0,1:T(4,128)S(1)}, s32[8,4]{0,1:T(4,128)}, u32[]{:S(2)}) copy-start(s32[8,4]{0,1:T(4,128)} %param.12) | copy-start | bytes 388
  0.6 31.5 %copy-start.8 = (s32[8,4]{0,1:T(4,128)S(1)}, s32[8,4]{0,1:T(4,128)}, u32[]{:S(2)}) copy-start(s32[8,4]{0,1:T(4,128)} %param.13) | copy-start | bytes 388
  0.7 10.4 %collective-permute-start.1 = (bf16[256,512]{1,0:T(8,128)(2,1)}, bf16[256,512]{1,0:T(8,128)(2,1)S(1)}, u32[]{:S(2)}, u32[]{:S(2)}) collective-permute-start(bf16[256,512]{1,0:T(8,128)(2,1)} %refs_0_.1), channel_id=1, source_target_pairs={{0,2},{1,3},{2,0},{3,1},{4,6},{5,7},{6,4},{7,5},{8,10},{9,11},{10,... | collective-permute-start | bytes 786440 | tf_op jit(solution)/shard_map/ppermute | solution.py:204
  3.7 11.5 %collective-permute-start = (bf16[256,512]{1,0:T(8,128)(2,1)}, bf16[256,512]{1,0:T(8,128)(2,1)S(1)}, u32[]{:S(2)}, u32[]{:S(2)}) collective-permute-start(bf16[256,512]{1,0:T(8,128)(2,1)} %refs_0_.1), channel_id=1, source_target_pairs={{0,1},{1,0},{2,3},{3,2},{4,5},{5,4},{6,7},{7,6},{8,9},{9,8},{10,11... | collective-permute-start | bytes 786440 | tf_op jit(solution)/shard_map/ppermute | solution.py:204
  3.7 11.5 %collective-permute-start.2 = (bf16[256,512]{1,0:T(8,128)(2,1)}, bf16[256,512]{1,0:T(8,128)(2,1)S(1)}, u32[]{:S(2)}, u32[]{:S(2)}) collective-permute-start(bf16[256,512]{1,0:T(8,128)(2,1)} %refs_0_.1), channel_id=1, source_target_pairs={{0,3},{1,2},{2,1},{3,0},{4,7},{5,6},{6,5},{7,4},{8,11},{9,10},{10,... | collective-permute-start | bytes 786440 | tf_op jit(solution)/shard_map/ppermute | solution.py:204
  5.8 14.5 %collective-permute-start.3 = (bf16[256,256]{1,0:T(8,128)(2,1)}, bf16[256,256]{1,0:T(8,128)(2,1)S(1)}, u32[]{:S(2)}, u32[]{:S(2)}) collective-permute-start(bf16[256,256]{1,0:T(8,128)(2,1)} %get-tuple-element.34), channel_id=1, source_target_pairs={{0,8},{4,12},{8,0},{12,4},{16,24},{20,28},{24,16},{28,20},{1,9},{5... | collective-permute-start | bytes 393224 | tf_op jit(solution)/shard_map/ppermute | solution.py:198
  7.8 13.0 %collective-permute-start.4 = (bf16[256,256]{1,0:T(8,128)(2,1)}, bf16[256,256]{1,0:T(8,128)(2,1)S(1)}, u32[]{:S(2)}, u32[]{:S(2)}) collective-permute-start(bf16[256,256]{1,0:T(8,128)(2,1)} %get-tuple-element.35), channel_id=1, source_target_pairs={{0,16},{4,20},{8,24},{12,28},{16,0},{20,4},{24,8},{28,12},{1,17},{... | collective-permute-start | bytes 393224 | tf_op jit(solution)/shard_map/ppermute | solution.py:198
  11.0 9.7 %collective-permute-start.5 = (bf16[256,256]{1,0:T(8,128)(2,1)}, bf16[256,256]{1,0:T(8,128)(2,1)S(1)}, u32[]{:S(2)}, u32[]{:S(2)}) collective-permute-start(bf16[256,256]{1,0:T(8,128)(2,1)} %get-tuple-element.36), channel_id=1, source_target_pairs={{0,24},{4,28},{8,16},{12,20},{16,8},{20,12},{24,0},{28,4},{1,25},{... | collective-permute-start | bytes 393224 | tf_op jit(solution)/shard_map/ppermute | solution.py:198
  15.2 1.6 %copy-start = (bf16[512,2048]{1,0:T(8,128)(2,1)S(1)}, bf16[512,2048]{1,0:T(8,128)(2,1)}, u32[]{:S(2)}) copy-start(bf16[512,2048]{1,0:T(8,128)(2,1)} %refs_8_.1) | copy-start | bytes 6291460
  16.8 0.9 copy-start.2
  18.7 2.1 %copy-start.4 = (bf16[256,256]{1,0:T(8,128)(2,1)S(1)}, bf16[256,256]{1,0:T(8,128)(2,1)}, u32[]{:S(2)}) copy-start(bf16[256,256]{1,0:T(8,128)(2,1)} %get-tuple-element.41.refs_4_) | copy-start | bytes 393220
  20.3 52.7 %copy-start.1 = (bf16[512,2048]{1,0:T(8,128)(2,1)S(1)}, bf16[512,2048]{1,0:T(8,128)(2,1)}, u32[]{:S(2)}) copy-start(bf16[512,2048]{1,0:T(8,128)(2,1)} %refs_8_.1) | copy-start | bytes 6291460
  20.7 6.8 %collective-permute-start.9 = (bf16[256,256]{1,0:T(8,128)(2,1)S(1)}, bf16[256,256]{1,0:T(8,128)(2,1)S(1)}, u32[]{:S(2)}, u32[]{:S(2)}) collective-permute-start(bf16[256,256]{1,0:T(8,128)(2,1)S(1)} %copy-done.4), channel_id=1, source_target_pairs={{0,4},{4,0},{8,12},{12,8},{16,20},{20,16},{24,28},{28,24},{1,5},{5... | collective-permute-start | bytes 393224 | tf_op jit(solution)/shard_map/ppermute | solution.py:201
  22.3 7.3 %collective-permute-start.10 = (bf16[256,256]{1,0:T(8,128)(2,1)S(1)}, bf16[256,256]{1,0:T(8,128)(2,1)S(1)}, u32[]{:S(2)}, u32[]{:S(2)}) collective-permute-start(bf16[256,256]{1,0:T(8,128)(2,1)S(1)} %collective-permute-done.3.refs_5_), channel_id=1, source_target_pairs={{0,4},{4,0},{8,12},{12,8},{16,20},{20,16},{24,28},{28,24},{1,5},{5... | collective-permute-start | bytes 393224 | tf_op jit(solution)/shard_map/ppermute | solution.py:201
  22.8 12.7 %collective-permute-start.6 = (bf16[256,384]{1,0:T(8,128)(2,1)}, bf16[256,384]{1,0:T(8,128)(2,1)S(1)}, u32[]{:S(2)}, u32[]{:S(2)}) collective-permute-start(bf16[256,384]{1,0:T(8,128)(2,1)} %get-tuple-element.38), channel_id=1, source_target_pairs={{0,8},{4,12},{8,0},{12,4},{16,24},{20,28},{24,16},{28,20},{1,9},{5... | collective-permute-start | bytes 589832 | tf_op jit(solution)/shard_map/ppermute | solution.py:198
  25.1 17.4 %collective-permute-start.7 = (bf16[256,384]{1,0:T(8,128)(2,1)}, bf16[256,384]{1,0:T(8,128)(2,1)S(1)}, u32[]{:S(2)}, u32[]{:S(2)}) collective-permute-start(bf16[256,384]{1,0:T(8,128)(2,1)} %get-tuple-element.39), channel_id=1, source_target_pairs={{0,16},{4,20},{8,24},{12,28},{16,0},{20,4},{24,8},{28,12},{1,17},{... | collective-permute-start | bytes 589832 | tf_op jit(solution)/shard_map/ppermute | solution.py:198
  26.6 15.9 %collective-permute-start.8 = (bf16[256,384]{1,0:T(8,128)(2,1)}, bf16[256,384]{1,0:T(8,128)(2,1)S(1)}, u32[]{:S(2)}, u32[]{:S(2)}) collective-permute-start(bf16[256,384]{1,0:T(8,128)(2,1)} %get-tuple-element.40), channel_id=1, source_target_pairs={{0,24},{4,28},{8,16},{12,20},{16,8},{20,12},{24,0},{28,4},{1,25},{... | collective-permute-start | bytes 589832 | tf_op jit(solution)/shard_map/ppermute | solution.py:198
  27.6 5.1 %collective-permute-start.11 = (bf16[256,256]{1,0:T(8,128)(2,1)S(1)}, bf16[256,256]{1,0:T(8,128)(2,1)}, u32[]{:S(2)}, u32[]{:S(2)}) collective-permute-start(bf16[256,256]{1,0:T(8,128)(2,1)S(1)} %collective-permute-done.4.refs_6_), channel_id=1, source_target_pairs={{0,4},{4,0},{8,12},{12,8},{16,20},{20,16},{24,28},{28,24},{1,5},{5... | collective-permute-start | bytes 393224 | tf_op jit(solution)/shard_map/ppermute | solution.py:201
  30.3 5.2 %collective-permute-start.12 = (bf16[256,256]{1,0:T(8,128)(2,1)S(1)}, bf16[256,256]{1,0:T(8,128)(2,1)}, u32[]{:S(2)}, u32[]{:S(2)}) collective-permute-start(bf16[256,256]{1,0:T(8,128)(2,1)S(1)} %collective-permute-done.5.refs_7_), channel_id=1, source_target_pairs={{0,4},{4,0},{8,12},{12,8},{16,20},{20,16},{24,28},{28,24},{1,5},{5... | collective-permute-start | bytes 393224 | tf_op jit(solution)/shard_map/ppermute | solution.py:201
  48.8 14.0 %collective-permute-start.13 = (bf16[4,256,256]{2,1,0:T(8,128)(2,1)S(1)}, bf16[4,256,256]{2,1,0:T(8,128)(2,1)S(1)}, u32[]{:S(2)}, u32[]{:S(2)}) collective-permute-start(bf16[4,256,256]{2,1,0:T(8,128)(2,1)S(1)} %get-tuple-element.47), channel_id=1, source_target_pairs={{0,4},{4,0},{8,12},{12,8},{16,20},{20,16},{24,28},{28,24},{1,5},{5... | collective-permute-start | bytes 1572872 | tf_op jit(solution)/shard_map/ppermute | solution.py:201
  50.4 10.9 %collective-permute-start.19 = (bf16[4,256,128]{2,1,0:T(8,128)(2,1)S(1)}, bf16[4,256,128]{2,1,0:T(8,128)(2,1)S(1)}, u32[]{:S(2)}, u32[]{:S(2)}) collective-permute-start(bf16[4,256,128]{2,1,0:T(8,128)(2,1)S(1)} %get-tuple-element.52.refs_0_), channel_id=1, source_target_pairs={{0,24},{4,28},{8,16},{12,20},{16,8},{20,12},{24,0},{28,4},{1,25},{... | collective-permute-start | bytes 786440 | tf_op jit(solution)/shard_map/ppermute | solution.py:198
  52.6 20.4 %collective-permute-start.18 = (bf16[4,256,128]{2,1,0:T(8,128)(2,1)S(1)}, bf16[4,256,128]{2,1,0:T(8,128)(2,1)S(1)}, u32[]{:S(2)}, u32[]{:S(2)}) collective-permute-start(bf16[4,256,128]{2,1,0:T(8,128)(2,1)S(1)} %get-tuple-element.52.refs_0_), channel_id=1, source_target_pairs={{0,16},{4,20},{8,24},{12,28},{16,0},{20,4},{24,8},{28,12},{1,17},{... | collective-permute-start | bytes 786440 | tf_op jit(solution)/shard_map/ppermute | solution.py:198
  54.7 18.2 %collective-permute-start.17 = (bf16[4,256,128]{2,1,0:T(8,128)(2,1)S(1)}, bf16[4,256,128]{2,1,0:T(8,128)(2,1)S(1)}, u32[]{:S(2)}, u32[]{:S(2)}) collective-permute-start(bf16[4,256,128]{2,1,0:T(8,128)(2,1)S(1)} %get-tuple-element.52.refs_0_), channel_id=1, source_target_pairs={{0,8},{4,12},{8,0},{12,4},{16,24},{20,28},{24,16},{28,20},{1,9},{5... | collective-permute-start | bytes 786440 | tf_op jit(solution)/shard_map/ppermute | solution.py:198
  54.8 18.2 %collective-permute-start.22 = (bf16[4,256,128]{2,1,0:T(8,128)(2,1)S(1)}, bf16[4,256,128]{2,1,0:T(8,128)(2,1)S(1)}, u32[]{:S(2)}, u32[]{:S(2)}) collective-permute-start(bf16[4,256,128]{2,1,0:T(8,128)(2,1)S(1)} %get-tuple-element.53.refs_4_), channel_id=1, source_target_pairs={{0,3},{1,2},{2,1},{3,0},{4,7},{5,6},{6,5},{7,4},{8,11},{9,10},{10,... | collective-permute-start | bytes 786440 | tf_op jit(solution)/shard_map/ppermute | solution.py:204
  61.4 11.6 %collective-permute-start.21 = (bf16[4,256,128]{2,1,0:T(8,128)(2,1)S(1)}, bf16[4,256,128]{2,1,0:T(8,128)(2,1)S(1)}, u32[]{:S(2)}, u32[]{:S(2)}) collective-permute-start(bf16[4,256,128]{2,1,0:T(8,128)(2,1)S(1)} %get-tuple-element.53.refs_4_), channel_id=1, source_target_pairs={{0,2},{1,3},{2,0},{3,1},{4,6},{5,7},{6,4},{7,5},{8,10},{9,11},{10,... | collective-permute-start | bytes 786440 | tf_op jit(solution)/shard_map/ppermute | solution.py:204
  62.9 10.1 %collective-permute-start.20 = (bf16[4,256,128]{2,1,0:T(8,128)(2,1)S(1)}, bf16[4,256,128]{2,1,0:T(8,128)(2,1)S(1)}, u32[]{:S(2)}, u32[]{:S(2)}) collective-permute-start(bf16[4,256,128]{2,1,0:T(8,128)(2,1)S(1)} %get-tuple-element.53.refs_4_), channel_id=1, source_target_pairs={{0,1},{1,0},{2,3},{3,2},{4,5},{5,4},{6,7},{7,6},{8,9},{9,8},{10,11... | collective-permute-start | bytes 786440 | tf_op jit(solution)/shard_map/ppermute | solution.py:204
  74.6 2.0 %collective-permute-start.23 = (bf16[256,1024]{1,0:T(8,128)(2,1)S(1)}, bf16[256,1024]{1,0:T(8,128)(2,1)S(1)}, u32[]{:S(2)}, u32[]{:S(2)}) collective-permute-start(bf16[256,1024]{1,0:T(8,128)(2,1)S(1)} %get-tuple-element.55), channel_id=1, source_target_pairs={{0,1},{1,0},{2,3},{3,2},{4,5},{5,4},{6,7},{7,6},{8,9},{9,8},{10,11... | collective-permute-start | bytes 1572872 | tf_op jit(solution)/shard_map/ppermute | solution.py:204
  74.7 24.2 %collective-permute-start.25 = (bf16[256,512]{1,0:T(8,128)(2,1)S(1)}, bf16[256,512]{1,0:T(8,128)(2,1)S(1)}, u32[]{:S(2)}, u32[]{:S(2)}) collective-permute-start(bf16[256,512]{1,0:T(8,128)(2,1)S(1)} %get-tuple-element.58), channel_id=1, source_target_pairs={{0,4},{4,0},{8,12},{12,8},{16,20},{20,16},{24,28},{28,24},{1,5},{5... | collective-permute-start | bytes 786440 | tf_op jit(solution)/shard_map/ppermute | solution.py:201
  76.7 22.3 %collective-permute-start.24 = (bf16[256,512]{1,0:T(8,128)(2,1)S(1)}, bf16[256,512]{1,0:T(8,128)(2,1)S(1)}, u32[]{:S(2)}, u32[]{:S(2)}) collective-permute-start(bf16[256,512]{1,0:T(8,128)(2,1)S(1)} %add_convert_fusion), channel_id=1, source_target_pairs={{0,2},{1,3},{2,0},{3,1},{4,6},{5,7},{6,4},{7,5},{8,10},{9,11},{10,... | collective-permute-start | bytes 786440 | tf_op jit(solution)/shard_map/ppermute | solution.py:204
  78.3 11.3 %collective-permute-start.14 = (bf16[256,384]{1,0:T(8,128)(2,1)S(1)}, bf16[256,384]{1,0:T(8,128)(2,1)S(1)}, u32[]{:S(2)}, u32[]{:S(2)}) collective-permute-start(bf16[256,384]{1,0:T(8,128)(2,1)S(1)} %get-tuple-element.49), channel_id=1, source_target_pairs={{0,8},{4,12},{8,0},{12,4},{16,24},{20,28},{24,16},{28,20},{1,9},{5... | collective-permute-start | bytes 589832 | tf_op jit(solution)/shard_map/ppermute | solution.py:198
  81.8 17.2 %collective-permute-start.15 = (bf16[256,384]{1,0:T(8,128)(2,1)S(1)}, bf16[256,384]{1,0:T(8,128)(2,1)S(1)}, u32[]{:S(2)}, u32[]{:S(2)}) collective-permute-start(bf16[256,384]{1,0:T(8,128)(2,1)S(1)} %get-tuple-element.50), channel_id=1, source_target_pairs={{0,16},{4,20},{8,24},{12,28},{16,0},{20,4},{24,8},{28,12},{1,17},{... | collective-permute-start | bytes 589832 | tf_op jit(solution)/shard_map/ppermute | solution.py:198
  81.8 17.2 %collective-permute-start.16 = (bf16[256,384]{1,0:T(8,128)(2,1)S(1)}, bf16[256,384]{1,0:T(8,128)(2,1)S(1)}, u32[]{:S(2)}, u32[]{:S(2)}) collective-permute-start(bf16[256,384]{1,0:T(8,128)(2,1)S(1)} %get-tuple-element.51), channel_id=1, source_target_pairs={{0,24},{4,28},{8,16},{12,20},{16,8},{20,12},{24,0},{28,4},{1,25},{... | collective-permute-start | bytes 589832 | tf_op jit(solution)/shard_map/ppermute | solution.py:198
  (3 other events, 2.5 us)

commit v3 on v2

v3 whole, which is shorter than its diff:
```python
import functools
import math

import jax
import jax.numpy as jnp
from jax import lax
from jax.experimental import pallas as pl
from jax.experimental.pallas import tpu as pltpu
from jax.sharding import PartitionSpec as P

DH = 128
BLOCK = 128
F32 = jnp.float32
BF16 = jnp.bfloat16
HIDDEN = -1e30
VMEM = pl.BlockSpec(memory_space=pltpu.VMEM)
ANY = pl.BlockSpec(memory_space=pl.ANY)
HBM = pl.BlockSpec(memory_space=pltpu.HBM)
SMEM = pl.BlockSpec(memory_space=pltpu.SMEM)


def dot(left, right, dims):
    return lax.dot_general(left, right, ((dims[:1], dims[1:]), ((), ())), preferred_element_type=F32)


def lanes(block, width):
    return pl.ds(pl.multiple_of(block * width, width), width)


def call(body, outs, operands, specs=None, scratch=(), limit=20):
    return list(pl.pallas_call(
        body,
        out_shape=outs,
        in_specs=specs or [VMEM] * len(operands),
        out_specs=[VMEM] * len(outs),
        scratch_shapes=list(scratch),
        compiler_params=pltpu.CompilerParams(vmem_limit_bytes=limit * 2**20),
        cost_estimate=pl.CostEstimate(flops=1, bytes_accessed=1, transcendentals=0),
    )(*operands))


def shape(dims, dtype):
    return jax.ShapeDtypeStruct(dims, dtype)


def cut_body(A, B, k_ref, v_ref, *outs):
    a = lax.axis_index("seg") % A
    for m in range(A):
        head = lanes(a ^ m, DH)
        outs[m][:, :DH] = k_ref[:, head]
        outs[m][:, DH:] = v_ref[:, head]


def cot_piece(full, A, B, other, half):
    total = full.shape[1]
    part, own = total // (A * 2), total // (A * B)
    if own == part:
        return full[:, lanes(half * A + other, part)]
    row = lax.broadcasted_iota(jnp.int32, (part * A, part), 0)
    col = lax.broadcasted_iota(jnp.int32, (part * A, part), 1)
    pick = (row == (col // own * A + other) * own + col % own).astype(BF16)
    return dot(full[:, lanes(half, part * A)], pick, (1, 0)).astype(BF16)


def slope_body(A, B, H, *refs):
    grads, weight_ref, q_ref, refs = refs[:H], refs[H], refs[H + 1], refs[H + 2 :]
    outs, full, mixed = refs[:A], refs[-2], refs[-1]
    a = lax.axis_index("seg") % A
    h = lax.axis_index("head")
    width = grads[0].shape[1]
    for k in range(H):
        full[:, lanes(h ^ k, width)] = grads[k][...]
    mixed[...] = dot(full[...], weight_ref[...], (1, 1)).astype(BF16)
    for m in range(A):
        head = lanes(a ^ m, DH)
        outs[m][:, :DH] = q_ref[:, head]
        outs[m][:, DH : 2 * DH] = mixed[:, head]
        outs[m][:, 2 * DH :] = cot_piece(full, A, B, a ^ m, h % 2)


def pack_body(A, *refs):
    for m in range(A):
        refs[A + m // (A - 1)][m % (A - 1)] = refs[m][...]


def attend_body(A, B, R, score_scale, owner_ref, block_ref, *refs):
    pair = B == 2
    piece_refs, own_refs, others, refs = refs[:A], refs[A : 2 * A], refs[2 * A : -10], refs[-10:]
    attn_ref, dq_ref, own_ref, cache_ref, carry_ref, cot_ref, q_all, da_all, kv, kvcat = refs
    SEG = piece_refs[0].shape[0]
    parts = SEG // BLOCK
    count = 2 * SEG + R * BLOCK
    seg = lax.axis_index("seg")
    a, b = seg % A, seg // A
    for m in range(A):
        q_all[m] = piece_refs[m][:, :DH]
        da_all[m] = piece_refs[m][:, DH : 2 * DH]
        cot_ref[m] = piece_refs[m][:, 2 * DH :]
    if pair:
        for m in range(A):
            for part in range(parts):
                rows = slice(part * BLOCK, (part + 1) * BLOCK)
                kv[m * parts + part] = own_refs[m][rows, :]
                kv[(A + m) * parts + part] = others[m // (A - 1)][m % (A - 1), rows, :]
    else:
        kv = others[0]

    def place(other_a, other_b):
        slot = (other_b ^ b) * A + (other_a ^ a) if pair else other_b * A + (other_a ^ a)
        return slot * parts

    def segment(m):
        seg_a = a ^ m
        s = b * A + seg_a
        prev_a = jnp.where(seg_a == 0, A - 1, seg_a - 1)
        prev_b = jnp.where(seg_a == 0, (b + B - 1) % B, b)
        far = count - SEG
        column = lax.broadcasted_iota(jnp.int32, (1, far), 1)
        hidden = (column < SEG) & (s == 0)
        for part in range(parts):
            at = part * BLOCK
            kvcat[at : at + BLOCK] = kv[place(seg_a, b) + part]
            kvcat[SEG + at : SEG + at + BLOCK] = kv[place(prev_a, prev_b) + part]
        for j in range(R):
            at = SEG + j * BLOCK
            owner, block = owner_ref[s, j], block_ref[s, j]
            kvcat[SEG + at : SEG + at + BLOCK] = kv[place(owner % A, owner // A) + jnp.maximum(block, 0)]
            hidden |= (column >= at) & (column < at + BLOCK) & (block < 0)
        bias = jnp.where(hidden, HIDDEN, 0.0)
        q, da = q_all[m], da_all[m]
        keys, values = kvcat[:, :DH], kvcat[:, DH:]
        near_keys, far_keys, near_values, far_values = keys[:SEG], keys[SEG:], values[:SEG], values[SEG:]
        row = lax.broadcasted_iota(jnp.int32, (SEG, SEG), 0)
        col = lax.broadcasted_iota(jnp.int32, (SEG, SEG), 1)
        scale = score_scale * math.log2(math.e)
        near = jnp.where(row >= col, dot(q, near_keys, (1, 1)) * scale, HIDDEN)
        rest = dot(q, far_keys, (1, 1)) * scale + bias
        top = jnp.maximum(jnp.max(near, -1, keepdims=True), jnp.max(rest, -1, keepdims=True))
        near, rest = jnp.exp2(near - top), jnp.exp2(rest - top)
        inverse = 1.0 / (jnp.sum(near, -1, keepdims=True) + jnp.sum(rest, -1, keepdims=True))
        near, rest = near * inverse, rest * inverse
        near_rounded, rounded = near.astype(BF16), rest.astype(BF16)
        attn = (dot(near_rounded, near_values, (1, 0)) + dot(rounded, far_values, (1, 0))).astype(BF16)
        attn_ref[m] = attn
        row_delta = jnp.sum(da.astype(F32) * attn.astype(F32), -1, keepdims=True)
        near_slopes = (near * (dot(da, near_values, (1, 1)) - row_delta)).astype(BF16)
        slopes = (rest * (dot(da, far_values, (1, 1)) - row_delta)).astype(BF16)
        dq_ref[m] = (score_scale * (dot(near_slopes, near_keys, (1, 0)) + dot(slopes, far_keys, (1, 0)))).astype(BF16)
        own_ref[m, :, :DH] = score_scale * dot(near_slopes, q, (0, 0))
        own_ref[m, :, DH:] = dot(near_rounded, da, (0, 0))
        dk = (score_scale * dot(slopes[:, :SEG], q, (0, 0))).astype(BF16)
        dv = dot(rounded[:, :SEG], da, (0, 0)).astype(BF16)
        cache_ref[prev_a ^ a, :, :DH] = dk
        cache_ref[prev_a ^ a, :, DH:] = dv

        @pl.when(seg_a == 0)
        def _():
            carry_ref[:, :DH] = dk
            carry_ref[:, DH:] = dv

    if pair:
        for m in range(A):
            segment(m)
    else:
        lax.fori_loop(0, A, lambda m, _: segment(m), None)


def project_body(A, B, H, *refs):
    attns, gs, weight_ref, refs = refs[:A], refs[A : A + 2], refs[A + 2], refs[A + 4 :]
    keep_ref, pass_ref, send_ref, *proj_refs = refs[:-3]
    own, mixed, cots = refs[-3:]
    seg = lax.axis_index("seg")
    a, b = seg % A, seg // A
    h = lax.axis_index("head")
    SEG = attns[0].shape[1]
    for m in range(A):
        head = lanes(a ^ m, DH)
        own[:, head] = attns[m][m]
        for i in range(A):
            mixed[(m ^ i) * SEG : (m ^ i) * SEG + SEG, head] = attns[m][i]
    width = keep_ref.shape[1]
    keep_ref[...] = dot(own[...], weight_ref[:, lanes(h, width)], (1, 0))
    pass_ref[...] = dot(own[...], weight_ref[:, lanes(h ^ 2, width)], (1, 0))
    for k in (1, 3):
        at = k // 2 * width
        send_ref[:, at : at + width] = dot(own[...], weight_ref[:, lanes(h ^ k, width)], (1, 0)).astype(BF16)
    piece = gs[0].shape[2]
    for k in range(2):
        for m in range(A):
            cots[m * SEG : (m + 1) * SEG, lanes(h % 2 ^ k, piece)] = gs[k][m]
    if B == 2:
        rows = piece
        proj_refs[0][...] = dot(cots[:, lanes(b, rows)], mixed[...], (0, 0))
        proj_refs[1][...] = dot(cots[:, lanes(1 - b, rows)], mixed[...], (0, 0)).astype(BF16)
    else:
        proj_refs[0][...] = dot(cots[...], mixed[...], (0, 0))


def merge_body(A, dq_ref, own_ref, cache_ref, carry_ref, *outs):
    a = lax.axis_index("seg") % A
    for m in range(A):
        outs[m][:, :DH] = dq_ref[m]
        late = jnp.where(a ^ m == A - 1, carry_ref[...], cache_ref[m])
        outs[m][:, DH:] = (own_ref[m] + late.astype(F32)).astype(BF16)


def place_body(A, B, *refs):
    pieces, terms, projs, outs = refs[:A], refs[A : A + 3], refs[A + 3 : -5], refs[-5:]
    a = lax.axis_index("seg") % A
    for m in range(A):
        for i in range(3):
            outs[1 + i][:, lanes(a ^ m, DH)] = pieces[m][:, i * DH : (i + 1) * DH]
    outs[0][...] = sum(term[...].astype(F32) for term in terms).astype(BF16)
    outs[4][...] = sum(term[...].astype(F32) for term in projs)


def per_device(queries, keys, values, out_grad, out_weight, retr_owner, retr_block):
    n, H = lax.axis_size("seg"), lax.axis_size("head")
    SEG, width = queries.shape
    A = width // DH
    B = n // A
    R = retr_owner.shape[1]
    D = out_weight.shape[1]
    score_scale = 1.0 / math.sqrt(DH)

    def over_a(x, m):
        return lax.ppermute(x, "seg", [(i, i // A * A + (i % A ^ m)) for i in range(n)])

    def over_b(x):
        return lax.ppermute(x, "seg", [(i, (i + A) % n) for i in range(n)])

    def back_b(x):
        return lax.ppermute(x, "seg", [(i, i - A) for i in range(A, n)])

    def over_head(x, k):
        return lax.ppermute(x, "head", [(i, i ^ k) for i in range(H)])

    def exchange(pieces):
        moved = {m: over_a(pieces[m], m) for m in reversed(range(1, A))}
        return [pieces[0]] + [moved[m] for m in range(1, A)]

    def direct(x):
        return [x] + [over_head(x, k) for k in range(1, H)]

    grads = direct(out_grad)

    cut = functools.partial(cut_body, A, B)
    kvs = exchange(call(cut, [shape((SEG, 2 * DH), BF16)] * A, [keys, values]))
    kv = call(
        functools.partial(pack_body, A), [shape((A - 1, SEG, 2 * DH), BF16), shape((1, SEG, 2 * DH), BF16)], kvs
    )
    if B == 2:
        kv = [over_b(piece) for piece in kv]
    else:
        groups = [[j * A + i for j in range(B)] for i in range(A)]
        kv = lax.all_gather(jnp.concatenate(kv), "seg", axis_index_groups=groups)
        kv = [kv.reshape(B * A * (SEG // BLOCK), BLOCK, 2 * DH)]
    sloped = call(
        functools.partial(slope_body, A, B, H),
        [shape((SEG, 2 * DH + width // 2), BF16)] * A,
        [*grads, out_weight, queries],
        scratch=[pltpu.VMEM((SEG, D), BF16), pltpu.VMEM((SEG, width), BF16)],
    )
    pieces = exchange(sloped)
    count = 2 * SEG + R * BLOCK
    attn, dq, own, cache, carry, cot = call(
        functools.partial(attend_body, A, B, R, score_scale),
        [
            shape((A, SEG, DH), BF16),
            shape((A, SEG, DH), BF16),
            shape((A, SEG, 2 * DH), F32),
            shape((A, SEG, 2 * DH), BF16),
            shape((SEG, 2 * DH), BF16),
            shape((A, SEG, width // 2), BF16),
        ],
        [retr_owner, retr_block, *pieces, *kvs, *kv],
        specs=[SMEM] * 2 + [VMEM] * (2 * A + len(kv)),
        scratch=[
            pltpu.VMEM((A, SEG, DH), BF16),
            pltpu.VMEM((A, SEG, DH), BF16),
            pltpu.VMEM((2 * A * (SEG // BLOCK), BLOCK, 2 * DH), BF16),
            pltpu.VMEM((count, 2 * DH), BF16),
        ],
    )
    attns = exchange([attn] * A)
    carried = back_b(carry)
    gs = [cot, over_head(cot, 1)]
    merged = call(
        functools.partial(merge_body, A), [shape((SEG, 3 * DH), BF16)] * A, [dq, own, cache, carried]
    )
    partials = [shape((SEG, D // H), F32)] * 2 + [shape((SEG, D // 2), BF16)]
    rows = D // A
    if B == 2:
        projs = [shape((rows // 2, width), F32), shape((rows // 2, width), BF16)]
    else:
        projs = [shape((rows, width), F32)]
    keep, passed, send, *proj = call(
        functools.partial(project_body, A, B, H),
        partials + projs,
        [*attns, *gs, out_weight, merged[0]],
        specs=[VMEM] * (A + 3) + [ANY],
        scratch=[
            pltpu.VMEM((SEG, width), BF16),
            pltpu.VMEM((A * SEG, width), BF16),
            pltpu.VMEM((A * SEG, rows), BF16),
        ],
    )
    moved = exchange(merged)
    block = D // H
    received = over_head(send, 1)
    passed = (passed + received[:, block:].astype(F32)).astype(BF16)
    if B == 2:
        proj = [proj[0], over_b(proj[1])]
    else:
        proj = [lax.psum_scatter(proj[0], "seg", scatter_dimension=0, axis_index_groups=groups, tiled=True)]
    return tuple(
        call(
            functools.partial(place_body, A, B),
            [shape((SEG, width), BF16)] * 4 + [shape(proj[0].shape, F32)],
            [*moved, keep, received[:, :block], over_head(passed, 2), *proj],
        )
    )


def solution(mesh):
    both = P("seg", "head")
    return jax.shard_map(
        per_device,
        mesh=mesh,
        in_specs=(both, both, both, both, P("head", None), P(), P()),
        out_specs=(both,) * 5,
        check_vma=False,
    )
```

time: 101 us -> 97.5 us (0.965)
  starting transfers between devices: 37.6 us -> 28.9 us
  waiting for transfers between devices: 44.5 us -> 50 us
    ppermute x18 -> x16, starting transfers between devices: 31.3 us -> 25 us  [the longest x12 18.8 us: over_a(): lax.ppermute(x, 'seg', [(i, i // A * A + (i % A ^ m)) for i in range(n)])]
    ppermute x18 -> x16, waiting for transfers between devices: 42.5 us -> 48.7 us  [the longest x12 30 us: over_a(): lax.ppermute(x, 'seg', [(i, i // A * A + (i % A ^ m)) for i in range(n)])]
    ppermute x8 -> x6, starting transfers between devices: 6.34 us -> 3.88 us  [over_head(): return lax.ppermute(x, 'head', [(i, i ^ k) for i in range(H)])]
    unnamed x20 -> x18, local copies, waits for them, and re-layouts: 5.23 us -> 5.56 us
    pallas_call x6 -> x7, Pallas kernels: 12.1 us -> 11.9 us  [call(): pl.pallas_call(body, out_shape=outs, in_specs=specs or [VMEM] * len(opera...]
  transfers between devices with their start and end apart: 26 -> 22, of which waited for: 11 -> 12; matrix products, arithmetic and copies ran while one was open for 0% -> 0% of each run, Pallas kernels for 4% -> 3%
where the time goes in v3:
time: 97.5 us; the launch traced here: 97.2 us
  waiting for transfers between devices  50 us (51%)
  starting transfers between devices  28.9 us (30%)
  Pallas kernels  11.9 us (12%)
  local copies, waits for them, and re-layouts  5.57 us (6%)
    ppermute x12, waiting for transfers between devices, over_a(): lax.ppermute(x, 'seg', [(i, i // A * A + (i % A ^ m)) for i in range(n)])  30 us
    ppermute x12, starting transfers between devices, over_a(): lax.ppermute(x, 'seg', [(i, i // A * A + (i % A ^ m)) for i in range(n)])  18.8 us
    pallas_call x7, Pallas kernels, call(): pl.pallas_call(body, out_shape=outs, in_specs=specs or [VMEM] * len(opera...  11.9 us
    ppermute x3, waiting for transfers between devices, over_b(): return lax.ppermute(x, 'seg', [(i, (i + A) % n) for i in range(n)])  11.9 us
    ppermute x1, waiting for transfers between devices, back_b(): return lax.ppermute(x, 'seg', [(i, i - A) for i in range(A, n)])  6.76 us
    unnamed x18, local copies, waits for them, and re-layouts  5.56 us
    ppermute x3, starting transfers between devices, over_b(): return lax.ppermute(x, 'seg', [(i, (i + A) % n) for i in range(n)])  4.88 us
    ppermute x6, starting transfers between devices, over_head(): return lax.ppermute(x, 'head', [(i, i ^ k) for i in range(H)])  3.88 us
  transfers between devices with their start and end apart: 22, of which 12 were waited for; matrix products, arithmetic and copies ran while one was open for 0% of the time, Pallas kernels for 3%

profile of v3, /device:TPU:0, one launch (start us, length us, event | category | flops | bytes accessed | tf_op | source)
XLA Modules:
  0.0 97.2 jit_solution(11361868932408481888)
XLA Ops:
  2.7 3.0 %collective-permute-start.6 = (bf16[256,256]{1,0:T(8,128)(2,1)S(1)}, bf16[256,256]{1,0:T(8,128)(2,1)S(1)}, u32[]{:S(2)}, u32[]{:S(2)}) collective-permute-start(bf16[256,256]{1,0:T(8,128)(2,1)S(1)} %get-tuple-element.35), channel_id=1, source_target_pairs={{0,4},{4,0},{8,12},{12,8},{16,20},{20,16},{24,28},{28,24},{1,5},{5... | collective-permute-start | bytes 393224 | tf_op jit(solution)/shard_map/ppermute | solution.py:227
  5.7 1.5 %collective-permute-start.1 = (bf16[256,512]{1,0:T(8,128)(2,1)}, bf16[256,512]{1,0:T(8,128)(2,1)S(1)}, u32[]{:S(2)}, u32[]{:S(2)}) collective-permute-start(bf16[256,512]{1,0:T(8,128)(2,1)} %refs_0_.1), channel_id=1, source_target_pairs={{0,2},{1,3},{2,0},{3,1},{4,6},{5,7},{6,4},{7,5},{8,10},{9,11},{10,... | collective-permute-start | bytes 786440 | tf_op jit(solution)/shard_map/ppermute | solution.py:236
  7.8 1.6 %collective-permute-start.7 = (bf16[256,256]{1,0:T(8,128)(2,1)S(1)}, bf16[256,256]{1,0:T(8,128)(2,1)S(1)}, u32[]{:S(2)}, u32[]{:S(2)}) collective-permute-start(bf16[256,256]{1,0:T(8,128)(2,1)S(1)} %get-tuple-element.36), channel_id=1, source_target_pairs={{0,8},{4,12},{8,0},{12,4},{16,24},{20,28},{24,16},{28,20},{1,9},{5... | collective-permute-start | bytes 393224 | tf_op jit(solution)/shard_map/ppermute | solution.py:227
  9.4 2.5 %collective-permute-start.8 = (bf16[256,256]{1,0:T(8,128)(2,1)S(1)}, bf16[256,256]{1,0:T(8,128)(2,1)S(1)}, u32[]{:S(2)}, u32[]{:S(2)}) collective-permute-start(bf16[256,256]{1,0:T(8,128)(2,1)S(1)} %get-tuple-element.37), channel_id=1, source_target_pairs={{0,12},{4,8},{8,4},{12,0},{16,28},{20,24},{24,20},{28,16},{1,13},{... | collective-permute-start | bytes 393224 | tf_op jit(solution)/shard_map/ppermute | solution.py:227
  11.9 2.3 %collective-permute-done.7.refs_2_.refs_6_ = bf16[256,256]{1,0:T(8,128)(2,1)S(1)} collective-permute-done((bf16[256,256]{1,0:T(8,128)(2,1)S(1)}, bf16[256,256]{1,0:T(8,128)(2,1)S(1)}, u32[]{:S(2)}, u32[]{:S(2)}) %collective-permute-start.7) | collective-permute-done | bytes 131104 | tf_op jit(solution)/shard_map/ppermute | solution.py:227
  14.2 1.7 %collective-permute-done.8.refs_3_.refs_7_ = bf16[256,256]{1,0:T(8,128)(2,1)S(1)} collective-permute-done((bf16[256,256]{1,0:T(8,128)(2,1)S(1)}, bf16[256,256]{1,0:T(8,128)(2,1)S(1)}, u32[]{:S(2)}, u32[]{:S(2)}) %collective-permute-start.8) | collective-permute-done | bytes 131104 | tf_op jit(solution)/shard_map/ppermute | solution.py:227
  16.7 2.7 %collective-permute-start.9 = (bf16[3,256,256]{2,1,0:T(8,128)(2,1)}, bf16[3,256,256]{2,1,0:T(8,128)(2,1)S(1)}, u32[]{:S(2)}, u32[]{:S(2)}) collective-permute-start(bf16[3,256,256]{2,1,0:T(8,128)(2,1)} %get-tuple-element.38), channel_id=1, source_target_pairs={{0,16},{4,20},{8,24},{12,28},{16,0},{20,4},{24,8},{28,12},{1,17},{... | collective-permute-start | bytes 1179656 | tf_op jit(solution)/shard_map/ppermute | solution.py:230
  19.4 1.6 %copy-done = bf16[512,2048]{1,0:T(8,128)(2,1)S(1)} copy-done((bf16[512,2048]{1,0:T(8,128)(2,1)S(1)}, bf16[512,2048]{1,0:T(8,128)(2,1)}, u32[]{:S(2)}) %copy-start) | copy-done | bytes 2097176
  22.9 1.7 %shard_map.110 = (bf16[256,512]{1,0:T(8,128)(2,1)S(1)}, bf16[256,512]{1,0:T(8,128)(2,1)}, bf16[256,512]{1,0:T(8,128)(2,1)}, bf16[256,512]{1,0:T(8,128)(2,1)}) custom-call(bf16[256,512]{1,0:T(8,128)(2,1)S(1)} %copy-done.4, bf16[256,512]{1,0:T(8,128)(2,1)S(1)} %collective-permute-done.refs_1_, bf16[256,512]{1,0:T(8,128)(2,1)S(1)} %collective-permute-done.1.refs_2_, ...), custom_call_target="tpu_custom_call" | custom-call | flops 1 | bytes 1 | tf_op jit(solution)/shard_map/pallas_call | solution.py:31
  24.6 1.5 %collective-permute-start.3 = (bf16[256,512]{1,0:T(8,128)(2,1)}, bf16[256,512]{1,0:T(8,128)(2,1)S(1)}, u32[]{:S(2)}, u32[]{:S(2)}) collective-permute-start(bf16[256,512]{1,0:T(8,128)(2,1)} %get-tuple-element.31), channel_id=1, source_target_pairs={{0,4},{4,0},{8,12},{12,8},{16,20},{20,16},{24,28},{28,24},{1,5},{5... | collective-permute-start | bytes 786440 | tf_op jit(solution)/shard_map/ppermute | solution.py:227
  26.1 1.6 %collective-permute-start.4 = (bf16[256,512]{1,0:T(8,128)(2,1)}, bf16[256,512]{1,0:T(8,128)(2,1)}, u32[]{:S(2)}, u32[]{:S(2)}) collective-permute-start(bf16[256,512]{1,0:T(8,128)(2,1)} %get-tuple-element.32), channel_id=1, source_target_pairs={{0,8},{4,12},{8,0},{12,4},{16,24},{20,28},{24,16},{28,20},{1,9},{5... | collective-permute-start | bytes 786440 | tf_op jit(solution)/shard_map/ppermute | solution.py:227
  28.1 1.6 %collective-permute-start.10 = (bf16[1,256,256]{2,1,0:T(8,128)(2,1)}, bf16[1,256,256]{2,1,0:T(8,128)(2,1)}, u32[]{:S(2)}, u32[]{:S(2)}) collective-permute-start(bf16[1,256,256]{2,1,0:T(8,128)(2,1)} %get-tuple-element.39), channel_id=1, source_target_pairs={{0,16},{4,20},{8,24},{12,28},{16,0},{20,4},{24,8},{28,12},{1,17},{... | collective-permute-start | bytes 393224 | tf_op jit(solution)/shard_map/ppermute | solution.py:230
  29.8 11.9 %collective-permute-done.10.refs_9_ = bf16[1,256,256]{2,1,0:T(8,128)(2,1)} collective-permute-done((bf16[1,256,256]{2,1,0:T(8,128)(2,1)}, bf16[1,256,256]{2,1,0:T(8,128)(2,1)}, u32[]{:S(2)}, u32[]{:S(2)}) %collective-permute-start.10) | collective-permute-done | bytes 131104 | tf_op jit(solution)/shard_map/ppermute | solution.py:230
  41.7 3.7 %collective-permute-done.4.refs_2_ = bf16[256,512]{1,0:T(8,128)(2,1)} collective-permute-done((bf16[256,512]{1,0:T(8,128)(2,1)}, bf16[256,512]{1,0:T(8,128)(2,1)}, u32[]{:S(2)}, u32[]{:S(2)}) %collective-permute-start.4) | collective-permute-done | bytes 262176 | tf_op jit(solution)/shard_map/ppermute | solution.py:227
  45.4 4.4 %collective-permute-done.5.refs_3_ = bf16[256,512]{1,0:T(8,128)(2,1)} collective-permute-done((bf16[256,512]{1,0:T(8,128)(2,1)}, bf16[256,512]{1,0:T(8,128)(2,1)}, u32[]{:S(2)}, u32[]{:S(2)}) %collective-permute-start.5) | collective-permute-done | bytes 262176 | tf_op jit(solution)/shard_map/ppermute | solution.py:227
  49.7 6.3 %shard_map.113 = (bf16[4,256,128]{2,1,0:T(8,128)(2,1)S(1)}, bf16[4,256,128]{2,1,0:T(8,128)(2,1)S(1)}, f32[4,256,256]{2,1,0:T(8,128)S(1)}, bf16[4,256,256]{2,1,0:...) custom-call(s32[8,4]{1,0:T(8,128)S(1)} %copy.12.owner_ref, s32[8,4]{1,0:T(8,128)S(1)} %copy.13.block_ref, ...), custom_call_target="tpu_custom_call" | custom-call | flops 1 | bytes 1 | tf_op jit(solution)/shard_map/pallas_call | solution.py:31
  56.2 2.4 %collective-permute-start.16 = (bf16[4,256,128]{2,1,0:T(8,128)(2,1)S(1)}, bf16[4,256,128]{2,1,0:T(8,128)(2,1)S(1)}, u32[]{:S(2)}, u32[]{:S(2)}) collective-permute-start(bf16[4,256,128]{2,1,0:T(8,128)(2,1)S(1)} %get-tuple-element.48.refs_0_), channel_id=1, source_target_pairs={{0,8},{4,12},{8,0},{12,4},{16,24},{20,28},{24,16},{28,20},{1,9},{5... | collective-permute-start | bytes 786440 | tf_op jit(solution)/shard_map/ppermute | solution.py:227
  58.5 1.1 %collective-permute-start.15 = (bf16[4,256,128]{2,1,0:T(8,128)(2,1)S(1)}, bf16[4,256,128]{2,1,0:T(8,128)(2,1)S(1)}, u32[]{:S(2)}, u32[]{:S(2)}) collective-permute-start(bf16[4,256,128]{2,1,0:T(8,128)(2,1)S(1)} %get-tuple-element.48.refs_0_), channel_id=1, source_target_pairs={{0,4},{4,0},{8,12},{12,8},{16,20},{20,16},{24,28},{28,24},{1,5},{5... | collective-permute-start | bytes 786440 | tf_op jit(solution)/shard_map/ppermute | solution.py:227
  59.7 1.3 %collective-permute-start.11 = (bf16[256,256]{1,0:T(8,128)(2,1)S(1)}, bf16[256,256]{1,0:T(8,128)(2,1)S(1)}, u32[]{:S(2)}, u32[]{:S(2)}) collective-permute-start(bf16[256,256]{1,0:T(8,128)(2,1)S(1)} %get-tuple-element.43), channel_id=1, source_target_pairs={{16,0},{20,4},{24,8},{28,12},{17,1},{21,5},{25,9},{29,13},{18,2},{... | collective-permute-start | bytes 393224 | tf_op jit(solution)/shard_map/ppermute | solution.py:233
  61.0 6.8 %collective-permute-done.11.carry_ref = bf16[256,256]{1,0:T(8,128)(2,1)S(1)} collective-permute-done((bf16[256,256]{1,0:T(8,128)(2,1)S(1)}, bf16[256,256]{1,0:T(8,128)(2,1)S(1)}, u32[]{:S(2)}, u32[]{:S(2)}) %collective-permute-start.11) | collective-permute-done | bytes 131104 | tf_op jit(solution)/shard_map/ppermute | solution.py:233
  67.9 1.2 %collective-permute-done.17.refs_3_ = bf16[4,256,128]{2,1,0:T(8,128)(2,1)S(1)} collective-permute-done((bf16[4,256,128]{2,1,0:T(8,128)(2,1)S(1)}, bf16[4,256,128]{2,1,0:T(8,128)(2,1)S(1)}, u32[]{:S(2)}, u32[]{:S(2)}) %collective-permute-start.17) | collective-permute-done | bytes 262176 | tf_op jit(solution)/shard_map/ppermute | solution.py:227
  69.0 4.6 %collective-permute-done.16.refs_2_ = bf16[4,256,128]{2,1,0:T(8,128)(2,1)S(1)} collective-permute-done((bf16[4,256,128]{2,1,0:T(8,128)(2,1)S(1)}, bf16[4,256,128]{2,1,0:T(8,128)(2,1)S(1)}, u32[]{:S(2)}, u32[]{:S(2)}) %collective-permute-start.16) | collective-permute-done | bytes 262176 | tf_op jit(solution)/shard_map/ppermute | solution.py:227
  73.7 1.5 %shard_map.115 = (f32[256,512]{1,0:T(8,128)S(1)}, f32[256,512]{1,0:T(8,128)S(1)}, bf16[256,1024]{1,0:T(8,128)(2,1)S(1)}, f32[256,512]{1,0:T(8,128)S(1)}, bf16[256,512]{1,0:T(8,128)(2,1)S(1)}) custom-call(bf16[4,256,128]{2,1,0:T(8,128)(2,1)S(1)} %get-tuple-element.48.refs_0_, bf16[4,256,128]{2,1,0:T(8,128)(2,1)S(1)} %collective-permute-done.15.refs_1_, ...), custom_call_target="tpu_custom_call" | custom-call | flops 1 | bytes 1 | tf_op jit(solution)/shard_map/pallas_call | solution.py:31
  75.8 1.3 %collective-permute-done.19 = bf16[256,1024]{1,0:T(8,128)(2,1)S(1)} collective-permute-done((bf16[256,1024]{1,0:T(8,128)(2,1)S(1)}, bf16[256,1024]{1,0:T(8,128)(2,1)S(1)}, u32[]{:S(2)}, u32[]{:S(2)}) %collective-permute-start.19) | collective-permute-done | bytes 524320 | tf_op jit(solution)/shard_map/ppermute | solution.py:236
  77.2 1.6 %collective-permute-start.20 = (bf16[256,512]{1,0:T(8,128)(2,1)S(1)}, bf16[256,512]{1,0:T(8,128)(2,1)S(1)}, u32[]{:S(2)}, u32[]{:S(2)}) collective-permute-start(bf16[256,512]{1,0:T(8,128)(2,1)S(1)} %add_convert_fusion), channel_id=1, source_target_pairs={{0,2},{1,3},{2,0},{3,1},{4,6},{5,7},{6,4},{7,5},{8,10},{9,11},{10,... | collective-permute-start | bytes 786440 | tf_op jit(solution)/shard_map/ppermute | solution.py:236
  78.8 1.1 %collective-permute-start.12 = (bf16[256,384]{1,0:T(8,128)(2,1)S(1)}, bf16[256,384]{1,0:T(8,128)(2,1)S(1)}, u32[]{:S(2)}, u32[]{:S(2)}) collective-permute-start(bf16[256,384]{1,0:T(8,128)(2,1)S(1)} %get-tuple-element.45), channel_id=1, source_target_pairs={{0,4},{4,0},{8,12},{12,8},{16,20},{20,16},{24,28},{28,24},{1,5},{5... | collective-permute-start | bytes 589832 | tf_op jit(solution)/shard_map/ppermute | solution.py:227
  79.9 2.5 %collective-permute-start.13 = (bf16[256,384]{1,0:T(8,128)(2,1)S(1)}, bf16[256,384]{1,0:T(8,128)(2,1)S(1)}, u32[]{:S(2)}, u32[]{:S(2)}) collective-permute-start(bf16[256,384]{1,0:T(8,128)(2,1)S(1)} %get-tuple-element.46), channel_id=1, source_target_pairs={{0,8},{4,12},{8,0},{12,4},{16,24},{20,28},{24,16},{28,20},{1,9},{5... | collective-permute-start | bytes 589832 | tf_op jit(solution)/shard_map/ppermute | solution.py:227
  82.5 1.0 %collective-permute-start.14 = (bf16[256,384]{1,0:T(8,128)(2,1)S(1)}, bf16[256,384]{1,0:T(8,128)(2,1)S(1)}, u32[]{:S(2)}, u32[]{:S(2)}) collective-permute-start(bf16[256,384]{1,0:T(8,128)(2,1)S(1)} %get-tuple-element.47), channel_id=1, source_target_pairs={{0,12},{4,8},{8,4},{12,0},{16,28},{20,24},{24,20},{28,16},{1,13},{... | collective-permute-start | bytes 589832 | tf_op jit(solution)/shard_map/ppermute | solution.py:227
  83.5 2.0 %collective-permute-done.12.refs_1_ = bf16[256,384]{1,0:T(8,128)(2,1)S(1)} collective-permute-done((bf16[256,384]{1,0:T(8,128)(2,1)S(1)}, bf16[256,384]{1,0:T(8,128)(2,1)S(1)}, u32[]{:S(2)}, u32[]{:S(2)}) %collective-permute-start.12) | collective-permute-done | bytes 196640 | tf_op jit(solution)/shard_map/ppermute | solution.py:227
  85.5 5.6 %collective-permute-done.13.refs_2_ = bf16[256,384]{1,0:T(8,128)(2,1)S(1)} collective-permute-done((bf16[256,384]{1,0:T(8,128)(2,1)S(1)}, bf16[256,384]{1,0:T(8,128)(2,1)S(1)}, u32[]{:S(2)}, u32[]{:S(2)}) %collective-permute-start.13) | collective-permute-done | bytes 196640 | tf_op jit(solution)/shard_map/ppermute | solution.py:227
  91.0 4.8 %collective-permute-done.14.refs_3_ = bf16[256,384]{1,0:T(8,128)(2,1)S(1)} collective-permute-done((bf16[256,384]{1,0:T(8,128)(2,1)S(1)}, bf16[256,384]{1,0:T(8,128)(2,1)S(1)}, u32[]{:S(2)}, u32[]{:S(2)}) %collective-permute-start.14) | collective-permute-done | bytes 196640 | tf_op jit(solution)/shard_map/ppermute | solution.py:227
  95.9 1.4 %shard_map.116 = (bf16[256,512]{1,0:T(8,128)(2,1)}, bf16[256,512]{1,0:T(8,128)(2,1)}, bf16[256,512]{1,0:T(8,128)(2,1)}, bf16[256,512]{1,0:T(8,128)(2,1)}, f32[256,512]{1,0:T(8,128)}) custom-call(bf16[256,384]{1,0:T(8,128)(2,1)S(1)} %get-tuple-element.44.refs_7_.refs_0_, bf16[256,384]{1,0:T(8,128)(2,1)S(1)} %collective-permute-done.12.refs_1_, ...), custom_call_target="tpu_custom_call" | custom-call | flops 1 | bytes 1 | tf_op jit(solution)/shard_map/pallas_call | solution.py:31
  (39 shorter events, 7.0 us)
Async XLA Ops:
  0.6 1.0 copy-start.2
  1.6 0.9 copy-start.3
  2.6 27.0 %copy-start.6 = (s32[8,4]{0,1:T(4,128)S(1)}, s32[8,4]{0,1:T(4,128)}, u32[]{:S(2)}) copy-start(s32[8,4]{0,1:T(4,128)} %param.12) | copy-start | bytes 388
  2.6 27.1 %copy-start.7 = (s32[8,4]{0,1:T(4,128)S(1)}, s32[8,4]{0,1:T(4,128)}, u32[]{:S(2)}) copy-start(s32[8,4]{0,1:T(4,128)} %param.13) | copy-start | bytes 388
  2.7 6.8 %collective-permute-start.6 = (bf16[256,256]{1,0:T(8,128)(2,1)S(1)}, bf16[256,256]{1,0:T(8,128)(2,1)S(1)}, u32[]{:S(2)}, u32[]{:S(2)}) collective-permute-start(bf16[256,256]{1,0:T(8,128)(2,1)S(1)} %get-tuple-element.35), channel_id=1, source_target_pairs={{0,4},{4,0},{8,12},{12,8},{16,20},{20,16},{24,28},{28,24},{1,5},{5... | collective-permute-start | bytes 393224 | tf_op jit(solution)/shard_map/ppermute | solution.py:227
  5.7 13.7 %collective-permute-start.1 = (bf16[256,512]{1,0:T(8,128)(2,1)}, bf16[256,512]{1,0:T(8,128)(2,1)S(1)}, u32[]{:S(2)}, u32[]{:S(2)}) collective-permute-start(bf16[256,512]{1,0:T(8,128)(2,1)} %refs_0_.1), channel_id=1, source_target_pairs={{0,2},{1,3},{2,0},{3,1},{4,6},{5,7},{6,4},{7,5},{8,10},{9,11},{10,... | collective-permute-start | bytes 786440 | tf_op jit(solution)/shard_map/ppermute | solution.py:236
  7.2 12.2 %collective-permute-start = (bf16[256,512]{1,0:T(8,128)(2,1)}, bf16[256,512]{1,0:T(8,128)(2,1)S(1)}, u32[]{:S(2)}, u32[]{:S(2)}) collective-permute-start(bf16[256,512]{1,0:T(8,128)(2,1)} %refs_0_.1), channel_id=1, source_target_pairs={{0,1},{1,0},{2,3},{3,2},{4,5},{5,4},{6,7},{7,6},{8,9},{9,8},{10,11... | collective-permute-start | bytes 786440 | tf_op jit(solution)/shard_map/ppermute | solution.py:236
  7.2 12.2 %collective-permute-start.2 = (bf16[256,512]{1,0:T(8,128)(2,1)}, bf16[256,512]{1,0:T(8,128)(2,1)S(1)}, u32[]{:S(2)}, u32[]{:S(2)}) collective-permute-start(bf16[256,512]{1,0:T(8,128)(2,1)} %refs_0_.1), channel_id=1, source_target_pairs={{0,3},{1,2},{2,1},{3,0},{4,7},{5,6},{6,5},{7,4},{8,11},{9,10},{10,... | collective-permute-start | bytes 786440 | tf_op jit(solution)/shard_map/ppermute | solution.py:236
  7.8 6.4 %collective-permute-start.7 = (bf16[256,256]{1,0:T(8,128)(2,1)S(1)}, bf16[256,256]{1,0:T(8,128)(2,1)S(1)}, u32[]{:S(2)}, u32[]{:S(2)}) collective-permute-start(bf16[256,256]{1,0:T(8,128)(2,1)S(1)} %get-tuple-element.36), channel_id=1, source_target_pairs={{0,8},{4,12},{8,0},{12,4},{16,24},{20,28},{24,16},{28,20},{1,9},{5... | collective-permute-start | bytes 393224 | tf_op jit(solution)/shard_map/ppermute | solution.py:227
  9.4 6.4 %collective-permute-start.8 = (bf16[256,256]{1,0:T(8,128)(2,1)S(1)}, bf16[256,256]{1,0:T(8,128)(2,1)S(1)}, u32[]{:S(2)}, u32[]{:S(2)}) collective-permute-start(bf16[256,256]{1,0:T(8,128)(2,1)S(1)} %get-tuple-element.37), channel_id=1, source_target_pairs={{0,12},{4,8},{8,4},{12,0},{16,28},{20,24},{24,20},{28,16},{1,13},{... | collective-permute-start | bytes 393224 | tf_op jit(solution)/shard_map/ppermute | solution.py:227
  16.7 33.1 %collective-permute-start.9 = (bf16[3,256,256]{2,1,0:T(8,128)(2,1)}, bf16[3,256,256]{2,1,0:T(8,128)(2,1)S(1)}, u32[]{:S(2)}, u32[]{:S(2)}) collective-permute-start(bf16[3,256,256]{2,1,0:T(8,128)(2,1)} %get-tuple-element.38), channel_id=1, source_target_pairs={{0,16},{4,20},{8,24},{12,28},{16,0},{20,4},{24,8},{28,12},{1,17},{... | collective-permute-start | bytes 1179656 | tf_op jit(solution)/shard_map/ppermute | solution.py:230
  19.4 1.6 %copy-start = (bf16[512,2048]{1,0:T(8,128)(2,1)S(1)}, bf16[512,2048]{1,0:T(8,128)(2,1)}, u32[]{:S(2)}) copy-start(bf16[512,2048]{1,0:T(8,128)(2,1)} %refs_6_.1) | copy-start | bytes 6291460
  21.0 0.9 copy-start.4
  22.0 0.9 copy-start.5
  24.6 49.1 %copy-start.1 = (bf16[512,2048]{1,0:T(8,128)(2,1)S(1)}, bf16[512,2048]{1,0:T(8,128)(2,1)}, u32[]{:S(2)}) copy-start(bf16[512,2048]{1,0:T(8,128)(2,1)} %refs_6_.1) | copy-start | bytes 6291460
  24.6 17.1 %collective-permute-start.3 = (bf16[256,512]{1,0:T(8,128)(2,1)}, bf16[256,512]{1,0:T(8,128)(2,1)S(1)}, u32[]{:S(2)}, u32[]{:S(2)}) collective-permute-start(bf16[256,512]{1,0:T(8,128)(2,1)} %get-tuple-element.31), channel_id=1, source_target_pairs={{0,4},{4,0},{8,12},{12,8},{16,20},{20,16},{24,28},{28,24},{1,5},{5... | collective-permute-start | bytes 786440 | tf_op jit(solution)/shard_map/ppermute | solution.py:227
  26.1 19.3 %collective-permute-start.4 = (bf16[256,512]{1,0:T(8,128)(2,1)}, bf16[256,512]{1,0:T(8,128)(2,1)}, u32[]{:S(2)}, u32[]{:S(2)}) collective-permute-start(bf16[256,512]{1,0:T(8,128)(2,1)} %get-tuple-element.32), channel_id=1, source_target_pairs={{0,8},{4,12},{8,0},{12,4},{16,24},{20,28},{24,16},{28,20},{1,9},{5... | collective-permute-start | bytes 786440 | tf_op jit(solution)/shard_map/ppermute | solution.py:227
  27.7 22.0 %collective-permute-start.5 = (bf16[256,512]{1,0:T(8,128)(2,1)}, bf16[256,512]{1,0:T(8,128)(2,1)}, u32[]{:S(2)}, u32[]{:S(2)}) collective-permute-start(bf16[256,512]{1,0:T(8,128)(2,1)} %get-tuple-element.33), channel_id=1, source_target_pairs={{0,12},{4,8},{8,4},{12,0},{16,28},{20,24},{24,20},{28,16},{1,13},{... | collective-permute-start | bytes 786440 | tf_op jit(solution)/shard_map/ppermute | solution.py:227
  28.1 13.6 %collective-permute-start.10 = (bf16[1,256,256]{2,1,0:T(8,128)(2,1)}, bf16[1,256,256]{2,1,0:T(8,128)(2,1)}, u32[]{:S(2)}, u32[]{:S(2)}) collective-permute-start(bf16[1,256,256]{2,1,0:T(8,128)(2,1)} %get-tuple-element.39), channel_id=1, source_target_pairs={{0,16},{4,20},{8,24},{12,28},{16,0},{20,4},{24,8},{28,12},{1,17},{... | collective-permute-start | bytes 393224 | tf_op jit(solution)/shard_map/ppermute | solution.py:230
  56.0 17.6 %collective-permute-start.18 = (bf16[4,256,256]{2,1,0:T(8,128)(2,1)S(1)}, bf16[4,256,256]{2,1,0:T(8,128)(2,1)S(1)}, u32[]{:S(2)}, u32[]{:S(2)}) collective-permute-start(bf16[4,256,256]{2,1,0:T(8,128)(2,1)S(1)} %get-tuple-element.49.refs_4_), channel_id=1, source_target_pairs={{0,1},{1,0},{2,3},{3,2},{4,5},{5,4},{6,7},{7,6},{8,9},{9,8},{10,11... | collective-permute-start | bytes 1572872 | tf_op jit(solution)/shard_map/ppermute | solution.py:236
  56.1 12.9 %collective-permute-start.17 = (bf16[4,256,128]{2,1,0:T(8,128)(2,1)S(1)}, bf16[4,256,128]{2,1,0:T(8,128)(2,1)S(1)}, u32[]{:S(2)}, u32[]{:S(2)}) collective-permute-start(bf16[4,256,128]{2,1,0:T(8,128)(2,1)S(1)} %get-tuple-element.48.refs_0_), channel_id=1, source_target_pairs={{0,12},{4,8},{8,4},{12,0},{16,28},{20,24},{24,20},{28,16},{1,13},{... | collective-permute-start | bytes 786440 | tf_op jit(solution)/shard_map/ppermute | solution.py:227
  56.2 17.4 %collective-permute-start.16 = (bf16[4,256,128]{2,1,0:T(8,128)(2,1)S(1)}, bf16[4,256,128]{2,1,0:T(8,128)(2,1)S(1)}, u32[]{:S(2)}, u32[]{:S(2)}) collective-permute-start(bf16[4,256,128]{2,1,0:T(8,128)(2,1)S(1)} %get-tuple-element.48.refs_0_), channel_id=1, source_target_pairs={{0,8},{4,12},{8,0},{12,4},{16,24},{20,28},{24,16},{28,20},{1,9},{5... | collective-permute-start | bytes 786440 | tf_op jit(solution)/shard_map/ppermute | solution.py:227
  58.5 15.1 %collective-permute-start.15 = (bf16[4,256,128]{2,1,0:T(8,128)(2,1)S(1)}, bf16[4,256,128]{2,1,0:T(8,128)(2,1)S(1)}, u32[]{:S(2)}, u32[]{:S(2)}) collective-permute-start(bf16[4,256,128]{2,1,0:T(8,128)(2,1)S(1)} %get-tuple-element.48.refs_0_), channel_id=1, source_target_pairs={{0,4},{4,0},{8,12},{12,8},{16,20},{20,16},{24,28},{28,24},{1,5},{5... | collective-permute-start | bytes 786440 | tf_op jit(solution)/shard_map/ppermute | solution.py:227
  59.7 8.0 %collective-permute-start.11 = (bf16[256,256]{1,0:T(8,128)(2,1)S(1)}, bf16[256,256]{1,0:T(8,128)(2,1)S(1)}, u32[]{:S(2)}, u32[]{:S(2)}) collective-permute-start(bf16[256,256]{1,0:T(8,128)(2,1)S(1)} %get-tuple-element.43), channel_id=1, source_target_pairs={{16,0},{20,4},{24,8},{28,12},{17,1},{21,5},{25,9},{29,13},{18,2},{... | collective-permute-start | bytes 393224 | tf_op jit(solution)/shard_map/ppermute | solution.py:233
  75.2 2.0 %collective-permute-start.19 = (bf16[256,1024]{1,0:T(8,128)(2,1)S(1)}, bf16[256,1024]{1,0:T(8,128)(2,1)S(1)}, u32[]{:S(2)}, u32[]{:S(2)}) collective-permute-start(bf16[256,1024]{1,0:T(8,128)(2,1)S(1)} %get-tuple-element.51), channel_id=1, source_target_pairs={{0,1},{1,0},{2,3},{3,2},{4,5},{5,4},{6,7},{7,6},{8,9},{9,8},{10,11... | collective-permute-start | bytes 1572872 | tf_op jit(solution)/shard_map/ppermute | solution.py:236
  75.3 20.6 %collective-permute-start.21 = (bf16[256,512]{1,0:T(8,128)(2,1)S(1)}, bf16[256,512]{1,0:T(8,128)(2,1)S(1)}, u32[]{:S(2)}, u32[]{:S(2)}) collective-permute-start(bf16[256,512]{1,0:T(8,128)(2,1)S(1)} %get-tuple-element.54), channel_id=1, source_target_pairs={{0,16},{4,20},{8,24},{12,28},{16,0},{20,4},{24,8},{28,12},{1,17},{... | collective-permute-start | bytes 786440 | tf_op jit(solution)/shard_map/ppermute | solution.py:230
  77.2 18.6 %collective-permute-start.20 = (bf16[256,512]{1,0:T(8,128)(2,1)S(1)}, bf16[256,512]{1,0:T(8,128)(2,1)S(1)}, u32[]{:S(2)}, u32[]{:S(2)}) collective-permute-start(bf16[256,512]{1,0:T(8,128)(2,1)S(1)} %add_convert_fusion), channel_id=1, source_target_pairs={{0,2},{1,3},{2,0},{3,1},{4,6},{5,7},{6,4},{7,5},{8,10},{9,11},{10,... | collective-permute-start | bytes 786440 | tf_op jit(solution)/shard_map/ppermute | solution.py:236
  78.8 6.7 %collective-permute-start.12 = (bf16[256,384]{1,0:T(8,128)(2,1)S(1)}, bf16[256,384]{1,0:T(8,128)(2,1)S(1)}, u32[]{:S(2)}, u32[]{:S(2)}) collective-permute-start(bf16[256,384]{1,0:T(8,128)(2,1)S(1)} %get-tuple-element.45), channel_id=1, source_target_pairs={{0,4},{4,0},{8,12},{12,8},{16,20},{20,16},{24,28},{28,24},{1,5},{5... | collective-permute-start | bytes 589832 | tf_op jit(solution)/shard_map/ppermute | solution.py:227
  79.9 11.1 %collective-permute-start.13 = (bf16[256,384]{1,0:T(8,128)(2,1)S(1)}, bf16[256,384]{1,0:T(8,128)(2,1)S(1)}, u32[]{:S(2)}, u32[]{:S(2)}) collective-permute-start(bf16[256,384]{1,0:T(8,128)(2,1)S(1)} %get-tuple-element.46), channel_id=1, source_target_pairs={{0,8},{4,12},{8,0},{12,4},{16,24},{20,28},{24,16},{28,20},{1,9},{5... | collective-permute-start | bytes 589832 | tf_op jit(solution)/shard_map/ppermute | solution.py:227
  82.5 13.4 %collective-permute-start.14 = (bf16[256,384]{1,0:T(8,128)(2,1)S(1)}, bf16[256,384]{1,0:T(8,128)(2,1)S(1)}, u32[]{:S(2)}, u32[]{:S(2)}) collective-permute-start(bf16[256,384]{1,0:T(8,128)(2,1)S(1)} %get-tuple-element.47), channel_id=1, source_target_pairs={{0,12},{4,8},{8,4},{12,0},{16,28},{20,24},{24,20},{28,16},{1,13},{... | collective-permute-start | bytes 589832 | tf_op jit(solution)/shard_map/ppermute | solution.py:227

commit v4 on v3

v4 whole, which is shorter than its diff:
```python
import functools
import math

import jax
import jax.numpy as jnp
from jax import lax
from jax.experimental import pallas as pl
from jax.experimental.pallas import tpu as pltpu
from jax.sharding import PartitionSpec as P

DH = 128
BLOCK = 128
F32 = jnp.float32
BF16 = jnp.bfloat16
HIDDEN = -1e30
VMEM = pl.BlockSpec(memory_space=pltpu.VMEM)
ANY = pl.BlockSpec(memory_space=pl.ANY)
HBM = pl.BlockSpec(memory_space=pltpu.HBM)
SMEM = pl.BlockSpec(memory_space=pltpu.SMEM)


def dot(left, right, dims):
    return lax.dot_general(left, right, ((dims[:1], dims[1:]), ((), ())), preferred_element_type=F32)


def lanes(block, width):
    return pl.ds(pl.multiple_of(block * width, width), width)


def call(body, outs, operands, specs=None, scratch=(), limit=20, flops=1):
    return list(pl.pallas_call(
        body,
        out_shape=outs,
        in_specs=specs or [VMEM] * len(operands),
        out_specs=[VMEM] * len(outs),
        scratch_shapes=list(scratch),
        compiler_params=pltpu.CompilerParams(vmem_limit_bytes=limit * 2**20),
        cost_estimate=pl.CostEstimate(flops=flops, bytes_accessed=1, transcendentals=0),
    )(*operands))


def shape(dims, dtype):
    return jax.ShapeDtypeStruct(dims, dtype)


def cut_body(A, B, k_ref, v_ref, *outs):
    a = lax.axis_index("seg") % A
    for m in range(A):
        head = lanes(a ^ m, DH)
        outs[m][:, :DH] = k_ref[:, head]
        outs[m][:, DH:] = v_ref[:, head]


def cot_piece(full, A, B, H, other, h):
    total = full.shape[1]
    part, own = total // (A * H), total // (A * B)
    if own % part == 0:
        split = own // part
        return full[:, lanes(((h // split) * A + other) * split + h % split, part)]
    row = lax.broadcasted_iota(jnp.int32, (part * A, part), 0)
    col = lax.broadcasted_iota(jnp.int32, (part * A, part), 1)
    pick = (row == (col // own * A + other) * own + col % own).astype(BF16)
    return dot(full[:, lanes(h, part * A)], pick, (1, 0)).astype(BF16)


def slope_body(A, B, H, *refs):
    grads, weight_ref, q_ref, refs = refs[:H], refs[H], refs[H + 1], refs[H + 2 :]
    outs, full, mixed = refs[:A], refs[-2], refs[-1]
    a = lax.axis_index("seg") % A
    h = lax.axis_index("head")
    width = grads[0].shape[1]
    for k in range(H):
        full[:, lanes(h ^ k, width)] = grads[k][...]
    mixed[...] = dot(full[...], weight_ref[...], (1, 1)).astype(BF16)
    for m in range(A):
        head = lanes(a ^ m, DH)
        outs[m][:, :DH] = q_ref[:, head]
        outs[m][:, DH : 2 * DH] = mixed[:, head]
        outs[m][:, 2 * DH :] = cot_piece(full, A, B, H, a ^ m, h)


def pack_body(A, *refs):
    for m in range(A):
        refs[-1][A - 1 - m] = refs[m][...]


def collect_body(*refs):
    for m, ref in enumerate(refs[:-1]):
        refs[-1][m] = ref[:, 2 * DH :]


def join_body(*refs):
    for i, ref in enumerate(refs[:-1]):
        refs[-1][i] = ref[...]


def stage_body(*refs):
    half = len(refs) // 2
    for source, target in zip(refs[:half], refs[half:]):
        target[...] = source[...]


def forward_body(A, B, R, score_scale, owner_ref, block_ref, *refs):
    pair = B == 2
    piece_refs, own_refs, other_ref, refs = refs[:A][::-1], refs[A : 2 * A], refs[2 * A], refs[2 * A + 1 :]
    attn_ref, kvcat, weights_ref, kv = refs
    SEG = piece_refs[0].shape[0]
    parts = SEG // BLOCK
    count = 2 * SEG + R * BLOCK
    seg = lax.axis_index("seg")
    a, b = seg % A, seg // A
    if pair:
        for m in range(A):
            for part in range(parts):
                rows = slice(part * BLOCK, (part + 1) * BLOCK)
                kv[m * parts + part] = own_refs[m][rows, :]
                kv[(A + m) * parts + part] = other_ref[m, rows, :]
    else:
        kv = other_ref

    def place(other_a, other_b):
        slot = (other_b ^ b) * A + (other_a ^ a) if pair else other_b * A + (other_a ^ a)
        return slot * parts

    for m in range(A):
        seg_a = a ^ m
        s = b * A + seg_a
        prev_a = jnp.where(seg_a == 0, A - 1, seg_a - 1)
        prev_b = jnp.where(seg_a == 0, (b + B - 1) % B, b)
        far = count - SEG
        column = lax.broadcasted_iota(jnp.int32, (1, far), 1)
        hidden = (column < SEG) & (s == 0)
        for part in range(parts):
            at = part * BLOCK
            kvcat[m, at : at + BLOCK] = kv[place(seg_a, b) + part]
            kvcat[m, SEG + at : SEG + at + BLOCK] = kv[place(prev_a, prev_b) + part]
        for j in range(R):
            at = SEG + j * BLOCK
            owner, block = owner_ref[s, j], block_ref[s, j]
            kvcat[m, SEG + at : SEG + at + BLOCK] = kv[place(owner % A, owner // A) + jnp.maximum(block, 0)]
            hidden |= (column >= at) & (column < at + BLOCK) & (block < 0)
        bias = jnp.where(hidden, HIDDEN, 0.0)
        q = piece_refs[m][:, :DH]
        row = lax.broadcasted_iota(jnp.int32, (SEG, SEG), 0)
        col = lax.broadcasted_iota(jnp.int32, (SEG, SEG), 1)
        scale = score_scale * math.log2(math.e)
        near = jnp.where(row >= col, dot(q, kvcat[m, :SEG, :DH], (1, 1)) * scale, HIDDEN)
        rest = dot(q, kvcat[m, SEG:, :DH], (1, 1)) * scale + bias
        top = jnp.maximum(jnp.max(near, -1, keepdims=True), jnp.max(rest, -1, keepdims=True))
        near, rest = jnp.exp2(near - top), jnp.exp2(rest - top)
        inverse = 1.0 / (jnp.sum(near, -1, keepdims=True) + jnp.sum(rest, -1, keepdims=True))
        near, rest = near * inverse, rest * inverse
        weights_ref[m, :, :SEG] = near.astype(weights_ref.dtype)
        weights_ref[m, :, SEG:] = rest.astype(weights_ref.dtype)
        near, rest = near.astype(BF16), rest.astype(BF16)
        attn_ref[m] = (dot(near, kvcat[m, :SEG, DH:], (1, 0)) + dot(rest, kvcat[m, SEG:, DH:], (1, 0))).astype(BF16)


def backward_body(A, B, score_scale, attn_ref, kvcat, weights_ref, *refs):
    piece_refs, (dq_ref, own_ref, cache_ref, carry_ref) = refs[:A], refs[A:]
    SEG = piece_refs[0].shape[0]
    a = lax.axis_index("seg") % A
    for m in range(A):
        seg_a = a ^ m
        prev_a = jnp.where(seg_a == 0, A - 1, seg_a - 1)
        q, da = piece_refs[m][:, :DH], piece_refs[m][:, DH : 2 * DH]
        row_delta = jnp.sum(da.astype(F32) * attn_ref[m].astype(F32), -1, keepdims=True)
        weights = weights_ref[m]
        rounded = weights.astype(BF16)
        slopes = (weights.astype(F32) * (dot(da, kvcat[m, :, DH:], (1, 1)) - row_delta)).astype(BF16)
        dq_ref[m] = (score_scale * dot(slopes, kvcat[m, :, :DH], (1, 0))).astype(BF16)
        dk = score_scale * dot(slopes[:, : 2 * SEG], q, (0, 0))
        dv = dot(rounded[:, : 2 * SEG], da, (0, 0))
        own_ref[m, :, :DH] = dk[:SEG]
        own_ref[m, :, DH:] = dv[:SEG]
        dk, dv = dk[SEG:].astype(BF16), dv[SEG:].astype(BF16)
        cache_ref[prev_a ^ a, :, :DH] = dk
        cache_ref[prev_a ^ a, :, DH:] = dv

        @pl.when(seg_a == 0)
        def _():
            carry_ref[:, :DH] = dk
            carry_ref[:, DH:] = dv


def project_body(A, B, H, *refs):
    attns, gs, weight_ref, refs = refs[:A][::-1], refs[A : A + 2], refs[A + 2], refs[A + 4 :]
    keep_ref, pass_ref, send_ref, *proj_refs = refs[:-3]
    own, mixed, cots = refs[-3:]
    seg = lax.axis_index("seg")
    a, b = seg % A, seg // A
    h = lax.axis_index("head")
    SEG = attns[0].shape[1]
    for m in range(A):
        head = lanes(a ^ m, DH)
        own[:, head] = attns[m][m]
        for i in range(A):
            mixed[(m ^ i) * SEG : (m ^ i) * SEG + SEG, head] = attns[m][i]
    width = keep_ref.shape[1]
    keep_ref[...] = dot(own[...], weight_ref[:, lanes(h, width)], (1, 0))
    pass_ref[...] = dot(own[...], weight_ref[:, lanes(h ^ 2, width)], (1, 0))
    for k in (1, 3):
        at = k // 2 * width
        send_ref[:, at : at + width] = dot(own[...], weight_ref[:, lanes(h ^ k, width)], (1, 0)).astype(BF16)
    piece = gs[0].shape[3]
    for k in range(H):
        for m in range(A):
            cots[m * SEG : (m + 1) * SEG, lanes(h ^ k, piece)] = gs[k % 2][k // 2, m]
    if B == 2:
        rows = piece * H // 2
        proj_refs[0][...] = dot(cots[:, lanes(b, rows)], mixed[...], (0, 0))
        proj_refs[1][...] = dot(cots[:, lanes(1 - b, rows)], mixed[...], (0, 0)).astype(BF16)
    else:
        proj_refs[0][...] = dot(cots[...], mixed[...], (0, 0))


def merge_body(A, dq_ref, own_ref, cache_ref, carry_ref, *outs):
    a = lax.axis_index("seg") % A
    for m in range(A):
        outs[m][:, :DH] = dq_ref[m]
        late = jnp.where(a ^ m == A - 1, carry_ref[...], cache_ref[m])
        outs[m][:, DH:] = (own_ref[m] + late.astype(F32)).astype(BF16)


def place_body(A, B, *refs):
    pieces, projs, outs = refs[:A][::-1], refs[A:-4], refs[-4:]
    a = lax.axis_index("seg") % A
    for m in range(A):
        for i in range(3):
            outs[i][:, lanes(a ^ m, DH)] = pieces[m][:, i * DH : (i + 1) * DH]
    outs[3][...] = sum(term[...].astype(F32) for term in projs)


def per_device(queries, keys, values, out_grad, out_weight, retr_owner, retr_block):
    n, H = lax.axis_size("seg"), lax.axis_size("head")
    SEG, width = queries.shape
    A = width // DH
    B = n // A
    R = retr_owner.shape[1]
    D = out_weight.shape[1]
    score_scale = 1.0 / math.sqrt(DH)

    def over_a(x, m):
        return lax.ppermute(x, "seg", [(i, i // A * A + (i % A ^ m)) for i in range(n)])

    def over_b(x):
        return lax.ppermute(x, "seg", [(i, (i + A) % n) for i in range(n)])

    def back_b(x):
        return lax.ppermute(x, "seg", [(i, i - A) for i in range(A, n)])

    def over_head(x, k):
        return lax.ppermute(x, "head", [(i, i ^ k) for i in range(H)])

    def exchange(pieces):
        moved = {m: over_a(pieces[m], m) for m in reversed(range(1, A))}
        return [pieces[0]] + [moved[m] for m in range(1, A)]

    def direct(x):
        return [x] + [over_head(x, k) for k in range(1, H)]

    grads = direct(out_grad)

    cut = functools.partial(cut_body, A, B)
    kvs = exchange(call(cut, [shape((SEG, 2 * DH), BF16)] * A, [keys, values]))
    staged = call(stage_body, [shape(x.shape, BF16) for x in (out_weight, queries, out_grad)], [out_weight, queries, out_grad])
    kv = call(
        functools.partial(pack_body, A),
        [shape((A, SEG, 2 * DH), BF16)],
        [*kvs[::-1], staged[0]],
        specs=[VMEM] * A + [ANY],
    )[0]
    out_weight, queries, grads[0] = staged
    if B == 2:
        kv = over_b(kv)
    else:
        groups = [[j * A + i for j in range(B)] for i in range(A)]
        kv = lax.all_gather(kv, "seg", axis_index_groups=groups)
        kv = kv.reshape(B * A * (SEG // BLOCK), BLOCK, 2 * DH)
    sloped = call(
        functools.partial(slope_body, A, B, H),
        [shape((SEG, 2 * DH + width // H), BF16)] * A,
        [*grads, out_weight, queries],
        scratch=[pltpu.VMEM((SEG, D), BF16), pltpu.VMEM((SEG, width), BF16)],
        flops=10**9,
    )
    pieces = exchange(sloped)
    count = 2 * SEG + R * BLOCK
    cot = call(collect_body, [shape((A, SEG, width // H), BF16)], pieces)[0]
    far_cot = over_head(cot, 2)
    limit = 20 if B == 2 else 60
    attn, kvcat, weights = call(
        functools.partial(forward_body, A, B, R, score_scale),
        [shape((A, SEG, DH), BF16), shape((A, count, 2 * DH), BF16), shape((A, SEG, count), F32)],
        [retr_owner, retr_block, *pieces[::-1], *kvs, kv],
        specs=[SMEM] * 2 + [VMEM] * (2 * A + 1),
        scratch=[pltpu.VMEM((2 * A * (SEG // BLOCK), BLOCK, 2 * DH), BF16)],
        limit=limit,
        flops=10**11,
    )
    dq, own, cache, carry = call(
        functools.partial(backward_body, A, B, score_scale),
        [
            shape((A, SEG, DH), BF16),
            shape((A, SEG, 2 * DH), F32),
            shape((A, SEG, 2 * DH), BF16),
            shape((SEG, 2 * DH), BF16),
        ],
        [attn, kvcat, weights, *pieces],
        limit=limit,
        flops=10**11,
    )
    attns = exchange([attn] * A)
    carried = back_b(carry)
    cots = call(join_body, [shape((2, *cot.shape), BF16)], [cot, far_cot])[0]
    gs = [cots, over_head(cots, 1)]
    merged = call(
        functools.partial(merge_body, A), [shape((SEG, 3 * DH), BF16)] * A, [dq, own, cache, carried]
    )
    partials = [shape((SEG, D // H), F32)] * 2 + [shape((SEG, D // 2), BF16)]
    rows = D // A
    if B == 2:
        projs = [shape((rows // 2, width), F32), shape((rows // 2, width), BF16)]
    else:
        projs = [shape((rows, width), F32)]
    keep, passed, send, *proj = call(
        functools.partial(project_body, A, B, H),
        partials + projs,
        [*attns[::-1], *gs, out_weight, merged[0]],
        specs=[VMEM] * (A + 3) + [ANY],
        scratch=[
            pltpu.VMEM((SEG, width), BF16),
            pltpu.VMEM((A * SEG, width), BF16),
            pltpu.VMEM((A * SEG, rows), BF16),
        ],
    )
    moved = exchange(merged)
    block = D // H
    received = over_head(send, 1)
    passed = (passed + received[:, block:].astype(F32)).astype(BF16)
    if B == 2:
        proj = [proj[0], over_b(proj[1])]
    else:
        proj = [lax.psum_scatter(proj[0], "seg", scatter_dimension=0, axis_index_groups=groups, tiled=True)]
    *placed, proj_grad_t = call(
        functools.partial(place_body, A, B),
        [shape((SEG, width), BF16)] * 3 + [shape(proj[0].shape, F32)],
        [*moved[::-1], *proj],
        flops=10**11,
    )
    placed[0], keep = lax.optimization_barrier((placed[0], keep))
    layer_out = keep + received[:, :block].astype(F32) + over_head(passed, 2).astype(F32)
    return (layer_out.astype(BF16), *placed, proj_grad_t)


def solution(mesh):
    both = P("seg", "head")
    return jax.shard_map(
        per_device,
        mesh=mesh,
        in_specs=(both, both, both, both, P("head", None), P(), P()),
        out_specs=(both,) * 5,
        check_vma=False,
    )
```

time: 97.5 us -> 88.8 us (0.911)
  waiting for transfers between devices: 50 us -> 45.5 us
  starting transfers between devices: 28.9 us -> 25.6 us
  Pallas kernels: 11.9 us -> 10.1 us
    ppermute x3 -> x2, waiting for transfers between devices: 11.9 us -> 0.01 us  [over_b(): return lax.ppermute(x, 'seg', [(i, (i + A) % n) for i in range(n)])]
    ppermute x6 -> x7, waiting for transfers between devices: 1.33 us -> 5.51 us  [over_head(): return lax.ppermute(x, 'head', [(i, i ^ k) for i in range(H)])]
    ppermute x12, starting transfers between devices: 18.8 us -> 15.2 us  [over_a(): lax.ppermute(x, 'seg', [(i, i // A * A + (i % A ^ m)) for i in range(n)])]
    ppermute x12, waiting for transfers between devices: 30 us -> 32.4 us  [over_a(): lax.ppermute(x, 'seg', [(i, i // A * A + (i % A ^ m)) for i in range(n)])]
    pallas_call x7 -> x11, Pallas kernels: 11.9 us -> 10.1 us  [call(): pl.pallas_call(body, out_shape=outs, in_specs=specs or [VMEM] * len(opera...]
    ppermute x6 -> x7, starting transfers between devices: 3.88 us -> 4.28 us  [over_head(): return lax.ppermute(x, 'head', [(i, i ^ k) for i in range(H)])]
    ppermute x3 -> x2, starting transfers between devices: 4.88 us -> 4.81 us  [over_b(): return lax.ppermute(x, 'seg', [(i, (i + A) % n) for i in range(n)])]
    unnamed x18 -> x20, local copies, waits for them, and re-layouts: 5.56 us -> 5.56 us
  transfers between devices with their start and end apart: 22 -> 22, of which waited for: 12 -> 9; matrix products, arithmetic and copies ran while one was open for 0% -> 0% of each run, Pallas kernels for 3% -> 9%
where the time goes in v4:
time: 88.8 us; the launch traced here: 88.5 us
  waiting for transfers between devices  45.5 us (51%)
  starting transfers between devices  25.6 us (29%)
  Pallas kernels  10.1 us (11%)
  local copies, waits for them, and re-layouts  5.56 us (6%)
    ppermute x12, waiting for transfers between devices, over_a(): lax.ppermute(x, 'seg', [(i, i // A * A + (i % A ^ m)) for i in range(n)])  32.4 us
    ppermute x12, starting transfers between devices, over_a(): lax.ppermute(x, 'seg', [(i, i // A * A + (i % A ^ m)) for i in range(n)])  15.2 us
    pallas_call x11, Pallas kernels, call(): pl.pallas_call(body, out_shape=outs, in_specs=specs or [VMEM] * len(opera...  10.1 us
    ppermute x1, waiting for transfers between devices, back_b(): return lax.ppermute(x, 'seg', [(i, i - A) for i in range(A, n)])  7.67 us
    unnamed x20, local copies, waits for them, and re-layouts  5.56 us
    ppermute x7, waiting for transfers between devices, over_head(): return lax.ppermute(x, 'head', [(i, i ^ k) for i in range(H)])  5.51 us
    ppermute x2, starting transfers between devices, over_b(): return lax.ppermute(x, 'seg', [(i, (i + A) % n) for i in range(n)])  4.81 us
    ppermute x7, starting transfers between devices, over_head(): return lax.ppermute(x, 'head', [(i, i ^ k) for i in range(H)])  4.28 us
  transfers between devices with their start and end apart: 22, of which 9 were waited for; matrix products, arithmetic and copies ran while one was open for 0% of the time, Pallas kernels for 9%

profile of v4, /device:TPU:0, one launch (start us, length us, event | category | flops | bytes accessed | tf_op | source)
XLA Modules:
  0.0 88.5 jit_solution(1685943118330199292)
XLA Ops:
  0.6 0.9 %copy-done.5 = bf16[256,512]{1,0:T(8,128)(2,1)S(1)} copy-done((bf16[256,512]{1,0:T(8,128)(2,1)S(1)}, bf16[256,512]{1,0:T(8,128)(2,1)}, u32[]{:S(2)}) %copy-start.5) | copy-done | bytes 262168
  1.6 0.9 %copy-done.6 = bf16[256,512]{1,0:T(8,128)(2,1)S(1)} copy-done((bf16[256,512]{1,0:T(8,128)(2,1)S(1)}, bf16[256,512]{1,0:T(8,128)(2,1)}, u32[]{:S(2)}) %copy-start.6) | copy-done | bytes 262168
  2.6 3.0 %collective-permute-start.6 = (bf16[256,256]{1,0:T(8,128)(2,1)S(1)}, bf16[256,256]{1,0:T(8,128)(2,1)S(1)}, u32[]{:S(2)}, u32[]{:S(2)}) collective-permute-start(bf16[256,256]{1,0:T(8,128)(2,1)S(1)} %get-tuple-element.46), channel_id=1, source_target_pairs={{0,4},{4,0},{8,12},{12,8},{16,20},{20,16},{24,28},{28,24},{1,5},{5... | collective-permute-start | bytes 393224 | tf_op jit(solution)/shard_map/ppermute | solution.py:244
  5.7 1.6 %collective-permute-start.7 = (bf16[256,256]{1,0:T(8,128)(2,1)S(1)}, bf16[256,256]{1,0:T(8,128)(2,1)S(1)}, u32[]{:S(2)}, u32[]{:S(2)}) collective-permute-start(bf16[256,256]{1,0:T(8,128)(2,1)S(1)} %get-tuple-element.47), channel_id=1, source_target_pairs={{0,8},{4,12},{8,0},{12,4},{16,24},{20,28},{24,16},{28,20},{1,9},{5... | collective-permute-start | bytes 393224 | tf_op jit(solution)/shard_map/ppermute | solution.py:244
  7.2 1.9 %collective-permute-start.1 = (bf16[256,512]{1,0:T(8,128)(2,1)}, bf16[256,512]{1,0:T(8,128)(2,1)S(1)}, u32[]{:S(2)}, u32[]{:S(2)}) collective-permute-start(bf16[256,512]{1,0:T(8,128)(2,1)} %refs_2_.1), channel_id=1, source_target_pairs={{0,2},{1,3},{2,0},{3,1},{4,6},{5,7},{6,4},{7,5},{8,10},{9,11},{10,... | collective-permute-start | bytes 786440 | tf_op jit(solution)/shard_map/ppermute | solution.py:253
  9.4 1.6 %copy-done.2 = bf16[512,2048]{1,0:T(8,128)(2,1)S(1)} copy-done((bf16[512,2048]{1,0:T(8,128)(2,1)S(1)}, bf16[512,2048]{1,0:T(8,128)(2,1)}, u32[]{:S(2)}) %copy-start.2) | copy-done | bytes 2097176
  11.0 0.9 %copy-done.3 = bf16[256,512]{1,0:T(8,128)(2,1)S(1)} copy-done((bf16[256,512]{1,0:T(8,128)(2,1)S(1)}, bf16[256,512]{1,0:T(8,128)(2,1)}, u32[]{:S(2)}) %copy-start.3) | copy-done | bytes 262168
  12.0 0.9 %copy-done.4 = bf16[256,512]{1,0:T(8,128)(2,1)S(1)} copy-done((bf16[256,512]{1,0:T(8,128)(2,1)S(1)}, bf16[256,512]{1,0:T(8,128)(2,1)}, u32[]{:S(2)}) %copy-start.4) | copy-done | bytes 262168
  13.3 2.8 %collective-permute-start.9 = (bf16[4,256,256]{2,1,0:T(8,128)(2,1)S(1)}, bf16[4,256,256]{2,1,0:T(8,128)(2,1)S(1)}, u32[]{:S(2)}, u32[]{:S(2)}) collective-permute-start(bf16[4,256,256]{2,1,0:T(8,128)(2,1)S(1)} %shard_map.113), channel_id=1, source_target_pairs={{0,16},{4,20},{8,24},{12,28},{16,0},{20,4},{24,8},{28,12},{1,17},{... | collective-permute-start | bytes 1572872 | tf_op jit(solution)/shard_map/ppermute | solution.py:247
  16.1 0.5 collective-permute-done.1.refs_2_
  16.6 5.0 %collective-permute-done.2.refs_3_ = bf16[256,512]{1,0:T(8,128)(2,1)S(1)} collective-permute-done((bf16[256,512]{1,0:T(8,128)(2,1)}, bf16[256,512]{1,0:T(8,128)(2,1)S(1)}, u32[]{:S(2)}, u32[]{:S(2)}) %collective-permute-start.2) | collective-permute-done | bytes 262176 | tf_op jit(solution)/shard_map/ppermute | solution.py:253
  21.6 0.9 %shard_map.111 = (bf16[256,384]{1,0:T(8,128)(2,1)S(1)}, bf16[256,384]{1,0:T(8,128)(2,1)S(1)}, bf16[256,384]{1,0:T(8,128)(2,1)S(1)}, bf16[256,384]{1,0:T(8,128)(2,1)S(1)}) custom-call(bf16[256,512]{1,0:T(8,128)(2,1)S(1)} %get-tuple-element.38.refs_0_, bf16[256,512]{1,0:T(8,128)(2,1)S(1)} %collective-permute-done.refs_1_, ...), custom_call_target="tpu_custom_call" | custom-call | flops 1000000000 | bytes 1 | tf_op jit(solution)/shard_map/pallas_call | solution.py:31
  22.5 2.8 %collective-permute-start.3 = (bf16[256,384]{1,0:T(8,128)(2,1)S(1)}, bf16[256,384]{1,0:T(8,128)(2,1)S(1)}, u32[]{:S(2)}, u32[]{:S(2)}) collective-permute-start(bf16[256,384]{1,0:T(8,128)(2,1)S(1)} %get-tuple-element.41), channel_id=1, source_target_pairs={{0,12},{4,8},{8,4},{12,0},{16,28},{20,24},{24,20},{28,16},{1,13},{... | collective-permute-start | bytes 589832 | tf_op jit(solution)/shard_map/ppermute | solution.py:244
  26.3 6.1 %collective-permute-done.3.refs_0_.refs_3_ = bf16[256,384]{1,0:T(8,128)(2,1)S(1)} collective-permute-done((bf16[256,384]{1,0:T(8,128)(2,1)S(1)}, bf16[256,384]{1,0:T(8,128)(2,1)S(1)}, u32[]{:S(2)}, u32[]{:S(2)}) %collective-permute-start.3) | collective-permute-done | bytes 196640 | tf_op jit(solution)/shard_map/ppermute | solution.py:244
  32.4 12.9 %collective-permute-done.4.refs_1_.refs_2_ = bf16[256,384]{1,0:T(8,128)(2,1)S(1)} collective-permute-done((bf16[256,384]{1,0:T(8,128)(2,1)S(1)}, bf16[256,384]{1,0:T(8,128)(2,1)S(1)}, u32[]{:S(2)}, u32[]{:S(2)}) %collective-permute-start.4) | collective-permute-done | bytes 196640 | tf_op jit(solution)/shard_map/ppermute | solution.py:244
  45.3 1.4 %collective-permute-start.17 = (bf16[4,256,128]{2,1,0:T(8,128)(2,1)S(1)}, bf16[4,256,128]{2,1,0:T(8,128)(2,1)S(1)}, u32[]{:S(2)}, u32[]{:S(2)}) collective-permute-start(bf16[4,256,128]{2,1,0:T(8,128)(2,1)S(1)} %shard_map.117.refs_0_), channel_id=1, source_target_pairs={{0,2},{1,3},{2,0},{3,1},{4,6},{5,7},{6,4},{7,5},{8,10},{9,11},{10,... | collective-permute-start | bytes 786440 | tf_op jit(solution)/shard_map/ppermute | solution.py:253
  46.7 3.5 %shard_map.114 = (bf16[4,256,128]{2,1,0:T(8,128)(2,1)S(1)}, bf16[4,1024,256]{2,1,0:T(8,128)(2,1)S(1)}, f32[4,256,1024]{2,1,0:T(8,128)S(1)}) custom-call(s32[8,4]{1,0:T(8,128)S(1)} %copy.12.owner_ref, s32[8,4]{1,0:T(8,128)S(1)} %copy.13.block_ref, bf16[256,384]{1,0:T(8,128)(2,1)S(1)} %collective-permute-done.3.refs_0_.refs_3_, ...), custom_call_target="tpu_custom_call" | custom-call | flops 99999997952 | bytes 1 | tf_op jit(solution)/shard_map/pallas_call | solution.py:31
  50.3 2.3 %collective-permute-start.15 = (bf16[4,256,128]{2,1,0:T(8,128)(2,1)S(1)}, bf16[4,256,128]{2,1,0:T(8,128)(2,1)S(1)}, u32[]{:S(2)}, u32[]{:S(2)}) collective-permute-start(bf16[4,256,128]{2,1,0:T(8,128)(2,1)S(1)} %get-tuple-element.49.attn_ref.refs_3_), channel_id=1, source_target_pairs={{0,8},{4,12},{8,0},{12,4},{16,24},{20,28},{24,16},{28,20},{1,9},{5... | collective-permute-start | bytes 786440 | tf_op jit(solution)/shard_map/ppermute | solution.py:244
  52.5 1.2 %collective-permute-start.16 = (bf16[4,256,128]{2,1,0:T(8,128)(2,1)S(1)}, bf16[4,256,128]{2,1,0:T(8,128)(2,1)S(1)}, u32[]{:S(2)}, u32[]{:S(2)}) collective-permute-start(bf16[4,256,128]{2,1,0:T(8,128)(2,1)S(1)} %get-tuple-element.49.attn_ref.refs_3_), channel_id=1, source_target_pairs={{0,4},{4,0},{8,12},{12,8},{16,20},{20,16},{24,28},{28,24},{1,5},{5... | collective-permute-start | bytes 786440 | tf_op jit(solution)/shard_map/ppermute | solution.py:244
  53.9 2.4 %shard_map.115 = (bf16[4,256,128]{2,1,0:T(8,128)(2,1)S(1)}, f32[4,256,256]{2,1,0:T(8,128)S(1)}, bf16[4,256,256]{2,1,0:T(8,128)(2,1)S(1)}, bf16[256,256]{1,0:T(8,128)(2,1)S(1)}) custom-call(bf16[4,256,128]{2,1,0:T(8,128)(2,1)S(1)} %get-tuple-element.49.attn_ref.refs_3_, bf16[4,1024,256]{2,1,0:T(8,128)(2,1)S(1)} %get-tuple-element.50.kvcat, ...), custom_call_target="tpu_custom_call" | custom-call | flops 99999997952 | bytes 1 | tf_op jit(solution)/shard_map/pallas_call | solution.py:31
  56.2 1.3 %collective-permute-start.10 = (bf16[256,256]{1,0:T(8,128)(2,1)S(1)}, bf16[256,256]{1,0:T(8,128)(2,1)S(1)}, u32[]{:S(2)}, u32[]{:S(2)}) collective-permute-start(bf16[256,256]{1,0:T(8,128)(2,1)S(1)} %get-tuple-element.55), channel_id=1, source_target_pairs={{16,0},{20,4},{24,8},{28,12},{17,1},{21,5},{25,9},{29,13},{18,2},{... | collective-permute-start | bytes 393224 | tf_op jit(solution)/shard_map/ppermute | solution.py:250
  57.5 7.7 %collective-permute-done.10.carry_ref = bf16[256,256]{1,0:T(8,128)(2,1)S(1)} collective-permute-done((bf16[256,256]{1,0:T(8,128)(2,1)S(1)}, bf16[256,256]{1,0:T(8,128)(2,1)S(1)}, u32[]{:S(2)}, u32[]{:S(2)}) %collective-permute-start.10) | collective-permute-done | bytes 131104 | tf_op jit(solution)/shard_map/ppermute | solution.py:250
  65.4 1.3 %collective-permute-done.15.refs_1_ = bf16[4,256,128]{2,1,0:T(8,128)(2,1)S(1)} collective-permute-done((bf16[4,256,128]{2,1,0:T(8,128)(2,1)S(1)}, bf16[4,256,128]{2,1,0:T(8,128)(2,1)S(1)}, u32[]{:S(2)}, u32[]{:S(2)}) %collective-permute-start.15) | collective-permute-done | bytes 262176 | tf_op jit(solution)/shard_map/ppermute | solution.py:244
  66.7 1.6 %shard_map.119 = (f32[256,512]{1,0:T(8,128)S(1)}, f32[256,512]{1,0:T(8,128)S(1)}, bf16[256,1024]{1,0:T(8,128)(2,1)S(1)}, f32[256,512]{1,0:T(8,128)S(1)}, bf16[256,512]{1,0:T(8,128)(2,1)S(1)}) custom-call(bf16[4,256,128]{2,1,0:T(8,128)(2,1)S(1)} %collective-permute-done.14.refs_0_, bf16[4,256,128]{2,1,0:T(8,128)(2,1)S(1)} %collective-permute-done.15.refs_1_, ...), custom_call_target="tpu_custom_call" | custom-call | flops 1 | bytes 1 | tf_op jit(solution)/shard_map/pallas_call | solution.py:31
  68.4 2.0 %collective-permute-start.19 = (bf16[256,512]{1,0:T(8,128)(2,1)S(1)}, bf16[256,512]{1,0:T(8,128)(2,1)S(1)}, u32[]{:S(2)}, u32[]{:S(2)}) collective-permute-start(bf16[256,512]{1,0:T(8,128)(2,1)S(1)} %get-tuple-element.61), channel_id=1, source_target_pairs={{0,16},{4,20},{8,24},{12,28},{16,0},{20,4},{24,8},{28,12},{1,17},{... | collective-permute-start | bytes 786440 | tf_op jit(solution)/shard_map/ppermute | solution.py:247
  70.4 2.0 %collective-permute-start.11 = (bf16[256,384]{1,0:T(8,128)(2,1)S(1)}, bf16[256,384]{1,0:T(8,128)(2,1)S(1)}, u32[]{:S(2)}, u32[]{:S(2)}) collective-permute-start(bf16[256,384]{1,0:T(8,128)(2,1)S(1)} %get-tuple-element.56), channel_id=1, source_target_pairs={{0,12},{4,8},{8,4},{12,0},{16,28},{20,24},{24,20},{28,16},{1,13},{... | collective-permute-start | bytes 589832 | tf_op jit(solution)/shard_map/ppermute | solution.py:244
  72.7 1.2 %collective-permute-start.13 = (bf16[256,384]{1,0:T(8,128)(2,1)S(1)}, bf16[256,384]{1,0:T(8,128)(2,1)S(1)}, u32[]{:S(2)}, u32[]{:S(2)}) collective-permute-start(bf16[256,384]{1,0:T(8,128)(2,1)S(1)} %get-tuple-element.58), channel_id=1, source_target_pairs={{0,4},{4,0},{8,12},{12,8},{16,20},{20,16},{24,28},{28,24},{1,5},{5... | collective-permute-start | bytes 589832 | tf_op jit(solution)/shard_map/ppermute | solution.py:244
  73.9 0.6 collective-permute-start.21
  74.5 6.8 %collective-permute-done.11.refs_0_ = bf16[256,384]{1,0:T(8,128)(2,1)S(1)} collective-permute-done((bf16[256,384]{1,0:T(8,128)(2,1)S(1)}, bf16[256,384]{1,0:T(8,128)(2,1)S(1)}, u32[]{:S(2)}, u32[]{:S(2)}) %collective-permute-start.11) | collective-permute-done | bytes 196640 | tf_op jit(solution)/shard_map/ppermute | solution.py:244
  81.3 5.2 %collective-permute-done.12.refs_1_ = bf16[256,384]{1,0:T(8,128)(2,1)S(1)} collective-permute-done((bf16[256,384]{1,0:T(8,128)(2,1)S(1)}, bf16[256,384]{1,0:T(8,128)(2,1)S(1)}, u32[]{:S(2)}, u32[]{:S(2)}) %collective-permute-start.12) | collective-permute-done | bytes 196640 | tf_op jit(solution)/shard_map/ppermute | solution.py:244
  86.5 1.2 %shard_map.120 = (bf16[256,512]{1,0:T(8,128)(2,1)}, bf16[256,512]{1,0:T(8,128)(2,1)}, bf16[256,512]{1,0:T(8,128)(2,1)}, f32[256,512]{1,0:T(8,128)}) custom-call(bf16[256,384]{1,0:T(8,128)(2,1)S(1)} %collective-permute-done.11.refs_0_, bf16[256,384]{1,0:T(8,128)(2,1)S(1)} %collective-permute-done.12.refs_1_, ...), custom_call_target="tpu_custom_call" | custom-call | flops 99999997952 | bytes 1 | tf_op jit(solution)/shard_map/pallas_call | solution.py:31
  87.7 0.8 add_convert_fusion
  (45 shorter events, 2.6 us)
Async XLA Ops:
  0.6 1.0 %copy-start.5 = (bf16[256,512]{1,0:T(8,128)(2,1)S(1)}, bf16[256,512]{1,0:T(8,128)(2,1)}, u32[]{:S(2)}) copy-start(bf16[256,512]{1,0:T(8,128)(2,1)} %k_ref.1) | copy-start | bytes 786436
  1.6 0.9 %copy-start.6 = (bf16[256,512]{1,0:T(8,128)(2,1)S(1)}, bf16[256,512]{1,0:T(8,128)(2,1)}, u32[]{:S(2)}) copy-start(bf16[256,512]{1,0:T(8,128)(2,1)} %v_ref.1) | copy-start | bytes 786436
  2.6 6.5 %collective-permute-start.6 = (bf16[256,256]{1,0:T(8,128)(2,1)S(1)}, bf16[256,256]{1,0:T(8,128)(2,1)S(1)}, u32[]{:S(2)}, u32[]{:S(2)}) collective-permute-start(bf16[256,256]{1,0:T(8,128)(2,1)S(1)} %get-tuple-element.46), channel_id=1, source_target_pairs={{0,4},{4,0},{8,12},{12,8},{16,20},{20,16},{24,28},{28,24},{1,5},{5... | collective-permute-start | bytes 393224 | tf_op jit(solution)/shard_map/ppermute | solution.py:244
  5.7 7.5 %collective-permute-start.7 = (bf16[256,256]{1,0:T(8,128)(2,1)S(1)}, bf16[256,256]{1,0:T(8,128)(2,1)S(1)}, u32[]{:S(2)}, u32[]{:S(2)}) collective-permute-start(bf16[256,256]{1,0:T(8,128)(2,1)S(1)} %get-tuple-element.47), channel_id=1, source_target_pairs={{0,8},{4,12},{8,0},{12,4},{16,24},{20,28},{24,16},{28,20},{1,9},{5... | collective-permute-start | bytes 393224 | tf_op jit(solution)/shard_map/ppermute | solution.py:244
  7.2 6.0 %collective-permute-start.8 = (bf16[256,256]{1,0:T(8,128)(2,1)S(1)}, bf16[256,256]{1,0:T(8,128)(2,1)S(1)}, u32[]{:S(2)}, u32[]{:S(2)}) collective-permute-start(bf16[256,256]{1,0:T(8,128)(2,1)S(1)} %get-tuple-element.48), channel_id=1, source_target_pairs={{0,12},{4,8},{8,4},{12,0},{16,28},{20,24},{24,20},{28,16},{1,13},{... | collective-permute-start | bytes 393224 | tf_op jit(solution)/shard_map/ppermute | solution.py:244
  7.2 8.9 %collective-permute-start = (bf16[256,512]{1,0:T(8,128)(2,1)}, bf16[256,512]{1,0:T(8,128)(2,1)S(1)}, u32[]{:S(2)}, u32[]{:S(2)}) collective-permute-start(bf16[256,512]{1,0:T(8,128)(2,1)} %refs_2_.1), channel_id=1, source_target_pairs={{0,1},{1,0},{2,3},{3,2},{4,5},{5,4},{6,7},{7,6},{8,9},{9,8},{10,11... | collective-permute-start | bytes 786440 | tf_op jit(solution)/shard_map/ppermute | solution.py:253
  7.2 9.4 %collective-permute-start.1 = (bf16[256,512]{1,0:T(8,128)(2,1)}, bf16[256,512]{1,0:T(8,128)(2,1)S(1)}, u32[]{:S(2)}, u32[]{:S(2)}) collective-permute-start(bf16[256,512]{1,0:T(8,128)(2,1)} %refs_2_.1), channel_id=1, source_target_pairs={{0,2},{1,3},{2,0},{3,1},{4,6},{5,7},{6,4},{7,5},{8,10},{9,11},{10,... | collective-permute-start | bytes 786440 | tf_op jit(solution)/shard_map/ppermute | solution.py:253
  9.2 12.4 %collective-permute-start.2 = (bf16[256,512]{1,0:T(8,128)(2,1)}, bf16[256,512]{1,0:T(8,128)(2,1)S(1)}, u32[]{:S(2)}, u32[]{:S(2)}) collective-permute-start(bf16[256,512]{1,0:T(8,128)(2,1)} %refs_2_.1), channel_id=1, source_target_pairs={{0,3},{1,2},{2,1},{3,0},{4,7},{5,6},{6,5},{7,4},{8,11},{9,10},{10,... | collective-permute-start | bytes 786440 | tf_op jit(solution)/shard_map/ppermute | solution.py:253
  9.4 1.6 %copy-start.2 = (bf16[512,2048]{1,0:T(8,128)(2,1)S(1)}, bf16[512,2048]{1,0:T(8,128)(2,1)}, u32[]{:S(2)}) copy-start(bf16[512,2048]{1,0:T(8,128)(2,1)} %refs_0_.1) | copy-start | bytes 6291460
  11.0 0.9 %copy-start.3 = (bf16[256,512]{1,0:T(8,128)(2,1)S(1)}, bf16[256,512]{1,0:T(8,128)(2,1)}, u32[]{:S(2)}) copy-start(bf16[256,512]{1,0:T(8,128)(2,1)} %refs_1_.1) | copy-start | bytes 786436
  12.0 0.9 %copy-start.4 = (bf16[256,512]{1,0:T(8,128)(2,1)S(1)}, bf16[256,512]{1,0:T(8,128)(2,1)}, u32[]{:S(2)}) copy-start(bf16[256,512]{1,0:T(8,128)(2,1)} %refs_2_.1) | copy-start | bytes 786436
  13.1 9.4 %copy-start = (bf16[512,2048]{1,0:T(8,128)(2,1)}, bf16[512,2048]{1,0:T(8,128)(2,1)S(1)}, u32[]{:S(2)}) copy-start(bf16[512,2048]{1,0:T(8,128)(2,1)S(1)} %get-tuple-element.39.refs_4_.refs_6_) | copy-start | bytes 6291460
  13.3 12.8 %copy-start.7 = (s32[8,4]{0,1:T(4,128)S(1)}, s32[8,4]{0,1:T(4,128)}, u32[]{:S(2)}) copy-start(s32[8,4]{0,1:T(4,128)} %param.12) | copy-start | bytes 388
  13.3 12.9 %copy-start.8 = (s32[8,4]{0,1:T(4,128)S(1)}, s32[8,4]{0,1:T(4,128)}, u32[]{:S(2)}) copy-start(s32[8,4]{0,1:T(4,128)} %param.13) | copy-start | bytes 388
  13.3 33.4 %collective-permute-start.9 = (bf16[4,256,256]{2,1,0:T(8,128)(2,1)S(1)}, bf16[4,256,256]{2,1,0:T(8,128)(2,1)S(1)}, u32[]{:S(2)}, u32[]{:S(2)}) collective-permute-start(bf16[4,256,256]{2,1,0:T(8,128)(2,1)S(1)} %shard_map.113), channel_id=1, source_target_pairs={{0,16},{4,20},{8,24},{12,28},{16,0},{20,4},{24,8},{28,12},{1,17},{... | collective-permute-start | bytes 1572872 | tf_op jit(solution)/shard_map/ppermute | solution.py:247
  22.5 9.8 %collective-permute-start.3 = (bf16[256,384]{1,0:T(8,128)(2,1)S(1)}, bf16[256,384]{1,0:T(8,128)(2,1)S(1)}, u32[]{:S(2)}, u32[]{:S(2)}) collective-permute-start(bf16[256,384]{1,0:T(8,128)(2,1)S(1)} %get-tuple-element.41), channel_id=1, source_target_pairs={{0,12},{4,8},{8,4},{12,0},{16,28},{20,24},{24,20},{28,16},{1,13},{... | collective-permute-start | bytes 589832 | tf_op jit(solution)/shard_map/ppermute | solution.py:244
  25.3 20.0 %collective-permute-start.4 = (bf16[256,384]{1,0:T(8,128)(2,1)S(1)}, bf16[256,384]{1,0:T(8,128)(2,1)S(1)}, u32[]{:S(2)}, u32[]{:S(2)}) collective-permute-start(bf16[256,384]{1,0:T(8,128)(2,1)S(1)} %get-tuple-element.42), channel_id=1, source_target_pairs={{0,8},{4,12},{8,0},{12,4},{16,24},{20,28},{24,16},{28,20},{1,9},{5... | collective-permute-start | bytes 589832 | tf_op jit(solution)/shard_map/ppermute | solution.py:244
  25.8 19.5 %collective-permute-start.5 = (bf16[256,384]{1,0:T(8,128)(2,1)S(1)}, bf16[256,384]{1,0:T(8,128)(2,1)S(1)}, u32[]{:S(2)}, u32[]{:S(2)}) collective-permute-start(bf16[256,384]{1,0:T(8,128)(2,1)S(1)} %get-tuple-element.43), channel_id=1, source_target_pairs={{0,4},{4,0},{8,12},{12,8},{16,20},{20,16},{24,28},{28,24},{1,5},{5... | collective-permute-start | bytes 589832 | tf_op jit(solution)/shard_map/ppermute | solution.py:244
  45.3 8.4 %collective-permute-start.17 = (bf16[4,256,128]{2,1,0:T(8,128)(2,1)S(1)}, bf16[4,256,128]{2,1,0:T(8,128)(2,1)S(1)}, u32[]{:S(2)}, u32[]{:S(2)}) collective-permute-start(bf16[4,256,128]{2,1,0:T(8,128)(2,1)S(1)} %shard_map.117.refs_0_), channel_id=1, source_target_pairs={{0,2},{1,3},{2,0},{3,1},{4,6},{5,7},{6,4},{7,5},{8,10},{9,11},{10,... | collective-permute-start | bytes 786440 | tf_op jit(solution)/shard_map/ppermute | solution.py:253
  50.2 15.2 %collective-permute-start.14 = (bf16[4,256,128]{2,1,0:T(8,128)(2,1)S(1)}, bf16[4,256,128]{2,1,0:T(8,128)(2,1)S(1)}, u32[]{:S(2)}, u32[]{:S(2)}) collective-permute-start(bf16[4,256,128]{2,1,0:T(8,128)(2,1)S(1)} %get-tuple-element.49.attn_ref.refs_3_), channel_id=1, source_target_pairs={{0,12},{4,8},{8,4},{12,0},{16,28},{20,24},{24,20},{28,16},{1,13},{... | collective-permute-start | bytes 786440 | tf_op jit(solution)/shard_map/ppermute | solution.py:244
  50.3 16.4 %collective-permute-start.15 = (bf16[4,256,128]{2,1,0:T(8,128)(2,1)S(1)}, bf16[4,256,128]{2,1,0:T(8,128)(2,1)S(1)}, u32[]{:S(2)}, u32[]{:S(2)}) collective-permute-start(bf16[4,256,128]{2,1,0:T(8,128)(2,1)S(1)} %get-tuple-element.49.attn_ref.refs_3_), channel_id=1, source_target_pairs={{0,8},{4,12},{8,0},{12,4},{16,24},{20,28},{24,16},{28,20},{1,9},{5... | collective-permute-start | bytes 786440 | tf_op jit(solution)/shard_map/ppermute | solution.py:244
  52.5 14.1 %collective-permute-start.16 = (bf16[4,256,128]{2,1,0:T(8,128)(2,1)S(1)}, bf16[4,256,128]{2,1,0:T(8,128)(2,1)S(1)}, u32[]{:S(2)}, u32[]{:S(2)}) collective-permute-start(bf16[4,256,128]{2,1,0:T(8,128)(2,1)S(1)} %get-tuple-element.49.attn_ref.refs_3_), channel_id=1, source_target_pairs={{0,4},{4,0},{8,12},{12,8},{16,20},{20,16},{24,28},{28,24},{1,5},{5... | collective-permute-start | bytes 786440 | tf_op jit(solution)/shard_map/ppermute | solution.py:244
  53.8 12.9 %collective-permute-start.18 = (bf16[2,4,256,128]{3,2,1,0:T(8,128)(2,1)S(1)}, bf16[2,4,256,128]{3,2,1,0:T(8,128)(2,1)S(1)}, u32[]{:S(2)}, u32[]{:S(2)}) collective-permute-start(bf16[2,4,256,128]{3,2,1,0:T(8,128)(2,1)S(1)} %shard_map.118.refs_4_), channel_id=1, source_target_pairs={{0,1},{1,0},{2,3},{3,2},{4,5},{5,4},{6,7},{7,6},{8,9},{9,8},{10,11... | collective-permute-start | bytes 1572872 | tf_op jit(solution)/shard_map/ppermute | solution.py:253
  53.9 12.8 %copy-start.1 = (bf16[512,2048]{1,0:T(8,128)(2,1)S(1)}, bf16[512,2048]{1,0:T(8,128)(2,1)}, u32[]{:S(2)}) copy-start(bf16[512,2048]{1,0:T(8,128)(2,1)} %copy-done) | copy-start | bytes 6291460
  56.2 9.0 %collective-permute-start.10 = (bf16[256,256]{1,0:T(8,128)(2,1)S(1)}, bf16[256,256]{1,0:T(8,128)(2,1)S(1)}, u32[]{:S(2)}, u32[]{:S(2)}) collective-permute-start(bf16[256,256]{1,0:T(8,128)(2,1)S(1)} %get-tuple-element.55), channel_id=1, source_target_pairs={{16,0},{20,4},{24,8},{28,12},{17,1},{21,5},{25,9},{29,13},{18,2},{... | collective-permute-start | bytes 393224 | tf_op jit(solution)/shard_map/ppermute | solution.py:250
  68.3 5.6 %collective-permute-start.20 = (bf16[256,1024]{1,0:T(8,128)(2,1)S(1)}, bf16[256,1024]{1,0:T(8,128)(2,1)S(1)}, u32[]{:S(2)}, u32[]{:S(2)}) collective-permute-start(bf16[256,1024]{1,0:T(8,128)(2,1)S(1)} %get-tuple-element.65), channel_id=1, source_target_pairs={{0,1},{1,0},{2,3},{3,2},{4,5},{5,4},{6,7},{7,6},{8,9},{9,8},{10,11... | collective-permute-start | bytes 1572872 | tf_op jit(solution)/shard_map/ppermute | solution.py:253
  68.4 18.1 %collective-permute-start.19 = (bf16[256,512]{1,0:T(8,128)(2,1)S(1)}, bf16[256,512]{1,0:T(8,128)(2,1)S(1)}, u32[]{:S(2)}, u32[]{:S(2)}) collective-permute-start(bf16[256,512]{1,0:T(8,128)(2,1)S(1)} %get-tuple-element.61), channel_id=1, source_target_pairs={{0,16},{4,20},{8,24},{12,28},{16,0},{20,4},{24,8},{28,12},{1,17},{... | collective-permute-start | bytes 786440 | tf_op jit(solution)/shard_map/ppermute | solution.py:247
  70.4 10.9 %collective-permute-start.11 = (bf16[256,384]{1,0:T(8,128)(2,1)S(1)}, bf16[256,384]{1,0:T(8,128)(2,1)S(1)}, u32[]{:S(2)}, u32[]{:S(2)}) collective-permute-start(bf16[256,384]{1,0:T(8,128)(2,1)S(1)} %get-tuple-element.56), channel_id=1, source_target_pairs={{0,12},{4,8},{8,4},{12,0},{16,28},{20,24},{24,20},{28,16},{1,13},{... | collective-permute-start | bytes 589832 | tf_op jit(solution)/shard_map/ppermute | solution.py:244
  72.3 14.1 %collective-permute-start.12 = (bf16[256,384]{1,0:T(8,128)(2,1)S(1)}, bf16[256,384]{1,0:T(8,128)(2,1)S(1)}, u32[]{:S(2)}, u32[]{:S(2)}) collective-permute-start(bf16[256,384]{1,0:T(8,128)(2,1)S(1)} %get-tuple-element.57), channel_id=1, source_target_pairs={{0,8},{4,12},{8,0},{12,4},{16,24},{20,28},{24,16},{28,20},{1,9},{5... | collective-permute-start | bytes 589832 | tf_op jit(solution)/shard_map/ppermute | solution.py:244
  72.7 13.8 %collective-permute-start.13 = (bf16[256,384]{1,0:T(8,128)(2,1)S(1)}, bf16[256,384]{1,0:T(8,128)(2,1)S(1)}, u32[]{:S(2)}, u32[]{:S(2)}) collective-permute-start(bf16[256,384]{1,0:T(8,128)(2,1)S(1)} %get-tuple-element.58), channel_id=1, source_target_pairs={{0,4},{4,0},{8,12},{12,8},{16,20},{20,16},{24,28},{28,24},{1,5},{5... | collective-permute-start | bytes 589832 | tf_op jit(solution)/shard_map/ppermute | solution.py:244
  73.9 13.8 %collective-permute-start.21 = (bf16[256,512]{1,0:T(8,128)(2,1)S(1)}, bf16[256,512]{1,0:T(8,128)(2,1)S(1)}, u32[]{:S(2)}, u32[]{:S(2)}) collective-permute-start(bf16[256,512]{1,0:T(8,128)(2,1)S(1)} %add_convert_fusion.1), channel_id=1, source_target_pairs={{0,2},{1,3},{2,0},{3,1},{4,6},{5,7},{6,4},{7,5},{8,10},{9,11},{10,... | collective-permute-start | bytes 786440 | tf_op jit(solution)/shard_map/ppermute | solution.py:253

commit v5 on v4

--- a/solution.py
+++ b/solution.py
@@ -80,8 +80,8 @@
 
 
 def pack_body(A, *refs):
-    for m in range(A):
-        refs[-1][A - 1 - m] = refs[m][...]
+    for m in range(1, A):
+        refs[-1][m - 1] = refs[A - 1 - m][...]
 
 
 def collect_body(*refs):
@@ -102,7 +102,7 @@
 
 def forward_body(A, B, R, score_scale, owner_ref, block_ref, *refs):
     pair = B == 2
-    piece_refs, own_refs, other_ref, refs = refs[:A][::-1], refs[A : 2 * A], refs[2 * A], refs[2 * A + 1 :]
+    piece_refs, own_refs, others, refs = refs[:A][::-1], refs[A : 2 * A], refs[2 * A : -4], refs[-4:]
     attn_ref, kvcat, weights_ref, kv = refs
     SEG = piece_refs[0].shape[0]
     parts = SEG // BLOCK
@@ -114,9 +114,9 @@
             for part in range(parts):
                 rows = slice(part * BLOCK, (part + 1) * BLOCK)
                 kv[m * parts + part] = own_refs[m][rows, :]
-                kv[(A + m) * parts + part] = other_ref[m, rows, :]
-    else:
-        kv = other_ref
+                kv[(A + m) * parts + part] = others[1][m - 1, rows, :] if m else others[0][rows, :]
+    else:
+        kv = others[0]
 
     def place(other_a, other_b):
         slot = (other_b ^ b) * A + (other_a ^ a) if pair else other_b * A + (other_a ^ a)
@@ -256,33 +256,32 @@
         moved = {m: over_a(pieces[m], m) for m in reversed(range(1, A))}
         return [pieces[0]] + [moved[m] for m in range(1, A)]
 
-    def direct(x):
-        return [x] + [over_head(x, k) for k in range(1, H)]
-
-    grads = direct(out_grad)
+    grads = [out_grad, over_head(out_grad, 1), over_head(out_grad, 2)]
+    grads += [over_head(grads[2], 1)]
 
     cut = functools.partial(cut_body, A, B)
     kvs = exchange(call(cut, [shape((SEG, 2 * DH), BF16)] * A, [keys, values]))
     staged = call(stage_body, [shape(x.shape, BF16) for x in (out_weight, queries, out_grad)], [out_weight, queries, out_grad])
+    early = [over_b(kvs[0])] if B == 2 else []
     kv = call(
         functools.partial(pack_body, A),
-        [shape((A, SEG, 2 * DH), BF16)],
-        [*kvs[::-1], staged[0]],
-        specs=[VMEM] * A + [ANY],
+        [shape((A - 1, SEG, 2 * DH), BF16)],
+        [*kvs[:0:-1], *early, staged[0]],
+        specs=[VMEM] * (A - 1) + [ANY] * (1 + len(early)),
     )[0]
     out_weight, queries, grads[0] = staged
     if B == 2:
-        kv = over_b(kv)
+        kv = [*early, over_b(kv)]
     else:
         groups = [[j * A + i for j in range(B)] for i in range(A)]
-        kv = lax.all_gather(kv, "seg", axis_index_groups=groups)
-        kv = kv.reshape(B * A * (SEG // BLOCK), BLOCK, 2 * DH)
+        kv = lax.all_gather(jnp.concatenate([kvs[0][None], kv]), "seg", axis_index_groups=groups)
+        kv = [kv.reshape(B * A * (SEG // BLOCK), BLOCK, 2 * DH)]
     sloped = call(
         functools.partial(slope_body, A, B, H),
         [shape((SEG, 2 * DH + width // H), BF16)] * A,
         [*grads, out_weight, queries],
         scratch=[pltpu.VMEM((SEG, D), BF16), pltpu.VMEM((SEG, width), BF16)],
-        flops=10**9,
+        flops=2 * 10**8,
     )
     pieces = exchange(sloped)
     count = 2 * SEG + R * BLOCK
@@ -292,8 +291,8 @@
     attn, kvcat, weights = call(
         functools.partial(forward_body, A, B, R, score_scale),
         [shape((A, SEG, DH), BF16), shape((A, count, 2 * DH), BF16), shape((A, SEG, count), F32)],
-        [retr_owner, retr_block, *pieces[::-1], *kvs, kv],
-        specs=[SMEM] * 2 + [VMEM] * (2 * A + 1),
+        [retr_owner, retr_block, *pieces[::-1], *kvs, *kv],
+        specs=[SMEM] * 2 + [VMEM] * (2 * A + len(kv)),
         scratch=[pltpu.VMEM((2 * A * (SEG // BLOCK), BLOCK, 2 * DH), BF16)],
         limit=limit,
         flops=10**11,

time: 88.8 us -> 84.2 us (0.948)
  waiting for transfers between devices: 45.5 us -> 40.3 us
    ppermute x7, waiting for transfers between devices: 5.51 us -> 0.02 us  [over_head(): return lax.ppermute(x, 'head', [(i, i ^ k) for i in range(H)])]
    ppermute x12, waiting for transfers between devices: 32.4 us -> 27.4 us  [over_a(): lax.ppermute(x, 'seg', [(i, i // A * A + (i % A ^ m)) for i in range(n)])]
    ppermute x2 -> x3, waiting for transfers between devices: 0.01 us -> 2.7 us  [over_b(): return lax.ppermute(x, 'seg', [(i, (i + A) % n) for i in range(n)])]
    ppermute x1, waiting for transfers between devices: 7.67 us -> 10.2 us  [back_b(): return lax.ppermute(x, 'seg', [(i, i - A) for i in range(A, n)])]
    ppermute x7, starting transfers between devices: 4.28 us -> 5.81 us  [over_head(): return lax.ppermute(x, 'head', [(i, i ^ k) for i in range(H)])]
    ppermute x2 -> x3, starting transfers between devices: 4.81 us -> 3.84 us  [over_b(): return lax.ppermute(x, 'seg', [(i, (i + A) % n) for i in range(n)])]
  transfers between devices with their start and end apart: 22 -> 23, of which waited for: 9 -> 6; matrix products, arithmetic and copies ran while one was open for 0% -> 0% of each run, Pallas kernels for 9% -> 10%
where the time goes in v5:
time: 84.2 us; the launch traced here: 83.9 us
  waiting for transfers between devices  40.3 us (48%)
  starting transfers between devices  26.2 us (31%)
  Pallas kernels  10.1 us (12%)
  local copies, waits for them, and re-layouts  5.57 us (7%)
  other arithmetic  0.88 us (1%)
  between operations  0.85 us (1%)
    ppermute x12, waiting for transfers between devices, over_a(): lax.ppermute(x, 'seg', [(i, i // A * A + (i % A ^ m)) for i in range(n)])  27.4 us
    ppermute x12, starting transfers between devices, over_a(): lax.ppermute(x, 'seg', [(i, i // A * A + (i % A ^ m)) for i in range(n)])  15.3 us
    ppermute x1, waiting for transfers between devices, back_b(): return lax.ppermute(x, 'seg', [(i, i - A) for i in range(A, n)])  10.2 us
    pallas_call x11, Pallas kernels, call(): pl.pallas_call(body, out_shape=outs, in_specs=specs or [VMEM] * len(opera...  10.1 us
    ppermute x7, starting transfers between devices, over_head(): return lax.ppermute(x, 'head', [(i, i ^ k) for i in range(H)])  5.81 us
    unnamed x20, local copies, waits for them, and re-layouts  5.57 us
    ppermute x3, starting transfers between devices, over_b(): return lax.ppermute(x, 'seg', [(i, (i + A) % n) for i in range(n)])  3.84 us
    ppermute x3, waiting for transfers between devices, over_b(): return lax.ppermute(x, 'seg', [(i, (i + A) % n) for i in range(n)])  2.7 us
  transfers between devices with their start and end apart: 23, of which 6 were waited for; matrix products, arithmetic and copies ran while one was open for 0% of the time, Pallas kernels for 10%

profile of v5, /device:TPU:0, one launch (start us, length us, event | category | flops | bytes accessed | tf_op | source)
XLA Modules:
  0.0 83.9 jit_solution(5781258783779742604)
XLA Ops:
  0.6 3.0 %collective-permute-start.1 = (bf16[256,512]{1,0:T(8,128)(2,1)}, bf16[256,512]{1,0:T(8,128)(2,1)S(1)}, u32[]{:S(2)}, u32[]{:S(2)}) collective-permute-start(bf16[256,512]{1,0:T(8,128)(2,1)} %refs_2_.1), channel_id=1, source_target_pairs={{0,2},{1,3},{2,0},{3,1},{4,6},{5,7},{6,4},{7,5},{8,10},{9,11},{10,... | collective-permute-start | bytes 786440 | tf_op jit(solution)/shard_map/ppermute | solution.py:253
  3.6 0.9 %copy-done.5 = bf16[256,512]{1,0:T(8,128)(2,1)S(1)} copy-done((bf16[256,512]{1,0:T(8,128)(2,1)S(1)}, bf16[256,512]{1,0:T(8,128)(2,1)}, u32[]{:S(2)}) %copy-start.5) | copy-done | bytes 262168
  4.6 0.9 %copy-done.6 = bf16[256,512]{1,0:T(8,128)(2,1)S(1)} copy-done((bf16[256,512]{1,0:T(8,128)(2,1)S(1)}, bf16[256,512]{1,0:T(8,128)(2,1)}, u32[]{:S(2)}) %copy-start.6) | copy-done | bytes 262168
  5.6 2.7 %collective-permute-start.9 = (bf16[256,256]{1,0:T(8,128)(2,1)S(1)}, bf16[256,256]{1,0:T(8,128)(2,1)S(1)}, u32[]{:S(2)}, u32[]{:S(2)}) collective-permute-start(bf16[256,256]{1,0:T(8,128)(2,1)S(1)} %get-tuple-element.45.refs_4_), channel_id=1, source_target_pairs={{0,16},{4,20},{8,24},{12,28},{16,0},{20,4},{24,8},{28,12},{1,17},{... | collective-permute-start | bytes 393224 | tf_op jit(solution)/shard_map/ppermute | solution.py:247
  8.3 1.5 %collective-permute-start.6 = (bf16[256,256]{1,0:T(8,128)(2,1)S(1)}, bf16[256,256]{1,0:T(8,128)(2,1)S(1)}, u32[]{:S(2)}, u32[]{:S(2)}) collective-permute-start(bf16[256,256]{1,0:T(8,128)(2,1)S(1)} %get-tuple-element.46), channel_id=1, source_target_pairs={{0,4},{4,0},{8,12},{12,8},{16,20},{20,16},{24,28},{28,24},{1,5},{5... | collective-permute-start | bytes 393224 | tf_op jit(solution)/shard_map/ppermute | solution.py:244
  9.8 1.6 %collective-permute-start.7 = (bf16[256,256]{1,0:T(8,128)(2,1)S(1)}, bf16[256,256]{1,0:T(8,128)(2,1)S(1)}, u32[]{:S(2)}, u32[]{:S(2)}) collective-permute-start(bf16[256,256]{1,0:T(8,128)(2,1)S(1)} %get-tuple-element.47), channel_id=1, source_target_pairs={{0,8},{4,12},{8,0},{12,4},{16,24},{20,28},{24,16},{28,20},{1,9},{5... | collective-permute-start | bytes 393224 | tf_op jit(solution)/shard_map/ppermute | solution.py:244
  11.8 2.7 %collective-permute-done.9.refs_3_.refs_8_ = bf16[256,256]{1,0:T(8,128)(2,1)S(1)} collective-permute-done((bf16[256,256]{1,0:T(8,128)(2,1)S(1)}, bf16[256,256]{1,0:T(8,128)(2,1)S(1)}, u32[]{:S(2)}, u32[]{:S(2)}) %collective-permute-start.9) | collective-permute-done | bytes 131104 | tf_op jit(solution)/shard_map/ppermute | solution.py:247
  15.0 1.6 %copy-done.2 = bf16[512,2048]{1,0:T(8,128)(2,1)S(1)} copy-done((bf16[512,2048]{1,0:T(8,128)(2,1)S(1)}, bf16[512,2048]{1,0:T(8,128)(2,1)}, u32[]{:S(2)}) %copy-start.2) | copy-done | bytes 2097176
  16.6 0.9 %copy-done.3 = bf16[256,512]{1,0:T(8,128)(2,1)S(1)} copy-done((bf16[256,512]{1,0:T(8,128)(2,1)S(1)}, bf16[256,512]{1,0:T(8,128)(2,1)}, u32[]{:S(2)}) %copy-start.3) | copy-done | bytes 262168
  17.5 0.9 %copy-done.4 = bf16[256,512]{1,0:T(8,128)(2,1)S(1)} copy-done((bf16[256,512]{1,0:T(8,128)(2,1)S(1)}, bf16[256,512]{1,0:T(8,128)(2,1)}, u32[]{:S(2)}) %copy-start.4) | copy-done | bytes 262168
  18.7 1.1 %collective-permute-start.10 = (bf16[3,256,256]{2,1,0:T(8,128)(2,1)S(1)}, bf16[3,256,256]{2,1,0:T(8,128)(2,1)S(1)}, u32[]{:S(2)}, u32[]{:S(2)}) collective-permute-start(bf16[3,256,256]{2,1,0:T(8,128)(2,1)S(1)} %shard_map.113), channel_id=1, source_target_pairs={{0,16},{4,20},{8,24},{12,28},{16,0},{20,4},{24,8},{28,12},{1,17},{... | collective-permute-start | bytes 1179656 | tf_op jit(solution)/shard_map/ppermute | solution.py:247
  19.9 0.9 %shard_map.111 = (bf16[256,384]{1,0:T(8,128)(2,1)S(1)}, bf16[256,384]{1,0:T(8,128)(2,1)S(1)}, bf16[256,384]{1,0:T(8,128)(2,1)S(1)}, bf16[256,384]{1,0:T(8,128)(2,1)S(1)}) custom-call(bf16[256,512]{1,0:T(8,128)(2,1)S(1)} %get-tuple-element.38.refs_0_, bf16[256,512]{1,0:T(8,128)(2,1)S(1)} %collective-permute-done.refs_1_, ...), custom_call_target="tpu_custom_call" | custom-call | flops 200000000 | bytes 1 | tf_op jit(solution)/shard_map/pallas_call | solution.py:31
  20.8 4.0 %collective-permute-start.3 = (bf16[256,384]{1,0:T(8,128)(2,1)S(1)}, bf16[256,384]{1,0:T(8,128)(2,1)S(1)}, u32[]{:S(2)}, u32[]{:S(2)}) collective-permute-start(bf16[256,384]{1,0:T(8,128)(2,1)S(1)} %get-tuple-element.41), channel_id=1, source_target_pairs={{0,12},{4,8},{8,4},{12,0},{16,28},{20,24},{24,20},{28,16},{1,13},{... | collective-permute-start | bytes 589832 | tf_op jit(solution)/shard_map/ppermute | solution.py:244
  24.8 0.6 collective-permute-start.5
  25.6 8.1 %collective-permute-done.3.refs_0_.refs_3_ = bf16[256,384]{1,0:T(8,128)(2,1)S(1)} collective-permute-done((bf16[256,384]{1,0:T(8,128)(2,1)S(1)}, bf16[256,384]{1,0:T(8,128)(2,1)S(1)}, u32[]{:S(2)}, u32[]{:S(2)}) %collective-permute-start.3) | collective-permute-done | bytes 196640 | tf_op jit(solution)/shard_map/ppermute | solution.py:244
  33.7 6.7 %collective-permute-done.4.refs_1_.refs_2_ = bf16[256,384]{1,0:T(8,128)(2,1)S(1)} collective-permute-done((bf16[256,384]{1,0:T(8,128)(2,1)S(1)}, bf16[256,384]{1,0:T(8,128)(2,1)S(1)}, u32[]{:S(2)}, u32[]{:S(2)}) %collective-permute-start.4) | collective-permute-done | bytes 196640 | tf_op jit(solution)/shard_map/ppermute | solution.py:244
  40.4 0.5 collective-permute-start.18
  41.0 3.5 %shard_map.114 = (bf16[4,256,128]{2,1,0:T(8,128)(2,1)S(1)}, bf16[4,1024,256]{2,1,0:T(8,128)(2,1)S(1)}, f32[4,256,1024]{2,1,0:T(8,128)S(1)}) custom-call(s32[8,4]{1,0:T(8,128)S(1)} %copy.12.owner_ref, s32[8,4]{1,0:T(8,128)S(1)} %copy.13.block_ref, bf16[256,384]{1,0:T(8,128)(2,1)S(1)} %collective-permute-done.3.refs_0_.refs_3_, ...), custom_call_target="tpu_custom_call" | custom-call | flops 99999997952 | bytes 1 | tf_op jit(solution)/shard_map/pallas_call | solution.py:31
  44.4 0.6 collective-permute-start.15
  45.1 2.5 %collective-permute-start.16 = (bf16[4,256,128]{2,1,0:T(8,128)(2,1)S(1)}, bf16[4,256,128]{2,1,0:T(8,128)(2,1)S(1)}, u32[]{:S(2)}, u32[]{:S(2)}) collective-permute-start(bf16[4,256,128]{2,1,0:T(8,128)(2,1)S(1)} %get-tuple-element.49.attn_ref.refs_3_), channel_id=1, source_target_pairs={{0,8},{4,12},{8,0},{12,4},{16,24},{20,28},{24,16},{28,20},{1,9},{5... | collective-permute-start | bytes 786440 | tf_op jit(solution)/shard_map/ppermute | solution.py:244
  48.1 2.4 %shard_map.115 = (bf16[4,256,128]{2,1,0:T(8,128)(2,1)S(1)}, f32[4,256,256]{2,1,0:T(8,128)S(1)}, bf16[4,256,256]{2,1,0:T(8,128)(2,1)S(1)}, bf16[256,256]{1,0:T(8,128)(2,1)S(1)}) custom-call(bf16[4,256,128]{2,1,0:T(8,128)(2,1)S(1)} %get-tuple-element.49.attn_ref.refs_3_, bf16[4,1024,256]{2,1,0:T(8,128)(2,1)S(1)} %get-tuple-element.50.kvcat, ...), custom_call_target="tpu_custom_call" | custom-call | flops 99999997952 | bytes 1 | tf_op jit(solution)/shard_map/pallas_call | solution.py:31
  50.5 1.3 %collective-permute-start.11 = (bf16[256,256]{1,0:T(8,128)(2,1)S(1)}, bf16[256,256]{1,0:T(8,128)(2,1)S(1)}, u32[]{:S(2)}, u32[]{:S(2)}) collective-permute-start(bf16[256,256]{1,0:T(8,128)(2,1)S(1)} %get-tuple-element.55), channel_id=1, source_target_pairs={{16,0},{20,4},{24,8},{28,12},{17,1},{21,5},{25,9},{29,13},{18,2},{... | collective-permute-start | bytes 393224 | tf_op jit(solution)/shard_map/ppermute | solution.py:250
  51.8 10.2 %collective-permute-done.11.carry_ref = bf16[256,256]{1,0:T(8,128)(2,1)S(1)} collective-permute-done((bf16[256,256]{1,0:T(8,128)(2,1)S(1)}, bf16[256,256]{1,0:T(8,128)(2,1)S(1)}, u32[]{:S(2)}, u32[]{:S(2)}) %collective-permute-start.11) | collective-permute-done | bytes 131104 | tf_op jit(solution)/shard_map/ppermute | solution.py:250
  62.2 1.6 %shard_map.119 = (f32[256,512]{1,0:T(8,128)S(1)}, f32[256,512]{1,0:T(8,128)S(1)}, bf16[256,1024]{1,0:T(8,128)(2,1)S(1)}, f32[256,512]{1,0:T(8,128)S(1)}, bf16[256,512]{1,0:T(8,128)(2,1)S(1)}) custom-call(bf16[4,256,128]{2,1,0:T(8,128)(2,1)S(1)} %collective-permute-done.15.refs_0_, bf16[4,256,128]{2,1,0:T(8,128)(2,1)S(1)} %collective-permute-done.16.refs_1_, ...), custom_call_target="tpu_custom_call" | custom-call | flops 1 | bytes 1 | tf_op jit(solution)/shard_map/pallas_call | solution.py:31
  64.0 0.7 collective-permute-start.12
  64.7 2.2 %collective-permute-start.13 = (bf16[256,384]{1,0:T(8,128)(2,1)S(1)}, bf16[256,384]{1,0:T(8,128)(2,1)S(1)}, u32[]{:S(2)}, u32[]{:S(2)}) collective-permute-start(bf16[256,384]{1,0:T(8,128)(2,1)S(1)} %get-tuple-element.57), channel_id=1, source_target_pairs={{0,8},{4,12},{8,0},{12,4},{16,24},{20,28},{24,16},{28,20},{1,9},{5... | collective-permute-start | bytes 589832 | tf_op jit(solution)/shard_map/ppermute | solution.py:244
  66.9 0.6 collective-permute-start.14
  67.6 1.6 %collective-permute-start.22 = (bf16[256,512]{1,0:T(8,128)(2,1)S(1)}, bf16[256,512]{1,0:T(8,128)(2,1)S(1)}, u32[]{:S(2)}, u32[]{:S(2)}) collective-permute-start(bf16[256,512]{1,0:T(8,128)(2,1)S(1)} %add_convert_fusion.1), channel_id=1, source_target_pairs={{0,2},{1,3},{2,0},{3,1},{4,6},{5,7},{6,4},{7,5},{8,10},{9,11},{10,... | collective-permute-start | bytes 786440 | tf_op jit(solution)/shard_map/ppermute | solution.py:253
  69.2 5.8 %collective-permute-done.12.refs_0_ = bf16[256,384]{1,0:T(8,128)(2,1)S(1)} collective-permute-done((bf16[256,384]{1,0:T(8,128)(2,1)S(1)}, bf16[256,384]{1,0:T(8,128)(2,1)S(1)}, u32[]{:S(2)}, u32[]{:S(2)}) %collective-permute-start.12) | collective-permute-done | bytes 196640 | tf_op jit(solution)/shard_map/ppermute | solution.py:244
  75.0 6.9 %collective-permute-done.13.refs_1_ = bf16[256,384]{1,0:T(8,128)(2,1)S(1)} collective-permute-done((bf16[256,384]{1,0:T(8,128)(2,1)S(1)}, bf16[256,384]{1,0:T(8,128)(2,1)S(1)}, u32[]{:S(2)}, u32[]{:S(2)}) %collective-permute-start.13) | collective-permute-done | bytes 196640 | tf_op jit(solution)/shard_map/ppermute | solution.py:244
  81.9 1.2 %shard_map.120 = (bf16[256,512]{1,0:T(8,128)(2,1)}, bf16[256,512]{1,0:T(8,128)(2,1)}, bf16[256,512]{1,0:T(8,128)(2,1)}, f32[256,512]{1,0:T(8,128)}) custom-call(bf16[256,384]{1,0:T(8,128)(2,1)S(1)} %collective-permute-done.12.refs_0_, bf16[256,384]{1,0:T(8,128)(2,1)S(1)} %collective-permute-done.13.refs_1_, ...), custom_call_target="tpu_custom_call" | custom-call | flops 99999997952 | bytes 1 | tf_op jit(solution)/shard_map/pallas_call | solution.py:31
  83.1 0.8 add_convert_fusion
  (47 shorter events, 2.4 us)
Async XLA Ops:
  0.6 13.8 %collective-permute-start.1 = (bf16[256,512]{1,0:T(8,128)(2,1)}, bf16[256,512]{1,0:T(8,128)(2,1)S(1)}, u32[]{:S(2)}, u32[]{:S(2)}) collective-permute-start(bf16[256,512]{1,0:T(8,128)(2,1)} %refs_2_.1), channel_id=1, source_target_pairs={{0,2},{1,3},{2,0},{3,1},{4,6},{5,7},{6,4},{7,5},{8,10},{9,11},{10,... | collective-permute-start | bytes 786440 | tf_op jit(solution)/shard_map/ppermute | solution.py:253
  3.6 0.9 %copy-start.5 = (bf16[256,512]{1,0:T(8,128)(2,1)S(1)}, bf16[256,512]{1,0:T(8,128)(2,1)}, u32[]{:S(2)}) copy-start(bf16[256,512]{1,0:T(8,128)(2,1)} %k_ref.1) | copy-start | bytes 786436
  4.6 0.9 %copy-start.6 = (bf16[256,512]{1,0:T(8,128)(2,1)S(1)}, bf16[256,512]{1,0:T(8,128)(2,1)}, u32[]{:S(2)}) copy-start(bf16[256,512]{1,0:T(8,128)(2,1)} %v_ref.1) | copy-start | bytes 786436
  5.6 8.8 %collective-permute-start.9 = (bf16[256,256]{1,0:T(8,128)(2,1)S(1)}, bf16[256,256]{1,0:T(8,128)(2,1)S(1)}, u32[]{:S(2)}, u32[]{:S(2)}) collective-permute-start(bf16[256,256]{1,0:T(8,128)(2,1)S(1)} %get-tuple-element.45.refs_4_), channel_id=1, source_target_pairs={{0,16},{4,20},{8,24},{12,28},{16,0},{20,4},{24,8},{28,12},{1,17},{... | collective-permute-start | bytes 393224 | tf_op jit(solution)/shard_map/ppermute | solution.py:247
  8.3 10.4 %collective-permute-start.6 = (bf16[256,256]{1,0:T(8,128)(2,1)S(1)}, bf16[256,256]{1,0:T(8,128)(2,1)S(1)}, u32[]{:S(2)}, u32[]{:S(2)}) collective-permute-start(bf16[256,256]{1,0:T(8,128)(2,1)S(1)} %get-tuple-element.46), channel_id=1, source_target_pairs={{0,4},{4,0},{8,12},{12,8},{16,20},{20,16},{24,28},{28,24},{1,5},{5... | collective-permute-start | bytes 393224 | tf_op jit(solution)/shard_map/ppermute | solution.py:244
  9.8 8.9 %collective-permute-start.7 = (bf16[256,256]{1,0:T(8,128)(2,1)S(1)}, bf16[256,256]{1,0:T(8,128)(2,1)S(1)}, u32[]{:S(2)}, u32[]{:S(2)}) collective-permute-start(bf16[256,256]{1,0:T(8,128)(2,1)S(1)} %get-tuple-element.47), channel_id=1, source_target_pairs={{0,8},{4,12},{8,0},{12,4},{16,24},{20,28},{24,16},{28,20},{1,9},{5... | collective-permute-start | bytes 393224 | tf_op jit(solution)/shard_map/ppermute | solution.py:244
  11.4 7.3 %collective-permute-start.8 = (bf16[256,256]{1,0:T(8,128)(2,1)S(1)}, bf16[256,256]{1,0:T(8,128)(2,1)S(1)}, u32[]{:S(2)}, u32[]{:S(2)}) collective-permute-start(bf16[256,256]{1,0:T(8,128)(2,1)S(1)} %get-tuple-element.48), channel_id=1, source_target_pairs={{0,12},{4,8},{8,4},{12,0},{16,28},{20,24},{24,20},{28,16},{1,13},{... | collective-permute-start | bytes 393224 | tf_op jit(solution)/shard_map/ppermute | solution.py:244
  14.5 5.4 %collective-permute-start = (bf16[256,512]{1,0:T(8,128)(2,1)}, bf16[256,512]{1,0:T(8,128)(2,1)S(1)}, u32[]{:S(2)}, u32[]{:S(2)}) collective-permute-start(bf16[256,512]{1,0:T(8,128)(2,1)} %refs_2_.1), channel_id=1, source_target_pairs={{0,1},{1,0},{2,3},{3,2},{4,5},{5,4},{6,7},{7,6},{8,9},{9,8},{10,11... | collective-permute-start | bytes 786440 | tf_op jit(solution)/shard_map/ppermute | solution.py:253
  14.5 5.4 %collective-permute-start.2 = (bf16[256,512]{1,0:T(8,128)(2,1)S(1)}, bf16[256,512]{1,0:T(8,128)(2,1)S(1)}, u32[]{:S(2)}, u32[]{:S(2)}) collective-permute-start(bf16[256,512]{1,0:T(8,128)(2,1)S(1)} %collective-permute-done.1.refs_2_), channel_id=1, source_target_pairs={{0,1},{1,0},{2,3},{3,2},{4,5},{5,4},{6,7},{7,6},{8,9},{9,8},{10,11... | collective-permute-start | bytes 786440 | tf_op jit(solution)/shard_map/ppermute | solution.py:253
  15.0 1.6 %copy-start.2 = (bf16[512,2048]{1,0:T(8,128)(2,1)S(1)}, bf16[512,2048]{1,0:T(8,128)(2,1)}, u32[]{:S(2)}) copy-start(bf16[512,2048]{1,0:T(8,128)(2,1)} %refs_0_.1) | copy-start | bytes 6291460
  16.6 0.9 %copy-start.3 = (bf16[256,512]{1,0:T(8,128)(2,1)S(1)}, bf16[256,512]{1,0:T(8,128)(2,1)}, u32[]{:S(2)}) copy-start(bf16[256,512]{1,0:T(8,128)(2,1)} %refs_1_.1) | copy-start | bytes 786436
  17.5 0.9 %copy-start.4 = (bf16[256,512]{1,0:T(8,128)(2,1)S(1)}, bf16[256,512]{1,0:T(8,128)(2,1)}, u32[]{:S(2)}) copy-start(bf16[256,512]{1,0:T(8,128)(2,1)} %refs_2_.1) | copy-start | bytes 786436
  18.6 2.2 %copy-start = (bf16[512,2048]{1,0:T(8,128)(2,1)}, bf16[512,2048]{1,0:T(8,128)(2,1)S(1)}, u32[]{:S(2)}) copy-start(bf16[512,2048]{1,0:T(8,128)(2,1)S(1)} %get-tuple-element.39.refs_4_.refs_6_) | copy-start | bytes 6291460
  18.7 6.8 %copy-start.7 = (s32[8,4]{0,1:T(4,128)S(1)}, s32[8,4]{0,1:T(4,128)}, u32[]{:S(2)}) copy-start(s32[8,4]{0,1:T(4,128)} %param.12) | copy-start | bytes 388
  18.7 6.8 %copy-start.8 = (s32[8,4]{0,1:T(4,128)S(1)}, s32[8,4]{0,1:T(4,128)}, u32[]{:S(2)}) copy-start(s32[8,4]{0,1:T(4,128)} %param.13) | copy-start | bytes 388
  18.7 22.2 %collective-permute-start.10 = (bf16[3,256,256]{2,1,0:T(8,128)(2,1)S(1)}, bf16[3,256,256]{2,1,0:T(8,128)(2,1)S(1)}, u32[]{:S(2)}, u32[]{:S(2)}) collective-permute-start(bf16[3,256,256]{2,1,0:T(8,128)(2,1)S(1)} %shard_map.113), channel_id=1, source_target_pairs={{0,16},{4,20},{8,24},{12,28},{16,0},{20,4},{24,8},{28,12},{1,17},{... | collective-permute-start | bytes 1179656 | tf_op jit(solution)/shard_map/ppermute | solution.py:247
  20.8 12.9 %collective-permute-start.3 = (bf16[256,384]{1,0:T(8,128)(2,1)S(1)}, bf16[256,384]{1,0:T(8,128)(2,1)S(1)}, u32[]{:S(2)}, u32[]{:S(2)}) collective-permute-start(bf16[256,384]{1,0:T(8,128)(2,1)S(1)} %get-tuple-element.41), channel_id=1, source_target_pairs={{0,12},{4,8},{8,4},{12,0},{16,28},{20,24},{24,20},{28,16},{1,13},{... | collective-permute-start | bytes 589832 | tf_op jit(solution)/shard_map/ppermute | solution.py:244
  24.8 15.5 %collective-permute-start.4 = (bf16[256,384]{1,0:T(8,128)(2,1)S(1)}, bf16[256,384]{1,0:T(8,128)(2,1)S(1)}, u32[]{:S(2)}, u32[]{:S(2)}) collective-permute-start(bf16[256,384]{1,0:T(8,128)(2,1)S(1)} %get-tuple-element.42), channel_id=1, source_target_pairs={{0,8},{4,12},{8,0},{12,4},{16,24},{20,28},{24,16},{28,20},{1,9},{5... | collective-permute-start | bytes 589832 | tf_op jit(solution)/shard_map/ppermute | solution.py:244
  24.8 15.5 %collective-permute-start.5 = (bf16[256,384]{1,0:T(8,128)(2,1)S(1)}, bf16[256,384]{1,0:T(8,128)(2,1)S(1)}, u32[]{:S(2)}, u32[]{:S(2)}) collective-permute-start(bf16[256,384]{1,0:T(8,128)(2,1)S(1)} %get-tuple-element.43), channel_id=1, source_target_pairs={{0,4},{4,0},{8,12},{12,8},{16,20},{20,16},{24,28},{28,24},{1,5},{5... | collective-permute-start | bytes 589832 | tf_op jit(solution)/shard_map/ppermute | solution.py:244
  40.4 7.6 %collective-permute-start.18 = (bf16[4,256,128]{2,1,0:T(8,128)(2,1)S(1)}, bf16[4,256,128]{2,1,0:T(8,128)(2,1)S(1)}, u32[]{:S(2)}, u32[]{:S(2)}) collective-permute-start(bf16[4,256,128]{2,1,0:T(8,128)(2,1)S(1)} %shard_map.117.refs_0_), channel_id=1, source_target_pairs={{0,2},{1,3},{2,0},{3,1},{4,6},{5,7},{6,4},{7,5},{8,10},{9,11},{10,... | collective-permute-start | bytes 786440 | tf_op jit(solution)/shard_map/ppermute | solution.py:253
  44.4 17.7 %collective-permute-start.15 = (bf16[4,256,128]{2,1,0:T(8,128)(2,1)S(1)}, bf16[4,256,128]{2,1,0:T(8,128)(2,1)S(1)}, u32[]{:S(2)}, u32[]{:S(2)}) collective-permute-start(bf16[4,256,128]{2,1,0:T(8,128)(2,1)S(1)} %get-tuple-element.49.attn_ref.refs_3_), channel_id=1, source_target_pairs={{0,12},{4,8},{8,4},{12,0},{16,28},{20,24},{24,20},{28,16},{1,13},{... | collective-permute-start | bytes 786440 | tf_op jit(solution)/shard_map/ppermute | solution.py:244
  45.1 17.1 %collective-permute-start.16 = (bf16[4,256,128]{2,1,0:T(8,128)(2,1)S(1)}, bf16[4,256,128]{2,1,0:T(8,128)(2,1)S(1)}, u32[]{:S(2)}, u32[]{:S(2)}) collective-permute-start(bf16[4,256,128]{2,1,0:T(8,128)(2,1)S(1)} %get-tuple-element.49.attn_ref.refs_3_), channel_id=1, source_target_pairs={{0,8},{4,12},{8,0},{12,4},{16,24},{20,28},{24,16},{28,20},{1,9},{5... | collective-permute-start | bytes 786440 | tf_op jit(solution)/shard_map/ppermute | solution.py:244
  47.5 14.6 %collective-permute-start.17 = (bf16[4,256,128]{2,1,0:T(8,128)(2,1)S(1)}, bf16[4,256,128]{2,1,0:T(8,128)(2,1)S(1)}, u32[]{:S(2)}, u32[]{:S(2)}) collective-permute-start(bf16[4,256,128]{2,1,0:T(8,128)(2,1)S(1)} %get-tuple-element.49.attn_ref.refs_3_), channel_id=1, source_target_pairs={{0,4},{4,0},{8,12},{12,8},{16,20},{20,16},{24,28},{28,24},{1,5},{5... | collective-permute-start | bytes 786440 | tf_op jit(solution)/shard_map/ppermute | solution.py:244
  48.0 14.1 %collective-permute-start.19 = (bf16[2,4,256,128]{3,2,1,0:T(8,128)(2,1)S(1)}, bf16[2,4,256,128]{3,2,1,0:T(8,128)(2,1)S(1)}, u32[]{:S(2)}, u32[]{:S(2)}) collective-permute-start(bf16[2,4,256,128]{3,2,1,0:T(8,128)(2,1)S(1)} %shard_map.118.refs_4_), channel_id=1, source_target_pairs={{0,1},{1,0},{2,3},{3,2},{4,5},{5,4},{6,7},{7,6},{8,9},{9,8},{10,11... | collective-permute-start | bytes 1572872 | tf_op jit(solution)/shard_map/ppermute | solution.py:253
  48.1 14.1 %copy-start.1 = (bf16[512,2048]{1,0:T(8,128)(2,1)S(1)}, bf16[512,2048]{1,0:T(8,128)(2,1)}, u32[]{:S(2)}) copy-start(bf16[512,2048]{1,0:T(8,128)(2,1)} %copy-done) | copy-start | bytes 6291460
  50.5 11.5 %collective-permute-start.11 = (bf16[256,256]{1,0:T(8,128)(2,1)S(1)}, bf16[256,256]{1,0:T(8,128)(2,1)S(1)}, u32[]{:S(2)}, u32[]{:S(2)}) collective-permute-start(bf16[256,256]{1,0:T(8,128)(2,1)S(1)} %get-tuple-element.55), channel_id=1, source_target_pairs={{16,0},{20,4},{24,8},{28,12},{17,1},{21,5},{25,9},{29,13},{18,2},{... | collective-permute-start | bytes 393224 | tf_op jit(solution)/shard_map/ppermute | solution.py:250
  63.8 3.7 %collective-permute-start.21 = (bf16[256,1024]{1,0:T(8,128)(2,1)S(1)}, bf16[256,1024]{1,0:T(8,128)(2,1)S(1)}, u32[]{:S(2)}, u32[]{:S(2)}) collective-permute-start(bf16[256,1024]{1,0:T(8,128)(2,1)S(1)} %get-tuple-element.65), channel_id=1, source_target_pairs={{0,1},{1,0},{2,3},{3,2},{4,5},{5,4},{6,7},{7,6},{8,9},{9,8},{10,11... | collective-permute-start | bytes 1572872 | tf_op jit(solution)/shard_map/ppermute | solution.py:253
  63.9 18.0 %collective-permute-start.20 = (bf16[256,512]{1,0:T(8,128)(2,1)S(1)}, bf16[256,512]{1,0:T(8,128)(2,1)S(1)}, u32[]{:S(2)}, u32[]{:S(2)}) collective-permute-start(bf16[256,512]{1,0:T(8,128)(2,1)S(1)} %get-tuple-element.61), channel_id=1, source_target_pairs={{0,16},{4,20},{8,24},{12,28},{16,0},{20,4},{24,8},{28,12},{1,17},{... | collective-permute-start | bytes 786440 | tf_op jit(solution)/shard_map/ppermute | solution.py:247
  64.0 11.0 %collective-permute-start.12 = (bf16[256,384]{1,0:T(8,128)(2,1)S(1)}, bf16[256,384]{1,0:T(8,128)(2,1)S(1)}, u32[]{:S(2)}, u32[]{:S(2)}) collective-permute-start(bf16[256,384]{1,0:T(8,128)(2,1)S(1)} %get-tuple-element.56), channel_id=1, source_target_pairs={{0,12},{4,8},{8,4},{12,0},{16,28},{20,24},{24,20},{28,16},{1,13},{... | collective-permute-start | bytes 589832 | tf_op jit(solution)/shard_map/ppermute | solution.py:244
  64.7 17.2 %collective-permute-start.13 = (bf16[256,384]{1,0:T(8,128)(2,1)S(1)}, bf16[256,384]{1,0:T(8,128)(2,1)S(1)}, u32[]{:S(2)}, u32[]{:S(2)}) collective-permute-start(bf16[256,384]{1,0:T(8,128)(2,1)S(1)} %get-tuple-element.57), channel_id=1, source_target_pairs={{0,8},{4,12},{8,0},{12,4},{16,24},{20,28},{24,16},{28,20},{1,9},{5... | collective-permute-start | bytes 589832 | tf_op jit(solution)/shard_map/ppermute | solution.py:244
  66.9 15.0 %collective-permute-start.14 = (bf16[256,384]{1,0:T(8,128)(2,1)S(1)}, bf16[256,384]{1,0:T(8,128)(2,1)S(1)}, u32[]{:S(2)}, u32[]{:S(2)}) collective-permute-start(bf16[256,384]{1,0:T(8,128)(2,1)S(1)} %get-tuple-element.58), channel_id=1, source_target_pairs={{0,4},{4,0},{8,12},{12,8},{16,20},{20,16},{24,28},{28,24},{1,5},{5... | collective-permute-start | bytes 589832 | tf_op jit(solution)/shard_map/ppermute | solution.py:244
  67.6 15.5 %collective-permute-start.22 = (bf16[256,512]{1,0:T(8,128)(2,1)S(1)}, bf16[256,512]{1,0:T(8,128)(2,1)S(1)}, u32[]{:S(2)}, u32[]{:S(2)}) collective-permute-start(bf16[256,512]{1,0:T(8,128)(2,1)S(1)} %add_convert_fusion.1), channel_id=1, source_target_pairs={{0,2},{1,3},{2,0},{3,1},{4,6},{5,7},{6,4},{7,5},{8,10},{9,11},{10,... | collective-permute-start | bytes 786440 | tf_op jit(solution)/shard_map/ppermute | solution.py:253

commit v6 on v5

--- a/solution.py
+++ b/solution.py
@@ -13,6 +13,7 @@
 F32 = jnp.float32
 BF16 = jnp.bfloat16
 HIDDEN = -1e30
+TURN = (2, 3, 1, 0)
 VMEM = pl.BlockSpec(memory_space=pltpu.VMEM)
 ANY = pl.BlockSpec(memory_space=pl.ANY)
 HBM = pl.BlockSpec(memory_space=pltpu.HBM)
@@ -25,6 +26,14 @@
 
 def lanes(block, width):
     return pl.ds(pl.multiple_of(block * width, width), width)
+
+
+def turned(pieces):
+    return [pieces[m] for m in TURN]
+
+
+def straight(refs):
+    return [refs[TURN.index(m)] for m in range(len(TURN))]
 
 
 def call(body, outs, operands, specs=None, scratch=(), limit=20, flops=1):
@@ -64,13 +73,13 @@
 
 
 def slope_body(A, B, H, *refs):
-    grads, weight_ref, q_ref, refs = refs[:H], refs[H], refs[H + 1], refs[H + 2 :]
+    grads, weight_ref, q_ref, refs = refs[:2], refs[2], refs[3], refs[4:]
     outs, full, mixed = refs[:A], refs[-2], refs[-1]
     a = lax.axis_index("seg") % A
     h = lax.axis_index("head")
-    width = grads[0].shape[1]
+    width = grads[0].shape[2]
     for k in range(H):
-        full[:, lanes(h ^ k, width)] = grads[k][...]
+        full[:, lanes(h ^ k, width)] = grads[k % 2][k // 2]
     mixed[...] = dot(full[...], weight_ref[...], (1, 1)).astype(BF16)
     for m in range(A):
         head = lanes(a ^ m, DH)
@@ -81,7 +90,7 @@
 
 def pack_body(A, *refs):
     for m in range(1, A):
-        refs[-1][m - 1] = refs[A - 1 - m][...]
+        refs[-1][m - 1] = refs[TURN.index(m)][...]
 
 
 def collect_body(*refs):
@@ -102,7 +111,7 @@
 
 def forward_body(A, B, R, score_scale, owner_ref, block_ref, *refs):
     pair = B == 2
-    piece_refs, own_refs, others, refs = refs[:A][::-1], refs[A : 2 * A], refs[2 * A : -4], refs[-4:]
+    piece_refs, own_refs, others, refs = straight(refs[:A]), refs[A : 2 * A], refs[2 * A : -4], refs[-4:]
     attn_ref, kvcat, weights_ref, kv = refs
     SEG = piece_refs[0].shape[0]
     parts = SEG // BLOCK
@@ -184,7 +193,7 @@
 
 
 def project_body(A, B, H, *refs):
-    attns, gs, weight_ref, refs = refs[:A][::-1], refs[A : A + 2], refs[A + 2], refs[A + 4 :]
+    attns, gs, weight_ref, refs = straight(refs[:A]), refs[A : A + 2], refs[A + 2], refs[A + 3 :]
     keep_ref, pass_ref, send_ref, *proj_refs = refs[:-3]
     own, mixed, cots = refs[-3:]
     seg = lax.axis_index("seg")
@@ -222,13 +231,18 @@
         outs[m][:, DH:] = (own_ref[m] + late.astype(F32)).astype(BF16)
 
 
+def token_body(*refs):
+    refs[-1][...] = jnp.zeros_like(refs[-1])
+
+
 def place_body(A, B, *refs):
-    pieces, projs, outs = refs[:A][::-1], refs[A:-4], refs[-4:]
+    pieces, terms, projs, outs = straight(refs[:A]), refs[A : A + 3], refs[A + 3 : -6], refs[-5:]
     a = lax.axis_index("seg") % A
     for m in range(A):
         for i in range(3):
-            outs[i][:, lanes(a ^ m, DH)] = pieces[m][:, i * DH : (i + 1) * DH]
-    outs[3][...] = sum(term[...].astype(F32) for term in projs)
+            outs[1 + i][:, lanes(a ^ m, DH)] = pieces[m][:, i * DH : (i + 1) * DH]
+    outs[0][...] = sum(term[...].astype(F32) for term in terms).astype(BF16)
+    outs[4][...] = sum(term[...].astype(F32) for term in projs)
 
 
 def per_device(queries, keys, values, out_grad, out_weight, retr_owner, retr_block):
@@ -256,20 +270,24 @@
         moved = {m: over_a(pieces[m], m) for m in reversed(range(1, A))}
         return [pieces[0]] + [moved[m] for m in range(1, A)]
 
-    grads = [out_grad, over_head(out_grad, 1), over_head(out_grad, 2)]
-    grads += [over_head(grads[2], 1)]
 
     cut = functools.partial(cut_body, A, B)
-    kvs = exchange(call(cut, [shape((SEG, 2 * DH), BF16)] * A, [keys, values]))
+    kvs = call(cut, [shape((SEG, 2 * DH), BF16)] * A, [keys, values])
+    out_grad, kvs[0] = lax.optimization_barrier((out_grad, kvs[0]))
+    far_grad = over_head(out_grad, 2)
+    kvs = exchange(kvs)
     staged = call(stage_body, [shape(x.shape, BF16) for x in (out_weight, queries, out_grad)], [out_weight, queries, out_grad])
     early = [over_b(kvs[0])] if B == 2 else []
     kv = call(
         functools.partial(pack_body, A),
         [shape((A - 1, SEG, 2 * DH), BF16)],
-        [*kvs[:0:-1], *early, staged[0]],
+        [*turned(kvs)[:-1], *early, staged[0]],
         specs=[VMEM] * (A - 1) + [ANY] * (1 + len(early)),
+        flops=40 * 10**8,
     )[0]
-    out_weight, queries, grads[0] = staged
+    out_weight, queries, near_grad = staged
+    both = call(join_body, [shape((2, SEG, width), BF16)], [near_grad, far_grad])[0]
+    grads = [both, over_head(both, 1)]
     if B == 2:
         kv = [*early, over_b(kv)]
     else:
@@ -281,7 +299,7 @@
         [shape((SEG, 2 * DH + width // H), BF16)] * A,
         [*grads, out_weight, queries],
         scratch=[pltpu.VMEM((SEG, D), BF16), pltpu.VMEM((SEG, width), BF16)],
-        flops=2 * 10**8,
+        flops=1,
     )
     pieces = exchange(sloped)
     count = 2 * SEG + R * BLOCK
@@ -291,7 +309,7 @@
     attn, kvcat, weights = call(
         functools.partial(forward_body, A, B, R, score_scale),
         [shape((A, SEG, DH), BF16), shape((A, count, 2 * DH), BF16), shape((A, SEG, count), F32)],
-        [retr_owner, retr_block, *pieces[::-1], *kvs, *kv],
+        [retr_owner, retr_block, *turned(pieces), *kvs, *kv],
         specs=[SMEM] * 2 + [VMEM] * (2 * A + len(kv)),
         scratch=[pltpu.VMEM((2 * A * (SEG // BLOCK), BLOCK, 2 * DH), BF16)],
         limit=limit,
@@ -314,7 +332,10 @@
     cots = call(join_body, [shape((2, *cot.shape), BF16)], [cot, far_cot])[0]
     gs = [cots, over_head(cots, 1)]
     merged = call(
-        functools.partial(merge_body, A), [shape((SEG, 3 * DH), BF16)] * A, [dq, own, cache, carried]
+        functools.partial(merge_body, A),
+        [shape((SEG, 3 * DH), BF16)] * A,
+        [dq, own, cache, carried],
+        flops=10 * 10**9,
     )
     partials = [shape((SEG, D // H), F32)] * 2 + [shape((SEG, D // 2), BF16)]
     rows = D // A
@@ -325,8 +346,8 @@
     keep, passed, send, *proj = call(
         functools.partial(project_body, A, B, H),
         partials + projs,
-        [*attns[::-1], *gs, out_weight, merged[0]],
-        specs=[VMEM] * (A + 3) + [ANY],
+        [*turned(attns), *gs, out_weight],
+        specs=[VMEM] * (A + 3),
         scratch=[
             pltpu.VMEM((SEG, width), BF16),
             pltpu.VMEM((A * SEG, width), BF16),
@@ -341,15 +362,15 @@
         proj = [proj[0], over_b(proj[1])]
     else:
         proj = [lax.psum_scatter(proj[0], "seg", scatter_dimension=0, axis_index_groups=groups, tiled=True)]
-    *placed, proj_grad_t = call(
-        functools.partial(place_body, A, B),
-        [shape((SEG, width), BF16)] * 3 + [shape(proj[0].shape, F32)],
-        [*moved[::-1], *proj],
-        flops=10**11,
-    )
-    placed[0], keep = lax.optimization_barrier((placed[0], keep))
-    layer_out = keep + received[:, :block].astype(F32) + over_head(passed, 2).astype(F32)
-    return (layer_out.astype(BF16), *placed, proj_grad_t)
+    token = call(token_body, [shape((8, 128), F32)], [*moved[1:], *proj[1:]], specs=[ANY] * (A - 2 + len(proj)), flops=10**11)
+    return tuple(
+        call(
+            functools.partial(place_body, A, B),
+            [shape((SEG, width), BF16)] * 4 + [shape(proj[0].shape, F32)],
+            [*turned(moved), keep, received[:, :block], over_head(passed, 2), *proj, *token],
+            specs=[VMEM] * (A + 3 + len(proj)) + [ANY],
+        )
+    )
 
 
 def solution(mesh):

time: 84.2 us -> 78.4 us (0.931)
  waiting for transfers between devices: 40.3 us -> 33.5 us
  starting transfers between devices: 26.2 us -> 27.9 us
    ppermute x1, waiting for transfers between devices: 10.2 us -> 0.01 us  [back_b(): return lax.ppermute(x, 'seg', [(i, i - A) for i in range(A, n)])]
    ppermute x12, waiting for transfers between devices: 27.4 us -> 32 us  [over_a(): lax.ppermute(x, 'seg', [(i, i // A * A + (i % A ^ m)) for i in range(n)])]
    ppermute x3, starting transfers between devices: 3.84 us -> 7.18 us  [over_b(): return lax.ppermute(x, 'seg', [(i, (i + A) % n) for i in range(n)])]
    ppermute x3, waiting for transfers between devices: 2.7 us -> 1.4 us  [over_b(): return lax.ppermute(x, 'seg', [(i, (i + A) % n) for i in range(n)])]
    ppermute x12, starting transfers between devices: 15.3 us -> 14.3 us  [over_a(): lax.ppermute(x, 'seg', [(i, i // A * A + (i % A ^ m)) for i in range(n)])]
    ppermute x7 -> x6, starting transfers between devices: 5.81 us -> 5.18 us  [over_head(): return lax.ppermute(x, 'head', [(i, i ^ k) for i in range(H)])]
    pallas_call x11 -> x13, Pallas kernels: 10.1 us -> 10.3 us  [call(): pl.pallas_call(body, out_shape=outs, in_specs=specs or [VMEM] * len(opera...]
  transfers between devices with their start and end apart: 23 -> 22, of which waited for: 6 -> 10; matrix products, arithmetic and copies ran while one was open for 0% -> 0% of each run, Pallas kernels for 10% -> 11%
where the time goes in v6:
time: 78.4 us; the launch traced here: 78.1 us
  waiting for transfers between devices  33.5 us (43%)
  starting transfers between devices  27.9 us (36%)
  Pallas kernels  10.3 us (13%)
  local copies, waits for them, and re-layouts  5.58 us (7%)
  between operations  0.84 us (1%)
    ppermute x12, waiting for transfers between devices, over_a(): lax.ppermute(x, 'seg', [(i, i // A * A + (i % A ^ m)) for i in range(n)])  32 us
    ppermute x12, starting transfers between devices, over_a(): lax.ppermute(x, 'seg', [(i, i // A * A + (i % A ^ m)) for i in range(n)])  14.3 us
    pallas_call x13, Pallas kernels, call(): pl.pallas_call(body, out_shape=outs, in_specs=specs or [VMEM] * len(opera...  10.3 us
    ppermute x3, starting transfers between devices, over_b(): return lax.ppermute(x, 'seg', [(i, (i + A) % n) for i in range(n)])  7.18 us
    unnamed x20, local copies, waits for them, and re-layouts  5.56 us
    ppermute x6, starting transfers between devices, over_head(): return lax.ppermute(x, 'head', [(i, i ^ k) for i in range(H)])  5.18 us
  transfers between devices with their start and end apart: 22, of which 10 were waited for; matrix products, arithmetic and copies ran while one was open for 0% of the time, Pallas kernels for 11%

profile of v6, /device:TPU:0, one launch (start us, length us, event | category | flops | bytes accessed | tf_op | source)
XLA Modules:
  0.0 78.1 jit_solution(284300455245670533)
XLA Ops:
  0.6 0.9 %copy-done.5 = bf16[256,512]{1,0:T(8,128)(2,1)S(1)} copy-done((bf16[256,512]{1,0:T(8,128)(2,1)S(1)}, bf16[256,512]{1,0:T(8,128)(2,1)}, u32[]{:S(2)}) %copy-start.5) | copy-done | bytes 262168
  1.6 0.9 %copy-done.6 = bf16[256,512]{1,0:T(8,128)(2,1)S(1)} copy-done((bf16[256,512]{1,0:T(8,128)(2,1)S(1)}, bf16[256,512]{1,0:T(8,128)(2,1)}, u32[]{:S(2)}) %copy-start.6) | copy-done | bytes 262168
  2.6 3.0 %collective-permute-start = (bf16[256,512]{1,0:T(8,128)(2,1)}, bf16[256,512]{1,0:T(8,128)(2,1)S(1)}, u32[]{:S(2)}, u32[]{:S(2)}) collective-permute-start(bf16[256,512]{1,0:T(8,128)(2,1)} %refs_2_), channel_id=1, source_target_pairs={{0,2},{1,3},{2,0},{3,1},{4,6},{5,7},{6,4},{7,5},{8,10},{9,11},{10,... | collective-permute-start | bytes 786440 | tf_op jit(solution)/shard_map/ppermute | solution.py:267
  5.6 1.5 %collective-permute-start.5 = (bf16[256,256]{1,0:T(8,128)(2,1)S(1)}, bf16[256,256]{1,0:T(8,128)(2,1)S(1)}, u32[]{:S(2)}, u32[]{:S(2)}) collective-permute-start(bf16[256,256]{1,0:T(8,128)(2,1)S(1)} %get-tuple-element.44), channel_id=1, source_target_pairs={{0,4},{4,0},{8,12},{12,8},{16,20},{20,16},{24,28},{28,24},{1,5},{5... | collective-permute-start | bytes 393224 | tf_op jit(solution)/shard_map/ppermute | solution.py:258
  7.2 1.6 %collective-permute-start.6 = (bf16[256,256]{1,0:T(8,128)(2,1)S(1)}, bf16[256,256]{1,0:T(8,128)(2,1)S(1)}, u32[]{:S(2)}, u32[]{:S(2)}) collective-permute-start(bf16[256,256]{1,0:T(8,128)(2,1)S(1)} %get-tuple-element.45), channel_id=1, source_target_pairs={{0,8},{4,12},{8,0},{12,4},{16,24},{20,28},{24,16},{28,20},{1,9},{5... | collective-permute-start | bytes 393224 | tf_op jit(solution)/shard_map/ppermute | solution.py:258
  9.1 2.6 %collective-permute-start.8 = (bf16[256,256]{1,0:T(8,128)(2,1)S(1)}, bf16[256,256]{1,0:T(8,128)(2,1)S(1)}, u32[]{:S(2)}, u32[]{:S(2)}) collective-permute-start(bf16[256,256]{1,0:T(8,128)(2,1)S(1)} %get-tuple-element.43.refs_4_), channel_id=1, source_target_pairs={{0,16},{4,20},{8,24},{12,28},{16,0},{20,4},{24,8},{28,12},{1,17},{... | collective-permute-start | bytes 393224 | tf_op jit(solution)/shard_map/ppermute | solution.py:261
  11.7 1.6 %copy-done.2 = bf16[512,2048]{1,0:T(8,128)(2,1)S(1)} copy-done((bf16[512,2048]{1,0:T(8,128)(2,1)S(1)}, bf16[512,2048]{1,0:T(8,128)(2,1)}, u32[]{:S(2)}) %copy-start.2) | copy-done | bytes 2097176
  13.3 0.9 %copy-done.3 = bf16[256,512]{1,0:T(8,128)(2,1)S(1)} copy-done((bf16[256,512]{1,0:T(8,128)(2,1)S(1)}, bf16[256,512]{1,0:T(8,128)(2,1)}, u32[]{:S(2)}) %copy-start.3) | copy-done | bytes 262168
  14.3 0.9 %copy-done.4 = bf16[256,512]{1,0:T(8,128)(2,1)S(1)} copy-done((bf16[256,512]{1,0:T(8,128)(2,1)S(1)}, bf16[256,512]{1,0:T(8,128)(2,1)}, u32[]{:S(2)}) %copy-start.4) | copy-done | bytes 262168
  16.0 1.6 %collective-permute-done.7.refs_1_.refs_7_ = bf16[256,256]{1,0:T(8,128)(2,1)S(1)} collective-permute-done((bf16[256,256]{1,0:T(8,128)(2,1)S(1)}, bf16[256,256]{1,0:T(8,128)(2,1)S(1)}, u32[]{:S(2)}, u32[]{:S(2)}) %collective-permute-start.7) | collective-permute-done | bytes 131104 | tf_op jit(solution)/shard_map/ppermute | solution.py:258
  17.7 2.4 %collective-permute-start.9 = (bf16[3,256,256]{2,1,0:T(8,128)(2,1)S(1)}, bf16[3,256,256]{2,1,0:T(8,128)(2,1)S(1)}, u32[]{:S(2)}, u32[]{:S(2)}) collective-permute-start(bf16[3,256,256]{2,1,0:T(8,128)(2,1)S(1)} %shard_map.114), channel_id=1, source_target_pairs={{0,16},{4,20},{8,24},{12,28},{16,0},{20,4},{24,8},{28,12},{1,17},{... | collective-permute-start | bytes 1179656 | tf_op jit(solution)/shard_map/ppermute | solution.py:261
  21.1 1.5 %collective-permute-start.2 = (bf16[256,384]{1,0:T(8,128)(2,1)S(1)}, bf16[256,384]{1,0:T(8,128)(2,1)S(1)}, u32[]{:S(2)}, u32[]{:S(2)}) collective-permute-start(bf16[256,384]{1,0:T(8,128)(2,1)S(1)} %get-tuple-element.39), channel_id=1, source_target_pairs={{0,8},{4,12},{8,0},{12,4},{16,24},{20,28},{24,16},{28,20},{1,9},{5... | collective-permute-start | bytes 589832 | tf_op jit(solution)/shard_map/ppermute | solution.py:258
  22.6 1.1 %collective-permute-start.3 = (bf16[256,384]{1,0:T(8,128)(2,1)S(1)}, bf16[256,384]{1,0:T(8,128)(2,1)S(1)}, u32[]{:S(2)}, u32[]{:S(2)}) collective-permute-start(bf16[256,384]{1,0:T(8,128)(2,1)S(1)} %get-tuple-element.40), channel_id=1, source_target_pairs={{0,12},{4,8},{8,4},{12,0},{16,28},{20,24},{24,20},{28,16},{1,13},{... | collective-permute-start | bytes 589832 | tf_op jit(solution)/shard_map/ppermute | solution.py:258
  24.8 8.5 %collective-permute-done.2.refs_0_.refs_2_ = bf16[256,384]{1,0:T(8,128)(2,1)S(1)} collective-permute-done((bf16[256,384]{1,0:T(8,128)(2,1)S(1)}, bf16[256,384]{1,0:T(8,128)(2,1)S(1)}, u32[]{:S(2)}, u32[]{:S(2)}) %collective-permute-start.2) | collective-permute-done | bytes 196640 | tf_op jit(solution)/shard_map/ppermute | solution.py:258
  33.3 2.1 %collective-permute-done.3.refs_1_.refs_3_ = bf16[256,384]{1,0:T(8,128)(2,1)S(1)} collective-permute-done((bf16[256,384]{1,0:T(8,128)(2,1)S(1)}, bf16[256,384]{1,0:T(8,128)(2,1)S(1)}, u32[]{:S(2)}, u32[]{:S(2)}) %collective-permute-start.3) | collective-permute-done | bytes 196640 | tf_op jit(solution)/shard_map/ppermute | solution.py:258
  36.1 1.4 %collective-permute-done.9.refs_9_ = bf16[3,256,256]{2,1,0:T(8,128)(2,1)S(1)} collective-permute-done((bf16[3,256,256]{2,1,0:T(8,128)(2,1)S(1)}, bf16[3,256,256]{2,1,0:T(8,128)(2,1)S(1)}, u32[]{:S(2)}, u32[]{:S(2)}) %collective-permute-start.9) | collective-permute-done | bytes 393248 | tf_op jit(solution)/shard_map/ppermute | solution.py:261
  37.5 3.5 %shard_map.115 = (bf16[4,256,128]{2,1,0:T(8,128)(2,1)S(1)}, bf16[4,1024,256]{2,1,0:T(8,128)(2,1)S(1)}, f32[4,256,1024]{2,1,0:T(8,128)S(1)}) custom-call(s32[8,4]{1,0:T(8,128)S(1)} %copy.12.owner_ref, s32[8,4]{1,0:T(8,128)S(1)} %copy.13.block_ref, bf16[256,384]{1,0:T(8,128)(2,1)S(1)} %collective-permute-done.2.refs_0_.refs_2_, ...), custom_call_target="tpu_custom_call" | custom-call | flops 99999997952 | bytes 1 | tf_op jit(solution)/shard_map/pallas_call | solution.py:40
  40.9 1.1 %collective-permute-start.14 = (bf16[4,256,128]{2,1,0:T(8,128)(2,1)S(1)}, bf16[4,256,128]{2,1,0:T(8,128)(2,1)S(1)}, u32[]{:S(2)}, u32[]{:S(2)}) collective-permute-start(bf16[4,256,128]{2,1,0:T(8,128)(2,1)S(1)} %get-tuple-element.47.attn_ref.refs_3_), channel_id=1, source_target_pairs={{0,8},{4,12},{8,0},{12,4},{16,24},{20,28},{24,16},{28,20},{1,9},{5... | collective-permute-start | bytes 786440 | tf_op jit(solution)/shard_map/ppermute | solution.py:258
  42.0 2.6 %collective-permute-start.15 = (bf16[4,256,128]{2,1,0:T(8,128)(2,1)S(1)}, bf16[4,256,128]{2,1,0:T(8,128)(2,1)S(1)}, u32[]{:S(2)}, u32[]{:S(2)}) collective-permute-start(bf16[4,256,128]{2,1,0:T(8,128)(2,1)S(1)} %get-tuple-element.47.attn_ref.refs_3_), channel_id=1, source_target_pairs={{0,12},{4,8},{8,4},{12,0},{16,28},{20,24},{24,20},{28,16},{1,13},{... | collective-permute-start | bytes 786440 | tf_op jit(solution)/shard_map/ppermute | solution.py:258
  44.7 2.4 %shard_map.116 = (bf16[4,256,128]{2,1,0:T(8,128)(2,1)S(1)}, f32[4,256,256]{2,1,0:T(8,128)S(1)}, bf16[4,256,256]{2,1,0:T(8,128)(2,1)S(1)}, bf16[256,256]{1,0:T(8,128)(2,1)S(1)}) custom-call(bf16[4,256,128]{2,1,0:T(8,128)(2,1)S(1)} %get-tuple-element.47.attn_ref.refs_3_, bf16[4,1024,256]{2,1,0:T(8,128)(2,1)S(1)} %get-tuple-element.48.kvcat, ...), custom_call_target="tpu_custom_call" | custom-call | flops 99999997952 | bytes 1 | tf_op jit(solution)/shard_map/pallas_call | solution.py:40
  47.1 1.3 %collective-permute-start.10 = (bf16[256,256]{1,0:T(8,128)(2,1)S(1)}, bf16[256,256]{1,0:T(8,128)(2,1)S(1)}, u32[]{:S(2)}, u32[]{:S(2)}) collective-permute-start(bf16[256,256]{1,0:T(8,128)(2,1)S(1)} %get-tuple-element.53), channel_id=1, source_target_pairs={{16,0},{20,4},{24,8},{28,12},{17,1},{21,5},{25,9},{29,13},{18,2},{... | collective-permute-start | bytes 393224 | tf_op jit(solution)/shard_map/ppermute | solution.py:264
  48.4 1.8 %collective-permute-done.14.refs_0_ = bf16[4,256,128]{2,1,0:T(8,128)(2,1)S(1)} collective-permute-done((bf16[4,256,128]{2,1,0:T(8,128)(2,1)S(1)}, bf16[4,256,128]{2,1,0:T(8,128)(2,1)S(1)}, u32[]{:S(2)}, u32[]{:S(2)}) %collective-permute-start.14) | collective-permute-done | bytes 262176 | tf_op jit(solution)/shard_map/ppermute | solution.py:258
  50.2 3.1 %collective-permute-done.15.refs_1_ = bf16[4,256,128]{2,1,0:T(8,128)(2,1)S(1)} collective-permute-done((bf16[4,256,128]{2,1,0:T(8,128)(2,1)S(1)}, bf16[4,256,128]{2,1,0:T(8,128)(2,1)S(1)}, u32[]{:S(2)}, u32[]{:S(2)}) %collective-permute-start.15) | collective-permute-done | bytes 262176 | tf_op jit(solution)/shard_map/ppermute | solution.py:258
  53.3 1.9 %collective-permute-done.16.refs_2_ = bf16[4,256,128]{2,1,0:T(8,128)(2,1)S(1)} collective-permute-done((bf16[4,256,128]{2,1,0:T(8,128)(2,1)S(1)}, bf16[4,256,128]{2,1,0:T(8,128)(2,1)S(1)}, u32[]{:S(2)}, u32[]{:S(2)}) %collective-permute-start.16) | collective-permute-done | bytes 262176 | tf_op jit(solution)/shard_map/ppermute | solution.py:258
  55.2 1.6 %shard_map.120 = (f32[256,512]{1,0:T(8,128)S(1)}, f32[256,512]{1,0:T(8,128)S(1)}, bf16[256,1024]{1,0:T(8,128)(2,1)S(1)}, f32[256,512]{1,0:T(8,128)S(1)}, bf16[256,512]{1,0:T(8,128)(2,1)S(1)}) custom-call(bf16[4,256,128]{2,1,0:T(8,128)(2,1)S(1)} %collective-permute-done.14.refs_0_, bf16[4,256,128]{2,1,0:T(8,128)(2,1)S(1)} %collective-permute-done.15.refs_1_, ...), custom_call_target="tpu_custom_call" | custom-call | flops 1 | bytes 1 | tf_op jit(solution)/shard_map/pallas_call | solution.py:40
  56.9 2.2 %collective-permute-start.21 = (bf16[256,512]{1,0:T(8,128)(2,1)S(1)}, bf16[256,512]{1,0:T(8,128)(2,1)S(1)}, u32[]{:S(2)}, u32[]{:S(2)}) collective-permute-start(bf16[256,512]{1,0:T(8,128)(2,1)S(1)} %get-tuple-element.62), channel_id=1, source_target_pairs={{0,16},{4,20},{8,24},{12,28},{16,0},{20,4},{24,8},{28,12},{1,17},{... | collective-permute-start | bytes 786440 | tf_op jit(solution)/shard_map/ppermute | solution.py:261
  59.3 1.7 %collective-permute-start.11 = (bf16[256,384]{1,0:T(8,128)(2,1)S(1)}, bf16[256,384]{1,0:T(8,128)(2,1)S(1)}, u32[]{:S(2)}, u32[]{:S(2)}) collective-permute-start(bf16[256,384]{1,0:T(8,128)(2,1)S(1)} %get-tuple-element.54), channel_id=1, source_target_pairs={{0,8},{4,12},{8,0},{12,4},{16,24},{20,28},{24,16},{28,20},{1,9},{5... | collective-permute-start | bytes 589832 | tf_op jit(solution)/shard_map/ppermute | solution.py:258
  61.0 1.2 %collective-permute-start.12 = (bf16[256,384]{1,0:T(8,128)(2,1)S(1)}, bf16[256,384]{1,0:T(8,128)(2,1)S(1)}, u32[]{:S(2)}, u32[]{:S(2)}) collective-permute-start(bf16[256,384]{1,0:T(8,128)(2,1)S(1)} %get-tuple-element.55), channel_id=1, source_target_pairs={{0,12},{4,8},{8,4},{12,0},{16,28},{20,24},{24,20},{28,16},{1,13},{... | collective-permute-start | bytes 589832 | tf_op jit(solution)/shard_map/ppermute | solution.py:258
  62.9 1.4 %collective-permute-start.20 = (bf16[256,512]{1,0:T(8,128)(2,1)S(1)}, bf16[256,512]{1,0:T(8,128)(2,1)S(1)}, u32[]{:S(2)}, u32[]{:S(2)}) collective-permute-start(bf16[256,512]{1,0:T(8,128)(2,1)S(1)} %add_convert_fusion), channel_id=1, source_target_pairs={{0,2},{1,3},{2,0},{3,1},{4,6},{5,7},{6,4},{7,5},{8,10},{9,11},{10,... | collective-permute-start | bytes 786440 | tf_op jit(solution)/shard_map/ppermute | solution.py:267
  64.3 5.7 %collective-permute-done.11.refs_1_.refs_0_ = bf16[256,384]{1,0:T(8,128)(2,1)S(1)} collective-permute-done((bf16[256,384]{1,0:T(8,128)(2,1)S(1)}, bf16[256,384]{1,0:T(8,128)(2,1)S(1)}, u32[]{:S(2)}, u32[]{:S(2)}) %collective-permute-start.11) | collective-permute-done | bytes 196640 | tf_op jit(solution)/shard_map/ppermute | solution.py:258
  70.0 6.7 %collective-permute-done.12.refs_2_.refs_1_ = bf16[256,384]{1,0:T(8,128)(2,1)S(1)} collective-permute-done((bf16[256,384]{1,0:T(8,128)(2,1)S(1)}, bf16[256,384]{1,0:T(8,128)(2,1)S(1)}, u32[]{:S(2)}, u32[]{:S(2)}) %collective-permute-start.12) | collective-permute-done | bytes 196640 | tf_op jit(solution)/shard_map/ppermute | solution.py:258
  76.8 1.4 %shard_map.122 = (bf16[256,512]{1,0:T(8,128)(2,1)}, bf16[256,512]{1,0:T(8,128)(2,1)}, bf16[256,512]{1,0:T(8,128)(2,1)}, bf16[256,512]{1,0:T(8,128)(2,1)}, f32[256,512]{1,0:T(8,128)}) custom-call(bf16[256,384]{1,0:T(8,128)(2,1)S(1)} %collective-permute-done.11.refs_1_.refs_0_, bf16[256,384]{1,0:T(8,128)(2,1)S(1)} %collective-permute-done.12.refs_2_.refs_1_, ...), custom_call_target="tpu_custom_call" | custom-call | flops 1 | bytes 1 | tf_op jit(solution)/shard_map/pallas_call | solution.py:40
  (47 shorter events, 5.0 us)
Async XLA Ops:
  0.6 1.0 %copy-start.5 = (bf16[256,512]{1,0:T(8,128)(2,1)S(1)}, bf16[256,512]{1,0:T(8,128)(2,1)}, u32[]{:S(2)}) copy-start(bf16[256,512]{1,0:T(8,128)(2,1)} %k_ref.1) | copy-start | bytes 786436
  1.6 0.9 %copy-start.6 = (bf16[256,512]{1,0:T(8,128)(2,1)S(1)}, bf16[256,512]{1,0:T(8,128)(2,1)}, u32[]{:S(2)}) copy-start(bf16[256,512]{1,0:T(8,128)(2,1)} %v_ref.1) | copy-start | bytes 786436
  2.6 12.8 %collective-permute-start = (bf16[256,512]{1,0:T(8,128)(2,1)}, bf16[256,512]{1,0:T(8,128)(2,1)S(1)}, u32[]{:S(2)}, u32[]{:S(2)}) collective-permute-start(bf16[256,512]{1,0:T(8,128)(2,1)} %refs_2_), channel_id=1, source_target_pairs={{0,2},{1,3},{2,0},{3,1},{4,6},{5,7},{6,4},{7,5},{8,10},{9,11},{10,... | collective-permute-start | bytes 786440 | tf_op jit(solution)/shard_map/ppermute | solution.py:267
  5.6 9.9 %collective-permute-start.5 = (bf16[256,256]{1,0:T(8,128)(2,1)S(1)}, bf16[256,256]{1,0:T(8,128)(2,1)S(1)}, u32[]{:S(2)}, u32[]{:S(2)}) collective-permute-start(bf16[256,256]{1,0:T(8,128)(2,1)S(1)} %get-tuple-element.44), channel_id=1, source_target_pairs={{0,4},{4,0},{8,12},{12,8},{16,20},{20,16},{24,28},{28,24},{1,5},{5... | collective-permute-start | bytes 393224 | tf_op jit(solution)/shard_map/ppermute | solution.py:258
  7.2 8.9 %collective-permute-start.6 = (bf16[256,256]{1,0:T(8,128)(2,1)S(1)}, bf16[256,256]{1,0:T(8,128)(2,1)S(1)}, u32[]{:S(2)}, u32[]{:S(2)}) collective-permute-start(bf16[256,256]{1,0:T(8,128)(2,1)S(1)} %get-tuple-element.45), channel_id=1, source_target_pairs={{0,8},{4,12},{8,0},{12,4},{16,24},{20,28},{24,16},{28,20},{1,9},{5... | collective-permute-start | bytes 393224 | tf_op jit(solution)/shard_map/ppermute | solution.py:258
  8.7 9.0 %collective-permute-start.7 = (bf16[256,256]{1,0:T(8,128)(2,1)S(1)}, bf16[256,256]{1,0:T(8,128)(2,1)S(1)}, u32[]{:S(2)}, u32[]{:S(2)}) collective-permute-start(bf16[256,256]{1,0:T(8,128)(2,1)S(1)} %get-tuple-element.46), channel_id=1, source_target_pairs={{0,12},{4,8},{8,4},{12,0},{16,28},{20,24},{24,20},{28,16},{1,13},{... | collective-permute-start | bytes 393224 | tf_op jit(solution)/shard_map/ppermute | solution.py:258
  9.1 8.6 %collective-permute-start.8 = (bf16[256,256]{1,0:T(8,128)(2,1)S(1)}, bf16[256,256]{1,0:T(8,128)(2,1)S(1)}, u32[]{:S(2)}, u32[]{:S(2)}) collective-permute-start(bf16[256,256]{1,0:T(8,128)(2,1)S(1)} %get-tuple-element.43.refs_4_), channel_id=1, source_target_pairs={{0,16},{4,20},{8,24},{12,28},{16,0},{20,4},{24,8},{28,12},{1,17},{... | collective-permute-start | bytes 393224 | tf_op jit(solution)/shard_map/ppermute | solution.py:261
  11.7 1.6 %copy-start.2 = (bf16[512,2048]{1,0:T(8,128)(2,1)S(1)}, bf16[512,2048]{1,0:T(8,128)(2,1)}, u32[]{:S(2)}) copy-start(bf16[512,2048]{1,0:T(8,128)(2,1)} %refs_0_.1) | copy-start | bytes 6291460
  13.3 0.9 %copy-start.3 = (bf16[256,512]{1,0:T(8,128)(2,1)S(1)}, bf16[256,512]{1,0:T(8,128)(2,1)}, u32[]{:S(2)}) copy-start(bf16[256,512]{1,0:T(8,128)(2,1)} %refs_1_.1) | copy-start | bytes 786436
  14.3 0.9 %copy-start.4 = (bf16[256,512]{1,0:T(8,128)(2,1)S(1)}, bf16[256,512]{1,0:T(8,128)(2,1)}, u32[]{:S(2)}) copy-start(bf16[256,512]{1,0:T(8,128)(2,1)} %refs_2_) | copy-start | bytes 786436
  15.4 4.8 %copy-start = (bf16[512,2048]{1,0:T(8,128)(2,1)}, bf16[512,2048]{1,0:T(8,128)(2,1)S(1)}, u32[]{:S(2)}) copy-start(bf16[512,2048]{1,0:T(8,128)(2,1)S(1)} %get-tuple-element.37.refs_2_.refs_4_.refs_6_) | copy-start | bytes 6291460
  15.4 4.7 %collective-permute-start.1 = (bf16[2,256,512]{2,1,0:T(8,128)(2,1)S(1)}, bf16[2,256,512]{2,1,0:T(8,128)(2,1)S(1)}, u32[]{:S(2)}, u32[]{:S(2)}) collective-permute-start(bf16[2,256,512]{2,1,0:T(8,128)(2,1)S(1)} %shard_map.112.refs_0_), channel_id=1, source_target_pairs={{0,1},{1,0},{2,3},{3,2},{4,5},{5,4},{6,7},{7,6},{8,9},{9,8},{10,11... | collective-permute-start | bytes 1572872 | tf_op jit(solution)/shard_map/ppermute | solution.py:267
  17.7 6.9 %copy-start.7 = (s32[8,4]{0,1:T(4,128)S(1)}, s32[8,4]{0,1:T(4,128)}, u32[]{:S(2)}) copy-start(s32[8,4]{0,1:T(4,128)} %param.12) | copy-start | bytes 388
  17.7 7.0 %copy-start.8 = (s32[8,4]{0,1:T(4,128)S(1)}, s32[8,4]{0,1:T(4,128)}, u32[]{:S(2)}) copy-start(s32[8,4]{0,1:T(4,128)} %param.13) | copy-start | bytes 388
  17.7 19.7 %collective-permute-start.9 = (bf16[3,256,256]{2,1,0:T(8,128)(2,1)S(1)}, bf16[3,256,256]{2,1,0:T(8,128)(2,1)S(1)}, u32[]{:S(2)}, u32[]{:S(2)}) collective-permute-start(bf16[3,256,256]{2,1,0:T(8,128)(2,1)S(1)} %shard_map.114), channel_id=1, source_target_pairs={{0,16},{4,20},{8,24},{12,28},{16,0},{20,4},{24,8},{28,12},{1,17},{... | collective-permute-start | bytes 1179656 | tf_op jit(solution)/shard_map/ppermute | solution.py:261
  21.1 12.2 %collective-permute-start.2 = (bf16[256,384]{1,0:T(8,128)(2,1)S(1)}, bf16[256,384]{1,0:T(8,128)(2,1)S(1)}, u32[]{:S(2)}, u32[]{:S(2)}) collective-permute-start(bf16[256,384]{1,0:T(8,128)(2,1)S(1)} %get-tuple-element.39), channel_id=1, source_target_pairs={{0,8},{4,12},{8,0},{12,4},{16,24},{20,28},{24,16},{28,20},{1,9},{5... | collective-permute-start | bytes 589832 | tf_op jit(solution)/shard_map/ppermute | solution.py:258
  22.6 12.8 %collective-permute-start.3 = (bf16[256,384]{1,0:T(8,128)(2,1)S(1)}, bf16[256,384]{1,0:T(8,128)(2,1)S(1)}, u32[]{:S(2)}, u32[]{:S(2)}) collective-permute-start(bf16[256,384]{1,0:T(8,128)(2,1)S(1)} %get-tuple-element.40), channel_id=1, source_target_pairs={{0,12},{4,8},{8,4},{12,0},{16,28},{20,24},{24,20},{28,16},{1,13},{... | collective-permute-start | bytes 589832 | tf_op jit(solution)/shard_map/ppermute | solution.py:258
  23.7 11.7 %collective-permute-start.4 = (bf16[256,384]{1,0:T(8,128)(2,1)S(1)}, bf16[256,384]{1,0:T(8,128)(2,1)S(1)}, u32[]{:S(2)}, u32[]{:S(2)}) collective-permute-start(bf16[256,384]{1,0:T(8,128)(2,1)S(1)} %get-tuple-element.41), channel_id=1, source_target_pairs={{0,4},{4,0},{8,12},{12,8},{16,20},{20,16},{24,28},{28,24},{1,5},{5... | collective-permute-start | bytes 589832 | tf_op jit(solution)/shard_map/ppermute | solution.py:258
  35.5 9.1 %collective-permute-start.17 = (bf16[4,256,128]{2,1,0:T(8,128)(2,1)S(1)}, bf16[4,256,128]{2,1,0:T(8,128)(2,1)S(1)}, u32[]{:S(2)}, u32[]{:S(2)}) collective-permute-start(bf16[4,256,128]{2,1,0:T(8,128)(2,1)S(1)} %shard_map.118.refs_0_), channel_id=1, source_target_pairs={{0,2},{1,3},{2,0},{3,1},{4,6},{5,7},{6,4},{7,5},{8,10},{9,11},{10,... | collective-permute-start | bytes 786440 | tf_op jit(solution)/shard_map/ppermute | solution.py:267
  40.9 9.3 %collective-permute-start.14 = (bf16[4,256,128]{2,1,0:T(8,128)(2,1)S(1)}, bf16[4,256,128]{2,1,0:T(8,128)(2,1)S(1)}, u32[]{:S(2)}, u32[]{:S(2)}) collective-permute-start(bf16[4,256,128]{2,1,0:T(8,128)(2,1)S(1)} %get-tuple-element.47.attn_ref.refs_3_), channel_id=1, source_target_pairs={{0,8},{4,12},{8,0},{12,4},{16,24},{20,28},{24,16},{28,20},{1,9},{5... | collective-permute-start | bytes 786440 | tf_op jit(solution)/shard_map/ppermute | solution.py:258
  42.0 11.3 %collective-permute-start.15 = (bf16[4,256,128]{2,1,0:T(8,128)(2,1)S(1)}, bf16[4,256,128]{2,1,0:T(8,128)(2,1)S(1)}, u32[]{:S(2)}, u32[]{:S(2)}) collective-permute-start(bf16[4,256,128]{2,1,0:T(8,128)(2,1)S(1)} %get-tuple-element.47.attn_ref.refs_3_), channel_id=1, source_target_pairs={{0,12},{4,8},{8,4},{12,0},{16,28},{20,24},{24,20},{28,16},{1,13},{... | collective-permute-start | bytes 786440 | tf_op jit(solution)/shard_map/ppermute | solution.py:258
  44.6 10.6 %collective-permute-start.16 = (bf16[4,256,128]{2,1,0:T(8,128)(2,1)S(1)}, bf16[4,256,128]{2,1,0:T(8,128)(2,1)S(1)}, u32[]{:S(2)}, u32[]{:S(2)}) collective-permute-start(bf16[4,256,128]{2,1,0:T(8,128)(2,1)S(1)} %get-tuple-element.47.attn_ref.refs_3_), channel_id=1, source_target_pairs={{0,4},{4,0},{8,12},{12,8},{16,20},{20,16},{24,28},{28,24},{1,5},{5... | collective-permute-start | bytes 786440 | tf_op jit(solution)/shard_map/ppermute | solution.py:258
  44.6 10.6 %collective-permute-start.18 = (bf16[2,4,256,128]{3,2,1,0:T(8,128)(2,1)S(1)}, bf16[2,4,256,128]{3,2,1,0:T(8,128)(2,1)S(1)}, u32[]{:S(2)}, u32[]{:S(2)}) collective-permute-start(bf16[2,4,256,128]{3,2,1,0:T(8,128)(2,1)S(1)} %shard_map.119.refs_4_), channel_id=1, source_target_pairs={{0,1},{1,0},{2,3},{3,2},{4,5},{5,4},{6,7},{7,6},{8,9},{9,8},{10,11... | collective-permute-start | bytes 1572872 | tf_op jit(solution)/shard_map/ppermute | solution.py:267
  44.7 10.5 %copy-start.1 = (bf16[512,2048]{1,0:T(8,128)(2,1)S(1)}, bf16[512,2048]{1,0:T(8,128)(2,1)}, u32[]{:S(2)}) copy-start(bf16[512,2048]{1,0:T(8,128)(2,1)} %copy-done) | copy-start | bytes 6291460
  47.1 12.0 %collective-permute-start.10 = (bf16[256,256]{1,0:T(8,128)(2,1)S(1)}, bf16[256,256]{1,0:T(8,128)(2,1)S(1)}, u32[]{:S(2)}, u32[]{:S(2)}) collective-permute-start(bf16[256,256]{1,0:T(8,128)(2,1)S(1)} %get-tuple-element.53), channel_id=1, source_target_pairs={{16,0},{20,4},{24,8},{28,12},{17,1},{21,5},{25,9},{29,13},{18,2},{... | collective-permute-start | bytes 393224 | tf_op jit(solution)/shard_map/ppermute | solution.py:264
  56.9 6.0 %collective-permute-start.19 = (bf16[256,1024]{1,0:T(8,128)(2,1)S(1)}, bf16[256,1024]{1,0:T(8,128)(2,1)S(1)}, u32[]{:S(2)}, u32[]{:S(2)}) collective-permute-start(bf16[256,1024]{1,0:T(8,128)(2,1)S(1)} %get-tuple-element.59), channel_id=1, source_target_pairs={{0,1},{1,0},{2,3},{3,2},{4,5},{5,4},{6,7},{7,6},{8,9},{9,8},{10,11... | collective-permute-start | bytes 1572872 | tf_op jit(solution)/shard_map/ppermute | solution.py:267
  56.9 19.8 %collective-permute-start.21 = (bf16[256,512]{1,0:T(8,128)(2,1)S(1)}, bf16[256,512]{1,0:T(8,128)(2,1)S(1)}, u32[]{:S(2)}, u32[]{:S(2)}) collective-permute-start(bf16[256,512]{1,0:T(8,128)(2,1)S(1)} %get-tuple-element.62), channel_id=1, source_target_pairs={{0,16},{4,20},{8,24},{12,28},{16,0},{20,4},{24,8},{28,12},{1,17},{... | collective-permute-start | bytes 786440 | tf_op jit(solution)/shard_map/ppermute | solution.py:261
  59.3 10.7 %collective-permute-start.11 = (bf16[256,384]{1,0:T(8,128)(2,1)S(1)}, bf16[256,384]{1,0:T(8,128)(2,1)S(1)}, u32[]{:S(2)}, u32[]{:S(2)}) collective-permute-start(bf16[256,384]{1,0:T(8,128)(2,1)S(1)} %get-tuple-element.54), channel_id=1, source_target_pairs={{0,8},{4,12},{8,0},{12,4},{16,24},{20,28},{24,16},{28,20},{1,9},{5... | collective-permute-start | bytes 589832 | tf_op jit(solution)/shard_map/ppermute | solution.py:258
  61.0 15.7 %collective-permute-start.12 = (bf16[256,384]{1,0:T(8,128)(2,1)S(1)}, bf16[256,384]{1,0:T(8,128)(2,1)S(1)}, u32[]{:S(2)}, u32[]{:S(2)}) collective-permute-start(bf16[256,384]{1,0:T(8,128)(2,1)S(1)} %get-tuple-element.55), channel_id=1, source_target_pairs={{0,12},{4,8},{8,4},{12,0},{16,28},{20,24},{24,20},{28,16},{1,13},{... | collective-permute-start | bytes 589832 | tf_op jit(solution)/shard_map/ppermute | solution.py:258
  62.2 14.5 %collective-permute-start.13 = (bf16[256,384]{1,0:T(8,128)(2,1)S(1)}, bf16[256,384]{1,0:T(8,128)(2,1)S(1)}, u32[]{:S(2)}, u32[]{:S(2)}) collective-permute-start(bf16[256,384]{1,0:T(8,128)(2,1)S(1)} %get-tuple-element.56), channel_id=1, source_target_pairs={{0,4},{4,0},{8,12},{12,8},{16,20},{20,16},{24,28},{28,24},{1,5},{5... | collective-permute-start | bytes 589832 | tf_op jit(solution)/shard_map/ppermute | solution.py:258
  62.9 13.9 %collective-permute-start.20 = (bf16[256,512]{1,0:T(8,128)(2,1)S(1)}, bf16[256,512]{1,0:T(8,128)(2,1)S(1)}, u32[]{:S(2)}, u32[]{:S(2)}) collective-permute-start(bf16[256,512]{1,0:T(8,128)(2,1)S(1)} %add_convert_fusion), channel_id=1, source_target_pairs={{0,2},{1,3},{2,0},{3,1},{4,6},{5,7},{6,4},{7,5},{8,10},{9,11},{10,... | collective-permute-start | bytes 786440 | tf_op jit(solution)/shard_map/ppermute | solution.py:267

commit v7 on v6

--- a/solution.py
+++ b/solution.py
@@ -14,6 +14,7 @@
 BF16 = jnp.bfloat16
 HIDDEN = -1e30
 TURN = (2, 3, 1, 0)
+LAST = (3, 2, 1, 0)
 VMEM = pl.BlockSpec(memory_space=pltpu.VMEM)
 ANY = pl.BlockSpec(memory_space=pl.ANY)
 HBM = pl.BlockSpec(memory_space=pltpu.HBM)
@@ -28,12 +29,12 @@
     return pl.ds(pl.multiple_of(block * width, width), width)
 
 
-def turned(pieces):
-    return [pieces[m] for m in TURN]
-
-
-def straight(refs):
-    return [refs[TURN.index(m)] for m in range(len(TURN))]
+def turned(pieces, turn=TURN):
+    return [pieces[m] for m in turn]
+
+
+def straight(refs, turn=TURN):
+    return [refs[turn.index(m)] for m in range(len(turn))]
 
 
 def call(body, outs, operands, specs=None, scratch=(), limit=20, flops=1):
@@ -131,13 +132,17 @@
         slot = (other_b ^ b) * A + (other_a ^ a) if pair else other_b * A + (other_a ^ a)
         return slot * parts
 
-    for m in range(A):
+    row = lax.broadcasted_iota(jnp.int32, (SEG, SEG), 0)
+    col = lax.broadcasted_iota(jnp.int32, (SEG, SEG), 1)
+    scale = score_scale * math.log2(math.e)
+    far = count - SEG
+    column = lax.broadcasted_iota(jnp.int32, (1, far), 1)
+
+    def score(m):
         seg_a = a ^ m
         s = b * A + seg_a
         prev_a = jnp.where(seg_a == 0, A - 1, seg_a - 1)
         prev_b = jnp.where(seg_a == 0, (b + B - 1) % B, b)
-        far = count - SEG
-        column = lax.broadcasted_iota(jnp.int32, (1, far), 1)
         hidden = (column < SEG) & (s == 0)
         for part in range(parts):
             at = part * BLOCK
@@ -148,21 +153,25 @@
             owner, block = owner_ref[s, j], block_ref[s, j]
             kvcat[m, SEG + at : SEG + at + BLOCK] = kv[place(owner % A, owner // A) + jnp.maximum(block, 0)]
             hidden |= (column >= at) & (column < at + BLOCK) & (block < 0)
-        bias = jnp.where(hidden, HIDDEN, 0.0)
         q = piece_refs[m][:, :DH]
-        row = lax.broadcasted_iota(jnp.int32, (SEG, SEG), 0)
-        col = lax.broadcasted_iota(jnp.int32, (SEG, SEG), 1)
-        scale = score_scale * math.log2(math.e)
         near = jnp.where(row >= col, dot(q, kvcat[m, :SEG, :DH], (1, 1)) * scale, HIDDEN)
-        rest = dot(q, kvcat[m, SEG:, :DH], (1, 1)) * scale + bias
+        return near, dot(q, kvcat[m, SEG:, :DH], (1, 1)) * scale + jnp.where(hidden, HIDDEN, 0.0)
+
+    def mix(m, near, rest):
         top = jnp.maximum(jnp.max(near, -1, keepdims=True), jnp.max(rest, -1, keepdims=True))
         near, rest = jnp.exp2(near - top), jnp.exp2(rest - top)
         inverse = 1.0 / (jnp.sum(near, -1, keepdims=True) + jnp.sum(rest, -1, keepdims=True))
         near, rest = near * inverse, rest * inverse
-        weights_ref[m, :, :SEG] = near.astype(weights_ref.dtype)
-        weights_ref[m, :, SEG:] = rest.astype(weights_ref.dtype)
+        weights_ref[m, :, :SEG] = near
+        weights_ref[m, :, SEG:] = rest
         near, rest = near.astype(BF16), rest.astype(BF16)
         attn_ref[m] = (dot(near, kvcat[m, :SEG, DH:], (1, 0)) + dot(rest, kvcat[m, SEG:, DH:], (1, 0))).astype(BF16)
+
+    scores = score(0)
+    for m in range(A):
+        later = score(m + 1) if m + 1 < A else None
+        mix(m, *scores)
+        scores = later
 
 
 def backward_body(A, B, score_scale, attn_ref, kvcat, weights_ref, *refs):
@@ -236,7 +245,7 @@
 
 
 def place_body(A, B, *refs):
-    pieces, terms, projs, outs = straight(refs[:A]), refs[A : A + 3], refs[A + 3 : -6], refs[-5:]
+    pieces, terms, projs, outs = straight(refs[:A], LAST), refs[A : A + 3], refs[A + 3 : -6], refs[-5:]
     a = lax.axis_index("seg") % A
     for m in range(A):
         for i in range(3):
@@ -367,7 +376,7 @@
         call(
             functools.partial(place_body, A, B),
             [shape((SEG, width), BF16)] * 4 + [shape(proj[0].shape, F32)],
-            [*turned(moved), keep, received[:, :block], over_head(passed, 2), *proj, *token],
+            [*turned(moved, LAST), keep, received[:, :block], over_head(passed, 2), *proj, *token],
             specs=[VMEM] * (A + 3 + len(proj)) + [ANY],
         )
     )

time: 78.4 us -> 77.2 us (0.985)
  no operation moved by 1% of the time
where the time goes in v7:
time: 77.2 us; the launch traced here: 76.9 us
  waiting for transfers between devices  32.8 us (42%)
  starting transfers between devices  27.9 us (36%)
  Pallas kernels  9.69 us (13%)
  local copies, waits for them, and re-layouts  5.58 us (7%)
  between operations  0.84 us (1%)
    ppermute x12, waiting for transfers between devices, over_a(): lax.ppermute(x, 'seg', [(i, i // A * A + (i % A ^ m)) for i in range(n)])  31.4 us
    ppermute x12, starting transfers between devices, over_a(): lax.ppermute(x, 'seg', [(i, i // A * A + (i % A ^ m)) for i in range(n)])  14.3 us
    pallas_call x13, Pallas kernels, call(): pl.pallas_call(body, out_shape=outs, in_specs=specs or [VMEM] * len(opera...  9.69 us
    ppermute x3, starting transfers between devices, over_b(): return lax.ppermute(x, 'seg', [(i, (i + A) % n) for i in range(n)])  7.18 us
    unnamed x20, local copies, waits for them, and re-layouts  5.56 us
    ppermute x6, starting transfers between devices, over_head(): return lax.ppermute(x, 'head', [(i, i ^ k) for i in range(H)])  5.17 us
  transfers between devices with their start and end apart: 22, of which 10 were waited for; matrix products, arithmetic and copies ran while one was open for 0% of the time, Pallas kernels for 11%

profile of v7, /device:TPU:0, one launch (start us, length us, event | category | flops | bytes accessed | tf_op | source)
XLA Modules:
  0.0 76.9 jit_solution(1053598123819927030)
XLA Ops:
  0.6 0.9 %copy-done.5 = bf16[256,512]{1,0:T(8,128)(2,1)S(1)} copy-done((bf16[256,512]{1,0:T(8,128)(2,1)S(1)}, bf16[256,512]{1,0:T(8,128)(2,1)}, u32[]{:S(2)}) %copy-start.5) | copy-done | bytes 262168
  1.6 0.9 %copy-done.6 = bf16[256,512]{1,0:T(8,128)(2,1)S(1)} copy-done((bf16[256,512]{1,0:T(8,128)(2,1)S(1)}, bf16[256,512]{1,0:T(8,128)(2,1)}, u32[]{:S(2)}) %copy-start.6) | copy-done | bytes 262168
  2.6 3.0 %collective-permute-start = (bf16[256,512]{1,0:T(8,128)(2,1)}, bf16[256,512]{1,0:T(8,128)(2,1)S(1)}, u32[]{:S(2)}, u32[]{:S(2)}) collective-permute-start(bf16[256,512]{1,0:T(8,128)(2,1)} %refs_2_), channel_id=1, source_target_pairs={{0,2},{1,3},{2,0},{3,1},{4,6},{5,7},{6,4},{7,5},{8,10},{9,11},{10,... | collective-permute-start | bytes 786440 | tf_op jit(solution)/shard_map/ppermute | solution.py:276
  5.6 1.5 %collective-permute-start.5 = (bf16[256,256]{1,0:T(8,128)(2,1)S(1)}, bf16[256,256]{1,0:T(8,128)(2,1)S(1)}, u32[]{:S(2)}, u32[]{:S(2)}) collective-permute-start(bf16[256,256]{1,0:T(8,128)(2,1)S(1)} %get-tuple-element.44), channel_id=1, source_target_pairs={{0,4},{4,0},{8,12},{12,8},{16,20},{20,16},{24,28},{28,24},{1,5},{5... | collective-permute-start | bytes 393224 | tf_op jit(solution)/shard_map/ppermute | solution.py:267
  7.2 1.6 %collective-permute-start.6 = (bf16[256,256]{1,0:T(8,128)(2,1)S(1)}, bf16[256,256]{1,0:T(8,128)(2,1)S(1)}, u32[]{:S(2)}, u32[]{:S(2)}) collective-permute-start(bf16[256,256]{1,0:T(8,128)(2,1)S(1)} %get-tuple-element.45), channel_id=1, source_target_pairs={{0,8},{4,12},{8,0},{12,4},{16,24},{20,28},{24,16},{28,20},{1,9},{5... | collective-permute-start | bytes 393224 | tf_op jit(solution)/shard_map/ppermute | solution.py:267
  9.1 2.6 %collective-permute-start.8 = (bf16[256,256]{1,0:T(8,128)(2,1)S(1)}, bf16[256,256]{1,0:T(8,128)(2,1)S(1)}, u32[]{:S(2)}, u32[]{:S(2)}) collective-permute-start(bf16[256,256]{1,0:T(8,128)(2,1)S(1)} %get-tuple-element.43.refs_4_), channel_id=1, source_target_pairs={{0,16},{4,20},{8,24},{12,28},{16,0},{20,4},{24,8},{28,12},{1,17},{... | collective-permute-start | bytes 393224 | tf_op jit(solution)/shard_map/ppermute | solution.py:270
  11.7 1.6 %copy-done.2 = bf16[512,2048]{1,0:T(8,128)(2,1)S(1)} copy-done((bf16[512,2048]{1,0:T(8,128)(2,1)S(1)}, bf16[512,2048]{1,0:T(8,128)(2,1)}, u32[]{:S(2)}) %copy-start.2) | copy-done | bytes 2097176
  13.3 0.9 %copy-done.3 = bf16[256,512]{1,0:T(8,128)(2,1)S(1)} copy-done((bf16[256,512]{1,0:T(8,128)(2,1)S(1)}, bf16[256,512]{1,0:T(8,128)(2,1)}, u32[]{:S(2)}) %copy-start.3) | copy-done | bytes 262168
  14.3 0.9 %copy-done.4 = bf16[256,512]{1,0:T(8,128)(2,1)S(1)} copy-done((bf16[256,512]{1,0:T(8,128)(2,1)S(1)}, bf16[256,512]{1,0:T(8,128)(2,1)}, u32[]{:S(2)}) %copy-start.4) | copy-done | bytes 262168
  16.0 1.6 %collective-permute-done.7.refs_1_.refs_7_ = bf16[256,256]{1,0:T(8,128)(2,1)S(1)} collective-permute-done((bf16[256,256]{1,0:T(8,128)(2,1)S(1)}, bf16[256,256]{1,0:T(8,128)(2,1)S(1)}, u32[]{:S(2)}, u32[]{:S(2)}) %collective-permute-start.7) | collective-permute-done | bytes 131104 | tf_op jit(solution)/shard_map/ppermute | solution.py:267
  17.7 2.4 %collective-permute-start.9 = (bf16[3,256,256]{2,1,0:T(8,128)(2,1)S(1)}, bf16[3,256,256]{2,1,0:T(8,128)(2,1)S(1)}, u32[]{:S(2)}, u32[]{:S(2)}) collective-permute-start(bf16[3,256,256]{2,1,0:T(8,128)(2,1)S(1)} %shard_map.114), channel_id=1, source_target_pairs={{0,16},{4,20},{8,24},{12,28},{16,0},{20,4},{24,8},{28,12},{1,17},{... | collective-permute-start | bytes 1179656 | tf_op jit(solution)/shard_map/ppermute | solution.py:270
  21.1 1.5 %collective-permute-start.2 = (bf16[256,384]{1,0:T(8,128)(2,1)S(1)}, bf16[256,384]{1,0:T(8,128)(2,1)S(1)}, u32[]{:S(2)}, u32[]{:S(2)}) collective-permute-start(bf16[256,384]{1,0:T(8,128)(2,1)S(1)} %get-tuple-element.39), channel_id=1, source_target_pairs={{0,8},{4,12},{8,0},{12,4},{16,24},{20,28},{24,16},{28,20},{1,9},{5... | collective-permute-start | bytes 589832 | tf_op jit(solution)/shard_map/ppermute | solution.py:267
  22.6 1.1 %collective-permute-start.3 = (bf16[256,384]{1,0:T(8,128)(2,1)S(1)}, bf16[256,384]{1,0:T(8,128)(2,1)S(1)}, u32[]{:S(2)}, u32[]{:S(2)}) collective-permute-start(bf16[256,384]{1,0:T(8,128)(2,1)S(1)} %get-tuple-element.40), channel_id=1, source_target_pairs={{0,12},{4,8},{8,4},{12,0},{16,28},{20,24},{24,20},{28,16},{1,13},{... | collective-permute-start | bytes 589832 | tf_op jit(solution)/shard_map/ppermute | solution.py:267
  24.8 8.5 %collective-permute-done.2.refs_0_.refs_2_ = bf16[256,384]{1,0:T(8,128)(2,1)S(1)} collective-permute-done((bf16[256,384]{1,0:T(8,128)(2,1)S(1)}, bf16[256,384]{1,0:T(8,128)(2,1)S(1)}, u32[]{:S(2)}, u32[]{:S(2)}) %collective-permute-start.2) | collective-permute-done | bytes 196640 | tf_op jit(solution)/shard_map/ppermute | solution.py:267
  33.3 2.1 %collective-permute-done.3.refs_1_.refs_3_ = bf16[256,384]{1,0:T(8,128)(2,1)S(1)} collective-permute-done((bf16[256,384]{1,0:T(8,128)(2,1)S(1)}, bf16[256,384]{1,0:T(8,128)(2,1)S(1)}, u32[]{:S(2)}, u32[]{:S(2)}) %collective-permute-start.3) | collective-permute-done | bytes 196640 | tf_op jit(solution)/shard_map/ppermute | solution.py:267
  36.1 1.4 %collective-permute-done.9.refs_9_ = bf16[3,256,256]{2,1,0:T(8,128)(2,1)S(1)} collective-permute-done((bf16[3,256,256]{2,1,0:T(8,128)(2,1)S(1)}, bf16[3,256,256]{2,1,0:T(8,128)(2,1)S(1)}, u32[]{:S(2)}, u32[]{:S(2)}) %collective-permute-start.9) | collective-permute-done | bytes 393248 | tf_op jit(solution)/shard_map/ppermute | solution.py:270
  37.5 2.9 %shard_map.115 = (bf16[4,256,128]{2,1,0:T(8,128)(2,1)S(1)}, bf16[4,1024,256]{2,1,0:T(8,128)(2,1)S(1)}, f32[4,256,1024]{2,1,0:T(8,128)S(1)}) custom-call(s32[8,4]{1,0:T(8,128)S(1)} %copy.12.owner_ref, s32[8,4]{1,0:T(8,128)S(1)} %copy.13.block_ref, bf16[256,384]{1,0:T(8,128)(2,1)S(1)} %collective-permute-done.2.refs_0_.refs_2_, ...), custom_call_target="tpu_custom_call" | custom-call | flops 99999997952 | bytes 1 | tf_op jit(solution)/shard_map/pallas_call | solution.py:41
  40.3 1.1 %collective-permute-start.14 = (bf16[4,256,128]{2,1,0:T(8,128)(2,1)S(1)}, bf16[4,256,128]{2,1,0:T(8,128)(2,1)S(1)}, u32[]{:S(2)}, u32[]{:S(2)}) collective-permute-start(bf16[4,256,128]{2,1,0:T(8,128)(2,1)S(1)} %get-tuple-element.47.attn_ref.refs_3_), channel_id=1, source_target_pairs={{0,8},{4,12},{8,0},{12,4},{16,24},{20,28},{24,16},{28,20},{1,9},{5... | collective-permute-start | bytes 786440 | tf_op jit(solution)/shard_map/ppermute | solution.py:267
  41.4 2.6 %collective-permute-start.15 = (bf16[4,256,128]{2,1,0:T(8,128)(2,1)S(1)}, bf16[4,256,128]{2,1,0:T(8,128)(2,1)S(1)}, u32[]{:S(2)}, u32[]{:S(2)}) collective-permute-start(bf16[4,256,128]{2,1,0:T(8,128)(2,1)S(1)} %get-tuple-element.47.attn_ref.refs_3_), channel_id=1, source_target_pairs={{0,12},{4,8},{8,4},{12,0},{16,28},{20,24},{24,20},{28,16},{1,13},{... | collective-permute-start | bytes 786440 | tf_op jit(solution)/shard_map/ppermute | solution.py:267
  44.2 2.4 %shard_map.116 = (bf16[4,256,128]{2,1,0:T(8,128)(2,1)S(1)}, f32[4,256,256]{2,1,0:T(8,128)S(1)}, bf16[4,256,256]{2,1,0:T(8,128)(2,1)S(1)}, bf16[256,256]{1,0:T(8,128)(2,1)S(1)}) custom-call(bf16[4,256,128]{2,1,0:T(8,128)(2,1)S(1)} %get-tuple-element.47.attn_ref.refs_3_, bf16[4,1024,256]{2,1,0:T(8,128)(2,1)S(1)} %get-tuple-element.48.kvcat, ...), custom_call_target="tpu_custom_call" | custom-call | flops 99999997952 | bytes 1 | tf_op jit(solution)/shard_map/pallas_call | solution.py:41
  46.5 1.3 %collective-permute-start.10 = (bf16[256,256]{1,0:T(8,128)(2,1)S(1)}, bf16[256,256]{1,0:T(8,128)(2,1)S(1)}, u32[]{:S(2)}, u32[]{:S(2)}) collective-permute-start(bf16[256,256]{1,0:T(8,128)(2,1)S(1)} %get-tuple-element.53), channel_id=1, source_target_pairs={{16,0},{20,4},{24,8},{28,12},{17,1},{21,5},{25,9},{29,13},{18,2},{... | collective-permute-start | bytes 393224 | tf_op jit(solution)/shard_map/ppermute | solution.py:273
  47.8 1.8 %collective-permute-done.14.refs_0_ = bf16[4,256,128]{2,1,0:T(8,128)(2,1)S(1)} collective-permute-done((bf16[4,256,128]{2,1,0:T(8,128)(2,1)S(1)}, bf16[4,256,128]{2,1,0:T(8,128)(2,1)S(1)}, u32[]{:S(2)}, u32[]{:S(2)}) %collective-permute-start.14) | collective-permute-done | bytes 262176 | tf_op jit(solution)/shard_map/ppermute | solution.py:267
  49.6 3.1 %collective-permute-done.15.refs_1_ = bf16[4,256,128]{2,1,0:T(8,128)(2,1)S(1)} collective-permute-done((bf16[4,256,128]{2,1,0:T(8,128)(2,1)S(1)}, bf16[4,256,128]{2,1,0:T(8,128)(2,1)S(1)}, u32[]{:S(2)}, u32[]{:S(2)}) %collective-permute-start.15) | collective-permute-done | bytes 262176 | tf_op jit(solution)/shard_map/ppermute | solution.py:267
  52.7 1.9 %collective-permute-done.16.refs_2_ = bf16[4,256,128]{2,1,0:T(8,128)(2,1)S(1)} collective-permute-done((bf16[4,256,128]{2,1,0:T(8,128)(2,1)S(1)}, bf16[4,256,128]{2,1,0:T(8,128)(2,1)S(1)}, u32[]{:S(2)}, u32[]{:S(2)}) %collective-permute-start.16) | collective-permute-done | bytes 262176 | tf_op jit(solution)/shard_map/ppermute | solution.py:267
  54.7 1.6 %shard_map.120 = (f32[256,512]{1,0:T(8,128)S(1)}, f32[256,512]{1,0:T(8,128)S(1)}, bf16[256,1024]{1,0:T(8,128)(2,1)S(1)}, f32[256,512]{1,0:T(8,128)S(1)}, bf16[256,512]{1,0:T(8,128)(2,1)S(1)}) custom-call(bf16[4,256,128]{2,1,0:T(8,128)(2,1)S(1)} %collective-permute-done.14.refs_0_, bf16[4,256,128]{2,1,0:T(8,128)(2,1)S(1)} %collective-permute-done.15.refs_1_, ...), custom_call_target="tpu_custom_call" | custom-call | flops 1 | bytes 1 | tf_op jit(solution)/shard_map/pallas_call | solution.py:41
  56.4 2.2 %collective-permute-start.21 = (bf16[256,512]{1,0:T(8,128)(2,1)S(1)}, bf16[256,512]{1,0:T(8,128)(2,1)S(1)}, u32[]{:S(2)}, u32[]{:S(2)}) collective-permute-start(bf16[256,512]{1,0:T(8,128)(2,1)S(1)} %get-tuple-element.62), channel_id=1, source_target_pairs={{0,16},{4,20},{8,24},{12,28},{16,0},{20,4},{24,8},{28,12},{1,17},{... | collective-permute-start | bytes 786440 | tf_op jit(solution)/shard_map/ppermute | solution.py:270
  58.7 1.4 %collective-permute-start.11 = (bf16[256,384]{1,0:T(8,128)(2,1)S(1)}, bf16[256,384]{1,0:T(8,128)(2,1)S(1)}, u32[]{:S(2)}, u32[]{:S(2)}) collective-permute-start(bf16[256,384]{1,0:T(8,128)(2,1)S(1)} %get-tuple-element.54), channel_id=1, source_target_pairs={{0,12},{4,8},{8,4},{12,0},{16,28},{20,24},{24,20},{28,16},{1,13},{... | collective-permute-start | bytes 589832 | tf_op jit(solution)/shard_map/ppermute | solution.py:267
  60.2 1.5 %collective-permute-start.12 = (bf16[256,384]{1,0:T(8,128)(2,1)S(1)}, bf16[256,384]{1,0:T(8,128)(2,1)S(1)}, u32[]{:S(2)}, u32[]{:S(2)}) collective-permute-start(bf16[256,384]{1,0:T(8,128)(2,1)S(1)} %get-tuple-element.55), channel_id=1, source_target_pairs={{0,8},{4,12},{8,0},{12,4},{16,24},{20,28},{24,16},{28,20},{1,9},{5... | collective-permute-start | bytes 589832 | tf_op jit(solution)/shard_map/ppermute | solution.py:267
  62.4 1.4 %collective-permute-start.20 = (bf16[256,512]{1,0:T(8,128)(2,1)S(1)}, bf16[256,512]{1,0:T(8,128)(2,1)S(1)}, u32[]{:S(2)}, u32[]{:S(2)}) collective-permute-start(bf16[256,512]{1,0:T(8,128)(2,1)S(1)} %add_convert_fusion), channel_id=1, source_target_pairs={{0,2},{1,3},{2,0},{3,1},{4,6},{5,7},{6,4},{7,5},{8,10},{9,11},{10,... | collective-permute-start | bytes 786440 | tf_op jit(solution)/shard_map/ppermute | solution.py:276
  63.7 9.3 %collective-permute-done.11.refs_2_.refs_0_ = bf16[256,384]{1,0:T(8,128)(2,1)S(1)} collective-permute-done((bf16[256,384]{1,0:T(8,128)(2,1)S(1)}, bf16[256,384]{1,0:T(8,128)(2,1)S(1)}, u32[]{:S(2)}, u32[]{:S(2)}) %collective-permute-start.11) | collective-permute-done | bytes 196640 | tf_op jit(solution)/shard_map/ppermute | solution.py:267
  73.0 2.5 %collective-permute-done.12.refs_1_ = bf16[256,384]{1,0:T(8,128)(2,1)S(1)} collective-permute-done((bf16[256,384]{1,0:T(8,128)(2,1)S(1)}, bf16[256,384]{1,0:T(8,128)(2,1)S(1)}, u32[]{:S(2)}, u32[]{:S(2)}) %collective-permute-start.12) | collective-permute-done | bytes 196640 | tf_op jit(solution)/shard_map/ppermute | solution.py:267
  75.6 1.4 %shard_map.122 = (bf16[256,512]{1,0:T(8,128)(2,1)}, bf16[256,512]{1,0:T(8,128)(2,1)}, bf16[256,512]{1,0:T(8,128)(2,1)}, bf16[256,512]{1,0:T(8,128)(2,1)}, f32[256,512]{1,0:T(8,128)}) custom-call(bf16[256,384]{1,0:T(8,128)(2,1)S(1)} %collective-permute-done.11.refs_2_.refs_0_, bf16[256,384]{1,0:T(8,128)(2,1)S(1)} %collective-permute-done.12.refs_1_, ...), custom_call_target="tpu_custom_call" | custom-call | flops 1 | bytes 1 | tf_op jit(solution)/shard_map/pallas_call | solution.py:41
  (47 shorter events, 5.0 us)
Async XLA Ops:
  0.6 1.0 %copy-start.5 = (bf16[256,512]{1,0:T(8,128)(2,1)S(1)}, bf16[256,512]{1,0:T(8,128)(2,1)}, u32[]{:S(2)}) copy-start(bf16[256,512]{1,0:T(8,128)(2,1)} %k_ref.1) | copy-start | bytes 786436
  1.6 0.9 %copy-start.6 = (bf16[256,512]{1,0:T(8,128)(2,1)S(1)}, bf16[256,512]{1,0:T(8,128)(2,1)}, u32[]{:S(2)}) copy-start(bf16[256,512]{1,0:T(8,128)(2,1)} %v_ref.1) | copy-start | bytes 786436
  2.6 12.8 %collective-permute-start = (bf16[256,512]{1,0:T(8,128)(2,1)}, bf16[256,512]{1,0:T(8,128)(2,1)S(1)}, u32[]{:S(2)}, u32[]{:S(2)}) collective-permute-start(bf16[256,512]{1,0:T(8,128)(2,1)} %refs_2_), channel_id=1, source_target_pairs={{0,2},{1,3},{2,0},{3,1},{4,6},{5,7},{6,4},{7,5},{8,10},{9,11},{10,... | collective-permute-start | bytes 786440 | tf_op jit(solution)/shard_map/ppermute | solution.py:276
  5.6 9.9 %collective-permute-start.5 = (bf16[256,256]{1,0:T(8,128)(2,1)S(1)}, bf16[256,256]{1,0:T(8,128)(2,1)S(1)}, u32[]{:S(2)}, u32[]{:S(2)}) collective-permute-start(bf16[256,256]{1,0:T(8,128)(2,1)S(1)} %get-tuple-element.44), channel_id=1, source_target_pairs={{0,4},{4,0},{8,12},{12,8},{16,20},{20,16},{24,28},{28,24},{1,5},{5... | collective-permute-start | bytes 393224 | tf_op jit(solution)/shard_map/ppermute | solution.py:267
  7.2 8.9 %collective-permute-start.6 = (bf16[256,256]{1,0:T(8,128)(2,1)S(1)}, bf16[256,256]{1,0:T(8,128)(2,1)S(1)}, u32[]{:S(2)}, u32[]{:S(2)}) collective-permute-start(bf16[256,256]{1,0:T(8,128)(2,1)S(1)} %get-tuple-element.45), channel_id=1, source_target_pairs={{0,8},{4,12},{8,0},{12,4},{16,24},{20,28},{24,16},{28,20},{1,9},{5... | collective-permute-start | bytes 393224 | tf_op jit(solution)/shard_map/ppermute | solution.py:267
  8.7 9.0 %collective-permute-start.7 = (bf16[256,256]{1,0:T(8,128)(2,1)S(1)}, bf16[256,256]{1,0:T(8,128)(2,1)S(1)}, u32[]{:S(2)}, u32[]{:S(2)}) collective-permute-start(bf16[256,256]{1,0:T(8,128)(2,1)S(1)} %get-tuple-element.46), channel_id=1, source_target_pairs={{0,12},{4,8},{8,4},{12,0},{16,28},{20,24},{24,20},{28,16},{1,13},{... | collective-permute-start | bytes 393224 | tf_op jit(solution)/shard_map/ppermute | solution.py:267
  9.1 8.6 %collective-permute-start.8 = (bf16[256,256]{1,0:T(8,128)(2,1)S(1)}, bf16[256,256]{1,0:T(8,128)(2,1)S(1)}, u32[]{:S(2)}, u32[]{:S(2)}) collective-permute-start(bf16[256,256]{1,0:T(8,128)(2,1)S(1)} %get-tuple-element.43.refs_4_), channel_id=1, source_target_pairs={{0,16},{4,20},{8,24},{12,28},{16,0},{20,4},{24,8},{28,12},{1,17},{... | collective-permute-start | bytes 393224 | tf_op jit(solution)/shard_map/ppermute | solution.py:270
  11.7 1.6 %copy-start.2 = (bf16[512,2048]{1,0:T(8,128)(2,1)S(1)}, bf16[512,2048]{1,0:T(8,128)(2,1)}, u32[]{:S(2)}) copy-start(bf16[512,2048]{1,0:T(8,128)(2,1)} %refs_0_.1) | copy-start | bytes 6291460
  13.3 0.9 %copy-start.3 = (bf16[256,512]{1,0:T(8,128)(2,1)S(1)}, bf16[256,512]{1,0:T(8,128)(2,1)}, u32[]{:S(2)}) copy-start(bf16[256,512]{1,0:T(8,128)(2,1)} %refs_1_.1) | copy-start | bytes 786436
  14.3 0.9 %copy-start.4 = (bf16[256,512]{1,0:T(8,128)(2,1)S(1)}, bf16[256,512]{1,0:T(8,128)(2,1)}, u32[]{:S(2)}) copy-start(bf16[256,512]{1,0:T(8,128)(2,1)} %refs_2_) | copy-start | bytes 786436
  15.4 4.8 %copy-start = (bf16[512,2048]{1,0:T(8,128)(2,1)}, bf16[512,2048]{1,0:T(8,128)(2,1)S(1)}, u32[]{:S(2)}) copy-start(bf16[512,2048]{1,0:T(8,128)(2,1)S(1)} %get-tuple-element.37.refs_2_.refs_4_.refs_6_) | copy-start | bytes 6291460
  15.4 4.7 %collective-permute-start.1 = (bf16[2,256,512]{2,1,0:T(8,128)(2,1)S(1)}, bf16[2,256,512]{2,1,0:T(8,128)(2,1)S(1)}, u32[]{:S(2)}, u32[]{:S(2)}) collective-permute-start(bf16[2,256,512]{2,1,0:T(8,128)(2,1)S(1)} %shard_map.112.refs_0_), channel_id=1, source_target_pairs={{0,1},{1,0},{2,3},{3,2},{4,5},{5,4},{6,7},{7,6},{8,9},{9,8},{10,11... | collective-permute-start | bytes 1572872 | tf_op jit(solution)/shard_map/ppermute | solution.py:276
  17.7 6.9 %copy-start.7 = (s32[8,4]{0,1:T(4,128)S(1)}, s32[8,4]{0,1:T(4,128)}, u32[]{:S(2)}) copy-start(s32[8,4]{0,1:T(4,128)} %param.12) | copy-start | bytes 388
  17.7 7.0 %copy-start.8 = (s32[8,4]{0,1:T(4,128)S(1)}, s32[8,4]{0,1:T(4,128)}, u32[]{:S(2)}) copy-start(s32[8,4]{0,1:T(4,128)} %param.13) | copy-start | bytes 388
  17.7 19.7 %collective-permute-start.9 = (bf16[3,256,256]{2,1,0:T(8,128)(2,1)S(1)}, bf16[3,256,256]{2,1,0:T(8,128)(2,1)S(1)}, u32[]{:S(2)}, u32[]{:S(2)}) collective-permute-start(bf16[3,256,256]{2,1,0:T(8,128)(2,1)S(1)} %shard_map.114), channel_id=1, source_target_pairs={{0,16},{4,20},{8,24},{12,28},{16,0},{20,4},{24,8},{28,12},{1,17},{... | collective-permute-start | bytes 1179656 | tf_op jit(solution)/shard_map/ppermute | solution.py:270
  21.1 12.2 %collective-permute-start.2 = (bf16[256,384]{1,0:T(8,128)(2,1)S(1)}, bf16[256,384]{1,0:T(8,128)(2,1)S(1)}, u32[]{:S(2)}, u32[]{:S(2)}) collective-permute-start(bf16[256,384]{1,0:T(8,128)(2,1)S(1)} %get-tuple-element.39), channel_id=1, source_target_pairs={{0,8},{4,12},{8,0},{12,4},{16,24},{20,28},{24,16},{28,20},{1,9},{5... | collective-permute-start | bytes 589832 | tf_op jit(solution)/shard_map/ppermute | solution.py:267
  22.6 12.8 %collective-permute-start.3 = (bf16[256,384]{1,0:T(8,128)(2,1)S(1)}, bf16[256,384]{1,0:T(8,128)(2,1)S(1)}, u32[]{:S(2)}, u32[]{:S(2)}) collective-permute-start(bf16[256,384]{1,0:T(8,128)(2,1)S(1)} %get-tuple-element.40), channel_id=1, source_target_pairs={{0,12},{4,8},{8,4},{12,0},{16,28},{20,24},{24,20},{28,16},{1,13},{... | collective-permute-start | bytes 589832 | tf_op jit(solution)/shard_map/ppermute | solution.py:267
  23.7 11.7 %collective-permute-start.4 = (bf16[256,384]{1,0:T(8,128)(2,1)S(1)}, bf16[256,384]{1,0:T(8,128)(2,1)S(1)}, u32[]{:S(2)}, u32[]{:S(2)}) collective-permute-start(bf16[256,384]{1,0:T(8,128)(2,1)S(1)} %get-tuple-element.41), channel_id=1, source_target_pairs={{0,4},{4,0},{8,12},{12,8},{16,20},{20,16},{24,28},{28,24},{1,5},{5... | collective-permute-start | bytes 589832 | tf_op jit(solution)/shard_map/ppermute | solution.py:267
  35.5 8.6 %collective-permute-start.17 = (bf16[4,256,128]{2,1,0:T(8,128)(2,1)S(1)}, bf16[4,256,128]{2,1,0:T(8,128)(2,1)S(1)}, u32[]{:S(2)}, u32[]{:S(2)}) collective-permute-start(bf16[4,256,128]{2,1,0:T(8,128)(2,1)S(1)} %shard_map.118.refs_0_), channel_id=1, source_target_pairs={{0,2},{1,3},{2,0},{3,1},{4,6},{5,7},{6,4},{7,5},{8,10},{9,11},{10,... | collective-permute-start | bytes 786440 | tf_op jit(solution)/shard_map/ppermute | solution.py:276
  40.3 9.3 %collective-permute-start.14 = (bf16[4,256,128]{2,1,0:T(8,128)(2,1)S(1)}, bf16[4,256,128]{2,1,0:T(8,128)(2,1)S(1)}, u32[]{:S(2)}, u32[]{:S(2)}) collective-permute-start(bf16[4,256,128]{2,1,0:T(8,128)(2,1)S(1)} %get-tuple-element.47.attn_ref.refs_3_), channel_id=1, source_target_pairs={{0,8},{4,12},{8,0},{12,4},{16,24},{20,28},{24,16},{28,20},{1,9},{5... | collective-permute-start | bytes 786440 | tf_op jit(solution)/shard_map/ppermute | solution.py:267
  41.4 11.3 %collective-permute-start.15 = (bf16[4,256,128]{2,1,0:T(8,128)(2,1)S(1)}, bf16[4,256,128]{2,1,0:T(8,128)(2,1)S(1)}, u32[]{:S(2)}, u32[]{:S(2)}) collective-permute-start(bf16[4,256,128]{2,1,0:T(8,128)(2,1)S(1)} %get-tuple-element.47.attn_ref.refs_3_), channel_id=1, source_target_pairs={{0,12},{4,8},{8,4},{12,0},{16,28},{20,24},{24,20},{28,16},{1,13},{... | collective-permute-start | bytes 786440 | tf_op jit(solution)/shard_map/ppermute | solution.py:267
  44.0 10.7 %collective-permute-start.16 = (bf16[4,256,128]{2,1,0:T(8,128)(2,1)S(1)}, bf16[4,256,128]{2,1,0:T(8,128)(2,1)S(1)}, u32[]{:S(2)}, u32[]{:S(2)}) collective-permute-start(bf16[4,256,128]{2,1,0:T(8,128)(2,1)S(1)} %get-tuple-element.47.attn_ref.refs_3_), channel_id=1, source_target_pairs={{0,4},{4,0},{8,12},{12,8},{16,20},{20,16},{24,28},{28,24},{1,5},{5... | collective-permute-start | bytes 786440 | tf_op jit(solution)/shard_map/ppermute | solution.py:267
  44.1 10.6 %collective-permute-start.18 = (bf16[2,4,256,128]{3,2,1,0:T(8,128)(2,1)S(1)}, bf16[2,4,256,128]{3,2,1,0:T(8,128)(2,1)S(1)}, u32[]{:S(2)}, u32[]{:S(2)}) collective-permute-start(bf16[2,4,256,128]{3,2,1,0:T(8,128)(2,1)S(1)} %shard_map.119.refs_4_), channel_id=1, source_target_pairs={{0,1},{1,0},{2,3},{3,2},{4,5},{5,4},{6,7},{7,6},{8,9},{9,8},{10,11... | collective-permute-start | bytes 1572872 | tf_op jit(solution)/shard_map/ppermute | solution.py:276
  44.1 10.5 %copy-start.1 = (bf16[512,2048]{1,0:T(8,128)(2,1)S(1)}, bf16[512,2048]{1,0:T(8,128)(2,1)}, u32[]{:S(2)}) copy-start(bf16[512,2048]{1,0:T(8,128)(2,1)} %copy-done) | copy-start | bytes 6291460
  46.5 12.1 %collective-permute-start.10 = (bf16[256,256]{1,0:T(8,128)(2,1)S(1)}, bf16[256,256]{1,0:T(8,128)(2,1)S(1)}, u32[]{:S(2)}, u32[]{:S(2)}) collective-permute-start(bf16[256,256]{1,0:T(8,128)(2,1)S(1)} %get-tuple-element.53), channel_id=1, source_target_pairs={{16,0},{20,4},{24,8},{28,12},{17,1},{21,5},{25,9},{29,13},{18,2},{... | collective-permute-start | bytes 393224 | tf_op jit(solution)/shard_map/ppermute | solution.py:273
  56.3 6.0 %collective-permute-start.19 = (bf16[256,1024]{1,0:T(8,128)(2,1)S(1)}, bf16[256,1024]{1,0:T(8,128)(2,1)S(1)}, u32[]{:S(2)}, u32[]{:S(2)}) collective-permute-start(bf16[256,1024]{1,0:T(8,128)(2,1)S(1)} %get-tuple-element.59), channel_id=1, source_target_pairs={{0,1},{1,0},{2,3},{3,2},{4,5},{5,4},{6,7},{7,6},{8,9},{9,8},{10,11... | collective-permute-start | bytes 1572872 | tf_op jit(solution)/shard_map/ppermute | solution.py:276
  56.4 19.1 %collective-permute-start.21 = (bf16[256,512]{1,0:T(8,128)(2,1)S(1)}, bf16[256,512]{1,0:T(8,128)(2,1)S(1)}, u32[]{:S(2)}, u32[]{:S(2)}) collective-permute-start(bf16[256,512]{1,0:T(8,128)(2,1)S(1)} %get-tuple-element.62), channel_id=1, source_target_pairs={{0,16},{4,20},{8,24},{12,28},{16,0},{20,4},{24,8},{28,12},{1,17},{... | collective-permute-start | bytes 786440 | tf_op jit(solution)/shard_map/ppermute | solution.py:270
  58.7 14.3 %collective-permute-start.11 = (bf16[256,384]{1,0:T(8,128)(2,1)S(1)}, bf16[256,384]{1,0:T(8,128)(2,1)S(1)}, u32[]{:S(2)}, u32[]{:S(2)}) collective-permute-start(bf16[256,384]{1,0:T(8,128)(2,1)S(1)} %get-tuple-element.54), channel_id=1, source_target_pairs={{0,12},{4,8},{8,4},{12,0},{16,28},{20,24},{24,20},{28,16},{1,13},{... | collective-permute-start | bytes 589832 | tf_op jit(solution)/shard_map/ppermute | solution.py:267
  60.2 15.3 %collective-permute-start.12 = (bf16[256,384]{1,0:T(8,128)(2,1)S(1)}, bf16[256,384]{1,0:T(8,128)(2,1)S(1)}, u32[]{:S(2)}, u32[]{:S(2)}) collective-permute-start(bf16[256,384]{1,0:T(8,128)(2,1)S(1)} %get-tuple-element.55), channel_id=1, source_target_pairs={{0,8},{4,12},{8,0},{12,4},{16,24},{20,28},{24,16},{28,20},{1,9},{5... | collective-permute-start | bytes 589832 | tf_op jit(solution)/shard_map/ppermute | solution.py:267
  61.7 13.9 %collective-permute-start.13 = (bf16[256,384]{1,0:T(8,128)(2,1)S(1)}, bf16[256,384]{1,0:T(8,128)(2,1)S(1)}, u32[]{:S(2)}, u32[]{:S(2)}) collective-permute-start(bf16[256,384]{1,0:T(8,128)(2,1)S(1)} %get-tuple-element.56), channel_id=1, source_target_pairs={{0,4},{4,0},{8,12},{12,8},{16,20},{20,16},{24,28},{28,24},{1,5},{5... | collective-permute-start | bytes 589832 | tf_op jit(solution)/shard_map/ppermute | solution.py:267
  62.4 13.2 %collective-permute-start.20 = (bf16[256,512]{1,0:T(8,128)(2,1)S(1)}, bf16[256,512]{1,0:T(8,128)(2,1)S(1)}, u32[]{:S(2)}, u32[]{:S(2)}) collective-permute-start(bf16[256,512]{1,0:T(8,128)(2,1)S(1)} %add_convert_fusion), channel_id=1, source_target_pairs={{0,2},{1,3},{2,0},{3,1},{4,6},{5,7},{6,4},{7,5},{8,10},{9,11},{10,... | collective-permute-start | bytes 786440 | tf_op jit(solution)/shard_map/ppermute | solution.py:276

commit v8 on v7

--- a/solution.py
+++ b/solution.py
@@ -112,7 +112,7 @@
 
 def forward_body(A, B, R, score_scale, owner_ref, block_ref, *refs):
     pair = B == 2
-    piece_refs, own_refs, others, refs = straight(refs[:A]), refs[A : 2 * A], refs[2 * A : -4], refs[-4:]
+    piece_refs, own_refs, others, refs = straight(refs[:A], LAST), refs[A : 2 * A], refs[2 * A : -4], refs[-4:]
     attn_ref, kvcat, weights_ref, kv = refs
     SEG = piece_refs[0].shape[0]
     parts = SEG // BLOCK
@@ -318,7 +318,7 @@
     attn, kvcat, weights = call(
         functools.partial(forward_body, A, B, R, score_scale),
         [shape((A, SEG, DH), BF16), shape((A, count, 2 * DH), BF16), shape((A, SEG, count), F32)],
-        [retr_owner, retr_block, *turned(pieces), *kvs, *kv],
+        [retr_owner, retr_block, *turned(pieces, LAST), *kvs, *kv],
         specs=[SMEM] * 2 + [VMEM] * (2 * A + len(kv)),
         scratch=[pltpu.VMEM((2 * A * (SEG // BLOCK), BLOCK, 2 * DH), BF16)],
         limit=limit,

time: 77.2 us -> 76.6 us (level)
    ppermute x3, waiting for transfers between devices: 1.4 us -> 0.01 us  [over_b(): return lax.ppermute(x, 'seg', [(i, (i + A) % n) for i in range(n)])]
    ppermute x12, waiting for transfers between devices: 31.4 us -> 32.2 us  [over_a(): lax.ppermute(x, 'seg', [(i, i // A * A + (i % A ^ m)) for i in range(n)])]
where the time goes in v8:
time: 76.6 us; the launch traced here: 76.3 us
  waiting for transfers between devices  32.4 us (42%)
  starting transfers between devices  27.7 us (36%)
  Pallas kernels  9.7 us (13%)
  local copies, waits for them, and re-layouts  5.58 us (7%)
  between operations  0.84 us (1%)
    ppermute x12, waiting for transfers between devices, over_a(): lax.ppermute(x, 'seg', [(i, i // A * A + (i % A ^ m)) for i in range(n)])  32.2 us
    ppermute x12, starting transfers between devices, over_a(): lax.ppermute(x, 'seg', [(i, i // A * A + (i % A ^ m)) for i in range(n)])  14.1 us
    pallas_call x13, Pallas kernels, call(): pl.pallas_call(body, out_shape=outs, in_specs=specs or [VMEM] * len(opera...  9.7 us
    ppermute x3, starting transfers between devices, over_b(): return lax.ppermute(x, 'seg', [(i, (i + A) % n) for i in range(n)])  7.16 us
    unnamed x20, local copies, waits for them, and re-layouts  5.56 us
    ppermute x6, starting transfers between devices, over_head(): return lax.ppermute(x, 'head', [(i, i ^ k) for i in range(H)])  5.1 us
  transfers between devices with their start and end apart: 22, of which 10 were waited for; matrix products, arithmetic and copies ran while one was open for 0% of the time, Pallas kernels for 11%

profile of v8, /device:TPU:0, one launch (start us, length us, event | category | flops | bytes accessed | tf_op | source)
XLA Modules:
  0.0 76.3 jit_solution(9145922797739703472)
XLA Ops:
  0.6 0.9 %copy-done.5 = bf16[256,512]{1,0:T(8,128)(2,1)S(1)} copy-done((bf16[256,512]{1,0:T(8,128)(2,1)S(1)}, bf16[256,512]{1,0:T(8,128)(2,1)}, u32[]{:S(2)}) %copy-start.5) | copy-done | bytes 262168
  1.6 0.9 %copy-done.6 = bf16[256,512]{1,0:T(8,128)(2,1)S(1)} copy-done((bf16[256,512]{1,0:T(8,128)(2,1)S(1)}, bf16[256,512]{1,0:T(8,128)(2,1)}, u32[]{:S(2)}) %copy-start.6) | copy-done | bytes 262168
  2.6 3.0 %collective-permute-start = (bf16[256,512]{1,0:T(8,128)(2,1)}, bf16[256,512]{1,0:T(8,128)(2,1)S(1)}, u32[]{:S(2)}, u32[]{:S(2)}) collective-permute-start(bf16[256,512]{1,0:T(8,128)(2,1)} %refs_2_), channel_id=1, source_target_pairs={{0,2},{1,3},{2,0},{3,1},{4,6},{5,7},{6,4},{7,5},{8,10},{9,11},{10,... | collective-permute-start | bytes 786440 | tf_op jit(solution)/shard_map/ppermute | solution.py:276
  5.6 1.5 %collective-permute-start.5 = (bf16[256,256]{1,0:T(8,128)(2,1)S(1)}, bf16[256,256]{1,0:T(8,128)(2,1)S(1)}, u32[]{:S(2)}, u32[]{:S(2)}) collective-permute-start(bf16[256,256]{1,0:T(8,128)(2,1)S(1)} %get-tuple-element.44), channel_id=1, source_target_pairs={{0,4},{4,0},{8,12},{12,8},{16,20},{20,16},{24,28},{28,24},{1,5},{5... | collective-permute-start | bytes 393224 | tf_op jit(solution)/shard_map/ppermute | solution.py:267
  7.2 1.6 %collective-permute-start.6 = (bf16[256,256]{1,0:T(8,128)(2,1)S(1)}, bf16[256,256]{1,0:T(8,128)(2,1)S(1)}, u32[]{:S(2)}, u32[]{:S(2)}) collective-permute-start(bf16[256,256]{1,0:T(8,128)(2,1)S(1)} %get-tuple-element.45), channel_id=1, source_target_pairs={{0,8},{4,12},{8,0},{12,4},{16,24},{20,28},{24,16},{28,20},{1,9},{5... | collective-permute-start | bytes 393224 | tf_op jit(solution)/shard_map/ppermute | solution.py:267
  9.1 2.6 %collective-permute-start.8 = (bf16[256,256]{1,0:T(8,128)(2,1)S(1)}, bf16[256,256]{1,0:T(8,128)(2,1)S(1)}, u32[]{:S(2)}, u32[]{:S(2)}) collective-permute-start(bf16[256,256]{1,0:T(8,128)(2,1)S(1)} %get-tuple-element.43.refs_4_), channel_id=1, source_target_pairs={{0,16},{4,20},{8,24},{12,28},{16,0},{20,4},{24,8},{28,12},{1,17},{... | collective-permute-start | bytes 393224 | tf_op jit(solution)/shard_map/ppermute | solution.py:270
  11.7 1.6 %copy-done.2 = bf16[512,2048]{1,0:T(8,128)(2,1)S(1)} copy-done((bf16[512,2048]{1,0:T(8,128)(2,1)S(1)}, bf16[512,2048]{1,0:T(8,128)(2,1)}, u32[]{:S(2)}) %copy-start.2) | copy-done | bytes 2097176
  13.3 0.9 %copy-done.3 = bf16[256,512]{1,0:T(8,128)(2,1)S(1)} copy-done((bf16[256,512]{1,0:T(8,128)(2,1)S(1)}, bf16[256,512]{1,0:T(8,128)(2,1)}, u32[]{:S(2)}) %copy-start.3) | copy-done | bytes 262168
  14.3 0.9 %copy-done.4 = bf16[256,512]{1,0:T(8,128)(2,1)S(1)} copy-done((bf16[256,512]{1,0:T(8,128)(2,1)S(1)}, bf16[256,512]{1,0:T(8,128)(2,1)}, u32[]{:S(2)}) %copy-start.4) | copy-done | bytes 262168
  16.0 1.6 %collective-permute-done.7.refs_1_.refs_7_ = bf16[256,256]{1,0:T(8,128)(2,1)S(1)} collective-permute-done((bf16[256,256]{1,0:T(8,128)(2,1)S(1)}, bf16[256,256]{1,0:T(8,128)(2,1)S(1)}, u32[]{:S(2)}, u32[]{:S(2)}) %collective-permute-start.7) | collective-permute-done | bytes 131104 | tf_op jit(solution)/shard_map/ppermute | solution.py:267
  17.7 2.4 %collective-permute-start.9 = (bf16[3,256,256]{2,1,0:T(8,128)(2,1)S(1)}, bf16[3,256,256]{2,1,0:T(8,128)(2,1)S(1)}, u32[]{:S(2)}, u32[]{:S(2)}) collective-permute-start(bf16[3,256,256]{2,1,0:T(8,128)(2,1)S(1)} %shard_map.114), channel_id=1, source_target_pairs={{0,16},{4,20},{8,24},{12,28},{16,0},{20,4},{24,8},{28,12},{1,17},{... | collective-permute-start | bytes 1179656 | tf_op jit(solution)/shard_map/ppermute | solution.py:270
  21.1 2.6 %collective-permute-start.2 = (bf16[256,384]{1,0:T(8,128)(2,1)S(1)}, bf16[256,384]{1,0:T(8,128)(2,1)S(1)}, u32[]{:S(2)}, u32[]{:S(2)}) collective-permute-start(bf16[256,384]{1,0:T(8,128)(2,1)S(1)} %get-tuple-element.39), channel_id=1, source_target_pairs={{0,12},{4,8},{8,4},{12,0},{16,28},{20,24},{24,20},{28,16},{1,13},{... | collective-permute-start | bytes 589832 | tf_op jit(solution)/shard_map/ppermute | solution.py:267
  23.6 1.0 %collective-permute-start.4 = (bf16[256,384]{1,0:T(8,128)(2,1)S(1)}, bf16[256,384]{1,0:T(8,128)(2,1)S(1)}, u32[]{:S(2)}, u32[]{:S(2)}) collective-permute-start(bf16[256,384]{1,0:T(8,128)(2,1)S(1)} %get-tuple-element.41), channel_id=1, source_target_pairs={{0,4},{4,0},{8,12},{12,8},{16,20},{20,16},{24,28},{28,24},{1,5},{5... | collective-permute-start | bytes 589832 | tf_op jit(solution)/shard_map/ppermute | solution.py:267
  24.8 8.5 %collective-permute-done.2.refs_0_.refs_3_ = bf16[256,384]{1,0:T(8,128)(2,1)S(1)} collective-permute-done((bf16[256,384]{1,0:T(8,128)(2,1)S(1)}, bf16[256,384]{1,0:T(8,128)(2,1)S(1)}, u32[]{:S(2)}, u32[]{:S(2)}) %collective-permute-start.2) | collective-permute-done | bytes 196640 | tf_op jit(solution)/shard_map/ppermute | solution.py:267
  33.3 4.9 %collective-permute-done.3.refs_1_.refs_2_ = bf16[256,384]{1,0:T(8,128)(2,1)S(1)} collective-permute-done((bf16[256,384]{1,0:T(8,128)(2,1)S(1)}, bf16[256,384]{1,0:T(8,128)(2,1)S(1)}, u32[]{:S(2)}, u32[]{:S(2)}) %collective-permute-start.3) | collective-permute-done | bytes 196640 | tf_op jit(solution)/shard_map/ppermute | solution.py:267
  38.5 2.9 %shard_map.115 = (bf16[4,256,128]{2,1,0:T(8,128)(2,1)S(1)}, bf16[4,1024,256]{2,1,0:T(8,128)(2,1)S(1)}, f32[4,256,1024]{2,1,0:T(8,128)S(1)}) custom-call(s32[8,4]{1,0:T(8,128)S(1)} %copy.12.owner_ref, s32[8,4]{1,0:T(8,128)S(1)} %copy.13.block_ref, bf16[256,384]{1,0:T(8,128)(2,1)S(1)} %collective-permute-done.2.refs_0_.refs_3_, ...), custom_call_target="tpu_custom_call" | custom-call | flops 99999997952 | bytes 1 | tf_op jit(solution)/shard_map/pallas_call | solution.py:41
  41.5 1.9 %collective-permute-start.15 = (bf16[4,256,128]{2,1,0:T(8,128)(2,1)S(1)}, bf16[4,256,128]{2,1,0:T(8,128)(2,1)S(1)}, u32[]{:S(2)}, u32[]{:S(2)}) collective-permute-start(bf16[4,256,128]{2,1,0:T(8,128)(2,1)S(1)} %get-tuple-element.47.attn_ref.refs_3_), channel_id=1, source_target_pairs={{0,12},{4,8},{8,4},{12,0},{16,28},{20,24},{24,20},{28,16},{1,13},{... | collective-permute-start | bytes 786440 | tf_op jit(solution)/shard_map/ppermute | solution.py:267
  43.4 1.6 %collective-permute-start.16 = (bf16[4,256,128]{2,1,0:T(8,128)(2,1)S(1)}, bf16[4,256,128]{2,1,0:T(8,128)(2,1)S(1)}, u32[]{:S(2)}, u32[]{:S(2)}) collective-permute-start(bf16[4,256,128]{2,1,0:T(8,128)(2,1)S(1)} %get-tuple-element.47.attn_ref.refs_3_), channel_id=1, source_target_pairs={{0,4},{4,0},{8,12},{12,8},{16,20},{20,16},{24,28},{28,24},{1,5},{5... | collective-permute-start | bytes 786440 | tf_op jit(solution)/shard_map/ppermute | solution.py:267
  45.1 2.4 %shard_map.116 = (bf16[4,256,128]{2,1,0:T(8,128)(2,1)S(1)}, f32[4,256,256]{2,1,0:T(8,128)S(1)}, bf16[4,256,256]{2,1,0:T(8,128)(2,1)S(1)}, bf16[256,256]{1,0:T(8,128)(2,1)S(1)}) custom-call(bf16[4,256,128]{2,1,0:T(8,128)(2,1)S(1)} %get-tuple-element.47.attn_ref.refs_3_, bf16[4,1024,256]{2,1,0:T(8,128)(2,1)S(1)} %get-tuple-element.48.kvcat, ...), custom_call_target="tpu_custom_call" | custom-call | flops 99999997952 | bytes 1 | tf_op jit(solution)/shard_map/pallas_call | solution.py:41
  47.4 1.3 %collective-permute-start.10 = (bf16[256,256]{1,0:T(8,128)(2,1)S(1)}, bf16[256,256]{1,0:T(8,128)(2,1)S(1)}, u32[]{:S(2)}, u32[]{:S(2)}) collective-permute-start(bf16[256,256]{1,0:T(8,128)(2,1)S(1)} %get-tuple-element.53), channel_id=1, source_target_pairs={{16,0},{20,4},{24,8},{28,12},{17,1},{21,5},{25,9},{29,13},{18,2},{... | collective-permute-start | bytes 393224 | tf_op jit(solution)/shard_map/ppermute | solution.py:273
  48.7 1.9 %collective-permute-done.14.refs_0_ = bf16[4,256,128]{2,1,0:T(8,128)(2,1)S(1)} collective-permute-done((bf16[4,256,128]{2,1,0:T(8,128)(2,1)S(1)}, bf16[4,256,128]{2,1,0:T(8,128)(2,1)S(1)}, u32[]{:S(2)}, u32[]{:S(2)}) %collective-permute-start.14) | collective-permute-done | bytes 262176 | tf_op jit(solution)/shard_map/ppermute | solution.py:267
  50.7 2.0 %collective-permute-done.15.refs_1_ = bf16[4,256,128]{2,1,0:T(8,128)(2,1)S(1)} collective-permute-done((bf16[4,256,128]{2,1,0:T(8,128)(2,1)S(1)}, bf16[4,256,128]{2,1,0:T(8,128)(2,1)S(1)}, u32[]{:S(2)}, u32[]{:S(2)}) %collective-permute-start.15) | collective-permute-done | bytes 262176 | tf_op jit(solution)/shard_map/ppermute | solution.py:267
  52.7 1.9 %collective-permute-done.16.refs_2_ = bf16[4,256,128]{2,1,0:T(8,128)(2,1)S(1)} collective-permute-done((bf16[4,256,128]{2,1,0:T(8,128)(2,1)S(1)}, bf16[4,256,128]{2,1,0:T(8,128)(2,1)S(1)}, u32[]{:S(2)}, u32[]{:S(2)}) %collective-permute-start.16) | collective-permute-done | bytes 262176 | tf_op jit(solution)/shard_map/ppermute | solution.py:267
  54.7 1.6 %shard_map.120 = (f32[256,512]{1,0:T(8,128)S(1)}, f32[256,512]{1,0:T(8,128)S(1)}, bf16[256,1024]{1,0:T(8,128)(2,1)S(1)}, f32[256,512]{1,0:T(8,128)S(1)}, bf16[256,512]{1,0:T(8,128)(2,1)S(1)}) custom-call(bf16[4,256,128]{2,1,0:T(8,128)(2,1)S(1)} %collective-permute-done.14.refs_0_, bf16[4,256,128]{2,1,0:T(8,128)(2,1)S(1)} %collective-permute-done.15.refs_1_, ...), custom_call_target="tpu_custom_call" | custom-call | flops 1 | bytes 1 | tf_op jit(solution)/shard_map/pallas_call | solution.py:41
  56.4 2.2 %collective-permute-start.21 = (bf16[256,512]{1,0:T(8,128)(2,1)S(1)}, bf16[256,512]{1,0:T(8,128)(2,1)S(1)}, u32[]{:S(2)}, u32[]{:S(2)}) collective-permute-start(bf16[256,512]{1,0:T(8,128)(2,1)S(1)} %get-tuple-element.62), channel_id=1, source_target_pairs={{0,16},{4,20},{8,24},{12,28},{16,0},{20,4},{24,8},{28,12},{1,17},{... | collective-permute-start | bytes 786440 | tf_op jit(solution)/shard_map/ppermute | solution.py:270
  58.9 1.1 %collective-permute-start.11 = (bf16[256,384]{1,0:T(8,128)(2,1)S(1)}, bf16[256,384]{1,0:T(8,128)(2,1)S(1)}, u32[]{:S(2)}, u32[]{:S(2)}) collective-permute-start(bf16[256,384]{1,0:T(8,128)(2,1)S(1)} %get-tuple-element.54), channel_id=1, source_target_pairs={{0,12},{4,8},{8,4},{12,0},{16,28},{20,24},{24,20},{28,16},{1,13},{... | collective-permute-start | bytes 589832 | tf_op jit(solution)/shard_map/ppermute | solution.py:267
  60.0 1.1 %collective-permute-start.12 = (bf16[256,384]{1,0:T(8,128)(2,1)S(1)}, bf16[256,384]{1,0:T(8,128)(2,1)S(1)}, u32[]{:S(2)}, u32[]{:S(2)}) collective-permute-start(bf16[256,384]{1,0:T(8,128)(2,1)S(1)} %get-tuple-element.55), channel_id=1, source_target_pairs={{0,8},{4,12},{8,0},{12,4},{16,24},{20,28},{24,16},{28,20},{1,9},{5... | collective-permute-start | bytes 589832 | tf_op jit(solution)/shard_map/ppermute | solution.py:267
  61.1 1.4 %collective-permute-start.13 = (bf16[256,384]{1,0:T(8,128)(2,1)S(1)}, bf16[256,384]{1,0:T(8,128)(2,1)S(1)}, u32[]{:S(2)}, u32[]{:S(2)}) collective-permute-start(bf16[256,384]{1,0:T(8,128)(2,1)S(1)} %get-tuple-element.56), channel_id=1, source_target_pairs={{0,4},{4,0},{8,12},{12,8},{16,20},{20,16},{24,28},{28,24},{1,5},{5... | collective-permute-start | bytes 589832 | tf_op jit(solution)/shard_map/ppermute | solution.py:267
  62.5 1.6 %collective-permute-start.20 = (bf16[256,512]{1,0:T(8,128)(2,1)S(1)}, bf16[256,512]{1,0:T(8,128)(2,1)S(1)}, u32[]{:S(2)}, u32[]{:S(2)}) collective-permute-start(bf16[256,512]{1,0:T(8,128)(2,1)S(1)} %add_convert_fusion), channel_id=1, source_target_pairs={{0,2},{1,3},{2,0},{3,1},{4,6},{5,7},{6,4},{7,5},{8,10},{9,11},{10,... | collective-permute-start | bytes 786440 | tf_op jit(solution)/shard_map/ppermute | solution.py:276
  64.1 9.0 %collective-permute-done.11.refs_2_.refs_0_ = bf16[256,384]{1,0:T(8,128)(2,1)S(1)} collective-permute-done((bf16[256,384]{1,0:T(8,128)(2,1)S(1)}, bf16[256,384]{1,0:T(8,128)(2,1)S(1)}, u32[]{:S(2)}, u32[]{:S(2)}) %collective-permute-start.11) | collective-permute-done | bytes 196640 | tf_op jit(solution)/shard_map/ppermute | solution.py:267
  73.2 1.7 %collective-permute-done.12.refs_1_ = bf16[256,384]{1,0:T(8,128)(2,1)S(1)} collective-permute-done((bf16[256,384]{1,0:T(8,128)(2,1)S(1)}, bf16[256,384]{1,0:T(8,128)(2,1)S(1)}, u32[]{:S(2)}, u32[]{:S(2)}) %collective-permute-start.12) | collective-permute-done | bytes 196640 | tf_op jit(solution)/shard_map/ppermute | solution.py:267
  74.9 1.4 %shard_map.122 = (bf16[256,512]{1,0:T(8,128)(2,1)}, bf16[256,512]{1,0:T(8,128)(2,1)}, bf16[256,512]{1,0:T(8,128)(2,1)}, bf16[256,512]{1,0:T(8,128)(2,1)}, f32[256,512]{1,0:T(8,128)}) custom-call(bf16[256,384]{1,0:T(8,128)(2,1)S(1)} %collective-permute-done.11.refs_2_.refs_0_, bf16[256,384]{1,0:T(8,128)(2,1)S(1)} %collective-permute-done.12.refs_1_, ...), custom_call_target="tpu_custom_call" | custom-call | flops 1 | bytes 1 | tf_op jit(solution)/shard_map/pallas_call | solution.py:41
  (47 shorter events, 3.4 us)
Async XLA Ops:
  0.6 1.0 %copy-start.5 = (bf16[256,512]{1,0:T(8,128)(2,1)S(1)}, bf16[256,512]{1,0:T(8,128)(2,1)}, u32[]{:S(2)}) copy-start(bf16[256,512]{1,0:T(8,128)(2,1)} %k_ref.1) | copy-start | bytes 786436
  1.6 0.9 %copy-start.6 = (bf16[256,512]{1,0:T(8,128)(2,1)S(1)}, bf16[256,512]{1,0:T(8,128)(2,1)}, u32[]{:S(2)}) copy-start(bf16[256,512]{1,0:T(8,128)(2,1)} %v_ref.1) | copy-start | bytes 786436
  2.6 12.8 %collective-permute-start = (bf16[256,512]{1,0:T(8,128)(2,1)}, bf16[256,512]{1,0:T(8,128)(2,1)S(1)}, u32[]{:S(2)}, u32[]{:S(2)}) collective-permute-start(bf16[256,512]{1,0:T(8,128)(2,1)} %refs_2_), channel_id=1, source_target_pairs={{0,2},{1,3},{2,0},{3,1},{4,6},{5,7},{6,4},{7,5},{8,10},{9,11},{10,... | collective-permute-start | bytes 786440 | tf_op jit(solution)/shard_map/ppermute | solution.py:276
  5.6 9.9 %collective-permute-start.5 = (bf16[256,256]{1,0:T(8,128)(2,1)S(1)}, bf16[256,256]{1,0:T(8,128)(2,1)S(1)}, u32[]{:S(2)}, u32[]{:S(2)}) collective-permute-start(bf16[256,256]{1,0:T(8,128)(2,1)S(1)} %get-tuple-element.44), channel_id=1, source_target_pairs={{0,4},{4,0},{8,12},{12,8},{16,20},{20,16},{24,28},{28,24},{1,5},{5... | collective-permute-start | bytes 393224 | tf_op jit(solution)/shard_map/ppermute | solution.py:267
  7.2 8.9 %collective-permute-start.6 = (bf16[256,256]{1,0:T(8,128)(2,1)S(1)}, bf16[256,256]{1,0:T(8,128)(2,1)S(1)}, u32[]{:S(2)}, u32[]{:S(2)}) collective-permute-start(bf16[256,256]{1,0:T(8,128)(2,1)S(1)} %get-tuple-element.45), channel_id=1, source_target_pairs={{0,8},{4,12},{8,0},{12,4},{16,24},{20,28},{24,16},{28,20},{1,9},{5... | collective-permute-start | bytes 393224 | tf_op jit(solution)/shard_map/ppermute | solution.py:267
  8.7 9.0 %collective-permute-start.7 = (bf16[256,256]{1,0:T(8,128)(2,1)S(1)}, bf16[256,256]{1,0:T(8,128)(2,1)S(1)}, u32[]{:S(2)}, u32[]{:S(2)}) collective-permute-start(bf16[256,256]{1,0:T(8,128)(2,1)S(1)} %get-tuple-element.46), channel_id=1, source_target_pairs={{0,12},{4,8},{8,4},{12,0},{16,28},{20,24},{24,20},{28,16},{1,13},{... | collective-permute-start | bytes 393224 | tf_op jit(solution)/shard_map/ppermute | solution.py:267
  9.1 8.6 %collective-permute-start.8 = (bf16[256,256]{1,0:T(8,128)(2,1)S(1)}, bf16[256,256]{1,0:T(8,128)(2,1)S(1)}, u32[]{:S(2)}, u32[]{:S(2)}) collective-permute-start(bf16[256,256]{1,0:T(8,128)(2,1)S(1)} %get-tuple-element.43.refs_4_), channel_id=1, source_target_pairs={{0,16},{4,20},{8,24},{12,28},{16,0},{20,4},{24,8},{28,12},{1,17},{... | collective-permute-start | bytes 393224 | tf_op jit(solution)/shard_map/ppermute | solution.py:270
  11.7 1.6 %copy-start.2 = (bf16[512,2048]{1,0:T(8,128)(2,1)S(1)}, bf16[512,2048]{1,0:T(8,128)(2,1)}, u32[]{:S(2)}) copy-start(bf16[512,2048]{1,0:T(8,128)(2,1)} %refs_0_.1) | copy-start | bytes 6291460
  13.3 0.9 %copy-start.3 = (bf16[256,512]{1,0:T(8,128)(2,1)S(1)}, bf16[256,512]{1,0:T(8,128)(2,1)}, u32[]{:S(2)}) copy-start(bf16[256,512]{1,0:T(8,128)(2,1)} %refs_1_.1) | copy-start | bytes 786436
  14.3 0.9 %copy-start.4 = (bf16[256,512]{1,0:T(8,128)(2,1)S(1)}, bf16[256,512]{1,0:T(8,128)(2,1)}, u32[]{:S(2)}) copy-start(bf16[256,512]{1,0:T(8,128)(2,1)} %refs_2_) | copy-start | bytes 786436
  15.4 4.8 %copy-start = (bf16[512,2048]{1,0:T(8,128)(2,1)}, bf16[512,2048]{1,0:T(8,128)(2,1)S(1)}, u32[]{:S(2)}) copy-start(bf16[512,2048]{1,0:T(8,128)(2,1)S(1)} %get-tuple-element.37.refs_2_.refs_4_.refs_6_) | copy-start | bytes 6291460
  15.4 4.7 %collective-permute-start.1 = (bf16[2,256,512]{2,1,0:T(8,128)(2,1)S(1)}, bf16[2,256,512]{2,1,0:T(8,128)(2,1)S(1)}, u32[]{:S(2)}, u32[]{:S(2)}) collective-permute-start(bf16[2,256,512]{2,1,0:T(8,128)(2,1)S(1)} %shard_map.112.refs_0_), channel_id=1, source_target_pairs={{0,1},{1,0},{2,3},{3,2},{4,5},{5,4},{6,7},{7,6},{8,9},{9,8},{10,11... | collective-permute-start | bytes 1572872 | tf_op jit(solution)/shard_map/ppermute | solution.py:276
  17.7 6.9 %copy-start.7 = (s32[8,4]{0,1:T(4,128)S(1)}, s32[8,4]{0,1:T(4,128)}, u32[]{:S(2)}) copy-start(s32[8,4]{0,1:T(4,128)} %param.12) | copy-start | bytes 388
  17.7 7.0 %copy-start.8 = (s32[8,4]{0,1:T(4,128)S(1)}, s32[8,4]{0,1:T(4,128)}, u32[]{:S(2)}) copy-start(s32[8,4]{0,1:T(4,128)} %param.13) | copy-start | bytes 388
  17.7 20.8 %collective-permute-start.9 = (bf16[3,256,256]{2,1,0:T(8,128)(2,1)S(1)}, bf16[3,256,256]{2,1,0:T(8,128)(2,1)S(1)}, u32[]{:S(2)}, u32[]{:S(2)}) collective-permute-start(bf16[3,256,256]{2,1,0:T(8,128)(2,1)S(1)} %shard_map.114), channel_id=1, source_target_pairs={{0,16},{4,20},{8,24},{12,28},{16,0},{20,4},{24,8},{28,12},{1,17},{... | collective-permute-start | bytes 1179656 | tf_op jit(solution)/shard_map/ppermute | solution.py:270
  21.1 12.2 %collective-permute-start.2 = (bf16[256,384]{1,0:T(8,128)(2,1)S(1)}, bf16[256,384]{1,0:T(8,128)(2,1)S(1)}, u32[]{:S(2)}, u32[]{:S(2)}) collective-permute-start(bf16[256,384]{1,0:T(8,128)(2,1)S(1)} %get-tuple-element.39), channel_id=1, source_target_pairs={{0,12},{4,8},{8,4},{12,0},{16,28},{20,24},{24,20},{28,16},{1,13},{... | collective-permute-start | bytes 589832 | tf_op jit(solution)/shard_map/ppermute | solution.py:267
  23.6 14.6 %collective-permute-start.3 = (bf16[256,384]{1,0:T(8,128)(2,1)S(1)}, bf16[256,384]{1,0:T(8,128)(2,1)S(1)}, u32[]{:S(2)}, u32[]{:S(2)}) collective-permute-start(bf16[256,384]{1,0:T(8,128)(2,1)S(1)} %get-tuple-element.40), channel_id=1, source_target_pairs={{0,8},{4,12},{8,0},{12,4},{16,24},{20,28},{24,16},{28,20},{1,9},{5... | collective-permute-start | bytes 589832 | tf_op jit(solution)/shard_map/ppermute | solution.py:267
  23.6 14.6 %collective-permute-start.4 = (bf16[256,384]{1,0:T(8,128)(2,1)S(1)}, bf16[256,384]{1,0:T(8,128)(2,1)S(1)}, u32[]{:S(2)}, u32[]{:S(2)}) collective-permute-start(bf16[256,384]{1,0:T(8,128)(2,1)S(1)} %get-tuple-element.41), channel_id=1, source_target_pairs={{0,4},{4,0},{8,12},{12,8},{16,20},{20,16},{24,28},{28,24},{1,5},{5... | collective-permute-start | bytes 589832 | tf_op jit(solution)/shard_map/ppermute | solution.py:267
  38.3 6.7 %collective-permute-start.17 = (bf16[4,256,128]{2,1,0:T(8,128)(2,1)S(1)}, bf16[4,256,128]{2,1,0:T(8,128)(2,1)S(1)}, u32[]{:S(2)}, u32[]{:S(2)}) collective-permute-start(bf16[4,256,128]{2,1,0:T(8,128)(2,1)S(1)} %shard_map.118.refs_0_), channel_id=1, source_target_pairs={{0,2},{1,3},{2,0},{3,1},{4,6},{5,7},{6,4},{7,5},{8,10},{9,11},{10,... | collective-permute-start | bytes 786440 | tf_op jit(solution)/shard_map/ppermute | solution.py:276
  41.4 9.3 %collective-permute-start.14 = (bf16[4,256,128]{2,1,0:T(8,128)(2,1)S(1)}, bf16[4,256,128]{2,1,0:T(8,128)(2,1)S(1)}, u32[]{:S(2)}, u32[]{:S(2)}) collective-permute-start(bf16[4,256,128]{2,1,0:T(8,128)(2,1)S(1)} %get-tuple-element.47.attn_ref.refs_3_), channel_id=1, source_target_pairs={{0,8},{4,12},{8,0},{12,4},{16,24},{20,28},{24,16},{28,20},{1,9},{5... | collective-permute-start | bytes 786440 | tf_op jit(solution)/shard_map/ppermute | solution.py:267
  41.5 11.2 %collective-permute-start.15 = (bf16[4,256,128]{2,1,0:T(8,128)(2,1)S(1)}, bf16[4,256,128]{2,1,0:T(8,128)(2,1)S(1)}, u32[]{:S(2)}, u32[]{:S(2)}) collective-permute-start(bf16[4,256,128]{2,1,0:T(8,128)(2,1)S(1)} %get-tuple-element.47.attn_ref.refs_3_), channel_id=1, source_target_pairs={{0,12},{4,8},{8,4},{12,0},{16,28},{20,24},{24,20},{28,16},{1,13},{... | collective-permute-start | bytes 786440 | tf_op jit(solution)/shard_map/ppermute | solution.py:267
  43.4 11.3 %collective-permute-start.16 = (bf16[4,256,128]{2,1,0:T(8,128)(2,1)S(1)}, bf16[4,256,128]{2,1,0:T(8,128)(2,1)S(1)}, u32[]{:S(2)}, u32[]{:S(2)}) collective-permute-start(bf16[4,256,128]{2,1,0:T(8,128)(2,1)S(1)} %get-tuple-element.47.attn_ref.refs_3_), channel_id=1, source_target_pairs={{0,4},{4,0},{8,12},{12,8},{16,20},{20,16},{24,28},{28,24},{1,5},{5... | collective-permute-start | bytes 786440 | tf_op jit(solution)/shard_map/ppermute | solution.py:267
  45.0 9.7 %collective-permute-start.18 = (bf16[2,4,256,128]{3,2,1,0:T(8,128)(2,1)S(1)}, bf16[2,4,256,128]{3,2,1,0:T(8,128)(2,1)S(1)}, u32[]{:S(2)}, u32[]{:S(2)}) collective-permute-start(bf16[2,4,256,128]{3,2,1,0:T(8,128)(2,1)S(1)} %shard_map.119.refs_4_), channel_id=1, source_target_pairs={{0,1},{1,0},{2,3},{3,2},{4,5},{5,4},{6,7},{7,6},{8,9},{9,8},{10,11... | collective-permute-start | bytes 1572872 | tf_op jit(solution)/shard_map/ppermute | solution.py:276
  45.1 9.6 %copy-start.1 = (bf16[512,2048]{1,0:T(8,128)(2,1)S(1)}, bf16[512,2048]{1,0:T(8,128)(2,1)}, u32[]{:S(2)}) copy-start(bf16[512,2048]{1,0:T(8,128)(2,1)} %copy-done) | copy-start | bytes 6291460
  47.4 11.3 %collective-permute-start.10 = (bf16[256,256]{1,0:T(8,128)(2,1)S(1)}, bf16[256,256]{1,0:T(8,128)(2,1)S(1)}, u32[]{:S(2)}, u32[]{:S(2)}) collective-permute-start(bf16[256,256]{1,0:T(8,128)(2,1)S(1)} %get-tuple-element.53), channel_id=1, source_target_pairs={{16,0},{20,4},{24,8},{28,12},{17,1},{21,5},{25,9},{29,13},{18,2},{... | collective-permute-start | bytes 393224 | tf_op jit(solution)/shard_map/ppermute | solution.py:273
  56.3 6.1 %collective-permute-start.19 = (bf16[256,1024]{1,0:T(8,128)(2,1)S(1)}, bf16[256,1024]{1,0:T(8,128)(2,1)S(1)}, u32[]{:S(2)}, u32[]{:S(2)}) collective-permute-start(bf16[256,1024]{1,0:T(8,128)(2,1)S(1)} %get-tuple-element.59), channel_id=1, source_target_pairs={{0,1},{1,0},{2,3},{3,2},{4,5},{5,4},{6,7},{7,6},{8,9},{9,8},{10,11... | collective-permute-start | bytes 1572872 | tf_op jit(solution)/shard_map/ppermute | solution.py:276
  56.4 18.5 %collective-permute-start.21 = (bf16[256,512]{1,0:T(8,128)(2,1)S(1)}, bf16[256,512]{1,0:T(8,128)(2,1)S(1)}, u32[]{:S(2)}, u32[]{:S(2)}) collective-permute-start(bf16[256,512]{1,0:T(8,128)(2,1)S(1)} %get-tuple-element.62), channel_id=1, source_target_pairs={{0,16},{4,20},{8,24},{12,28},{16,0},{20,4},{24,8},{28,12},{1,17},{... | collective-permute-start | bytes 786440 | tf_op jit(solution)/shard_map/ppermute | solution.py:270
  58.9 14.3 %collective-permute-start.11 = (bf16[256,384]{1,0:T(8,128)(2,1)S(1)}, bf16[256,384]{1,0:T(8,128)(2,1)S(1)}, u32[]{:S(2)}, u32[]{:S(2)}) collective-permute-start(bf16[256,384]{1,0:T(8,128)(2,1)S(1)} %get-tuple-element.54), channel_id=1, source_target_pairs={{0,12},{4,8},{8,4},{12,0},{16,28},{20,24},{24,20},{28,16},{1,13},{... | collective-permute-start | bytes 589832 | tf_op jit(solution)/shard_map/ppermute | solution.py:267
  60.0 14.9 %collective-permute-start.12 = (bf16[256,384]{1,0:T(8,128)(2,1)S(1)}, bf16[256,384]{1,0:T(8,128)(2,1)S(1)}, u32[]{:S(2)}, u32[]{:S(2)}) collective-permute-start(bf16[256,384]{1,0:T(8,128)(2,1)S(1)} %get-tuple-element.55), channel_id=1, source_target_pairs={{0,8},{4,12},{8,0},{12,4},{16,24},{20,28},{24,16},{28,20},{1,9},{5... | collective-permute-start | bytes 589832 | tf_op jit(solution)/shard_map/ppermute | solution.py:267
  61.1 13.8 %collective-permute-start.13 = (bf16[256,384]{1,0:T(8,128)(2,1)S(1)}, bf16[256,384]{1,0:T(8,128)(2,1)S(1)}, u32[]{:S(2)}, u32[]{:S(2)}) collective-permute-start(bf16[256,384]{1,0:T(8,128)(2,1)S(1)} %get-tuple-element.56), channel_id=1, source_target_pairs={{0,4},{4,0},{8,12},{12,8},{16,20},{20,16},{24,28},{28,24},{1,5},{5... | collective-permute-start | bytes 589832 | tf_op jit(solution)/shard_map/ppermute | solution.py:267
  62.5 12.4 %collective-permute-start.20 = (bf16[256,512]{1,0:T(8,128)(2,1)S(1)}, bf16[256,512]{1,0:T(8,128)(2,1)S(1)}, u32[]{:S(2)}, u32[]{:S(2)}) collective-permute-start(bf16[256,512]{1,0:T(8,128)(2,1)S(1)} %add_convert_fusion), channel_id=1, source_target_pairs={{0,2},{1,3},{2,0},{3,1},{4,6},{5,7},{6,4},{7,5},{8,10},{9,11},{10,... | collective-permute-start | bytes 786440 | tf_op jit(solution)/shard_map/ppermute | solution.py:276

commit v9 on v8

--- a/solution.py
+++ b/solution.py
@@ -178,14 +178,17 @@
     piece_refs, (dq_ref, own_ref, cache_ref, carry_ref) = refs[:A], refs[A:]
     SEG = piece_refs[0].shape[0]
     a = lax.axis_index("seg") % A
+    raw = [dot(piece_refs[0][:, DH : 2 * DH], kvcat[0, :, DH:], (1, 1))]
     for m in range(A):
         seg_a = a ^ m
+        if m + 1 < A:
+            raw.append(dot(piece_refs[m + 1][:, DH : 2 * DH], kvcat[m + 1, :, DH:], (1, 1)))
         prev_a = jnp.where(seg_a == 0, A - 1, seg_a - 1)
         q, da = piece_refs[m][:, :DH], piece_refs[m][:, DH : 2 * DH]
         row_delta = jnp.sum(da.astype(F32) * attn_ref[m].astype(F32), -1, keepdims=True)
         weights = weights_ref[m]
         rounded = weights.astype(BF16)
-        slopes = (weights.astype(F32) * (dot(da, kvcat[m, :, DH:], (1, 1)) - row_delta)).astype(BF16)
+        slopes = (weights.astype(F32) * (raw[m] - row_delta)).astype(BF16)
         dq_ref[m] = (score_scale * dot(slopes, kvcat[m, :, :DH], (1, 0))).astype(BF16)
         dk = score_scale * dot(slopes[:, : 2 * SEG], q, (0, 0))
         dv = dot(rounded[:, : 2 * SEG], da, (0, 0))

time: 76.6 us -> 76.6 us (level)
  no operation moved by 1% of the time
where the time goes in v9:
time: 76.6 us; the launch traced here: 76.3 us
  waiting for transfers between devices  32.3 us (42%)
  starting transfers between devices  27.7 us (36%)
  Pallas kernels  9.82 us (13%)
  local copies, waits for them, and re-layouts  5.58 us (7%)
  between operations  0.84 us (1%)
    ppermute x12, waiting for transfers between devices, over_a(): lax.ppermute(x, 'seg', [(i, i // A * A + (i % A ^ m)) for i in range(n)])  32 us
    ppermute x12, starting transfers between devices, over_a(): lax.ppermute(x, 'seg', [(i, i // A * A + (i % A ^ m)) for i in range(n)])  14.1 us
    pallas_call x13, Pallas kernels, call(): pl.pallas_call(body, out_shape=outs, in_specs=specs or [VMEM] * len(opera...  9.82 us
    ppermute x3, starting transfers between devices, over_b(): return lax.ppermute(x, 'seg', [(i, (i + A) % n) for i in range(n)])  7.16 us
    unnamed x20, local copies, waits for them, and re-layouts  5.56 us
    ppermute x6, starting transfers between devices, over_head(): return lax.ppermute(x, 'head', [(i, i ^ k) for i in range(H)])  5.1 us
  transfers between devices with their start and end apart: 22, of which 10 were waited for; matrix products, arithmetic and copies ran while one was open for 0% of the time, Pallas kernels for 11%

profile of v9, /device:TPU:0, one launch (start us, length us, event | category | flops | bytes accessed | tf_op | source)
XLA Modules:
  0.0 76.3 jit_solution(17619831093597958578)
XLA Ops:
  0.6 0.9 %copy-done.5 = bf16[256,512]{1,0:T(8,128)(2,1)S(1)} copy-done((bf16[256,512]{1,0:T(8,128)(2,1)S(1)}, bf16[256,512]{1,0:T(8,128)(2,1)}, u32[]{:S(2)}) %copy-start.5) | copy-done | bytes 262168
  1.6 0.9 %copy-done.6 = bf16[256,512]{1,0:T(8,128)(2,1)S(1)} copy-done((bf16[256,512]{1,0:T(8,128)(2,1)S(1)}, bf16[256,512]{1,0:T(8,128)(2,1)}, u32[]{:S(2)}) %copy-start.6) | copy-done | bytes 262168
  2.6 3.0 %collective-permute-start = (bf16[256,512]{1,0:T(8,128)(2,1)}, bf16[256,512]{1,0:T(8,128)(2,1)S(1)}, u32[]{:S(2)}, u32[]{:S(2)}) collective-permute-start(bf16[256,512]{1,0:T(8,128)(2,1)} %refs_2_), channel_id=1, source_target_pairs={{0,2},{1,3},{2,0},{3,1},{4,6},{5,7},{6,4},{7,5},{8,10},{9,11},{10,... | collective-permute-start | bytes 786440 | tf_op jit(solution)/shard_map/ppermute | solution.py:279
  5.6 1.5 %collective-permute-start.5 = (bf16[256,256]{1,0:T(8,128)(2,1)S(1)}, bf16[256,256]{1,0:T(8,128)(2,1)S(1)}, u32[]{:S(2)}, u32[]{:S(2)}) collective-permute-start(bf16[256,256]{1,0:T(8,128)(2,1)S(1)} %get-tuple-element.44), channel_id=1, source_target_pairs={{0,4},{4,0},{8,12},{12,8},{16,20},{20,16},{24,28},{28,24},{1,5},{5... | collective-permute-start | bytes 393224 | tf_op jit(solution)/shard_map/ppermute | solution.py:270
  7.2 1.6 %collective-permute-start.6 = (bf16[256,256]{1,0:T(8,128)(2,1)S(1)}, bf16[256,256]{1,0:T(8,128)(2,1)S(1)}, u32[]{:S(2)}, u32[]{:S(2)}) collective-permute-start(bf16[256,256]{1,0:T(8,128)(2,1)S(1)} %get-tuple-element.45), channel_id=1, source_target_pairs={{0,8},{4,12},{8,0},{12,4},{16,24},{20,28},{24,16},{28,20},{1,9},{5... | collective-permute-start | bytes 393224 | tf_op jit(solution)/shard_map/ppermute | solution.py:270
  9.1 2.6 %collective-permute-start.8 = (bf16[256,256]{1,0:T(8,128)(2,1)S(1)}, bf16[256,256]{1,0:T(8,128)(2,1)S(1)}, u32[]{:S(2)}, u32[]{:S(2)}) collective-permute-start(bf16[256,256]{1,0:T(8,128)(2,1)S(1)} %get-tuple-element.43.refs_4_), channel_id=1, source_target_pairs={{0,16},{4,20},{8,24},{12,28},{16,0},{20,4},{24,8},{28,12},{1,17},{... | collective-permute-start | bytes 393224 | tf_op jit(solution)/shard_map/ppermute | solution.py:273
  11.7 1.6 %copy-done.2 = bf16[512,2048]{1,0:T(8,128)(2,1)S(1)} copy-done((bf16[512,2048]{1,0:T(8,128)(2,1)S(1)}, bf16[512,2048]{1,0:T(8,128)(2,1)}, u32[]{:S(2)}) %copy-start.2) | copy-done | bytes 2097176
  13.3 0.9 %copy-done.3 = bf16[256,512]{1,0:T(8,128)(2,1)S(1)} copy-done((bf16[256,512]{1,0:T(8,128)(2,1)S(1)}, bf16[256,512]{1,0:T(8,128)(2,1)}, u32[]{:S(2)}) %copy-start.3) | copy-done | bytes 262168
  14.3 0.9 %copy-done.4 = bf16[256,512]{1,0:T(8,128)(2,1)S(1)} copy-done((bf16[256,512]{1,0:T(8,128)(2,1)S(1)}, bf16[256,512]{1,0:T(8,128)(2,1)}, u32[]{:S(2)}) %copy-start.4) | copy-done | bytes 262168
  16.0 1.6 %collective-permute-done.7.refs_1_.refs_7_ = bf16[256,256]{1,0:T(8,128)(2,1)S(1)} collective-permute-done((bf16[256,256]{1,0:T(8,128)(2,1)S(1)}, bf16[256,256]{1,0:T(8,128)(2,1)S(1)}, u32[]{:S(2)}, u32[]{:S(2)}) %collective-permute-start.7) | collective-permute-done | bytes 131104 | tf_op jit(solution)/shard_map/ppermute | solution.py:270
  17.7 2.4 %collective-permute-start.9 = (bf16[3,256,256]{2,1,0:T(8,128)(2,1)S(1)}, bf16[3,256,256]{2,1,0:T(8,128)(2,1)S(1)}, u32[]{:S(2)}, u32[]{:S(2)}) collective-permute-start(bf16[3,256,256]{2,1,0:T(8,128)(2,1)S(1)} %shard_map.114), channel_id=1, source_target_pairs={{0,16},{4,20},{8,24},{12,28},{16,0},{20,4},{24,8},{28,12},{1,17},{... | collective-permute-start | bytes 1179656 | tf_op jit(solution)/shard_map/ppermute | solution.py:273
  21.1 2.6 %collective-permute-start.2 = (bf16[256,384]{1,0:T(8,128)(2,1)S(1)}, bf16[256,384]{1,0:T(8,128)(2,1)S(1)}, u32[]{:S(2)}, u32[]{:S(2)}) collective-permute-start(bf16[256,384]{1,0:T(8,128)(2,1)S(1)} %get-tuple-element.39), channel_id=1, source_target_pairs={{0,12},{4,8},{8,4},{12,0},{16,28},{20,24},{24,20},{28,16},{1,13},{... | collective-permute-start | bytes 589832 | tf_op jit(solution)/shard_map/ppermute | solution.py:270
  23.6 1.0 %collective-permute-start.4 = (bf16[256,384]{1,0:T(8,128)(2,1)S(1)}, bf16[256,384]{1,0:T(8,128)(2,1)S(1)}, u32[]{:S(2)}, u32[]{:S(2)}) collective-permute-start(bf16[256,384]{1,0:T(8,128)(2,1)S(1)} %get-tuple-element.41), channel_id=1, source_target_pairs={{0,4},{4,0},{8,12},{12,8},{16,20},{20,16},{24,28},{28,24},{1,5},{5... | collective-permute-start | bytes 589832 | tf_op jit(solution)/shard_map/ppermute | solution.py:270
  24.8 8.5 %collective-permute-done.2.refs_0_.refs_3_ = bf16[256,384]{1,0:T(8,128)(2,1)S(1)} collective-permute-done((bf16[256,384]{1,0:T(8,128)(2,1)S(1)}, bf16[256,384]{1,0:T(8,128)(2,1)S(1)}, u32[]{:S(2)}, u32[]{:S(2)}) %collective-permute-start.2) | collective-permute-done | bytes 196640 | tf_op jit(solution)/shard_map/ppermute | solution.py:270
  33.3 4.9 %collective-permute-done.3.refs_1_.refs_2_ = bf16[256,384]{1,0:T(8,128)(2,1)S(1)} collective-permute-done((bf16[256,384]{1,0:T(8,128)(2,1)S(1)}, bf16[256,384]{1,0:T(8,128)(2,1)S(1)}, u32[]{:S(2)}, u32[]{:S(2)}) %collective-permute-start.3) | collective-permute-done | bytes 196640 | tf_op jit(solution)/shard_map/ppermute | solution.py:270
  38.5 2.9 %shard_map.115 = (bf16[4,256,128]{2,1,0:T(8,128)(2,1)S(1)}, bf16[4,1024,256]{2,1,0:T(8,128)(2,1)S(1)}, f32[4,256,1024]{2,1,0:T(8,128)S(1)}) custom-call(s32[8,4]{1,0:T(8,128)S(1)} %copy.12.owner_ref, s32[8,4]{1,0:T(8,128)S(1)} %copy.13.block_ref, bf16[256,384]{1,0:T(8,128)(2,1)S(1)} %collective-permute-done.2.refs_0_.refs_3_, ...), custom_call_target="tpu_custom_call" | custom-call | flops 99999997952 | bytes 1 | tf_op jit(solution)/shard_map/pallas_call | solution.py:41
  41.5 1.9 %collective-permute-start.15 = (bf16[4,256,128]{2,1,0:T(8,128)(2,1)S(1)}, bf16[4,256,128]{2,1,0:T(8,128)(2,1)S(1)}, u32[]{:S(2)}, u32[]{:S(2)}) collective-permute-start(bf16[4,256,128]{2,1,0:T(8,128)(2,1)S(1)} %get-tuple-element.47.attn_ref.refs_3_), channel_id=1, source_target_pairs={{0,12},{4,8},{8,4},{12,0},{16,28},{20,24},{24,20},{28,16},{1,13},{... | collective-permute-start | bytes 786440 | tf_op jit(solution)/shard_map/ppermute | solution.py:270
  43.4 1.6 %collective-permute-start.16 = (bf16[4,256,128]{2,1,0:T(8,128)(2,1)S(1)}, bf16[4,256,128]{2,1,0:T(8,128)(2,1)S(1)}, u32[]{:S(2)}, u32[]{:S(2)}) collective-permute-start(bf16[4,256,128]{2,1,0:T(8,128)(2,1)S(1)} %get-tuple-element.47.attn_ref.refs_3_), channel_id=1, source_target_pairs={{0,4},{4,0},{8,12},{12,8},{16,20},{20,16},{24,28},{28,24},{1,5},{5... | collective-permute-start | bytes 786440 | tf_op jit(solution)/shard_map/ppermute | solution.py:270
  45.1 2.5 %shard_map.116 = (bf16[4,256,128]{2,1,0:T(8,128)(2,1)S(1)}, f32[4,256,256]{2,1,0:T(8,128)S(1)}, bf16[4,256,256]{2,1,0:T(8,128)(2,1)S(1)}, bf16[256,256]{1,0:T(8,128)(2,1)S(1)}) custom-call(bf16[4,256,128]{2,1,0:T(8,128)(2,1)S(1)} %get-tuple-element.47.attn_ref.refs_3_, bf16[4,1024,256]{2,1,0:T(8,128)(2,1)S(1)} %get-tuple-element.48.kvcat, ...), custom_call_target="tpu_custom_call" | custom-call | flops 99999997952 | bytes 1 | tf_op jit(solution)/shard_map/pallas_call | solution.py:41
  47.6 1.3 %collective-permute-start.10 = (bf16[256,256]{1,0:T(8,128)(2,1)S(1)}, bf16[256,256]{1,0:T(8,128)(2,1)S(1)}, u32[]{:S(2)}, u32[]{:S(2)}) collective-permute-start(bf16[256,256]{1,0:T(8,128)(2,1)S(1)} %get-tuple-element.53), channel_id=1, source_target_pairs={{16,0},{20,4},{24,8},{28,12},{17,1},{21,5},{25,9},{29,13},{18,2},{... | collective-permute-start | bytes 393224 | tf_op jit(solution)/shard_map/ppermute | solution.py:276
  48.9 1.8 %collective-permute-done.14.refs_0_ = bf16[4,256,128]{2,1,0:T(8,128)(2,1)S(1)} collective-permute-done((bf16[4,256,128]{2,1,0:T(8,128)(2,1)S(1)}, bf16[4,256,128]{2,1,0:T(8,128)(2,1)S(1)}, u32[]{:S(2)}, u32[]{:S(2)}) %collective-permute-start.14) | collective-permute-done | bytes 262176 | tf_op jit(solution)/shard_map/ppermute | solution.py:270
  50.7 2.0 %collective-permute-done.15.refs_1_ = bf16[4,256,128]{2,1,0:T(8,128)(2,1)S(1)} collective-permute-done((bf16[4,256,128]{2,1,0:T(8,128)(2,1)S(1)}, bf16[4,256,128]{2,1,0:T(8,128)(2,1)S(1)}, u32[]{:S(2)}, u32[]{:S(2)}) %collective-permute-start.15) | collective-permute-done | bytes 262176 | tf_op jit(solution)/shard_map/ppermute | solution.py:270
  52.7 1.9 %collective-permute-done.16.refs_2_ = bf16[4,256,128]{2,1,0:T(8,128)(2,1)S(1)} collective-permute-done((bf16[4,256,128]{2,1,0:T(8,128)(2,1)S(1)}, bf16[4,256,128]{2,1,0:T(8,128)(2,1)S(1)}, u32[]{:S(2)}, u32[]{:S(2)}) %collective-permute-start.16) | collective-permute-done | bytes 262176 | tf_op jit(solution)/shard_map/ppermute | solution.py:270
  54.7 1.6 %shard_map.120 = (f32[256,512]{1,0:T(8,128)S(1)}, f32[256,512]{1,0:T(8,128)S(1)}, bf16[256,1024]{1,0:T(8,128)(2,1)S(1)}, f32[256,512]{1,0:T(8,128)S(1)}, bf16[256,512]{1,0:T(8,128)(2,1)S(1)}) custom-call(bf16[4,256,128]{2,1,0:T(8,128)(2,1)S(1)} %collective-permute-done.14.refs_0_, bf16[4,256,128]{2,1,0:T(8,128)(2,1)S(1)} %collective-permute-done.15.refs_1_, ...), custom_call_target="tpu_custom_call" | custom-call | flops 1 | bytes 1 | tf_op jit(solution)/shard_map/pallas_call | solution.py:41
  56.4 2.2 %collective-permute-start.21 = (bf16[256,512]{1,0:T(8,128)(2,1)S(1)}, bf16[256,512]{1,0:T(8,128)(2,1)S(1)}, u32[]{:S(2)}, u32[]{:S(2)}) collective-permute-start(bf16[256,512]{1,0:T(8,128)(2,1)S(1)} %get-tuple-element.62), channel_id=1, source_target_pairs={{0,16},{4,20},{8,24},{12,28},{16,0},{20,4},{24,8},{28,12},{1,17},{... | collective-permute-start | bytes 786440 | tf_op jit(solution)/shard_map/ppermute | solution.py:273
  59.0 1.0 %collective-permute-start.11 = (bf16[256,384]{1,0:T(8,128)(2,1)S(1)}, bf16[256,384]{1,0:T(8,128)(2,1)S(1)}, u32[]{:S(2)}, u32[]{:S(2)}) collective-permute-start(bf16[256,384]{1,0:T(8,128)(2,1)S(1)} %get-tuple-element.54), channel_id=1, source_target_pairs={{0,12},{4,8},{8,4},{12,0},{16,28},{20,24},{24,20},{28,16},{1,13},{... | collective-permute-start | bytes 589832 | tf_op jit(solution)/shard_map/ppermute | solution.py:270
  60.0 1.2 %collective-permute-start.12 = (bf16[256,384]{1,0:T(8,128)(2,1)S(1)}, bf16[256,384]{1,0:T(8,128)(2,1)S(1)}, u32[]{:S(2)}, u32[]{:S(2)}) collective-permute-start(bf16[256,384]{1,0:T(8,128)(2,1)S(1)} %get-tuple-element.55), channel_id=1, source_target_pairs={{0,8},{4,12},{8,0},{12,4},{16,24},{20,28},{24,16},{28,20},{1,9},{5... | collective-permute-start | bytes 589832 | tf_op jit(solution)/shard_map/ppermute | solution.py:270
  61.2 1.4 %collective-permute-start.13 = (bf16[256,384]{1,0:T(8,128)(2,1)S(1)}, bf16[256,384]{1,0:T(8,128)(2,1)S(1)}, u32[]{:S(2)}, u32[]{:S(2)}) collective-permute-start(bf16[256,384]{1,0:T(8,128)(2,1)S(1)} %get-tuple-element.56), channel_id=1, source_target_pairs={{0,4},{4,0},{8,12},{12,8},{16,20},{20,16},{24,28},{28,24},{1,5},{5... | collective-permute-start | bytes 589832 | tf_op jit(solution)/shard_map/ppermute | solution.py:270
  62.6 1.6 %collective-permute-start.20 = (bf16[256,512]{1,0:T(8,128)(2,1)S(1)}, bf16[256,512]{1,0:T(8,128)(2,1)S(1)}, u32[]{:S(2)}, u32[]{:S(2)}) collective-permute-start(bf16[256,512]{1,0:T(8,128)(2,1)S(1)} %add_convert_fusion), channel_id=1, source_target_pairs={{0,2},{1,3},{2,0},{3,1},{4,6},{5,7},{6,4},{7,5},{8,10},{9,11},{10,... | collective-permute-start | bytes 786440 | tf_op jit(solution)/shard_map/ppermute | solution.py:279
  64.3 9.0 %collective-permute-done.11.refs_2_.refs_0_ = bf16[256,384]{1,0:T(8,128)(2,1)S(1)} collective-permute-done((bf16[256,384]{1,0:T(8,128)(2,1)S(1)}, bf16[256,384]{1,0:T(8,128)(2,1)S(1)}, u32[]{:S(2)}, u32[]{:S(2)}) %collective-permute-start.11) | collective-permute-done | bytes 196640 | tf_op jit(solution)/shard_map/ppermute | solution.py:270
  73.3 1.6 %collective-permute-done.12.refs_1_ = bf16[256,384]{1,0:T(8,128)(2,1)S(1)} collective-permute-done((bf16[256,384]{1,0:T(8,128)(2,1)S(1)}, bf16[256,384]{1,0:T(8,128)(2,1)S(1)}, u32[]{:S(2)}, u32[]{:S(2)}) %collective-permute-start.12) | collective-permute-done | bytes 196640 | tf_op jit(solution)/shard_map/ppermute | solution.py:270
  74.9 1.4 %shard_map.122 = (bf16[256,512]{1,0:T(8,128)(2,1)}, bf16[256,512]{1,0:T(8,128)(2,1)}, bf16[256,512]{1,0:T(8,128)(2,1)}, bf16[256,512]{1,0:T(8,128)(2,1)}, f32[256,512]{1,0:T(8,128)}) custom-call(bf16[256,384]{1,0:T(8,128)(2,1)S(1)} %collective-permute-done.11.refs_2_.refs_0_, bf16[256,384]{1,0:T(8,128)(2,1)S(1)} %collective-permute-done.12.refs_1_, ...), custom_call_target="tpu_custom_call" | custom-call | flops 1 | bytes 1 | tf_op jit(solution)/shard_map/pallas_call | solution.py:41
  (47 shorter events, 3.5 us)
Async XLA Ops:
  0.6 1.0 %copy-start.5 = (bf16[256,512]{1,0:T(8,128)(2,1)S(1)}, bf16[256,512]{1,0:T(8,128)(2,1)}, u32[]{:S(2)}) copy-start(bf16[256,512]{1,0:T(8,128)(2,1)} %k_ref.1) | copy-start | bytes 786436
  1.6 0.9 %copy-start.6 = (bf16[256,512]{1,0:T(8,128)(2,1)S(1)}, bf16[256,512]{1,0:T(8,128)(2,1)}, u32[]{:S(2)}) copy-start(bf16[256,512]{1,0:T(8,128)(2,1)} %v_ref.1) | copy-start | bytes 786436
  2.6 12.8 %collective-permute-start = (bf16[256,512]{1,0:T(8,128)(2,1)}, bf16[256,512]{1,0:T(8,128)(2,1)S(1)}, u32[]{:S(2)}, u32[]{:S(2)}) collective-permute-start(bf16[256,512]{1,0:T(8,128)(2,1)} %refs_2_), channel_id=1, source_target_pairs={{0,2},{1,3},{2,0},{3,1},{4,6},{5,7},{6,4},{7,5},{8,10},{9,11},{10,... | collective-permute-start | bytes 786440 | tf_op jit(solution)/shard_map/ppermute | solution.py:279
  5.6 9.9 %collective-permute-start.5 = (bf16[256,256]{1,0:T(8,128)(2,1)S(1)}, bf16[256,256]{1,0:T(8,128)(2,1)S(1)}, u32[]{:S(2)}, u32[]{:S(2)}) collective-permute-start(bf16[256,256]{1,0:T(8,128)(2,1)S(1)} %get-tuple-element.44), channel_id=1, source_target_pairs={{0,4},{4,0},{8,12},{12,8},{16,20},{20,16},{24,28},{28,24},{1,5},{5... | collective-permute-start | bytes 393224 | tf_op jit(solution)/shard_map/ppermute | solution.py:270
  7.2 8.9 %collective-permute-start.6 = (bf16[256,256]{1,0:T(8,128)(2,1)S(1)}, bf16[256,256]{1,0:T(8,128)(2,1)S(1)}, u32[]{:S(2)}, u32[]{:S(2)}) collective-permute-start(bf16[256,256]{1,0:T(8,128)(2,1)S(1)} %get-tuple-element.45), channel_id=1, source_target_pairs={{0,8},{4,12},{8,0},{12,4},{16,24},{20,28},{24,16},{28,20},{1,9},{5... | collective-permute-start | bytes 393224 | tf_op jit(solution)/shard_map/ppermute | solution.py:270
  8.7 9.0 %collective-permute-start.7 = (bf16[256,256]{1,0:T(8,128)(2,1)S(1)}, bf16[256,256]{1,0:T(8,128)(2,1)S(1)}, u32[]{:S(2)}, u32[]{:S(2)}) collective-permute-start(bf16[256,256]{1,0:T(8,128)(2,1)S(1)} %get-tuple-element.46), channel_id=1, source_target_pairs={{0,12},{4,8},{8,4},{12,0},{16,28},{20,24},{24,20},{28,16},{1,13},{... | collective-permute-start | bytes 393224 | tf_op jit(solution)/shard_map/ppermute | solution.py:270
  9.1 8.6 %collective-permute-start.8 = (bf16[256,256]{1,0:T(8,128)(2,1)S(1)}, bf16[256,256]{1,0:T(8,128)(2,1)S(1)}, u32[]{:S(2)}, u32[]{:S(2)}) collective-permute-start(bf16[256,256]{1,0:T(8,128)(2,1)S(1)} %get-tuple-element.43.refs_4_), channel_id=1, source_target_pairs={{0,16},{4,20},{8,24},{12,28},{16,0},{20,4},{24,8},{28,12},{1,17},{... | collective-permute-start | bytes 393224 | tf_op jit(solution)/shard_map/ppermute | solution.py:273
  11.7 1.6 %copy-start.2 = (bf16[512,2048]{1,0:T(8,128)(2,1)S(1)}, bf16[512,2048]{1,0:T(8,128)(2,1)}, u32[]{:S(2)}) copy-start(bf16[512,2048]{1,0:T(8,128)(2,1)} %refs_0_.1) | copy-start | bytes 6291460
  13.3 0.9 %copy-start.3 = (bf16[256,512]{1,0:T(8,128)(2,1)S(1)}, bf16[256,512]{1,0:T(8,128)(2,1)}, u32[]{:S(2)}) copy-start(bf16[256,512]{1,0:T(8,128)(2,1)} %refs_1_.1) | copy-start | bytes 786436
  14.3 0.9 %copy-start.4 = (bf16[256,512]{1,0:T(8,128)(2,1)S(1)}, bf16[256,512]{1,0:T(8,128)(2,1)}, u32[]{:S(2)}) copy-start(bf16[256,512]{1,0:T(8,128)(2,1)} %refs_2_) | copy-start | bytes 786436
  15.4 4.8 %copy-start = (bf16[512,2048]{1,0:T(8,128)(2,1)}, bf16[512,2048]{1,0:T(8,128)(2,1)S(1)}, u32[]{:S(2)}) copy-start(bf16[512,2048]{1,0:T(8,128)(2,1)S(1)} %get-tuple-element.37.refs_2_.refs_4_.refs_6_) | copy-start | bytes 6291460
  15.4 4.7 %collective-permute-start.1 = (bf16[2,256,512]{2,1,0:T(8,128)(2,1)S(1)}, bf16[2,256,512]{2,1,0:T(8,128)(2,1)S(1)}, u32[]{:S(2)}, u32[]{:S(2)}) collective-permute-start(bf16[2,256,512]{2,1,0:T(8,128)(2,1)S(1)} %shard_map.112.refs_0_), channel_id=1, source_target_pairs={{0,1},{1,0},{2,3},{3,2},{4,5},{5,4},{6,7},{7,6},{8,9},{9,8},{10,11... | collective-permute-start | bytes 1572872 | tf_op jit(solution)/shard_map/ppermute | solution.py:279
  17.7 6.9 %copy-start.7 = (s32[8,4]{0,1:T(4,128)S(1)}, s32[8,4]{0,1:T(4,128)}, u32[]{:S(2)}) copy-start(s32[8,4]{0,1:T(4,128)} %param.12) | copy-start | bytes 388
  17.7 7.0 %copy-start.8 = (s32[8,4]{0,1:T(4,128)S(1)}, s32[8,4]{0,1:T(4,128)}, u32[]{:S(2)}) copy-start(s32[8,4]{0,1:T(4,128)} %param.13) | copy-start | bytes 388
  17.7 20.8 %collective-permute-start.9 = (bf16[3,256,256]{2,1,0:T(8,128)(2,1)S(1)}, bf16[3,256,256]{2,1,0:T(8,128)(2,1)S(1)}, u32[]{:S(2)}, u32[]{:S(2)}) collective-permute-start(bf16[3,256,256]{2,1,0:T(8,128)(2,1)S(1)} %shard_map.114), channel_id=1, source_target_pairs={{0,16},{4,20},{8,24},{12,28},{16,0},{20,4},{24,8},{28,12},{1,17},{... | collective-permute-start | bytes 1179656 | tf_op jit(solution)/shard_map/ppermute | solution.py:273
  21.1 12.2 %collective-permute-start.2 = (bf16[256,384]{1,0:T(8,128)(2,1)S(1)}, bf16[256,384]{1,0:T(8,128)(2,1)S(1)}, u32[]{:S(2)}, u32[]{:S(2)}) collective-permute-start(bf16[256,384]{1,0:T(8,128)(2,1)S(1)} %get-tuple-element.39), channel_id=1, source_target_pairs={{0,12},{4,8},{8,4},{12,0},{16,28},{20,24},{24,20},{28,16},{1,13},{... | collective-permute-start | bytes 589832 | tf_op jit(solution)/shard_map/ppermute | solution.py:270
  23.6 14.6 %collective-permute-start.3 = (bf16[256,384]{1,0:T(8,128)(2,1)S(1)}, bf16[256,384]{1,0:T(8,128)(2,1)S(1)}, u32[]{:S(2)}, u32[]{:S(2)}) collective-permute-start(bf16[256,384]{1,0:T(8,128)(2,1)S(1)} %get-tuple-element.40), channel_id=1, source_target_pairs={{0,8},{4,12},{8,0},{12,4},{16,24},{20,28},{24,16},{28,20},{1,9},{5... | collective-permute-start | bytes 589832 | tf_op jit(solution)/shard_map/ppermute | solution.py:270
  23.6 14.6 %collective-permute-start.4 = (bf16[256,384]{1,0:T(8,128)(2,1)S(1)}, bf16[256,384]{1,0:T(8,128)(2,1)S(1)}, u32[]{:S(2)}, u32[]{:S(2)}) collective-permute-start(bf16[256,384]{1,0:T(8,128)(2,1)S(1)} %get-tuple-element.41), channel_id=1, source_target_pairs={{0,4},{4,0},{8,12},{12,8},{16,20},{20,16},{24,28},{28,24},{1,5},{5... | collective-permute-start | bytes 589832 | tf_op jit(solution)/shard_map/ppermute | solution.py:270
  38.3 6.7 %collective-permute-start.17 = (bf16[4,256,128]{2,1,0:T(8,128)(2,1)S(1)}, bf16[4,256,128]{2,1,0:T(8,128)(2,1)S(1)}, u32[]{:S(2)}, u32[]{:S(2)}) collective-permute-start(bf16[4,256,128]{2,1,0:T(8,128)(2,1)S(1)} %shard_map.118.refs_0_), channel_id=1, source_target_pairs={{0,2},{1,3},{2,0},{3,1},{4,6},{5,7},{6,4},{7,5},{8,10},{9,11},{10,... | collective-permute-start | bytes 786440 | tf_op jit(solution)/shard_map/ppermute | solution.py:279
  41.4 9.3 %collective-permute-start.14 = (bf16[4,256,128]{2,1,0:T(8,128)(2,1)S(1)}, bf16[4,256,128]{2,1,0:T(8,128)(2,1)S(1)}, u32[]{:S(2)}, u32[]{:S(2)}) collective-permute-start(bf16[4,256,128]{2,1,0:T(8,128)(2,1)S(1)} %get-tuple-element.47.attn_ref.refs_3_), channel_id=1, source_target_pairs={{0,8},{4,12},{8,0},{12,4},{16,24},{20,28},{24,16},{28,20},{1,9},{5... | collective-permute-start | bytes 786440 | tf_op jit(solution)/shard_map/ppermute | solution.py:270
  41.5 11.2 %collective-permute-start.15 = (bf16[4,256,128]{2,1,0:T(8,128)(2,1)S(1)}, bf16[4,256,128]{2,1,0:T(8,128)(2,1)S(1)}, u32[]{:S(2)}, u32[]{:S(2)}) collective-permute-start(bf16[4,256,128]{2,1,0:T(8,128)(2,1)S(1)} %get-tuple-element.47.attn_ref.refs_3_), channel_id=1, source_target_pairs={{0,12},{4,8},{8,4},{12,0},{16,28},{20,24},{24,20},{28,16},{1,13},{... | collective-permute-start | bytes 786440 | tf_op jit(solution)/shard_map/ppermute | solution.py:270
  43.4 11.3 %collective-permute-start.16 = (bf16[4,256,128]{2,1,0:T(8,128)(2,1)S(1)}, bf16[4,256,128]{2,1,0:T(8,128)(2,1)S(1)}, u32[]{:S(2)}, u32[]{:S(2)}) collective-permute-start(bf16[4,256,128]{2,1,0:T(8,128)(2,1)S(1)} %get-tuple-element.47.attn_ref.refs_3_), channel_id=1, source_target_pairs={{0,4},{4,0},{8,12},{12,8},{16,20},{20,16},{24,28},{28,24},{1,5},{5... | collective-permute-start | bytes 786440 | tf_op jit(solution)/shard_map/ppermute | solution.py:270
  45.0 9.7 %collective-permute-start.18 = (bf16[2,4,256,128]{3,2,1,0:T(8,128)(2,1)S(1)}, bf16[2,4,256,128]{3,2,1,0:T(8,128)(2,1)S(1)}, u32[]{:S(2)}, u32[]{:S(2)}) collective-permute-start(bf16[2,4,256,128]{3,2,1,0:T(8,128)(2,1)S(1)} %shard_map.119.refs_4_), channel_id=1, source_target_pairs={{0,1},{1,0},{2,3},{3,2},{4,5},{5,4},{6,7},{7,6},{8,9},{9,8},{10,11... | collective-permute-start | bytes 1572872 | tf_op jit(solution)/shard_map/ppermute | solution.py:279
  45.1 9.6 %copy-start.1 = (bf16[512,2048]{1,0:T(8,128)(2,1)S(1)}, bf16[512,2048]{1,0:T(8,128)(2,1)}, u32[]{:S(2)}) copy-start(bf16[512,2048]{1,0:T(8,128)(2,1)} %copy-done) | copy-start | bytes 6291460
  47.6 11.3 %collective-permute-start.10 = (bf16[256,256]{1,0:T(8,128)(2,1)S(1)}, bf16[256,256]{1,0:T(8,128)(2,1)S(1)}, u32[]{:S(2)}, u32[]{:S(2)}) collective-permute-start(bf16[256,256]{1,0:T(8,128)(2,1)S(1)} %get-tuple-element.53), channel_id=1, source_target_pairs={{16,0},{20,4},{24,8},{28,12},{17,1},{21,5},{25,9},{29,13},{18,2},{... | collective-permute-start | bytes 393224 | tf_op jit(solution)/shard_map/ppermute | solution.py:276
  56.3 6.2 %collective-permute-start.19 = (bf16[256,1024]{1,0:T(8,128)(2,1)S(1)}, bf16[256,1024]{1,0:T(8,128)(2,1)S(1)}, u32[]{:S(2)}, u32[]{:S(2)}) collective-permute-start(bf16[256,1024]{1,0:T(8,128)(2,1)S(1)} %get-tuple-element.59), channel_id=1, source_target_pairs={{0,1},{1,0},{2,3},{3,2},{4,5},{5,4},{6,7},{7,6},{8,9},{9,8},{10,11... | collective-permute-start | bytes 1572872 | tf_op jit(solution)/shard_map/ppermute | solution.py:279
  56.4 18.5 %collective-permute-start.21 = (bf16[256,512]{1,0:T(8,128)(2,1)S(1)}, bf16[256,512]{1,0:T(8,128)(2,1)S(1)}, u32[]{:S(2)}, u32[]{:S(2)}) collective-permute-start(bf16[256,512]{1,0:T(8,128)(2,1)S(1)} %get-tuple-element.62), channel_id=1, source_target_pairs={{0,16},{4,20},{8,24},{12,28},{16,0},{20,4},{24,8},{28,12},{1,17},{... | collective-permute-start | bytes 786440 | tf_op jit(solution)/shard_map/ppermute | solution.py:273
  59.0 14.3 %collective-permute-start.11 = (bf16[256,384]{1,0:T(8,128)(2,1)S(1)}, bf16[256,384]{1,0:T(8,128)(2,1)S(1)}, u32[]{:S(2)}, u32[]{:S(2)}) collective-permute-start(bf16[256,384]{1,0:T(8,128)(2,1)S(1)} %get-tuple-element.54), channel_id=1, source_target_pairs={{0,12},{4,8},{8,4},{12,0},{16,28},{20,24},{24,20},{28,16},{1,13},{... | collective-permute-start | bytes 589832 | tf_op jit(solution)/shard_map/ppermute | solution.py:270
  60.0 14.9 %collective-permute-start.12 = (bf16[256,384]{1,0:T(8,128)(2,1)S(1)}, bf16[256,384]{1,0:T(8,128)(2,1)S(1)}, u32[]{:S(2)}, u32[]{:S(2)}) collective-permute-start(bf16[256,384]{1,0:T(8,128)(2,1)S(1)} %get-tuple-element.55), channel_id=1, source_target_pairs={{0,8},{4,12},{8,0},{12,4},{16,24},{20,28},{24,16},{28,20},{1,9},{5... | collective-permute-start | bytes 589832 | tf_op jit(solution)/shard_map/ppermute | solution.py:270
  61.2 13.7 %collective-permute-start.13 = (bf16[256,384]{1,0:T(8,128)(2,1)S(1)}, bf16[256,384]{1,0:T(8,128)(2,1)S(1)}, u32[]{:S(2)}, u32[]{:S(2)}) collective-permute-start(bf16[256,384]{1,0:T(8,128)(2,1)S(1)} %get-tuple-element.56), channel_id=1, source_target_pairs={{0,4},{4,0},{8,12},{12,8},{16,20},{20,16},{24,28},{28,24},{1,5},{5... | collective-permute-start | bytes 589832 | tf_op jit(solution)/shard_map/ppermute | solution.py:270
  62.6 12.3 %collective-permute-start.20 = (bf16[256,512]{1,0:T(8,128)(2,1)S(1)}, bf16[256,512]{1,0:T(8,128)(2,1)S(1)}, u32[]{:S(2)}, u32[]{:S(2)}) collective-permute-start(bf16[256,512]{1,0:T(8,128)(2,1)S(1)} %add_convert_fusion), channel_id=1, source_target_pairs={{0,2},{1,3},{2,0},{3,1},{4,6},{5,7},{6,4},{7,5},{8,10},{9,11},{10,... | collective-permute-start | bytes 786440 | tf_op jit(solution)/shard_map/ppermute | solution.py:279
